TPU v7x, 512 devices: a whole 4x4x16 slice. The times are simulated.
512 devices in a mesh: batch: 16 (over y, z_hi), space: 32 (over x, z_lo, core).
Axes of the slice: x: 4, y: 4, z: 16 (z_hi: 4, z_lo: 4; z = z_hi * 4 + z_lo), core: 2. Of those that a mesh axis runs over, the one named last changes fastest.
Arguments:
- latent: bfloat16 [65536, 640], P(('batch', 'space')), parts along dimension 0, may hold values from -8 to 8
- timestep: int32 [16], P('batch'), parts along dimension 0, may hold values from 0 to 999
- norm1_gain: float32 [640], replicated, may hold values from 0.25 to 1.75
- norm1_shift: float32 [640], replicated, may hold values from -3 to 3
- conv_weight: bfloat16 [5760, 640], P('space'), may hold values from -0.078125 to 0.078125
- conv_bias: float32 [640], replicated, may hold values from -3 to 3
- time_weight: float32 [320, 640], replicated, may hold values from -0.5 to 0.5
- norm2_gain: float32 [640], replicated, may hold values from 0.25 to 1.75
- norm2_shift: float32 [640], replicated, may hold values from -3 to 3
- qkv_weight: bfloat16 [640, 960], replicated, may hold values from -0.25 to 0.25
- out_weight: bfloat16 [320, 640], replicated, may hold values from -0.3125 to 0.3125
- stale_kv: bfloat16 [2, 65536, 320], P(None, ('batch', 'space')), parts along dimension 1, may hold values from -6 to 6
Outputs:
- result: bfloat16 [65536, 640], P(('batch', 'space')), parts along dimension 0
- fresh_kv: bfloat16 [2, 65536, 320], P(None, ('batch', 'space')), parts along dimension 1
There are 16 independent parts, one for each index of `batch`. A program takes and returns all parts, laid end to end along the dimension named above; an argument that names none is the same for every part. Nothing has to cross between parts.
All inputs are finite; a program needn't handle non-finite values.
Results may differ from a plain program's by a relative error of at most 0.015.
Values may be sent and summed in bfloat16 or wider, within the bound.
No kernel may reach another device: no remote copies, remote signals or barrier semaphores. Data moves between devices by JAX's collectives and lax.ppermute only.
A program may use at most 64 MiB of HBM per device.

v0:
```python
import math

import jax
import jax.numpy as jnp
from jax import lax
from jax.sharding import PartitionSpec as P

GROUPS = 32
HEADS = 5
HEAD_DIM = 64
TFREQ = 320
GW = 128


def with_halo(value, sides, width):
    for axis, dim in sides:
        peers, length = (lax.axis_size(axis), value.shape[dim])
        up = [(i, (i + 1) % peers) for i in range(peers - 1)]
        down = [(j, i) for i, j in up]
        last = lax.slice_in_dim(value, length - width, length, axis=dim)
        first = lax.slice_in_dim(value, 0, width, axis=dim)
        before = lax.ppermute(last, axis, up)
        after = lax.ppermute(first, axis, down)
        value = jnp.concatenate([before, value, after], axis=dim)
    return value


def group_norm(values, gain, shift, eps):
    count, width = values.shape
    grouped = values.reshape(count, GROUPS, width // GROUPS)
    number = count * lax.axis_size("space") * (width // GROUPS)
    total = lax.psum(jnp.sum(grouped, axis=(0, 2)), "space")
    mean = total / number
    centered = grouped - mean[None, :, None]
    var = lax.psum(jnp.sum(centered * centered, axis=(0, 2)), "space") / number
    scaled = centered * lax.rsqrt(var + eps)[None, :, None]
    return scaled.reshape(count, width) * gain + shift


def time_embed(timestep, time_weight):
    half = TFREQ // 2
    index = jnp.arange(half, dtype=jnp.float32)
    freq = jnp.exp(-math.log(10000.0) * index / half)
    angle = timestep.astype(jnp.float32)[0] * freq
    feats = jnp.concatenate([jnp.cos(angle), jnp.sin(angle)])[None, :]
    return jnp.dot(feats, time_weight, precision=lax.Precision.HIGHEST)


def on_device(
    latent,
    timestep,
    norm1_gain,
    norm1_shift,
    conv_weight,
    conv_bias,
    time_weight,
    norm2_gain,
    norm2_shift,
    qkv_weight,
    out_weight,
    stale_kv,
):
    tok_dev, width = latent.shape
    row_count = tok_dev // GW
    base = latent.astype(jnp.float32)
    normed = jax.nn.silu(group_norm(base, norm1_gain, norm1_shift, 1e-05)).astype(jnp.bfloat16)
    normed = normed.reshape(row_count, GW, width)
    edged = with_halo(normed, (("space", 0),), 1)
    padded = jnp.pad(edged, ((0, 0), (1, 1), (0, 0)))
    windows = []
    for tap in range(9):
        down, across = (tap // 3, tap % 3)
        windows.append(
            padded[down : down + row_count, across : across + GW].reshape(tok_dev, width)
        )
    unfolded = jnp.concatenate(windows, axis=1)
    conv = jnp.dot(
        unfolded,
        lax.all_gather(conv_weight, "space", axis=0, tiled=True),
        preferred_element_type=jnp.float32,
    )
    mid = (base + conv + conv_bias + time_embed(timestep, time_weight)).astype(jnp.bfloat16)
    normed2 = group_norm(mid.astype(jnp.float32), norm2_gain, norm2_shift, 1e-06).astype(
        jnp.bfloat16
    )
    qkv = jnp.dot(normed2, qkv_weight, preferred_element_type=jnp.float32).astype(jnp.bfloat16)
    feats = qkv.shape[1] // 3
    query, key, value = (qkv[:, :feats], qkv[:, feats : 2 * feats], qkv[:, 2 * feats :])
    fresh_kv = jnp.stack([key, value])
    queries = query.reshape(tok_dev, HEADS, HEAD_DIM)
    scale = 1.0 / math.sqrt(HEAD_DIM)
    scores = (
        jnp.einsum(
            "qhd,khd->hqk",
            queries,
            key.reshape(tok_dev, HEADS, HEAD_DIM),
            preferred_element_type=jnp.float32,
        )
        * scale
    )
    peak = jnp.max(scores, axis=-1)
    expo = jnp.exp(scores - peak[:, :, None])
    total = jnp.sum(expo, axis=-1)
    mixed = jnp.einsum(
        "hqk,khd->hqd",
        expo.astype(jnp.bfloat16),
        value.reshape(tok_dev, HEADS, HEAD_DIM),
        preferred_element_type=jnp.float32,
    )
    own_start = lax.axis_index("space") * tok_dev
    keys = lax.all_gather(stale_kv[0], "space", axis=0, tiled=True)
    values = lax.all_gather(stale_kv[1], "space", axis=0, tiled=True)
    length = keys.shape[0]
    block = (
        jnp.einsum(
            "qhd,khd->hqk",
            queries,
            keys.reshape(length, HEADS, HEAD_DIM),
            preferred_element_type=jnp.float32,
        )
        * scale
    )
    position = jnp.arange(length, dtype=jnp.int32)
    keep = (position < own_start) | (position >= own_start + tok_dev)
    block = jnp.where(keep[None, None, :], block, -jnp.inf)
    peak_next = jnp.maximum(peak, jnp.max(block, axis=-1))
    factor = jnp.exp(peak - peak_next)
    weights = jnp.exp(block - peak_next[:, :, None])
    total_next = total * factor + jnp.sum(weights, axis=-1)
    mixed_next = mixed * factor[:, :, None] + jnp.einsum(
        "hqk,khd->hqd",
        weights.astype(jnp.bfloat16),
        values.reshape(length, HEADS, HEAD_DIM),
        preferred_element_type=jnp.float32,
    )
    attended = (
        (mixed_next / total_next[:, :, None])
        .transpose(1, 0, 2)
        .reshape(tok_dev, feats)
        .astype(jnp.bfloat16)
    )
    result = (
        mid.astype(jnp.float32) + jnp.dot(attended, out_weight, preferred_element_type=jnp.float32)
    ).astype(jnp.bfloat16)
    return (result, fresh_kv)


def solution(mesh):
    return jax.shard_map(
        on_device,
        mesh=mesh,
        in_specs=(
            P(("batch", "space"), None),
            P("batch"),
            P(),
            P(),
            P("space", None),
            P(),
            P(),
            P(),
            P(),
            P(),
            P(),
            P(None, ("batch", "space"), None),
        ),
        out_specs=(P(("batch", "space"), None), P(None, ("batch", "space"), None)),
        check_vma=False,
    )
```

profile of v0, /device:TPU:1, one launch (start us, length us, event | category | flops | bytes accessed | tf_op | source)
XLA Modules:
  0.0 341.4 jit_solution(892937285037293991)
XLA Ops:
  7.3 0.7 all-gather.11.cloned.1.call-update
  8.0 1.6 fusion.57
  9.7 1.0 convert_reduce_fusion
  10.7 0.1 reduce_sum.69
  10.8 74.5 %psum.28 = f32[32]{0:T(128)S(1)} all-reduce(f32[32]{0:T(128)S(1)} %reduce_sum.69), channel_id=1, replica_groups=mesh['batch'=16,'space'=32] {'space'}, use_global_device_ids=true, to_apply=%region_2.0 | all-reduce | flops 32 | bytes 256 | tf_op jit(solution)/shard_map/psum | solution.py:32
  85.5 1.0 fusion.26
  86.6 0.1 reduce_sum.75
  86.7 68.8 %psum.29 = f32[32]{0:T(128)S(1)} all-reduce(f32[32]{0:T(128)S(1)} %reduce_sum.75), channel_id=1, replica_groups=mesh['batch'=16,'space'=32] {'space'}, use_global_device_ids=true, to_apply=%region_5.6 | all-reduce | flops 32 | bytes 256 | tf_op jit(solution)/shard_map/psum | solution.py:35
  155.6 0.1 mul.96
  155.7 1.1 fusion.55
  156.8 1.9 collective-permute-start
  158.7 2.4 collective-permute-start.1
  161.9 1.7 convolution_reduce_fusion
  163.6 1.7 collective-permute-done.1
  165.3 0.1 fusion.23
  165.6 0.1 constant_dynamic-update-slice_fusion
  166.0 8.8 %reshape.125 = bf16[5760,640]{1,0:T(8,128)(2,1)} reshape(bf16[32,180,640]{2,1,0:T(8,128)(2,1)} %all-gather.11.cloned.1.call-done) | data formatting | bytes 14745600
  174.8 4.5 %fusion.58 = (f32[640]{0:T(1024)S(1)}, f32[128,640]{1,0:T(8,128)S(1)}) fusion(f32[640]{0:T(1024)S(1)} %convolution_reduce_fusion, f32[640]{0:T(1024)S(1)} %copy-done.6, bf16[128,5760]{1,0:T(8,128)(2,1)S(1)} %fusion.38, bf16[5760,640]{1,0:T(8,128)(2,1)} %reshape.125, bf16[128,640]{1,0:T(8,128)(2,1)S(1)} %copy-done.2), kind=kOutput, calls=%fused_computation.91 | convolution fusion | flops 944291200 | bytes 9346560 | tf_op jit(solution)/shard_map/dot_general | solution.py:77
  179.4 0.1 reduce_sum.94
  179.5 65.0 %psum.30 = f32[32]{0:T(128)S(1)} all-reduce(f32[32]{0:T(128)S(1)} %reduce_sum.94), channel_id=1, replica_groups=mesh['batch'=16,'space'=32] {'space'}, use_global_device_ids=true, to_apply=%region_8.9 | all-reduce | flops 32 | bytes 256 | tf_op jit(solution)/shard_map/psum | solution.py:32
  244.8 0.1 reduce_sum.97
  244.9 70.2 %psum.31 = f32[32]{0:T(128)S(1)} all-reduce(f32[32]{0:T(128)S(1)} %reduce_sum.97), channel_id=1, replica_groups=mesh['batch'=16,'space'=32] {'space'}, use_global_device_ids=true, to_apply=%region_11.12 | all-reduce | flops 32 | bytes 256 | tf_op jit(solution)/shard_map/psum | solution.py:35
  315.2 0.1 mul.106
  315.3 0.5 convolution_convert_fusion
  315.9 0.3 fusion.59
  316.2 3.4 fusion
  319.7 3.9 %copy-done.1 = f32[5,128,4096]{2,1,0:T(8,128)} copy-done((f32[5,128,4096]{2,1,0:T(8,128)}, f32[5,128,4096]{2,1,0:T(8,128)S(1)}, u32[]{:S(2)}) %copy-start.1) | copy-done | bytes 10485784
  323.6 2.3 fusion.1
  325.9 7.1 %fusion.14 = f32[128,5,64]{0,2,1:T(8,128)S(1)} fusion(bf16[4096,5,64]{0,2,1:T(8,128)(2,1)} %bitcast.86, f32[5,128,4096]{2,1,0:T(8,128)} %copy-done.1, f32[5,128]{1,0:T(8,128)S(1)} %max.18, pred[4096]{0:T(1024)(128)(4,1)S(1)} %fusion.49), kind=kOutput, calls=%fused_computation.22 | convolution fusion | flops 346030080 | bytes 13277696 | tf_op jit(solution)/shard_map/hqk,khd->hqd/dot_general | solution.py:130
  333.0 0.7 pad_maximum_fusion
  333.7 0.2 fusion.17
  333.9 1.0 fusion.8
  (57 shorter events, 1.7 us)
Async XLA Ops:
  7.2 308.1 %copy-start = (bf16[640,960]{0,1:T(8,128)(2,1)S(1)}, bf16[640,960]{0,1:T(8,128)(2,1)}, u32[]{:S(2)}) copy-start(bf16[640,960]{0,1:T(8,128)(2,1)} %param.21) | copy-start | bytes 3686404
  7.2 158.4 %copy-start.2 = (bf16[128,640]{1,0:T(8,128)(2,1)S(1)}, bf16[128,640]{1,0:T(8,128)(2,1)}, u32[]{:S(2)}) copy-start(bf16[128,640]{1,0:T(8,128)(2,1)} %param.12) | copy-start | bytes 491524
  7.2 158.4 %copy-start.5 = (f32[640]{0:T(1024)S(1)}, f32[640]{0:T(1024)}, u32[]{:S(2)}) copy-start(f32[640]{0:T(1024)} %param.14) | copy-start | bytes 7684
  7.2 158.4 %copy-start.4 = (f32[640]{0:T(1024)S(1)}, f32[640]{0:T(1024)}, u32[]{:S(2)}) copy-start(f32[640]{0:T(1024)} %param.15) | copy-start | bytes 7684
  7.2 158.8 %all-gather.11.cloned.1.call-start = ((), (), s32[]{:S(2)}) async-start(), calls=%async_computation.2 | async-start | bytes 7772160 | tf_op jit(solution)/shard_map/all_gather | solution.py:79
  7.9 308.2 %all-gather.7.cloned.1.call-start = ((), (), s32[]{:S(2)}) async-start(), calls=%async_computation | async-start | bytes 2703360 | tf_op jit(solution)/shard_map/all_gather | solution.py:111
  9.6 316.3 %all-gather.9.cloned.1.call-start = ((), (), s32[]{:S(2)}) async-start(), calls=%async_computation.1 | async-start | bytes 2703360 | tf_op jit(solution)/shard_map/all_gather | solution.py:112
  156.8 6.8 %collective-permute-start = (bf16[1,128,640]{2,1,0:T(8,128)(2,1)S(1)}, bf16[1,128,640]{2,1,0:T(8,128)(2,1)S(1)}, u32[]{:S(2)}, u32[]{:S(2)}) collective-permute-start(bf16[1,128,640]{2,1,0:T(8,128)(2,1)S(1)} %fusion.55), channel_id=1, source_target_pairs={{0,1},{1,2},{2,3},{3,4},{4,5},{5,6},{6,7},{7,8},{8,9},{9,10},{10,1... | collective-permute-start | bytes 491528 | tf_op jit(solution)/shard_map/ppermute | solution.py:22
  158.7 6.6 %collective-permute-start.1 = (bf16[1,128,640]{2,1,0:T(8,128)(2,1)S(1)}, bf16[1,128,640]{2,1,0:T(8,128)(2,1)S(1)}, u32[]{:S(2)}, u32[]{:S(2)}) collective-permute-start(bf16[1,128,640]{2,1,0:T(8,128)(2,1)S(1)} %fusion.55), channel_id=1, source_target_pairs={{1,0},{2,1},{3,2},{4,3},{5,4},{6,5},{7,6},{8,7},{9,8},{10,9},{11,1... | collective-permute-start | bytes 491528 | tf_op jit(solution)/shard_map/ppermute | solution.py:23
  166.0 8.8 %copy-start.6 = (f32[640]{0:T(1024)S(1)}, f32[640]{0:T(1024)}, u32[]{:S(2)}) copy-start(f32[640]{0:T(1024)} %param.17) | copy-start | bytes 7684
  174.8 140.5 %copy-start.7 = (f32[640]{0:T(1024)S(1)}, f32[640]{0:T(1024)}, u32[]{:S(2)}) copy-start(f32[640]{0:T(1024)} %param.20) | copy-start | bytes 7684
  174.8 140.5 %copy-start.8 = (f32[640]{0:T(1024)S(1)}, f32[640]{0:T(1024)}, u32[]{:S(2)}) copy-start(f32[640]{0:T(1024)} %param.19) | copy-start | bytes 7684
  319.6 4.0 %copy-start.1 = (f32[5,128,4096]{2,1,0:T(8,128)}, f32[5,128,4096]{2,1,0:T(8,128)S(1)}, u32[]{:S(2)}) copy-start(f32[5,128,4096]{2,1,0:T(8,128)S(1)} %get-tuple-element.16) | copy-start | bytes 31457284
  325.9 8.0 %copy-start.3 = (bf16[320,640]{1,0:T(8,128)(2,1)S(1)}, bf16[320,640]{1,0:T(8,128)(2,1)}, u32[]{:S(2)}) copy-start(bf16[320,640]{1,0:T(8,128)(2,1)} %param.22) | copy-start | bytes 1228804
Sparse Core Ops, SparseCore 0:
  10.2 79.2 all-gather.10
  92.1 70.1 all-gather.6
  165.0 70.6 all-gather.8
where the time goes:
time: 342 us; the launch traced here: 341 us
  blocking collectives  278 us (81%)
  matrix products  18.6 us (5%)
  local copies, waits for them, and re-layouts  15.7 us (5%)
  between operations  14.7 us (4%)
  other arithmetic  7.04 us (2%)
  starting transfers between devices  4.45 us (1%)
    psum x2, blocking collectives, group_norm(): total = lax.psum(jnp.sum(grouped, axis=(0, 2)), 'space')  139 us
    psum x2, blocking collectives, group_norm(): var = lax.psum(jnp.sum(centered * centered, axis=(0, 2)), 'space') / number  139 us
    unnamed x26, local copies, waits for them, and re-layouts  12.9 us
    dot_general x1, matrix products, on_device(): jnp.einsum('hqk,khd->hqd', weights.astype(jnp.bfloat16), values.reshape(l...  7.1 us
  transfers between devices with their start and end apart: 5, of which 1 were waited for; matrix products, arithmetic and copies ran while one was open for 8% of the time, Pallas kernels for 0%

commit v1 on v0

v1 whole, which is shorter than its diff:
```python
import math

import jax
import jax.numpy as jnp
from jax import lax
from jax.sharding import PartitionSpec as P

GROUPS = 32
HEADS = 5
HEAD_DIM = 64
TFREQ = 320
GW = 128


def local_stats(values):
    count, width = values.shape
    per = width // GROUPS
    mean = jnp.sum(values, axis=0).reshape(GROUPS, per).sum(axis=1) / (count * per)
    centered = values - jnp.repeat(mean, per)
    spread = jnp.sum(centered * centered, axis=0).reshape(GROUPS, per).sum(axis=1)
    return jnp.concatenate([mean, spread])


def merged_stats(values, eps):
    count, width = values.shape
    per = width // GROUPS
    peers = lax.axis_size("space")
    mine = local_stats(values)
    every = lax.all_to_all(
        jnp.broadcast_to(mine[None, None], (peers, 1, 2 * GROUPS)), "space", 0, 0, tiled=True
    )[:, 0]
    means, spreads = every[:, :GROUPS], every[:, GROUPS:]
    mean = jnp.mean(means, axis=0)
    shifted = means - mean
    var = (
        jnp.sum(spreads, axis=0) / (count * per) + jnp.sum(shifted * shifted, axis=0)
    ) / peers
    return jnp.repeat(mean, per), jnp.repeat(lax.rsqrt(var + eps), per)


def time_embed(timestep, time_weight):
    half = TFREQ // 2
    index = jnp.arange(half, dtype=jnp.float32)
    freq = jnp.exp(-math.log(10000.0) * index / half)
    angle = timestep.astype(jnp.float32)[0] * freq
    feats = jnp.concatenate([jnp.cos(angle), jnp.sin(angle)])[None, :]
    return jnp.dot(feats, time_weight, precision=lax.Precision.HIGHEST)


def on_device(
    latent,
    timestep,
    norm1_gain,
    norm1_shift,
    conv_weight,
    conv_bias,
    time_weight,
    norm2_gain,
    norm2_shift,
    qkv_weight,
    out_weight,
    stale_kv,
):
    tok_dev, width = latent.shape
    peers = lax.axis_size("space")
    me = lax.axis_index("space")
    rows = conv_weight.shape[0]
    sent = jnp.concatenate(
        [conv_weight, jnp.concatenate([stale_kv[0], stale_kv[1]], axis=1)], axis=0
    )
    whole = lax.all_gather(sent, "space", axis=0)
    up = [(i, i + 1) for i in range(peers - 1)]
    down = [(i + 1, i) for i in range(peers - 1)]
    before = lax.ppermute(latent, "space", up)
    after = lax.ppermute(latent, "space", down)
    base = latent.astype(jnp.float32)
    mean, scale1 = merged_stats(base, 1e-05)
    three = jnp.stack([before, latent, after]).astype(jnp.float32)
    normed = jax.nn.silu((three - mean) * scale1 * norm1_gain + norm1_shift).astype(jnp.bfloat16)
    inside = jnp.stack([me > 0, me >= 0, me < peers - 1])
    normed = jnp.where(inside[:, None, None], normed, 0)
    padded = jnp.pad(normed, ((0, 0), (1, 1), (0, 0)))
    windows = []
    for tap in range(9):
        down_, across = (tap // 3, tap % 3)
        windows.append(padded[down_, across : across + GW])
    unfolded = jnp.concatenate(windows, axis=1)
    bias = conv_bias + time_embed(timestep, time_weight)
    weight = whole[:, :rows].reshape(peers * rows, width)
    conv = jnp.dot(unfolded, weight, preferred_element_type=jnp.float32)
    mid = (base + conv + bias).astype(jnp.bfloat16)
    mid32 = mid.astype(jnp.float32)
    mean2, scale2 = merged_stats(mid32, 1e-06)
    normed2 = ((mid32 - mean2) * scale2 * norm2_gain + norm2_shift).astype(jnp.bfloat16)
    qkv = jnp.dot(normed2, qkv_weight, preferred_element_type=jnp.float32).astype(jnp.bfloat16)
    feats = qkv.shape[1] // 3
    query, key, value = (qkv[:, :feats], qkv[:, feats : 2 * feats], qkv[:, 2 * feats :])
    fresh_kv = jnp.stack([key, value])
    held = whole[:, rows:]
    own = (jnp.arange(peers) == me)[:, None, None]
    held = jnp.where(own, qkv[:, feats:], held).reshape(peers * tok_dev, 2 * feats)
    keys = held[:, :feats].reshape(-1, HEADS, HEAD_DIM)
    values = held[:, feats:].reshape(-1, HEADS, HEAD_DIM)
    queries = query.reshape(tok_dev, HEADS, HEAD_DIM)
    scores = jnp.einsum(
        "qhd,khd->hqk", queries, keys, preferred_element_type=jnp.float32
    ) * (1.0 / math.sqrt(HEAD_DIM))
    peak = jnp.max(scores, axis=-1, keepdims=True)
    expo = jnp.exp(scores - peak)
    total = jnp.sum(expo, axis=-1)
    mixed = jnp.einsum(
        "hqk,khd->hqd", expo.astype(jnp.bfloat16), values, preferred_element_type=jnp.float32
    )
    attended = (
        (mixed / total[:, :, None]).transpose(1, 0, 2).reshape(tok_dev, feats).astype(jnp.bfloat16)
    )
    result = (
        mid32 + jnp.dot(attended, out_weight, preferred_element_type=jnp.float32)
    ).astype(jnp.bfloat16)
    return (result, fresh_kv)


def solution(mesh):
    return jax.shard_map(
        on_device,
        mesh=mesh,
        in_specs=(
            P(("batch", "space"), None),
            P("batch"),
            P(),
            P(),
            P("space", None),
            P(),
            P(),
            P(),
            P(),
            P(),
            P(),
            P(None, ("batch", "space"), None),
        ),
        out_specs=(P(("batch", "space"), None), P(None, ("batch", "space"), None)),
        check_vma=False,
    )
```

time: 342 us -> 173 us (0.51)
  blocking collectives: 278 us -> 0 us
  waiting for transfers between devices: 2.49 us -> 76.5 us
  local copies, waits for them, and re-layouts: 15.7 us -> 34.2 us
  starting transfers between devices: 4.45 us -> 22.5 us
  matrix products: 18.6 us -> 11.9 us
  other arithmetic: 7.04 us -> 12.1 us
    psum x4 -> x0, blocking collectives: 278 us -> none  [the longest x2 139 us: group_norm(): total = lax.psum(jnp.sum(grouped, axis=(0, 2)), 'space')]
    all_gather x3 -> x1, waiting for transfers between devices: 0.06 us -> 63.7 us  [on_device(): whole = lax.all_gather(sent, 'space', axis=0)]
    all_to_all x0 -> x2, waiting for transfers between devices: none -> 12.8 us  [merged_stats(): lax.all_to_all(jnp.broadcast_to(mine[None, None], (peers, 1, 2 * GROUPS))...]
    all_to_all x0 -> x2, starting transfers between devices: none -> 12.4 us  [merged_stats(): lax.all_to_all(jnp.broadcast_to(mine[None, None], (peers, 1, 2 * GROUPS))...]
    slice x1 -> x5, local copies, waits for them, and re-layouts: 1.6 us -> 12.6 us  [the longest x1 6.74 us: on_device(): weight = whole[:, :rows].reshape(peers * rows, width)]
    reshape x0 -> x5, local copies, waits for them, and re-layouts: none -> 9.2 us  [the longest x1 8.82 us: on_device(): weight = whole[:, :rows].reshape(peers * rows, width)]
    ppermute x2, starting transfers between devices: 4.33 us -> 10.1 us  [the longest x1 5.12 us: on_device(): after = lax.ppermute(latent, 'space', down)]
    dot_general x5 -> x3, matrix products: 15.5 us -> 9.89 us  [the longest x1 4.47 us: on_device(): conv = jnp.dot(unfolded, weight, preferred_element_type=jnp.float32)]
  transfers between devices with their start and end apart: 5 -> 5, of which waited for: 1 -> 3; matrix products, arithmetic and copies ran while one was open for 8% -> 3% of each run, Pallas kernels for 0% -> 0%
where the time goes in v1:
time: 173 us; the launch traced here: 172 us
  waiting for transfers between devices  76.5 us (44%)
  local copies, waits for them, and re-layouts  34.2 us (20%)
  starting transfers between devices  22.5 us (13%)
  between operations  15.1 us (9%)
  other arithmetic  12.1 us (7%)
  matrix products  11.9 us (7%)
    all_gather x1, waiting for transfers between devices, on_device(): whole = lax.all_gather(sent, 'space', axis=0)  63.7 us
    all_to_all x2, waiting for transfers between devices, merged_stats(): lax.all_to_all(jnp.broadcast_to(mine[None, None], (peers, 1, 2 * GROUPS))...  12.8 us
    all_to_all x2, starting transfers between devices, merged_stats(): lax.all_to_all(jnp.broadcast_to(mine[None, None], (peers, 1, 2 * GROUPS))...  12.4 us
    unnamed x32, local copies, waits for them, and re-layouts  9.99 us
    reshape x1, local copies, waits for them, and re-layouts, on_device(): weight = whole[:, :rows].reshape(peers * rows, width)  8.82 us
    slice x1, local copies, waits for them, and re-layouts, on_device(): weight = whole[:, :rows].reshape(peers * rows, width)  6.74 us
    ppermute x1, starting transfers between devices, on_device(): after = lax.ppermute(latent, 'space', down)  5.12 us
    ppermute x1, starting transfers between devices, on_device(): before = lax.ppermute(latent, 'space', up)  4.97 us
  transfers between devices with their start and end apart: 5, of which 3 were waited for; matrix products, arithmetic and copies ran while one was open for 3% of the time, Pallas kernels for 0%

profile of v1, /device:TPU:1, one launch (start us, length us, event | category | flops | bytes accessed | tf_op | source)
XLA Modules:
  0.0 172.2 jit_solution(12987214832457999103)
XLA Ops:
  7.3 1.1 fusion.45
  8.4 0.1 copy.37
  8.5 0.1 copy.38
  8.6 1.8 %maximum_bitcast_fusion = bf16[1,308,640]{2,1,0:T(8,128)(2,1)} fusion(bf16[128,320]{1,0:T(8,128)(2,1)S(1)} %bitcast.81, bf16[128,320]{1,0:T(8,128)(2,1)S(1)} %bitcast.80, bf16[180,640]{1,0:T(8,128)(2,1)} %param.16), kind=kLoop, calls=%fused_computation.23 | loop fusion | flops 1182720 | bytes 788480
  10.5 5.0 %collective-permute-start = (bf16[128,640]{1,0:T(8,128)(2,1)}, bf16[128,640]{1,0:T(8,128)(2,1)S(1)}, u32[]{:S(2)}, u32[]{:S(2)}) collective-permute-start(bf16[128,640]{1,0:T(8,128)(2,1)} %param.12), channel_id=1, source_target_pairs={{0,1},{1,2},{2,3},{3,4},{4,5},{5,6},{6,7},{7,8},{8,9},{9,10},{10,1... | collective-permute-start | bytes 491528 | tf_op jit(solution)/shard_map/ppermute | solution.py:74
  15.4 5.1 %collective-permute-start.1 = (bf16[128,640]{1,0:T(8,128)(2,1)}, bf16[128,640]{1,0:T(8,128)(2,1)S(1)}, u32[]{:S(2)}, u32[]{:S(2)}) collective-permute-start(bf16[128,640]{1,0:T(8,128)(2,1)} %param.12), channel_id=1, source_target_pairs={{1,0},{2,1},{3,2},{4,3},{5,4},{6,5},{7,6},{8,7},{9,8},{10,9},{11,1... | collective-permute-start | bytes 491528 | tf_op jit(solution)/shard_map/ppermute | solution.py:75
  20.6 1.0 convert_reduce_fusion
  21.9 1.0 fusion.21
  23.0 0.1 reduce_sum.138
  23.2 0.6 broadcast_in_dim.68
  23.8 5.5 %all-to-all-start = ((f32[32,1,64]{2,1,0:T(1,128)}), f32[32,1,64]{2,1,0:T(1,128)S(1)}, u32[]{:S(2)}, u32[]{:S(2)}) async-start(f32[32,1,64]{2,1,0:T(1,128)} %broadcast_in_dim.68), calls=%async_computation | async-start | bytes 32768 | tf_op jit(solution)/shard_map/all_to_all | solution.py:29
  30.1 0.5 convolution_reduce_fusion
  30.8 5.7 %all-to-all-done = f32[32,1,64]{2,1,0:T(1,128)S(1)} async-done(((f32[32,1,64]{2,1,0:T(1,128)}), f32[32,1,64]{2,1,0:T(1,128)S(1)}, u32[]{:S(2)}, u32[]{:S(2)}) %all-to-all-start) | async-done | bytes 8224 | tf_op jit(solution)/shard_map/all_to_all | solution.py:29
  37.0 0.4 fusion.19
  37.8 63.7 %all-gather.4.cloned.1.call-done = bf16[32,308,640]{2,1,0:T(8,128)(2,1)} async-done(((bf16[1,308,640]{2,1,0:T(8,128)(2,1)}), bf16[32,308,640]{2,1,0:T(8,128)(2,1)}) %all-gather.4.cloned.1.call-update) | async-done | bytes 12615696 | tf_op jit(solution)/shard_map/all_gather | solution.py:71
  101.5 6.7 %slice.100 = bf16[32,180,640]{2,1,0:T(8,128)(2,1)} slice(bf16[32,308,640]{2,1,0:T(8,128)(2,1)} %all-gather.4.cloned.1.call-done), slice={[0:32], [0:180], [0:640]} | slice | bytes 14745600 | tf_op jit(solution)/shard_map/slice | solution.py:89
  108.2 8.8 %reshape.69 = bf16[5760,640]{1,0:T(8,128)(2,1)} reshape(bf16[32,180,640]{2,1,0:T(8,128)(2,1)} %slice.100) | data formatting | bytes 14745600 | tf_op jit(solution)/shard_map/reshape | solution.py:89
  117.1 4.5 %fusion.46 = (f32[640]{0:T(1024)S(1)}, f32[128,640]{1,0:T(8,128)S(1)}) fusion(f32[640]{0:T(1024)S(1)} %add.65, bf16[128,5760]{1,0:T(8,128)(2,1)S(1)} %fusion.33, bf16[5760,640]{1,0:T(8,128)(2,1)} %reshape.69, bf16[128,640]{1,0:T(8,128)(2,1)S(1)} %copy-done.2), kind=kOutput, calls=%fused_computation.82 | convolution fusion | flops 944209280 | bytes 9344000 | tf_op jit(solution)/shard_map/dot_general | solution.py:90
  122.3 0.6 broadcast_in_dim.73
  122.9 6.9 %all-to-all-start.1 = ((f32[32,1,64]{2,1,0:T(1,128)}), f32[32,1,64]{2,1,0:T(1,128)S(1)}, u32[]{:S(2)}, u32[]{:S(2)}) async-start(f32[32,1,64]{2,1,0:T(1,128)} %broadcast_in_dim.73), calls=%async_computation.1 | async-start | bytes 32768 | tf_op jit(solution)/shard_map/all_to_all | solution.py:29
  129.8 7.1 %all-to-all-done.1 = f32[32,1,64]{2,1,0:T(1,128)S(1)} async-done(((f32[32,1,64]{2,1,0:T(1,128)}), f32[32,1,64]{2,1,0:T(1,128)S(1)}, u32[]{:S(2)}, u32[]{:S(2)}) %all-to-all-start.1) | async-done | bytes 8224 | tf_op jit(solution)/shard_map/all_to_all | solution.py:29
  137.5 0.5 convolution_convert_fusion
  138.0 0.2 copy.34
  138.2 4.3 %slice_select_fusion = bf16[32,128,640]{2,1,0:T(8,128)(2,1)S(1)} fusion(bf16[32,308,640]{2,1,0:T(8,128)(2,1)} %all-gather.4.cloned.1.call-done, pred[32]{0:T(512)(128)(4,1)S(1)} %iota_compare_fusion, bf16[128,640]{1,0:T(8,128)(2,1)S(1)} %copy.34), kind=kLoop, calls=%fused_computation.5 | loop fusion | flops 2621440 | bytes 10649632 | tf_op jit(solution)/shard_map/jit(_where)/select_n | solution.py:101
  142.4 4.6 %fusion.44 = (bf16[4096,320]{1,0:T(8,128)(2,1)}, bf16[4096,320]{1,0:T(8,128)(2,1)}) fusion(bf16[4096,640]{1,0:T(8,128)(2,1)S(1)} %bitcast.75), kind=kLoop, calls=%fused_computation.80 | loop fusion | bytes 10485760 | tf_op jit(solution)/shard_map/slice | solution.py:102
  147.0 4.8 %copy.39 = bf16[4096,320]{0,1:T(8,128)(2,1)} copy(bf16[4096,320]{1,0:T(8,128)(2,1)} %get-tuple-element.6) | data formatting | bytes 5242880
  151.8 4.6 %copy.40 = bf16[4096,320]{0,1:T(8,128)(2,1)} copy(bf16[4096,320]{1,0:T(8,128)(2,1)} %get-tuple-element.7) | data formatting | bytes 5242880
  156.4 0.7 pad_maximum_fusion
  157.1 3.4 %multiply_reduce_fusion = (f32[5,128]{1,0:T(8,128)S(1)}, f32[5,128,4096]{2,1,0:T(8,128)S(1)}) fusion(bf16[128,5,64]{0,2,1:T(8,128)(2,1)S(1)} %bitcast.79, bf16[4096,5,64]{0,2,1:T(8,128)(2,1)} %bitcast.76), kind=kOutput, calls=%fused_computation.1 | convolution fusion | flops 340786560 | bytes 13191680 | tf_op jit(solution)/shard_map/qhd,khd->hqk/dot_general | solution.py:105
  160.5 1.8 %fusion = f32[5,128]{1,0:T(8,128)S(1)} fusion(f32[5,128,4096]{2,1,0:T(8,128)S(1)} %get-tuple-element.16, f32[5,128]{1,0:T(8,128)S(1)} %get-tuple-element.15), kind=kLoop, calls=%fused_computation.2 | loop fusion | flops 7863680 | bytes 10490880 | tf_op jit(solution)/shard_map/reduce_sum | solution.py:110
  162.3 2.0 %fusion.16 = bf16[128,5,64]{0,2,1:T(8,128)(2,1)S(1)} fusion(bf16[4096,5,64]{0,2,1:T(8,128)(2,1)S(1)} %bitcast.77, f32[5,128,4096]{2,1,0:T(8,128)S(1)} %get-tuple-element.16, f32[5,128]{1,0:T(8,128)S(1)} %get-tuple-element.15, f32[128,5]{0,1:T(8,128)S(1)} %bitcast.89), kind=kOutput, calls=%fused_computation.18 | convolution fusion | flops 343490560 | bytes 13194240 | tf_op jit(solution)/shard_map/hqk,khd->hqd/dot_general | solution.py:111
  164.4 1.0 fusion.7
  (73 shorter events, 3.0 us)
Async XLA Ops:
  7.2 130.3 %copy-start = (bf16[640,960]{0,1:T(8,128)(2,1)S(1)}, bf16[640,960]{0,1:T(8,128)(2,1)}, u32[]{:S(2)}) copy-start(bf16[640,960]{0,1:T(8,128)(2,1)} %param.21) | copy-start | bytes 3686404
  7.2 29.8 %copy-start.2 = (bf16[128,640]{1,0:T(8,128)(2,1)S(1)}, bf16[128,640]{1,0:T(8,128)(2,1)}, u32[]{:S(2)}) copy-start(bf16[128,640]{1,0:T(8,128)(2,1)} %param.12) | copy-start | bytes 491524
  7.2 22.9 %copy-start.3 = (f32[320,640]{1,0:T(8,128)S(1)}, f32[320,640]{1,0:T(8,128)}, u32[]{:S(2)}) copy-start(f32[320,640]{1,0:T(8,128)} %param.18) | copy-start | bytes 2457604
  7.2 23.5 %copy-start.9 = (f32[640]{0:T(1024)S(1)}, f32[640]{0:T(1024)}, u32[]{:S(2)}) copy-start(f32[640]{0:T(1024)} %param.17) | copy-start | bytes 7684
  7.2 29.8 %copy-start.6 = (f32[640]{0:T(1024)S(1)}, f32[640]{0:T(1024)}, u32[]{:S(2)}) copy-start(f32[640]{0:T(1024)} %param.14) | copy-start | bytes 7684
  7.2 29.8 %copy-start.5 = (f32[640]{0:T(1024)S(1)}, f32[640]{0:T(1024)}, u32[]{:S(2)}) copy-start(f32[640]{0:T(1024)} %param.15) | copy-start | bytes 7684
  7.2 94.3 %all-gather.4.cloned.1.call-start = ((), (), s32[]{:S(2)}) async-start(), calls=%async_computation.2 | async-start | bytes 13178880 | tf_op jit(solution)/shard_map/all_gather | solution.py:71
  10.5 26.5 %collective-permute-start = (bf16[128,640]{1,0:T(8,128)(2,1)}, bf16[128,640]{1,0:T(8,128)(2,1)S(1)}, u32[]{:S(2)}, u32[]{:S(2)}) collective-permute-start(bf16[128,640]{1,0:T(8,128)(2,1)} %param.12), channel_id=1, source_target_pairs={{0,1},{1,2},{2,3},{3,4},{4,5},{5,6},{6,7},{7,8},{8,9},{9,10},{10,1... | collective-permute-start | bytes 491528 | tf_op jit(solution)/shard_map/ppermute | solution.py:74
  15.4 21.5 %collective-permute-start.1 = (bf16[128,640]{1,0:T(8,128)(2,1)}, bf16[128,640]{1,0:T(8,128)(2,1)S(1)}, u32[]{:S(2)}, u32[]{:S(2)}) collective-permute-start(bf16[128,640]{1,0:T(8,128)(2,1)} %param.12), channel_id=1, source_target_pairs={{1,0},{2,1},{3,2},{4,3},{5,4},{6,5},{7,6},{8,7},{9,8},{10,9},{11,1... | collective-permute-start | bytes 491528 | tf_op jit(solution)/shard_map/ppermute | solution.py:75
  23.8 12.6 %all-to-all-start = ((f32[32,1,64]{2,1,0:T(1,128)}), f32[32,1,64]{2,1,0:T(1,128)S(1)}, u32[]{:S(2)}, u32[]{:S(2)}) async-start(f32[32,1,64]{2,1,0:T(1,128)} %broadcast_in_dim.68), calls=%async_computation | async-start | bytes 32768 | tf_op jit(solution)/shard_map/all_to_all | solution.py:29
  117.0 20.4 %copy-start.7 = (f32[640]{0:T(1024)S(1)}, f32[640]{0:T(1024)}, u32[]{:S(2)}) copy-start(f32[640]{0:T(1024)} %param.20) | copy-start | bytes 7684
  117.1 20.4 %copy-start.8 = (f32[640]{0:T(1024)S(1)}, f32[640]{0:T(1024)}, u32[]{:S(2)}) copy-start(f32[640]{0:T(1024)} %param.19) | copy-start | bytes 7684
  122.9 14.0 %all-to-all-start.1 = ((f32[32,1,64]{2,1,0:T(1,128)}), f32[32,1,64]{2,1,0:T(1,128)S(1)}, u32[]{:S(2)}, u32[]{:S(2)}) async-start(f32[32,1,64]{2,1,0:T(1,128)} %broadcast_in_dim.73), calls=%async_computation.1 | async-start | bytes 32768 | tf_op jit(solution)/shard_map/all_to_all | solution.py:29
  160.5 1.8 %copy-start.1 = (bf16[4096,320]{0,1:T(8,128)(2,1)S(1)}, bf16[4096,320]{0,1:T(8,128)(2,1)}, u32[]{:S(2)}) copy-start(bf16[4096,320]{0,1:T(8,128)(2,1)} %copy.40) | copy-start | bytes 7864324
  162.3 2.1 %copy-start.4 = (bf16[320,640]{1,0:T(8,128)(2,1)S(1)}, bf16[320,640]{1,0:T(8,128)(2,1)}, u32[]{:S(2)}) copy-start(bf16[320,640]{1,0:T(8,128)(2,1)} %param.22) | copy-start | bytes 1228804
Sparse Core Ops, SparseCore 0:
  10.6 90.8 all-gather.3

commit v2 on v1

v2 whole, which is shorter than its diff:
```python
import math

import jax
import jax.numpy as jnp
from jax import lax
from jax.experimental import pallas as pl
from jax.experimental.pallas import tpu as pltpu
from jax.sharding import PartitionSpec as P

GROUPS = 32
HEADS = 5
HEAD_DIM = 64
TFREQ = 320
GW = 128
PEERS = 32
Z_GROUPS = [[8 * x + 2 * z + c for z in range(4)] for x in range(4) for c in range(2)]
CORE_GROUPS = [[2 * k, 2 * k + 1] for k in range(16)]
RIGHT = [(i, (i + 8) % PEERS) for i in range(PEERS)]
LEFT = [(i, (i + 24) % PEERS) for i in range(PEERS)]
SWAP = [(i, i ^ 1) for i in range(PEERS)]
OUTER = [(i, i - 2) for i in range(2, PEERS, 2)] + [(i, i + 2) for i in range(1, PEERS - 2, 2)]
ROWS = 192
LOW = -1e30
VMEM = pl.BlockSpec(memory_space=pltpu.VMEM)
SMEM = pl.BlockSpec(memory_space=pltpu.SMEM)


def local_stats(values):
    count, width = values.shape
    per = width // GROUPS
    mean = jnp.sum(values, axis=0).reshape(GROUPS, per).sum(axis=1) / (count * per)
    centered = values - jnp.repeat(mean, per)
    spread = jnp.sum(centered * centered, axis=0).reshape(GROUPS, per).sum(axis=1)
    return jnp.concatenate([mean, spread])


def merged_stats(values, eps):
    count, width = values.shape
    per = width // GROUPS
    mine = local_stats(values)
    every = lax.all_to_all(
        jnp.broadcast_to(mine[None, None], (PEERS, 1, 2 * GROUPS)), "space", 0, 0, tiled=True
    )[:, 0]
    means, spreads = every[:, :GROUPS], every[:, GROUPS:]
    mean = jnp.mean(means, axis=0)
    shifted = means - mean
    var = (
        jnp.sum(spreads, axis=0) / (count * per) + jnp.sum(shifted * shifted, axis=0)
    ) / PEERS
    return jnp.repeat(mean, per), jnp.repeat(lax.rsqrt(var + eps), per)


def time_embed(timestep, time_weight):
    half = TFREQ // 2
    index = jnp.arange(half, dtype=jnp.float32)
    freq = jnp.exp(-math.log(10000.0) * index / half)
    angle = timestep.astype(jnp.float32)[0] * freq
    feats = jnp.concatenate([jnp.cos(angle), jnp.sin(angle)])[None, :]
    return jnp.dot(feats, time_weight, precision=lax.Precision.HIGHEST)


def dot32(a, b):
    return jnp.dot(a, b, preferred_element_type=jnp.float32)


def conv_near(x_ref, blocks_ref, own_ref, left_ref, right_ref, out_ref):
    x = x_ref[0]
    total = None
    for step, ref in ((0, own_ref), (3, left_ref), (1, right_ref)):
        first = 4 * ((x + step) & 3)
        for z in range(4):
            part = dot32(blocks_ref[first + z], ref[z])
            total = part if total is None else total + part
    out_ref[...] = total


def conv_far(x_ref, blocks_ref, low_ref, high_ref, near_ref, out_ref):
    first = 4 * ((x_ref[0] + 2) & 3)
    total = near_ref[...]
    for z in range(4):
        ref = low_ref if z < 2 else high_ref
        total = total + dot32(blocks_ref[first + z], ref[z % 2])
    out_ref[...] = total


def attend(z_ref, q_ref, own_ref, left_ref, right_ref, low_ref, high_ref, fresh_ref, out_ref):
    my_z = z_ref[0]
    count = fresh_ref.shape[0]
    lane = lax.broadcasted_iota(jnp.int32, (2 * count, 128), 1)
    row = lax.broadcasted_iota(jnp.int32, (2 * count, 4 * count), 0)
    block = lax.broadcasted_iota(jnp.int32, (2 * count, 4 * count), 1) // count
    replaced = (row < count) & (block == my_z)
    held = (own_ref, left_ref, right_ref, low_ref, high_ref)
    outs = []
    for head in range(HEADS):
        k_at = 128 * ((HEADS + head) // 2)
        v_at = 128 * (head // 2)
        q_at = 128 * ((1 + head) // 2)
        mine = (lane >= 64) if head % 2 == 0 else (lane < 64)
        query = jnp.where(mine, q_ref[:, q_at : q_at + 128].astype(jnp.float32), 0.0)
        query = query.astype(jnp.bfloat16)
        scores = []
        for ref in held:
            keys = ref[:, :, k_at : k_at + 128].reshape(-1, 128)
            scores.append(
                lax.dot_general(
                    query, keys, (((1,), (1,)), ((), ())), preferred_element_type=jnp.float32
                )
            )
        scores[0] = jnp.where(replaced, LOW, scores[0])
        fresh = lax.dot_general(
            query[:count],
            fresh_ref[:, k_at : k_at + 128],
            (((1,), (1,)), ((), ())),
            preferred_element_type=jnp.float32,
        )
        scores.append(jnp.concatenate([fresh, jnp.full((count, count), LOW, jnp.float32)], axis=0))
        peak = scores[0].max(axis=1, keepdims=True)
        for s in scores[1:]:
            peak = jnp.maximum(peak, s.max(axis=1, keepdims=True))
        total = jnp.zeros((2 * count, 1), jnp.float32)
        mixed = jnp.zeros((2 * count, 128), jnp.float32)
        for s, ref in zip(scores, held + (fresh_ref,), strict=True):
            weights = jnp.exp(s - peak)
            total = total + weights.sum(axis=1, keepdims=True)
            if ref is fresh_ref:
                values = ref[:, v_at : v_at + 128]
            else:
                values = ref[:, :, v_at : v_at + 128].reshape(-1, 128)
            mixed = mixed + dot32(weights.astype(jnp.bfloat16), values)
        outs.append((mixed, peak, total))
    out_ref[:, :128] = jnp.where(lane < 64, outs[0][0], outs[1][0])
    out_ref[:, 128:256] = jnp.where(lane < 64, outs[2][0], outs[3][0])
    last = jnp.where(lane < 64, outs[4][0], 0.0)
    for head in range(HEADS):
        last = jnp.where(lane == 64 + head, outs[head][1], last)
        last = jnp.where(lane == 72 + head, outs[head][2], last)
    out_ref[:, 256:] = last


def finish(own_ref, other_ref, mid_ref, weight_ref, out_ref):
    count = mid_ref.shape[0]
    lane = lax.broadcasted_iota(jnp.int32, (count, 128), 1)
    factors = []
    for head in range(HEADS):
        peak1 = own_ref[:, 320 + head : 321 + head]
        peak2 = other_ref[:, 320 + head : 321 + head]
        peak = jnp.maximum(peak1, peak2)
        one, two = jnp.exp(peak1 - peak), jnp.exp(peak2 - peak)
        total = own_ref[:, 328 + head : 329 + head] * one
        total = total + other_ref[:, 328 + head : 329 + head] * two
        factors.append((one / total, two / total))
    result = mid_ref[...].astype(jnp.float32)
    for tile in range(3):
        first = factors[2 * tile]
        second = factors[min(2 * tile + 1, HEADS - 1)]
        at = 128 * tile
        mixed = own_ref[:, at : at + 128] * jnp.where(lane < 64, first[0], second[0])
        mixed = mixed + other_ref[:, at : at + 128] * jnp.where(lane < 64, first[1], second[1])
        if tile == 2:
            mixed = jnp.where(lane < 64, mixed, 0.0)
        result = result + dot32(mixed.astype(jnp.bfloat16), weight_ref[at : at + 128])
    out_ref[...] = result.astype(jnp.bfloat16)


def call(kernel, shape, dtype, specs, *args):
    return pl.pallas_call(
        kernel,
        out_shape=jax.ShapeDtypeStruct(shape, dtype),
        in_specs=specs,
        out_specs=VMEM,
        compiler_params=pltpu.CompilerParams(vmem_limit_bytes=40 * 1024 * 1024),
    )(*args)


def on_device(
    latent,
    timestep,
    norm1_gain,
    norm1_shift,
    conv_weight,
    conv_bias,
    time_weight,
    norm2_gain,
    norm2_shift,
    qkv_weight,
    out_weight,
    stale_kv,
):
    tok_dev, width = latent.shape
    me = lax.axis_index("space")
    x, z, core = me // 8, (me // 2) % 4, me % 2
    x_at, z_at = x.reshape(1), z.reshape(1)
    rows = conv_weight.shape[0]

    outer = lax.ppermute(latent, "space", OUTER)
    base = latent.astype(jnp.float32)
    mean, scale1 = merged_stats(base, 1e-05)

    weight = jnp.pad(conv_weight, ((0, ROWS - rows), (0, 0)))
    own_w = lax.all_gather(weight, "space", axis=0, axis_index_groups=Z_GROUPS)
    left_w = lax.ppermute(own_w, "space", RIGHT)
    right_w = lax.ppermute(own_w, "space", LEFT)
    low_w = lax.ppermute(left_w[:2], "space", RIGHT)
    high_w = lax.ppermute(right_w[2:], "space", LEFT)

    stale = jnp.concatenate([stale_kv[1], stale_kv[0]], axis=1)
    stale, _ = lax.optimization_barrier((stale, own_w))
    own_kv = lax.all_gather(stale, "space", axis=0, axis_index_groups=Z_GROUPS)

    pair = lax.all_gather(
        jnp.stack([latent, outer]), "space", axis=0, axis_index_groups=CORE_GROUPS
    )
    four = jnp.stack([pair[1, 1], pair[0, 0], pair[1, 0], pair[0, 1]]).astype(jnp.float32)
    normed = jax.nn.silu((four - mean) * scale1 * norm1_gain + norm1_shift).astype(jnp.bfloat16)
    inside = jnp.stack([me >= 2, me >= 0, me >= 0, me < PEERS - 2])
    normed = jnp.where(inside[:, None, None], normed, 0)
    padded = jnp.pad(normed, ((0, 0), (1, 1), (0, 0)))
    unfolded = jnp.concatenate(
        [padded[t // 3 : t // 3 + 2, t % 3 : t % 3 + GW] for t in range(9)], axis=2
    )
    blocks = unfolded.reshape(2 * tok_dev, 16, 2, rows)
    blocks = lax.dynamic_index_in_dim(blocks, core, axis=2, keepdims=False).transpose(1, 0, 2)
    blocks = jnp.pad(blocks, ((0, 0), (0, 0), (0, ROWS - rows)))

    shape = (2 * tok_dev, width)
    near = call(
        conv_near, shape, jnp.float32, [SMEM] + [VMEM] * 4, x_at, blocks, own_w, left_w, right_w
    )
    sums = call(
        conv_far, shape, jnp.float32, [SMEM] + [VMEM] * 4, x_at, blocks, low_w, high_w, near
    )
    sums = sums.reshape(2, tok_dev, width)
    kept = lax.dynamic_index_in_dim(sums, core, axis=0, keepdims=False)
    given = lax.dynamic_index_in_dim(sums, 1 - core, axis=0, keepdims=False)
    conv = kept + lax.ppermute(given, "space", SWAP)

    own_kv, _ = lax.optimization_barrier((own_kv, sums))
    left_kv = lax.ppermute(own_kv, "space", RIGHT)
    right_kv = lax.ppermute(own_kv, "space", LEFT)
    low_kv = lax.ppermute(left_kv[:2], "space", RIGHT)
    high_kv = lax.ppermute(right_kv[2:], "space", LEFT)

    bias = conv_bias + time_embed(timestep, time_weight)
    mid = (base + conv + bias).astype(jnp.bfloat16)
    mid32 = mid.astype(jnp.float32)
    mean2, scale2 = merged_stats(mid32, 1e-06)
    normed2 = ((mid32 - mean2) * scale2 * norm2_gain + norm2_shift).astype(jnp.bfloat16)
    qkv = dot32(normed2, qkv_weight).astype(jnp.bfloat16)
    feats = qkv.shape[1] // 3
    query, key, value = (qkv[:, :feats], qkv[:, feats : 2 * feats], qkv[:, 2 * feats :])
    fresh_kv = jnp.stack([key, value])
    fresh = jnp.concatenate([value, key], axis=1)
    query = jnp.pad(query * (1.0 / math.sqrt(HEAD_DIM)), ((0, 0), (HEAD_DIM, 0)))
    both = jnp.concatenate([query, lax.ppermute(query, "space", SWAP)], axis=0)
    parts = call(
        attend,
        (2 * tok_dev, 384),
        jnp.float32,
        [SMEM] + [VMEM] * 7,
        z_at,
        both,
        own_kv,
        left_kv,
        right_kv,
        low_kv,
        high_kv,
        fresh,
    )
    other = lax.ppermute(parts[tok_dev:], "space", SWAP)
    project = jnp.pad(out_weight, ((0, 384 - feats), (0, 0)))
    result = call(
        finish, (tok_dev, width), jnp.bfloat16, [VMEM] * 4, parts[:tok_dev], other, mid, project
    )
    return (result, fresh_kv)


def solution(mesh):
    return jax.shard_map(
        on_device,
        mesh=mesh,
        in_specs=(
            P(("batch", "space"), None),
            P("batch"),
            P(),
            P(),
            P("space", None),
            P(),
            P(),
            P(),
            P(),
            P(),
            P(),
            P(None, ("batch", "space"), None),
        ),
        out_specs=(P(("batch", "space"), None), P(None, ("batch", "space"), None)),
        check_vma=False,
    )
```

time: 173 us -> 177 us (1.023)
  waiting for transfers between devices: 76.5 us -> 16.2 us
  blocking collectives: 0 us -> 39.7 us
  starting transfers between devices: 22.5 us -> 60.3 us
  between operations: 15.1 us -> 1.89 us
  matrix products: 11.9 us -> 1.05 us
  Pallas kernels: 0 us -> 10.3 us
  local copies, waits for them, and re-layouts: 34.2 us -> 40.6 us
  other arithmetic: 12.1 us -> 6.07 us
    all_gather x1 -> x0, waiting for transfers between devices: 63.7 us -> none  [on_device(): whole = lax.all_gather(sent, 'space', axis=0)]
    all_gather x0 -> x3, blocking collectives: none -> 39.7 us  [the longest x1 21.2 us: on_device(): own_w = lax.all_gather(weight, 'space', axis=0, axis_index_groups=Z_GROUPS)]
    ppermute x2 -> x12, starting transfers between devices: 10.1 us -> 43.3 us  [the longest x1 5.78 us: on_device(): other = lax.ppermute(parts[tok_dev:], 'space', SWAP)]
    ppermute x2 -> x12, waiting for transfers between devices: 0.01 us -> 12 us  [the longest x1 9.25 us: on_device(): right_kv = lax.ppermute(own_kv, 'space', LEFT)]
    dot_general x5 -> x1, matrix products: 11.3 us -> 0.53 us  [dot32(): return jnp.dot(a, b, preferred_element_type=jnp.float32)]
    pallas_call x0 -> x4, Pallas kernels: none -> 10.3 us  [call(): pl.pallas_call(kernel, out_shape=jax.ShapeDtypeStruct(shape, dtype), in_s...]
    slice x5, local copies, waits for them, and re-layouts: 12.6 us -> 2.85 us  [the longest x1 1.91 us: on_device(): high_w = lax.ppermute(right_w[2:], 'space', LEFT)]
    concatenate x1 -> x2, local copies, waits for them, and re-layouts: 0.05 us -> 9.31 us  [on_device(): jnp.concatenate([padded[t // 3:t // 3 + 2, t % 3:t % 3 + GW] for t in ran...]
  transfers between devices with their start and end apart: 5 -> 14, of which waited for: 3 -> 6; matrix products, arithmetic and copies ran while one was open for 3% -> 26% of each run, Pallas kernels for 0% -> 1%
where the time goes in v2:
time: 177 us; the launch traced here: 176 us
  starting transfers between devices  60.3 us (34%)
  local copies, waits for them, and re-layouts  40.6 us (23%)
  blocking collectives  39.7 us (22%)
  waiting for transfers between devices  16.2 us (9%)
  Pallas kernels  10.3 us (6%)
  other arithmetic  6.07 us (3%)
  between operations  1.89 us (1%)
    all_gather x1, blocking collectives, on_device(): own_w = lax.all_gather(weight, 'space', axis=0, axis_index_groups=Z_GROUPS)  21.2 us
    all_to_all x2, starting transfers between devices, merged_stats(): lax.all_to_all(jnp.broadcast_to(mine[None, None], (PEERS, 1, 2 * GROUPS))...  17 us
    all_gather x1, blocking collectives, on_device(): own_kv = lax.all_gather(stale, 'space', axis=0, axis_index_groups=Z_GROUPS)  15.8 us
    pallas_call x4, Pallas kernels, call(): pl.pallas_call(kernel, out_shape=jax.ShapeDtypeStruct(shape, dtype), in_s...  10.3 us
    concatenate x2, local copies, waits for them, and re-layouts, on_device(): jnp.concatenate([padded[t // 3:t // 3 + 2, t % 3:t % 3 + GW] for t in ran...  9.31 us
    ppermute x1, waiting for transfers between devices, on_device(): right_kv = lax.ppermute(own_kv, 'space', LEFT)  9.25 us
    reshape x1, local copies, waits for them, and re-layouts, on_device(): blocks = unfolded.reshape(2 * tok_dev, 16, 2, rows)  7.49 us
    unnamed x33, local copies, waits for them, and re-layouts  7.48 us
  transfers between devices with their start and end apart: 14, of which 6 were waited for; matrix products, arithmetic and copies ran while one was open for 26% of the time, Pallas kernels for 1%

profile of v2, /device:TPU:1, one launch (start us, length us, event | category | flops | bytes accessed | tf_op | source)
XLA Modules:
  0.0 176.2 jit_solution(7075627812033116667)
XLA Ops:
  0.7 1.1 pad.22
  1.7 21.2 %all-gather.1 = bf16[768,640]{1,0:T(8,128)(2,1)S(1)} all-gather(bf16[192,640]{1,0:T(8,128)(2,1)S(1)} %pad.22), channel_id=3, replica_groups={{0,2,4,6},{1,3,5,7},{8,10,12,14},{9,11,13,15},{16,18,20,22},{17,19,21,2..., dimensions={0}, use_global_device_ids=true | all-gather | bytes 1228800 | tf_op jit(solution)/shard_map/all_gather | solution.py:201
  23.0 2.8 %collective-permute-start.1 = (bf16[4,192,640]{2,1,0:T(8,128)(2,1)S(1)}, bf16[4,192,640]{2,1,0:T(8,128)(2,1)S(1)}, u32[]{:S(2)}, u32[]{:S(2)}) collective-permute-start(bf16[4,192,640]{2,1,0:T(8,128)(2,1)S(1)} %bitcast.45), channel_id=1, source_target_pairs={{0,8},{1,9},{2,10},{3,11},{4,12},{5,13},{6,14},{7,15},{8,16},{9,17... | collective-permute-start | bytes 2949128 | tf_op jit(solution)/shard_map/ppermute | solution.py:202
  25.8 3.6 %collective-permute-start.3 = (bf16[4,192,640]{2,1,0:T(8,128)(2,1)S(1)}, bf16[4,192,640]{2,1,0:T(8,128)(2,1)}, u32[]{:S(2)}, u32[]{:S(2)}) collective-permute-start(bf16[4,192,640]{2,1,0:T(8,128)(2,1)S(1)} %bitcast.46), channel_id=1, source_target_pairs={{0,24},{1,25},{2,26},{3,27},{4,28},{5,29},{6,30},{7,31},{8,0},{9,1... | collective-permute-start | bytes 2949128 | tf_op jit(solution)/shard_map/ppermute | solution.py:203
  29.5 3.0 %collective-permute-start = (bf16[128,640]{1,0:T(8,128)(2,1)}, bf16[128,640]{1,0:T(8,128)(2,1)S(1)}, u32[]{:S(2)}, u32[]{:S(2)}) collective-permute-start(bf16[128,640]{1,0:T(8,128)(2,1)} %param.12), channel_id=1, source_target_pairs={{2,0},{4,2},{6,4},{8,6},{10,8},{12,10},{14,12},{16,14},{18,16},{20... | collective-permute-start | bytes 491528 | tf_op jit(solution)/shard_map/ppermute | solution.py:196
  33.8 1.0 fusion.8
  35.7 9.8 %all-to-all-start = ((f32[32,1,64]{2,1,0:T(1,128)}), f32[32,1,64]{2,1,0:T(1,128)S(1)}, u32[]{:S(2)}, u32[]{:S(2)}) async-start(f32[32,1,64]{2,1,0:T(1,128)} %broadcast_in_dim.30), calls=%async_computation | async-start | bytes 32768 | tf_op jit(solution)/shard_map/all_to_all | solution.py:41
  48.4 4.2 %all-to-all-done = f32[32,1,64]{2,1,0:T(1,128)S(1)} async-done(((f32[32,1,64]{2,1,0:T(1,128)}), f32[32,1,64]{2,1,0:T(1,128)S(1)}, u32[]{:S(2)}, u32[]{:S(2)}) %all-to-all-start) | async-done | bytes 8224 | tf_op jit(solution)/shard_map/all_to_all | solution.py:41
  54.1 2.7 %all-gather = bf16[4,128,640]{2,1,0:T(8,128)(2,1)S(1)} all-gather(bf16[2,128,640]{2,1,0:T(8,128)(2,1)S(1)} %pad_maximum_fusion), channel_id=2, replica_groups={{0,1},{2,3},{4,5},{6,7},{8,9},{10,11},{12,13},{14,15},{16,17},{18,19},{..., dimensions={0}, use_global_device_ids=true | all-gather | bytes 983040 | tf_op jit(solution)/shard_map/all_gather | solution.py:211
  64.1 2.4 %collective-permute-start.2 = (bf16[2,192,640]{2,1,0:T(8,128)(2,1)}, bf16[2,192,640]{2,1,0:T(8,128)(2,1)}, u32[]{:S(2)}, u32[]{:S(2)}) collective-permute-start(bf16[2,192,640]{2,1,0:T(8,128)(2,1)} %slice.124), channel_id=1, source_target_pairs={{0,8},{1,9},{2,10},{3,11},{4,12},{5,13},{6,14},{7,15},{8,16},{9,17... | collective-permute-start | bytes 1474568 | tf_op jit(solution)/shard_map/ppermute | solution.py:204
  66.4 1.9 %slice.125 = bf16[2,192,640]{2,1,0:T(8,128)(2,1)} slice(bf16[4,192,640]{2,1,0:T(8,128)(2,1)} %collective-permute-done.3.right_ref), slice={[2:4], [0:192], [0:640]} | slice | bytes 983040 | tf_op jit(solution)/shard_map/slice | solution.py:205
  68.3 4.1 %collective-permute-start.4 = (bf16[2,192,640]{2,1,0:T(8,128)(2,1)}, bf16[2,192,640]{2,1,0:T(8,128)(2,1)}, u32[]{:S(2)}, u32[]{:S(2)}) collective-permute-start(bf16[2,192,640]{2,1,0:T(8,128)(2,1)} %slice.125), channel_id=1, source_target_pairs={{0,24},{1,25},{2,26},{3,27},{4,28},{5,29},{6,30},{7,31},{8,0},{9,1... | collective-permute-start | bytes 1474568 | tf_op jit(solution)/shard_map/ppermute | solution.py:205
  74.1 8.5 %copy.40 = bf16[2,128,5760]{1,0,2:T(2,128)(2,1)} copy(bf16[2,128,5760]{2,1,0:T(8,128)(2,1)} %fusion.6) | data formatting | bytes 5898240 | tf_op jit(solution)/shard_map/concatenate | solution.py:219
  82.6 7.5 %reshape.60 = bf16[256,16,2,180]{0,3,2,1:T(8,128)(2,1)} reshape(bf16[2,128,5760]{1,0,2:T(2,128)(2,1)} %copy.40) | data formatting | bytes 5898240 | tf_op jit(solution)/shard_map/reshape | solution.py:222
  90.1 2.6 %constant_dynamic-slice_fusion = bf16[256,16,1,180]{0,3,2,1:T(8,128)(2,1)} fusion(bf16[256,16,2,180]{0,3,2,1:T(8,128)(2,1)} %reshape.60, s32[]{:T(128)S(6)} %select_n.36), kind=kLoop, calls=%fused_computation.64 | loop fusion | bytes 2949124 | tf_op jit(solution)/shard_map/jit(dynamic_index_in_dim)/dynamic_slice | solution.py:223
  92.7 3.7 %copy.41 = bf16[256,16,1,180]{3,0,1,2:T(8,128)(2,1)} copy(bf16[256,16,1,180]{0,3,2,1:T(8,128)(2,1)} %constant_dynamic-slice_fusion) | data formatting | bytes 2949120 | tf_op jit(solution)/shard_map/jit(dynamic_index_in_dim)/dynamic_slice | solution.py:223
  96.4 2.0 %pad.21.blocks_ref = bf16[16,256,192]{2,1,0:T(8,128)(2,1)S(1)} pad(bf16[16,256,180]{2,1,0:T(8,128)(2,1)} %bitcast.53, bf16[]{:T(256)} %constant.89.clone.1), padding=0_0x0_0x0_12 | pad | bytes 3047426 | tf_op jit(solution)/shard_map/jit(_pad)/pad | solution.py:224
  98.3 2.6 %shard_map.131.near_ref = f32[256,640]{1,0:T(8,128)S(1)} custom-call(s32[1]{0:T(128)} %bitcast.1.x_ref, bf16[16,256,192]{2,1,0:T(8,128)(2,1)S(1)} %pad.21.blocks_ref, bf16[4,192,640]{2,1,0:T(8,128)(2,1)S(1)} %bitcast.47, bf16[4,192,640]{2,1,0:T(8,128)(2,1)S(1)} %collective-permute-done.1.left_ref, bf16[4,192,640]{2,1,0:T(8,128)(2,1)} %collective-permute-done.3.right_ref), custom_call_target="tpu_custom_call" | custom-call | tf_op jit(solution)/shard_map/pallas_call | solution.py:167
  101.0 1.8 %shard_map.132 = f32[256,640]{1,0:T(8,128)S(1)} custom-call(s32[1]{0:T(128)} %bitcast.1.x_ref, bf16[16,256,192]{2,1,0:T(8,128)(2,1)S(1)} %pad.21.blocks_ref, bf16[2,192,640]{2,1,0:T(8,128)(2,1)} %collective-permute-done.2.low_ref, bf16[2,192,640]{2,1,0:T(8,128)(2,1)} %collective-permute-done.4.high_ref, f32[256,640]{1,0:T(8,128)S(1)} %shard_map.131.near_ref), custom_call_target="tpu_custom_call" | custom-call | tf_op jit(solution)/shard_map/pallas_call | solution.py:167
  102.9 2.8 %collective-permute-start.5 = (f32[128,640]{1,0:T(8,128)S(1)}, f32[128,640]{1,0:T(8,128)S(1)}, u32[]{:S(2)}, u32[]{:S(2)}) collective-permute-start(f32[128,640]{1,0:T(8,128)S(1)} %dynamic-slice_bitcast_fusion), channel_id=1, source_target_pairs={{0,1},{1,0},{2,3},{3,2},{4,5},{5,4},{6,7},{7,6},{8,9},{9,8},{10,11... | collective-permute-start | bytes 983048 | tf_op jit(solution)/shard_map/ppermute | solution.py:236
  108.5 7.2 %all-to-all-start.1 = ((f32[32,1,64]{2,1,0:T(1,128)}), f32[32,1,64]{2,1,0:T(1,128)S(1)}, u32[]{:S(2)}, u32[]{:S(2)}) async-start(f32[32,1,64]{2,1,0:T(1,128)} %broadcast_in_dim.58), calls=%async_computation.1 | async-start | bytes 32768 | tf_op jit(solution)/shard_map/all_to_all | solution.py:41
  115.7 15.8 %all-gather.2 = bf16[512,640]{0,1:T(8,128)(2,1)S(1)} all-gather(bf16[128,640]{0,1:T(8,128)(2,1)S(1)} %pad_maximum_fusion.3), channel_id=4, replica_groups={{0,2,4,6},{1,3,5,7},{8,10,12,14},{9,11,13,15},{16,18,20,22},{17,19,21,2..., dimensions={0}, use_global_device_ids=true | all-gather | bytes 819200 | tf_op jit(solution)/shard_map/all_gather | solution.py:209
  131.8 4.4 %collective-permute-start.8 = (bf16[4,128,640]{2,1,0:T(8,128)(2,1)S(1)}, bf16[4,128,640]{2,1,0:T(8,128)(2,1)S(1)}, u32[]{:S(2)}, u32[]{:S(2)}) collective-permute-start(bf16[4,128,640]{2,1,0:T(8,128)(2,1)S(1)} %bitcast.50), channel_id=1, source_target_pairs={{0,24},{1,25},{2,26},{3,27},{4,28},{5,29},{6,30},{7,31},{8,0},{9,1... | collective-permute-start | bytes 1966088 | tf_op jit(solution)/shard_map/ppermute | solution.py:240
  136.2 1.9 %collective-permute-start.7 = (bf16[4,128,640]{2,1,0:T(8,128)(2,1)S(1)}, bf16[4,128,640]{2,1,0:T(8,128)(2,1)S(1)}, u32[]{:S(2)}, u32[]{:S(2)}) collective-permute-start(bf16[4,128,640]{2,1,0:T(8,128)(2,1)S(1)} %bitcast.51), channel_id=1, source_target_pairs={{0,8},{1,9},{2,10},{3,11},{4,12},{5,13},{6,14},{7,15},{8,16},{9,17... | collective-permute-start | bytes 1966088 | tf_op jit(solution)/shard_map/ppermute | solution.py:239
  139.2 9.2 %collective-permute-done.8.right_ref = bf16[4,128,640]{2,1,0:T(8,128)(2,1)S(1)} collective-permute-done((bf16[4,128,640]{2,1,0:T(8,128)(2,1)S(1)}, bf16[4,128,640]{2,1,0:T(8,128)(2,1)S(1)}, u32[]{:S(2)}, u32[]{:S(2)}) %collective-permute-start.8) | collective-permute-done | bytes 655392 | tf_op jit(solution)/shard_map/ppermute | solution.py:240
  148.5 5.3 %collective-permute-start.10 = (bf16[2,128,640]{2,1,0:T(8,128)(2,1)S(1)}, bf16[2,128,640]{2,1,0:T(8,128)(2,1)S(1)}, u32[]{:S(2)}, u32[]{:S(2)}) collective-permute-start(bf16[2,128,640]{2,1,0:T(8,128)(2,1)S(1)} %slice.130), channel_id=1, source_target_pairs={{0,24},{1,25},{2,26},{3,27},{4,28},{5,29},{6,30},{7,31},{8,0},{9,1... | collective-permute-start | bytes 983048 | tf_op jit(solution)/shard_map/ppermute | solution.py:242
  153.9 2.1 %collective-permute-start.9 = (bf16[2,128,640]{2,1,0:T(8,128)(2,1)S(1)}, bf16[2,128,640]{2,1,0:T(8,128)(2,1)S(1)}, u32[]{:S(2)}, u32[]{:S(2)}) collective-permute-start(bf16[2,128,640]{2,1,0:T(8,128)(2,1)S(1)} %slice.129), channel_id=1, source_target_pairs={{0,8},{1,9},{2,10},{3,11},{4,12},{5,13},{6,14},{7,15},{8,16},{9,17... | collective-permute-start | bytes 983048 | tf_op jit(solution)/shard_map/ppermute | solution.py:241
  156.1 5.0 %collective-permute-start.6 = (bf16[128,384]{1,0:T(8,128)(2,1)S(1)}, bf16[128,384]{1,0:T(8,128)(2,1)S(1)}, u32[]{:S(2)}, u32[]{:S(2)}) collective-permute-start(bf16[128,384]{1,0:T(8,128)(2,1)S(1)} %pad.23), channel_id=1, source_target_pairs={{0,1},{1,0},{2,3},{3,2},{4,5},{5,4},{6,7},{7,6},{8,9},{9,8},{10,11... | collective-permute-start | bytes 294920 | tf_op jit(solution)/shard_map/ppermute | solution.py:255
  162.0 1.4 collective-permute-done.9.low_ref
  163.4 4.6 %shard_map.133 = f32[256,384]{1,0:T(8,128)S(1)} custom-call(s32[1]{0:T(128)} %bitcast.z_ref, bf16[256,384]{1,0:T(8,128)(2,1)S(1)} %pad_maximum_fusion.1.q_ref, bf16[4,128,640]{2,1,0:T(8,128)(2,1)S(1)} %bitcast.52, bf16[4,128,640]{2,1,0:T(8,128)(2,1)S(1)} %collective-permute-done.7.left_ref, bf16[4,128,640]{2,1,0:T(8,128)(2,1)S(1)} %collective-permute-done.8.right_ref, ...), custom_call_target="tpu_custom_call" | custom-call | tf_op jit(solution)/shard_map/pallas_call | solution.py:167
  168.0 5.8 %collective-permute-start.11 = (f32[128,384]{1,0:T(8,128)S(1)}, f32[128,384]{1,0:T(8,128)S(1)}, u32[]{:S(2)}, u32[]{:S(2)}) collective-permute-start(f32[128,384]{1,0:T(8,128)S(1)} %get-tuple-element.28), channel_id=1, source_target_pairs={{0,1},{1,0},{2,3},{3,2},{4,5},{5,4},{6,7},{7,6},{8,9},{9,8},{10,11... | collective-permute-start | bytes 589832 | tf_op jit(solution)/shard_map/ppermute | solution.py:270
  174.9 1.3 shard_map.134
  (106 shorter events, 20.9 us)
Async XLA Ops:
  0.6 138.0 %copy-start = (bf16[640,960]{0,1:T(8,128)(2,1)S(1)}, bf16[640,960]{0,1:T(8,128)(2,1)}, u32[]{:S(2)}) copy-start(bf16[640,960]{0,1:T(8,128)(2,1)} %param.21) | copy-start | bytes 3686404
  0.6 56.2 %copy-start.5 = (f32[640]{0:T(1024)S(1)}, f32[640]{0:T(1024)}, u32[]{:S(2)}) copy-start(f32[640]{0:T(1024)} %param.14) | copy-start | bytes 7684
  0.7 56.2 %copy-start.4 = (f32[640]{0:T(1024)S(1)}, f32[640]{0:T(1024)}, u32[]{:S(2)}) copy-start(f32[640]{0:T(1024)} %param.15) | copy-start | bytes 7684
  23.0 40.2 %collective-permute-start.1 = (bf16[4,192,640]{2,1,0:T(8,128)(2,1)S(1)}, bf16[4,192,640]{2,1,0:T(8,128)(2,1)S(1)}, u32[]{:S(2)}, u32[]{:S(2)}) collective-permute-start(bf16[4,192,640]{2,1,0:T(8,128)(2,1)S(1)} %bitcast.45), channel_id=1, source_target_pairs={{0,8},{1,9},{2,10},{3,11},{4,12},{5,13},{6,14},{7,15},{8,16},{9,17... | collective-permute-start | bytes 2949128 | tf_op jit(solution)/shard_map/ppermute | solution.py:202
  25.8 40.6 %collective-permute-start.3 = (bf16[4,192,640]{2,1,0:T(8,128)(2,1)S(1)}, bf16[4,192,640]{2,1,0:T(8,128)(2,1)}, u32[]{:S(2)}, u32[]{:S(2)}) collective-permute-start(bf16[4,192,640]{2,1,0:T(8,128)(2,1)S(1)} %bitcast.46), channel_id=1, source_target_pairs={{0,24},{1,25},{2,26},{3,27},{4,28},{5,29},{6,30},{7,31},{8,0},{9,1... | collective-permute-start | bytes 2949128 | tf_op jit(solution)/shard_map/ppermute | solution.py:203
  29.5 23.7 %collective-permute-start = (bf16[128,640]{1,0:T(8,128)(2,1)}, bf16[128,640]{1,0:T(8,128)(2,1)S(1)}, u32[]{:S(2)}, u32[]{:S(2)}) collective-permute-start(bf16[128,640]{1,0:T(8,128)(2,1)} %param.12), channel_id=1, source_target_pairs={{2,0},{4,2},{6,4},{8,6},{10,8},{12,10},{14,12},{16,14},{18,16},{20... | collective-permute-start | bytes 491528 | tf_op jit(solution)/shard_map/ppermute | solution.py:196
  35.7 16.9 %all-to-all-start = ((f32[32,1,64]{2,1,0:T(1,128)}), f32[32,1,64]{2,1,0:T(1,128)S(1)}, u32[]{:S(2)}, u32[]{:S(2)}) async-start(f32[32,1,64]{2,1,0:T(1,128)} %broadcast_in_dim.30), calls=%async_computation | async-start | bytes 32768 | tf_op jit(solution)/shard_map/all_to_all | solution.py:41
  53.1 3.7 %copy-start.11 = (pred[4]{0:T(512)(128)(4,1)S(1)}, pred[4]{0:T(512)(128)(4,1)}, u32[]{:S(2)}) copy-start(pred[4]{0:T(512)(128)(4,1)} %pad_add_fusion) | copy-start | bytes 16
  64.1 36.9 %collective-permute-start.2 = (bf16[2,192,640]{2,1,0:T(8,128)(2,1)}, bf16[2,192,640]{2,1,0:T(8,128)(2,1)}, u32[]{:S(2)}, u32[]{:S(2)}) collective-permute-start(bf16[2,192,640]{2,1,0:T(8,128)(2,1)} %slice.124), channel_id=1, source_target_pairs={{0,8},{1,9},{2,10},{3,11},{4,12},{5,13},{6,14},{7,15},{8,16},{9,17... | collective-permute-start | bytes 1474568 | tf_op jit(solution)/shard_map/ppermute | solution.py:204
  68.3 32.7 %collective-permute-start.4 = (bf16[2,192,640]{2,1,0:T(8,128)(2,1)}, bf16[2,192,640]{2,1,0:T(8,128)(2,1)}, u32[]{:S(2)}, u32[]{:S(2)}) collective-permute-start(bf16[2,192,640]{2,1,0:T(8,128)(2,1)} %slice.125), channel_id=1, source_target_pairs={{0,24},{1,25},{2,26},{3,27},{4,28},{5,29},{6,30},{7,31},{8,0},{9,1... | collective-permute-start | bytes 1474568 | tf_op jit(solution)/shard_map/ppermute | solution.py:205
  100.9 4.8 %copy-start.9 = (f32[160]{0:T(256)S(1)}, f32[160]{0:T(256)}, u32[]{:S(2)}) copy-start(f32[160]{0:T(256)} %get-tuple-element.37) | copy-start | bytes 1924
  100.9 4.8 %copy-start.10 = (f32[160]{0:T(256)S(1)}, f32[160]{0:T(256)}, u32[]{:S(2)}) copy-start(f32[160]{0:T(256)} %get-tuple-element.38) | copy-start | bytes 1924
  100.9 4.9 %copy-start.2 = (f32[320,640]{1,0:T(8,128)S(1)}, f32[320,640]{1,0:T(8,128)}, u32[]{:S(2)}) copy-start(f32[320,640]{1,0:T(8,128)} %param.18) | copy-start | bytes 2457604
  101.0 5.4 %copy-start.8 = (f32[640]{0:T(1024)S(1)}, f32[640]{0:T(1024)}, u32[]{:S(2)}) copy-start(f32[640]{0:T(1024)} %param.17) | copy-start | bytes 7684
  101.0 6.0 %copy-start.1 = (bf16[128,640]{1,0:T(8,128)(2,1)S(1)}, bf16[128,640]{1,0:T(8,128)(2,1)}, u32[]{:S(2)}) copy-start(bf16[128,640]{1,0:T(8,128)(2,1)} %param.12) | copy-start | bytes 491524
  102.8 35.8 %copy-start.6 = (f32[640]{0:T(1024)S(1)}, f32[640]{0:T(1024)}, u32[]{:S(2)}) copy-start(f32[640]{0:T(1024)} %param.20) | copy-start | bytes 7684
  102.8 35.8 %copy-start.7 = (f32[640]{0:T(1024)S(1)}, f32[640]{0:T(1024)}, u32[]{:S(2)}) copy-start(f32[640]{0:T(1024)} %param.19) | copy-start | bytes 7684
  102.9 4.1 %collective-permute-start.5 = (f32[128,640]{1,0:T(8,128)S(1)}, f32[128,640]{1,0:T(8,128)S(1)}, u32[]{:S(2)}, u32[]{:S(2)}) collective-permute-start(f32[128,640]{1,0:T(8,128)S(1)} %dynamic-slice_bitcast_fusion), channel_id=1, source_target_pairs={{0,1},{1,0},{2,3},{3,2},{4,5},{5,4},{6,7},{7,6},{8,9},{9,8},{10,11... | collective-permute-start | bytes 983048 | tf_op jit(solution)/shard_map/ppermute | solution.py:236
  108.5 29.7 %all-to-all-start.1 = ((f32[32,1,64]{2,1,0:T(1,128)}), f32[32,1,64]{2,1,0:T(1,128)S(1)}, u32[]{:S(2)}, u32[]{:S(2)}) async-start(f32[32,1,64]{2,1,0:T(1,128)} %broadcast_in_dim.58), calls=%async_computation.1 | async-start | bytes 32768 | tf_op jit(solution)/shard_map/all_to_all | solution.py:41
  131.8 16.6 %collective-permute-start.8 = (bf16[4,128,640]{2,1,0:T(8,128)(2,1)S(1)}, bf16[4,128,640]{2,1,0:T(8,128)(2,1)S(1)}, u32[]{:S(2)}, u32[]{:S(2)}) collective-permute-start(bf16[4,128,640]{2,1,0:T(8,128)(2,1)S(1)} %bitcast.50), channel_id=1, source_target_pairs={{0,24},{1,25},{2,26},{3,27},{4,28},{5,29},{6,30},{7,31},{8,0},{9,1... | collective-permute-start | bytes 1966088 | tf_op jit(solution)/shard_map/ppermute | solution.py:240
  136.2 17.6 %collective-permute-start.7 = (bf16[4,128,640]{2,1,0:T(8,128)(2,1)S(1)}, bf16[4,128,640]{2,1,0:T(8,128)(2,1)S(1)}, u32[]{:S(2)}, u32[]{:S(2)}) collective-permute-start(bf16[4,128,640]{2,1,0:T(8,128)(2,1)S(1)} %bitcast.51), channel_id=1, source_target_pairs={{0,8},{1,9},{2,10},{3,11},{4,12},{5,13},{6,14},{7,15},{8,16},{9,17... | collective-permute-start | bytes 1966088 | tf_op jit(solution)/shard_map/ppermute | solution.py:239
  148.5 13.5 %collective-permute-start.10 = (bf16[2,128,640]{2,1,0:T(8,128)(2,1)S(1)}, bf16[2,128,640]{2,1,0:T(8,128)(2,1)S(1)}, u32[]{:S(2)}, u32[]{:S(2)}) collective-permute-start(bf16[2,128,640]{2,1,0:T(8,128)(2,1)S(1)} %slice.130), channel_id=1, source_target_pairs={{0,24},{1,25},{2,26},{3,27},{4,28},{5,29},{6,30},{7,31},{8,0},{9,1... | collective-permute-start | bytes 983048 | tf_op jit(solution)/shard_map/ppermute | solution.py:242
  153.9 20.0 %copy-start.3 = (bf16[320,640]{1,0:T(8,128)(2,1)S(1)}, bf16[320,640]{1,0:T(8,128)(2,1)}, u32[]{:S(2)}) copy-start(bf16[320,640]{1,0:T(8,128)(2,1)} %param.22) | copy-start | bytes 1228804
  153.9 9.5 %collective-permute-start.9 = (bf16[2,128,640]{2,1,0:T(8,128)(2,1)S(1)}, bf16[2,128,640]{2,1,0:T(8,128)(2,1)S(1)}, u32[]{:S(2)}, u32[]{:S(2)}) collective-permute-start(bf16[2,128,640]{2,1,0:T(8,128)(2,1)S(1)} %slice.129), channel_id=1, source_target_pairs={{0,8},{1,9},{2,10},{3,11},{4,12},{5,13},{6,14},{7,15},{8,16},{9,17... | collective-permute-start | bytes 983048 | tf_op jit(solution)/shard_map/ppermute | solution.py:241
  156.1 5.8 %collective-permute-start.6 = (bf16[128,384]{1,0:T(8,128)(2,1)S(1)}, bf16[128,384]{1,0:T(8,128)(2,1)S(1)}, u32[]{:S(2)}, u32[]{:S(2)}) collective-permute-start(bf16[128,384]{1,0:T(8,128)(2,1)S(1)} %pad.23), channel_id=1, source_target_pairs={{0,1},{1,0},{2,3},{3,2},{4,5},{5,4},{6,7},{7,6},{8,9},{9,8},{10,11... | collective-permute-start | bytes 294920 | tf_op jit(solution)/shard_map/ppermute | solution.py:255
  168.0 6.8 %collective-permute-start.11 = (f32[128,384]{1,0:T(8,128)S(1)}, f32[128,384]{1,0:T(8,128)S(1)}, u32[]{:S(2)}, u32[]{:S(2)}) collective-permute-start(f32[128,384]{1,0:T(8,128)S(1)} %get-tuple-element.28), channel_id=1, source_target_pairs={{0,1},{1,0},{2,3},{3,2},{4,5},{5,4},{6,7},{7,6},{8,9},{9,8},{10,11... | collective-permute-start | bytes 589832 | tf_op jit(solution)/shard_map/ppermute | solution.py:270

commit v3 on v2

v3 whole, which is shorter than its diff:
```python
import math

import jax
import jax.numpy as jnp
from jax import lax
from jax.experimental import pallas as pl
from jax.experimental.pallas import tpu as pltpu
from jax.sharding import PartitionSpec as P

GROUPS = 32
HEADS = 5
HEAD_DIM = 64
TFREQ = 320
PER = 20
PEERS = 32
Z_GROUPS = [[8 * x + 2 * z + c for z in range(4)] for x in range(4) for c in range(2)]
CORE_GROUPS = [[2 * k, 2 * k + 1] for k in range(16)]
RIGHT = [(i, (i + 8) % PEERS) for i in range(PEERS)]
LEFT = [(i, (i + 24) % PEERS) for i in range(PEERS)]
SWAP = [(i, i ^ 1) for i in range(PEERS)]
OUTER = [(i, i - 2) for i in range(2, PEERS, 2)] + [(i, i + 2) for i in range(1, PEERS - 2, 2)]
ROWS = 192
LOW = -1e30
VMEM = pl.BlockSpec(memory_space=pltpu.VMEM)
SMEM = pl.BlockSpec(memory_space=pltpu.SMEM)


def group_map(first, transposed=False):
    shape = (128, 640) if transposed else (640, 128)
    channel = lax.broadcasted_iota(jnp.int32, shape, 1 if transposed else 0)
    low = (lax.broadcasted_iota(jnp.int32, shape, 0 if transposed else 1) - first) * PER
    return ((channel >= low) & (channel < low + PER)).astype(jnp.float32)


def exact(a, b):
    return jnp.dot(
        a, b, precision=lax.Precision.HIGHEST, preferred_element_type=jnp.float32
    )


def local_stats(values):
    count, width = values.shape
    summed = jnp.broadcast_to(values.sum(axis=0, keepdims=True), (8, width))
    mean = exact(summed, group_map(0)) / (count * PER)
    centered = values - exact(mean, group_map(0, True))[:1]
    spread = (centered * centered).sum(axis=0, keepdims=True)
    return mean + exact(jnp.broadcast_to(spread, (8, width)), group_map(GROUPS))


def merged_stats(every_ref, count, eps):
    every = every_ref[...]
    average = every.sum(axis=0) / PEERS
    shifted = every - average[None]
    between = (shifted * shifted).sum(axis=0) / PEERS
    var = pltpu.roll(average, 128 - GROUPS, 1) / (count * PER) + between
    lane = lax.broadcasted_iota(jnp.int32, var.shape, 1)
    inverse = jnp.where(lane < GROUPS, lax.rsqrt(var + eps), 0.0)
    spreading = group_map(0, True)
    return exact(average, spreading)[:1], exact(inverse, spreading)[:1]


def exchanged(stats):
    return lax.all_to_all(stats, "space", 0, 0, tiled=True)


def first_stats(latent_ref, out_ref):
    stats = local_stats(latent_ref[...].astype(jnp.float32))
    out_ref[...] = jnp.broadcast_to(stats[None], out_ref.shape)


def prepare(where_ref, every_ref, pair_ref, gain_ref, shift_ref, out_ref, flat_ref):
    core, chip = where_ref[0], where_ref[1]
    count = pair_ref.shape[2]
    mean, inverse = merged_stats(every_ref, count, 1e-05)
    factor = inverse * gain_ref[...]
    token = lax.broadcasted_iota(jnp.int32, (count, 640), 0)
    flat_ref[:, 5760:] = jnp.zeros((2 * count, 128), jnp.bfloat16)
    for row, (holder, which) in enumerate(((1, 1), (0, 0), (1, 0), (0, 1))):
        value = pair_ref[holder, which].astype(jnp.float32)
        value = (value - mean) * factor + shift_ref[...]
        value = value / (1.0 + jnp.exp(-value))
        if row == 0:
            value = jnp.where(chip > 0, value, 0.0)
        if row == 3:
            value = jnp.where(chip < PEERS // 2 - 1, value, 0.0)
        value = value.astype(jnp.bfloat16).astype(jnp.float32)
        shifts = (
            jnp.where(token == 0, 0.0, pltpu.roll(value, 1, 0)),
            value,
            jnp.where(token == count - 1, 0.0, pltpu.roll(value, count - 1, 0)),
        )
        for across, shifted in enumerate(shifts):
            shifted = shifted.astype(jnp.bfloat16)
            for out in range(2):
                down = row - out
                if 0 <= down <= 2:
                    at = (3 * down + across) * 640
                    flat_ref[out * count : (out + 1) * count, at : at + 640] = shifted
    for parity in range(2):

        @pl.when(core == parity)
        def _():
            for index in range(16):
                at = 360 * index + 180 * parity
                low = at // 128 * 128
                wide = flat_ref[:, low : low + 384]
                out_ref[index] = wide[:, at - low : at - low + ROWS]


def time_embed(timestep, time_weight):
    half = TFREQ // 2
    index = jnp.arange(half, dtype=jnp.float32)
    freq = jnp.exp(-math.log(10000.0) * index / half)
    angle = timestep.astype(jnp.float32)[0] * freq
    feats = jnp.concatenate([jnp.cos(angle), jnp.sin(angle)])[None, :]
    return jnp.dot(feats, time_weight, precision=lax.Precision.HIGHEST)


def dot32(a, b):
    return jnp.dot(a, b, preferred_element_type=jnp.float32)


def dot_t(a, b):
    return lax.dot_general(
        a, b, (((1,), (1,)), ((), ())), preferred_element_type=jnp.float32
    )


def conv_near(where_ref, blocks_ref, own_ref, left_ref, right_ref, out_ref):
    x = where_ref[2]
    total = None
    for step, ref in ((0, own_ref), (3, left_ref), (1, right_ref)):
        first = 4 * ((x + step) & 3)
        for z in range(4):
            part = dot32(blocks_ref[first + z], ref[z])
            total = part if total is None else total + part
    out_ref[...] = total


def conv_far(where_ref, blocks_ref, low_ref, high_ref, near_ref, kept_ref, given_ref):
    first = 4 * ((where_ref[2] + 2) & 3)
    total = near_ref[...]
    for z in range(4):
        ref = low_ref if z < 2 else high_ref
        total = total + dot32(blocks_ref[first + z], ref[z % 2])
    count = kept_ref.shape[0]
    kept_ref[...] = jnp.where(where_ref[0] == 0, total[:count], total[count:])
    given_ref[...] = jnp.where(where_ref[0] == 0, total[count:], total[:count])


def middle(kept_ref, other_ref, latent_ref, bias_ref, mid_ref, stats_ref):
    conv = kept_ref[...] + other_ref[...]
    mid = (latent_ref[...].astype(jnp.float32) + conv + bias_ref[...]).astype(jnp.bfloat16)
    mid_ref[...] = mid
    stats = local_stats(mid.astype(jnp.float32))
    stats_ref[...] = jnp.broadcast_to(stats[None], stats_ref.shape)


def project(every_ref, mid_ref, gain_ref, shift_ref, weight_ref, query_ref, fresh_ref):
    mid = mid_ref[...].astype(jnp.float32)
    mean, inverse = merged_stats(every_ref, mid.shape[0], 1e-06)
    normed = ((mid - mean) * (inverse * gain_ref[...]) + shift_ref[...]).astype(jnp.bfloat16)
    query = dot_t(normed, weight_ref[:384])
    lane = lax.broadcasted_iota(jnp.int32, query.shape, 1)
    query = jnp.where(lane < HEADS * HEAD_DIM, query, 0.0).astype(jnp.bfloat16)
    query_ref[...] = query * jnp.bfloat16(1.0 / math.sqrt(HEAD_DIM))
    fresh_ref[...] = dot_t(weight_ref[HEADS * HEAD_DIM :], normed).astype(jnp.bfloat16)


def attend(
    where_ref,
    q_ref,
    other_ref,
    own_ref,
    left_ref,
    right_ref,
    low_ref,
    high_ref,
    fresh_ref,
    out_ref,
    given_ref,
):
    my_z = where_ref[3]
    count = q_ref.shape[0]
    lane = lax.broadcasted_iota(jnp.int32, (2 * count, 128), 1)
    row = lax.broadcasted_iota(jnp.int32, (2 * count, 4 * count), 0)
    block = lax.broadcasted_iota(jnp.int32, (2 * count, 4 * count), 1) // count
    replaced = (row < count) & (block == my_z)
    held = (own_ref, left_ref, right_ref, low_ref, high_ref)
    outs = []
    for head in range(HEADS):
        at = 128 * (head // 2)
        mine = (lane < 64) if head % 2 == 0 else (lane >= 64)
        query = jnp.concatenate(
            [q_ref[:, at : at + 128], other_ref[:, at : at + 128]], axis=0
        )
        query = jnp.where(mine, query.astype(jnp.float32), 0.0).astype(jnp.bfloat16)
        scores = []
        for ref in held:
            keys = [ref[z, at : at + 128] for z in range(ref.shape[0])]
            scores.append(dot32(query, jnp.concatenate(keys, axis=1)))
        scores[0] = jnp.where(replaced, LOW, scores[0])
        fresh = dot32(query[:count], fresh_ref[at : at + 128])
        scores.append(jnp.concatenate([fresh, jnp.full((count, count), LOW, jnp.float32)], axis=0))
        peak = scores[0].max(axis=1, keepdims=True)
        for s in scores[1:]:
            peak = jnp.maximum(peak, s.max(axis=1, keepdims=True))
        total = jnp.zeros((2 * count, 1), jnp.float32)
        mixed = jnp.zeros((2 * count, 128), jnp.float32)
        v_at = HEADS * HEAD_DIM + at
        for s, ref in zip(scores, held + (fresh_ref,), strict=True):
            weights = jnp.exp(s - peak)
            total = total + weights.sum(axis=1, keepdims=True)
            if ref is fresh_ref:
                values = ref[v_at : v_at + 128]
            else:
                values = [ref[z, v_at : v_at + 128] for z in range(ref.shape[0])]
                values = jnp.concatenate(values, axis=1)
            if head == HEADS - 1:
                values = jnp.concatenate([values, jnp.zeros_like(values)], axis=0)
            mixed = mixed + dot_t(weights.astype(jnp.bfloat16), values)
        outs.append((mixed, peak, total))
    last = jnp.where(lane < 64, outs[4][0], 0.0)
    for head in range(HEADS):
        last = jnp.where(lane == 64 + head, outs[head][1], last)
        last = jnp.where(lane == 72 + head, outs[head][2], last)
    tiles = (
        jnp.where(lane < 64, outs[0][0], outs[1][0]),
        jnp.where(lane < 64, outs[2][0], outs[3][0]),
        last,
    )
    for tile, value in enumerate(tiles):
        out_ref[:, 128 * tile : 128 * (tile + 1)] = value[:count]
        given_ref[:, 128 * tile : 128 * (tile + 1)] = value[count:]


def finish(own_ref, other_ref, mid_ref, weight_ref, out_ref):
    count = mid_ref.shape[0]
    lane = lax.broadcasted_iota(jnp.int32, (count, 128), 1)
    factors = []
    for head in range(HEADS):
        peak1 = own_ref[:, 320 + head : 321 + head]
        peak2 = other_ref[:, 320 + head : 321 + head]
        peak = jnp.maximum(peak1, peak2)
        one, two = jnp.exp(peak1 - peak), jnp.exp(peak2 - peak)
        total = own_ref[:, 328 + head : 329 + head] * one
        total = total + other_ref[:, 328 + head : 329 + head] * two
        factors.append((one / total, two / total))
    result = mid_ref[...].astype(jnp.float32)
    for tile in range(3):
        first = factors[2 * tile]
        second = factors[min(2 * tile + 1, HEADS - 1)]
        at = 128 * tile
        mixed = own_ref[:, at : at + 128] * jnp.where(lane < 64, first[0], second[0])
        mixed = mixed + other_ref[:, at : at + 128] * jnp.where(lane < 64, first[1], second[1])
        mixed = mixed.astype(jnp.bfloat16)
        if tile == 2:
            mixed = mixed[:, :HEAD_DIM]
        result = result + dot32(mixed, weight_ref[at : at + mixed.shape[1]])
    out_ref[...] = result.astype(jnp.bfloat16)


def call(kernel, outs, smem, *args, scratch=()):
    return pl.pallas_call(
        kernel,
        out_shape=[jax.ShapeDtypeStruct(shape, dtype) for shape, dtype in outs],
        in_specs=[SMEM] * smem + [VMEM] * (len(args) - smem),
        out_specs=[VMEM] * len(outs),
        scratch_shapes=list(scratch),
        compiler_params=pltpu.CompilerParams(vmem_limit_bytes=40 * 1024 * 1024),
    )(*args)


def on_device(
    latent,
    timestep,
    norm1_gain,
    norm1_shift,
    conv_weight,
    conv_bias,
    time_weight,
    norm2_gain,
    norm2_shift,
    qkv_weight,
    out_weight,
    stale_kv,
):
    tok_dev, width = latent.shape
    feats = qkv_weight.shape[1] // 3
    me = lax.axis_index("space")
    where = jnp.stack([me % 2, me // 2, me // 8, (me // 2) % 4])
    rows = conv_weight.shape[0]
    f32, bf16 = jnp.float32, jnp.bfloat16
    table = ((PEERS, 8, 128), f32)

    weight = jnp.pad(conv_weight, ((0, ROWS - rows), (0, 0)))
    own_w = lax.all_gather(weight, "space", axis=0, axis_index_groups=Z_GROUPS)
    left_w = lax.ppermute(own_w, "space", RIGHT)
    right_w = lax.ppermute(own_w, "space", LEFT)
    outer = lax.ppermute(latent, "space", OUTER)
    (stats1,) = call(first_stats, [table], 0, latent)
    every1 = exchanged(stats1)
    pair = lax.all_gather(
        jnp.stack([latent, outer]), "space", axis=0, axis_index_groups=CORE_GROUPS
    )
    stale = stale_kv.transpose(0, 2, 1).reshape(2 * feats, tok_dev)
    stale, _ = lax.optimization_barrier((stale, own_w))
    own_kv = lax.all_to_all(
        jnp.broadcast_to(stale[None], (4, 2 * feats, tok_dev)),
        "space",
        0,
        0,
        axis_index_groups=Z_GROUPS,
        tiled=True,
    )
    every1, pair, left_w, right_w = lax.optimization_barrier((every1, pair, left_w, right_w))
    low_w = lax.ppermute(left_w[:2], "space", RIGHT)
    high_w = lax.ppermute(right_w[2:], "space", LEFT)
    (blocks,) = call(
        prepare,
        [((16, 2 * tok_dev, ROWS), bf16)],
        1,
        where,
        every1,
        pair,
        norm1_gain[None],
        norm1_shift[None],
        scratch=[pltpu.VMEM((2 * tok_dev, 5760 + 128), bf16)],
    )
    own_kv, _ = lax.optimization_barrier((own_kv, blocks))
    left_kv = lax.ppermute(own_kv, "space", RIGHT)
    right_kv = lax.ppermute(own_kv, "space", LEFT)

    step, _ = lax.optimization_barrier((timestep, blocks))
    bias = (conv_bias + time_embed(step, time_weight)).reshape(1, width)
    (near,) = call(
        conv_near, [((2 * tok_dev, width), f32)], 1, where, blocks, own_w, left_w, right_w
    )
    kept, given = call(
        conv_far, [((tok_dev, width), f32)] * 2, 1, where, blocks, low_w, high_w, near
    )
    other = lax.ppermute(given, "space", SWAP)
    mid, stats2 = call(middle, [((tok_dev, width), bf16), table], 0, kept, other, latent, bias)
    every2 = exchanged(stats2)
    low_kv = lax.ppermute(left_kv[:2], "space", RIGHT)
    high_kv = lax.ppermute(right_kv[2:], "space", LEFT)

    query, fresh = call(
        project,
        [((tok_dev, 384), bf16), ((2 * feats, tok_dev), bf16)],
        0,
        every2,
        mid,
        norm2_gain[None],
        norm2_shift[None],
        qkv_weight.T,
    )
    fresh_kv = fresh.reshape(2, feats, tok_dev).transpose(0, 2, 1)
    mine, theirs = call(
        attend,
        [((tok_dev, 384), f32)] * 2,
        1,
        where,
        query,
        lax.ppermute(query, "space", SWAP),
        own_kv,
        left_kv,
        right_kv,
        low_kv,
        high_kv,
        fresh,
    )
    other = lax.ppermute(theirs, "space", SWAP)
    (result,) = call(finish, [((tok_dev, width), bf16)], 0, mine, other, mid, out_weight)
    return (result, fresh_kv)


def solution(mesh):
    return jax.shard_map(
        on_device,
        mesh=mesh,
        in_specs=(
            P(("batch", "space"), None),
            P("batch"),
            P(),
            P(),
            P("space", None),
            P(),
            P(),
            P(),
            P(),
            P(),
            P(),
            P(None, ("batch", "space"), None),
        ),
        out_specs=(P(("batch", "space"), None), P(None, ("batch", "space"), None)),
        check_vma=False,
    )
```

time: 177 us -> 143 us (0.81)
  local copies, waits for them, and re-layouts: 40.6 us -> 13.1 us
  blocking collectives: 39.7 us -> 26.1 us
  Pallas kernels: 10.3 us -> 18.8 us
  other arithmetic: 6.07 us -> 0.25 us
  starting transfers between devices: 60.3 us -> 64 us
    all_gather x1 -> x0, blocking collectives: 15.8 us -> none  [on_device(): own_kv = lax.all_gather(stale, 'space', axis=0, axis_index_groups=Z_GROUPS)]
    concatenate x2 -> x0, local copies, waits for them, and re-layouts: 9.31 us -> none  [on_device(): jnp.concatenate([padded[t // 3:t // 3 + 2, t % 3:t % 3 + GW] for t in ran...]
    ppermute x1, waiting for transfers between devices: 9.25 us -> 0.01 us  [on_device(): right_kv = lax.ppermute(own_kv, 'space', LEFT)]
    pallas_call x4 -> x8, Pallas kernels: 10.3 us -> 18.8 us  [call(): pl.pallas_call(kernel, out_shape=[jax.ShapeDtypeStruct(shape, dtype) for...]
    reshape x5 -> x0, local copies, waits for them, and re-layouts: 7.87 us -> none  [the longest x1 7.49 us: on_device(): blocks = unfolded.reshape(2 * tok_dev, 16, 2, rows)]
    all_to_all x2 -> x3, starting transfers between devices: 17 us -> 23.7 us  [the longest x2 18.6 us: exchanged(): return lax.all_to_all(stats, 'space', 0, 0, tiled=True)]
    dynamic_slice x2 -> x0, local copies, waits for them, and re-layouts: 6.3 us -> none  [on_device(): lax.dynamic_index_in_dim(blocks, core, axis=2, keepdims=False)]
    ppermute x1, waiting for transfers between devices: 0.01 us -> 5.3 us  [on_device(): left_w = lax.ppermute(own_w, 'space', RIGHT)]
  transfers between devices with their start and end apart: 14 -> 15, of which waited for: 6 -> 7; matrix products, arithmetic and copies ran while one was open for 26% -> 4% of each run, Pallas kernels for 1% -> 7%
where the time goes in v3:
time: 143 us; the launch traced here: 142 us
  starting transfers between devices  64 us (45%)
  blocking collectives  26.1 us (18%)
  Pallas kernels  18.8 us (13%)
  waiting for transfers between devices  17.1 us (12%)
  local copies, waits for them, and re-layouts  13.1 us (9%)
  between operations  1.74 us (1%)
    all_gather x1, blocking collectives, on_device(): own_w = lax.all_gather(weight, 'space', axis=0, axis_index_groups=Z_GROUPS)  19.6 us
    pallas_call x8, Pallas kernels, call(): pl.pallas_call(kernel, out_shape=[jax.ShapeDtypeStruct(shape, dtype) for...  18.8 us
    all_to_all x2, starting transfers between devices, exchanged(): return lax.all_to_all(stats, 'space', 0, 0, tiled=True)  18.6 us
    unnamed x38, local copies, waits for them, and re-layouts  6.65 us
    all_gather x1, blocking collectives, on_device(): lax.all_gather(jnp.stack([latent, outer]), 'space', axis=0, axis_index_gr...  6.48 us
    ppermute x1, starting transfers between devices, on_device(): other = lax.ppermute(given, 'space', SWAP)  5.95 us
    ppermute x1, waiting for transfers between devices, on_device(): left_w = lax.ppermute(own_w, 'space', RIGHT)  5.3 us
    all_to_all x1, starting transfers between devices, on_device(): lax.all_to_all(jnp.broadcast_to(stale[None], (4, 2 * feats, tok_dev)), 's...  5.06 us
  transfers between devices with their start and end apart: 15, of which 7 were waited for; matrix products, arithmetic and copies ran while one was open for 4% of the time, Pallas kernels for 7%

profile of v3, /device:TPU:1, one launch (start us, length us, event | category | flops | bytes accessed | tf_op | source)
XLA Modules:
  0.0 141.6 jit_solution(4427135514672383502)
XLA Ops:
  1.6 1.6 %shard_map.131 = f32[32,8,128]{2,1,0:T(8,128)} custom-call(bf16[128,640]{1,0:T(8,128)(2,1)S(1)} %copy-done.8), custom_call_target="tpu_custom_call" | custom-call | tf_op jit(solution)/shard_map/pallas_call | solution.py:264
  3.3 10.5 %all-to-all-start = ((f32[32,8,128]{2,1,0:T(8,128)}), f32[32,8,128]{2,1,0:T(8,128)S(1)}, u32[]{:S(2)}, u32[]{:S(2)}) async-start(f32[32,8,128]{2,1,0:T(8,128)} %shard_map.131), calls=%async_computation | async-start | bytes 262144 | tf_op jit(solution)/shard_map/all_to_all | solution.py:63
  14.8 19.6 %all-gather.1 = bf16[768,640]{1,0:T(8,128)(2,1)S(1)} all-gather(bf16[192,640]{1,0:T(8,128)(2,1)S(1)} %pad.4), channel_id=3, replica_groups={{0,2,4,6},{1,3,5,7},{8,10,12,14},{9,11,13,15},{16,18,20,22},{17,19,21,2..., dimensions={0}, use_global_device_ids=true | all-gather | bytes 1228800 | tf_op jit(solution)/shard_map/all_gather | solution.py:297
  35.4 5.1 %all-to-all-start.2 = ((bf16[4,640,128]{2,1,0:T(8,128)(2,1)}), bf16[4,640,128]{2,1,0:T(8,128)(2,1)}, u32[]{:S(2)}, u32[]{:S(2)}) async-start(bf16[4,640,128]{2,1,0:T(8,128)(2,1)} %broadcast_in_dim.24), calls=%async_computation.2 | async-start | bytes 1310720 | tf_op jit(solution)/shard_map/all_to_all | solution.py:308
  40.4 3.3 %collective-permute-start.1 = (bf16[4,192,640]{2,1,0:T(8,128)(2,1)S(1)}, bf16[4,192,640]{2,1,0:T(8,128)(2,1)S(1)}, u32[]{:S(2)}, u32[]{:S(2)}) collective-permute-start(bf16[4,192,640]{2,1,0:T(8,128)(2,1)S(1)} %bitcast.18), channel_id=1, source_target_pairs={{0,8},{1,9},{2,10},{3,11},{4,12},{5,13},{6,14},{7,15},{8,16},{9,17... | collective-permute-start | bytes 2949128 | tf_op jit(solution)/shard_map/ppermute | solution.py:298
  43.7 3.3 %collective-permute-start.2 = (bf16[4,192,640]{2,1,0:T(8,128)(2,1)S(1)}, bf16[4,192,640]{2,1,0:T(8,128)(2,1)S(1)}, u32[]{:S(2)}, u32[]{:S(2)}) collective-permute-start(bf16[4,192,640]{2,1,0:T(8,128)(2,1)S(1)} %bitcast.19), channel_id=1, source_target_pairs={{0,24},{1,25},{2,26},{3,27},{4,28},{5,29},{6,30},{7,31},{8,0},{9,1... | collective-permute-start | bytes 2949128 | tf_op jit(solution)/shard_map/ppermute | solution.py:299
  47.1 3.4 %collective-permute-start = (bf16[128,640]{1,0:T(8,128)(2,1)S(1)}, bf16[128,640]{1,0:T(8,128)(2,1)S(1)}, u32[]{:S(2)}, u32[]{:S(2)}) collective-permute-start(bf16[128,640]{1,0:T(8,128)(2,1)S(1)} %copy-done.9), channel_id=1, source_target_pairs={{2,0},{4,2},{6,4},{8,6},{10,8},{12,10},{14,12},{16,14},{18,16},{20... | collective-permute-start | bytes 491528 | tf_op jit(solution)/shard_map/ppermute | solution.py:300
  50.5 3.0 %collective-permute-done = bf16[128,640]{1,0:T(8,128)(2,1)S(1)} collective-permute-done((bf16[128,640]{1,0:T(8,128)(2,1)S(1)}, bf16[128,640]{1,0:T(8,128)(2,1)S(1)}, u32[]{:S(2)}, u32[]{:S(2)}) %collective-permute-start) | collective-permute-done | bytes 163872 | tf_op jit(solution)/shard_map/ppermute | solution.py:300
  53.5 6.5 %all-gather = bf16[4,128,640]{2,1,0:T(8,128)(2,1)} all-gather(bf16[2,128,640]{2,1,0:T(8,128)(2,1)S(1)} %pad_maximum_fusion), channel_id=2, replica_groups={{0,1},{2,3},{4,5},{6,7},{8,9},{10,11},{12,13},{14,15},{16,17},{18,19},{..., dimensions={0}, use_global_device_ids=true | all-gather | bytes 983040 | tf_op jit(solution)/shard_map/all_gather | solution.py:303
  60.0 5.3 %collective-permute-done.1.left_ref = bf16[4,192,640]{2,1,0:T(8,128)(2,1)S(1)} collective-permute-done((bf16[4,192,640]{2,1,0:T(8,128)(2,1)S(1)}, bf16[4,192,640]{2,1,0:T(8,128)(2,1)S(1)}, u32[]{:S(2)}, u32[]{:S(2)}) %collective-permute-start.1) | collective-permute-done | bytes 983072 | tf_op jit(solution)/shard_map/ppermute | solution.py:298
  65.3 1.7 %collective-permute-done.2.right_ref = bf16[4,192,640]{2,1,0:T(8,128)(2,1)S(1)} collective-permute-done((bf16[4,192,640]{2,1,0:T(8,128)(2,1)S(1)}, bf16[4,192,640]{2,1,0:T(8,128)(2,1)S(1)}, u32[]{:S(2)}, u32[]{:S(2)}) %collective-permute-start.2) | collective-permute-done | bytes 983072 | tf_op jit(solution)/shard_map/ppermute | solution.py:299
  67.8 3.1 %collective-permute-start.3 = (bf16[2,192,640]{2,1,0:T(8,128)(2,1)}, bf16[2,192,640]{2,1,0:T(8,128)(2,1)}, u32[]{:S(2)}, u32[]{:S(2)}) collective-permute-start(bf16[2,192,640]{2,1,0:T(8,128)(2,1)} %slice.12), channel_id=1, source_target_pairs={{0,8},{1,9},{2,10},{3,11},{4,12},{5,13},{6,14},{7,15},{8,16},{9,17... | collective-permute-start | bytes 1474568 | tf_op jit(solution)/shard_map/ppermute | solution.py:317
  71.8 3.3 %collective-permute-start.4 = (bf16[2,192,640]{2,1,0:T(8,128)(2,1)}, bf16[2,192,640]{2,1,0:T(8,128)(2,1)}, u32[]{:S(2)}, u32[]{:S(2)}) collective-permute-start(bf16[2,192,640]{2,1,0:T(8,128)(2,1)} %slice.13), channel_id=1, source_target_pairs={{0,24},{1,25},{2,26},{3,27},{4,28},{5,29},{6,30},{7,31},{8,0},{9,1... | collective-permute-start | bytes 1474568 | tf_op jit(solution)/shard_map/ppermute | solution.py:318
  76.4 2.7 %shard_map.132.blocks_ref = bf16[16,256,192]{2,1,0:T(8,128)(2,1)S(1)} custom-call(s32[4]{0:T(128)S(1)} %pad_add_fusion.where_ref, f32[32,8,128]{2,1,0:T(8,128)S(1)} %all-to-all-done.every_ref, bf16[2,2,128,640]{3,2,1,0:T(8,128)(2,1)S(1)} %bitcast.21, f32[1,640]{1,0:T(1,128)S(1)} %broadcast_in_dim.20.gain_ref, f32[1,640]{1,0:T(1,128)S(1)} %broadcast_in_dim.21.shift_ref), custom_call_target="tpu_custom_call" | custom-call | tf_op jit(solution)/shard_map/pallas_call | solution.py:264
  79.1 3.3 %collective-permute-start.8 = (bf16[4,640,128]{2,1,0:T(8,128)(2,1)}, bf16[4,640,128]{2,1,0:T(8,128)(2,1)}, u32[]{:S(2)}, u32[]{:S(2)}) collective-permute-start(bf16[4,640,128]{2,1,0:T(8,128)(2,1)} %all-to-all-done.2.own_ref), channel_id=1, source_target_pairs={{0,24},{1,25},{2,26},{3,27},{4,28},{5,29},{6,30},{7,31},{8,0},{9,1... | collective-permute-start | bytes 1966088 | tf_op jit(solution)/shard_map/ppermute | solution.py:332
  82.5 1.9 %collective-permute-start.7 = (bf16[4,640,128]{2,1,0:T(8,128)(2,1)}, bf16[4,640,128]{2,1,0:T(8,128)(2,1)}, u32[]{:S(2)}, u32[]{:S(2)}) collective-permute-start(bf16[4,640,128]{2,1,0:T(8,128)(2,1)} %all-to-all-done.2.own_ref), channel_id=1, source_target_pairs={{0,8},{1,9},{2,10},{3,11},{4,12},{5,13},{6,14},{7,15},{8,16},{9,17... | collective-permute-start | bytes 1966088 | tf_op jit(solution)/shard_map/ppermute | solution.py:331
  86.3 1.2 copy-done.5
  87.5 1.2 copy-done.7
  88.7 1.9 %shard_map.133.near_ref = f32[256,640]{1,0:T(8,128)S(1)} custom-call(s32[4]{0:T(128)S(1)} %pad_add_fusion.where_ref, bf16[16,256,192]{2,1,0:T(8,128)(2,1)S(1)} %shard_map.132.blocks_ref, bf16[4,192,640]{2,1,0:T(8,128)(2,1)S(1)} %bitcast.20, bf16[4,192,640]{2,1,0:T(8,128)(2,1)S(1)} %copy-done.5, bf16[4,192,640]{2,1,0:T(8,128)(2,1)S(1)} %copy-done.7), custom_call_target="tpu_custom_call" | custom-call | tf_op jit(solution)/shard_map/pallas_call | solution.py:264
  90.6 1.8 %shard_map.134 = (f32[128,640]{1,0:T(8,128)S(1)}, f32[128,640]{1,0:T(8,128)S(1)}) custom-call(s32[4]{0:T(128)S(1)} %pad_add_fusion.where_ref, bf16[16,256,192]{2,1,0:T(8,128)(2,1)S(1)} %shard_map.132.blocks_ref, bf16[2,192,640]{2,1,0:T(8,128)(2,1)} %collective-permute-done.3.low_ref, bf16[2,192,640]{2,1,0:T(8,128)(2,1)} %collective-permute-done.4.high_ref, ...), custom_call_target="tpu_custom_call" | custom-call | tf_op jit(solution)/shard_map/pallas_call | solution.py:264
  92.4 5.9 %collective-permute-start.5 = (f32[128,640]{1,0:T(8,128)S(1)}, f32[128,640]{1,0:T(8,128)S(1)}, u32[]{:S(2)}, u32[]{:S(2)}) collective-permute-start(f32[128,640]{1,0:T(8,128)S(1)} %get-tuple-element.22), channel_id=1, source_target_pairs={{0,1},{1,0},{2,3},{3,2},{4,5},{5,4},{6,7},{7,6},{8,9},{9,8},{10,11... | collective-permute-start | bytes 983048 | tf_op jit(solution)/shard_map/ppermute | solution.py:342
  99.6 1.7 %shard_map.135 = (bf16[128,640]{1,0:T(8,128)(2,1)S(1)}, f32[32,8,128]{2,1,0:T(8,128)}) custom-call(f32[128,640]{1,0:T(8,128)S(1)} %get-tuple-element.21.kept_ref, f32[128,640]{1,0:T(8,128)S(1)} %collective-permute-done.5.other_ref, bf16[128,640]{1,0:T(8,128)(2,1)S(1)} %copy-done.9, f32[1,640]{1,0:T(1,128)S(1)} %add.19.bias_ref), custom_call_target="tpu_custom_call" | custom-call | tf_op jit(solution)/shard_map/pallas_call | solution.py:264
  101.3 8.1 %all-to-all-start.1 = ((f32[32,8,128]{2,1,0:T(8,128)}), f32[32,8,128]{2,1,0:T(8,128)S(1)}, u32[]{:S(2)}, u32[]{:S(2)}) async-start(f32[32,8,128]{2,1,0:T(8,128)} %get-tuple-element.24), calls=%async_computation.1 | async-start | bytes 262144 | tf_op jit(solution)/shard_map/all_to_all | solution.py:63
  110.4 4.5 %collective-permute-start.10 = (bf16[2,640,128]{2,1,0:T(8,128)(2,1)S(1)}, bf16[2,640,128]{2,1,0:T(8,128)(2,1)S(1)}, u32[]{:S(2)}, u32[]{:S(2)}) collective-permute-start(bf16[2,640,128]{2,1,0:T(8,128)(2,1)S(1)} %slice.17), channel_id=1, source_target_pairs={{0,24},{1,25},{2,26},{3,27},{4,28},{5,29},{6,30},{7,31},{8,0},{9,1... | collective-permute-start | bytes 983048 | tf_op jit(solution)/shard_map/ppermute | solution.py:346
  115.0 1.7 %slice.16 = bf16[2,640,128]{2,1,0:T(8,128)(2,1)} slice(bf16[4,640,128]{2,1,0:T(8,128)(2,1)} %collective-permute-done.7.left_ref), slice={[0:2], [0:640], [0:128]} | slice | bytes 655360 | tf_op jit(solution)/shard_map/slice | solution.py:345
  116.7 1.9 %collective-permute-start.9 = (bf16[2,640,128]{2,1,0:T(8,128)(2,1)}, bf16[2,640,128]{2,1,0:T(8,128)(2,1)S(1)}, u32[]{:S(2)}, u32[]{:S(2)}) collective-permute-start(bf16[2,640,128]{2,1,0:T(8,128)(2,1)} %slice.16), channel_id=1, source_target_pairs={{0,8},{1,9},{2,10},{3,11},{4,12},{5,13},{6,14},{7,15},{8,16},{9,17... | collective-permute-start | bytes 983048 | tf_op jit(solution)/shard_map/ppermute | solution.py:345
  118.7 1.6 %shard_map.136 = (bf16[128,384]{1,0:T(8,128)(2,1)S(1)}, bf16[640,128]{1,0:T(8,128)(2,1)}) custom-call(f32[32,8,128]{2,1,0:T(8,128)S(1)} %all-to-all-done.1.every_ref, bf16[128,640]{1,0:T(8,128)(2,1)S(1)} %get-tuple-element.25.mid_ref, f32[1,640]{1,0:T(1,128)S(1)} %broadcast_in_dim.22.gain_ref, f32[1,640]{1,0:T(1,128)S(1)} %broadcast_in_dim.23.shift_ref, ...), custom_call_target="tpu_custom_call" | custom-call | tf_op jit(solution)/shard_map/pallas_call | solution.py:264
  120.3 2.7 %collective-permute-start.6 = (bf16[128,384]{1,0:T(8,128)(2,1)S(1)}, bf16[128,384]{1,0:T(8,128)(2,1)S(1)}, u32[]{:S(2)}, u32[]{:S(2)}) collective-permute-start(bf16[128,384]{1,0:T(8,128)(2,1)S(1)} %get-tuple-element.26.q_ref), channel_id=1, source_target_pairs={{0,1},{1,0},{2,3},{3,2},{4,5},{5,4},{6,7},{7,6},{8,9},{9,8},{10,11... | collective-permute-start | bytes 294920 | tf_op jit(solution)/shard_map/ppermute | solution.py:365
  123.8 4.8 %collective-permute-done.9.low_ref = bf16[2,640,128]{2,1,0:T(8,128)(2,1)S(1)} collective-permute-done((bf16[2,640,128]{2,1,0:T(8,128)(2,1)}, bf16[2,640,128]{2,1,0:T(8,128)(2,1)S(1)}, u32[]{:S(2)}, u32[]{:S(2)}) %collective-permute-start.9) | collective-permute-done | bytes 327712 | tf_op jit(solution)/shard_map/ppermute | solution.py:345
  129.6 6.3 %shard_map.137 = (f32[128,384]{1,0:T(8,128)S(1)}, f32[128,384]{1,0:T(8,128)S(1)}) custom-call(s32[4]{0:T(128)S(1)} %pad_add_fusion.where_ref, bf16[128,384]{1,0:T(8,128)(2,1)S(1)} %get-tuple-element.26.q_ref, bf16[128,384]{1,0:T(8,128)(2,1)S(1)} %collective-permute-done.6.other_ref, bf16[4,640,128]{2,1,0:T(8,128)(2,1)} %all-to-all-done.2.own_ref, ...), custom_call_target="tpu_custom_call" | custom-call | tf_op jit(solution)/shard_map/pallas_call | solution.py:264
  135.8 3.4 %collective-permute-start.11 = (f32[128,384]{1,0:T(8,128)S(1)}, f32[128,384]{1,0:T(8,128)S(1)}, u32[]{:S(2)}, u32[]{:S(2)}) collective-permute-start(f32[128,384]{1,0:T(8,128)S(1)} %get-tuple-element.31), channel_id=1, source_target_pairs={{0,1},{1,0},{2,3},{3,2},{4,5},{5,4},{6,7},{7,6},{8,9},{9,8},{10,11... | collective-permute-start | bytes 589832 | tf_op jit(solution)/shard_map/ppermute | solution.py:373
  140.3 1.3 shard_map.138
  (64 shorter events, 12.1 us)
Async XLA Ops:
  0.6 97.9 %copy-start = (f32[320,640]{1,0:T(8,128)S(1)}, f32[320,640]{1,0:T(8,128)}, u32[]{:S(2)}) copy-start(f32[320,640]{1,0:T(8,128)} %param.18) | copy-start | bytes 2457604
  1.6 32.7 %copy-start.13 = (bf16[2,128,320]{1,2,0:T(8,128)(2,1)S(1)}, bf16[2,128,320]{1,2,0:T(8,128)(2,1)}, u32[]{:S(2)}) copy-start(bf16[2,128,320]{1,2,0:T(8,128)(2,1)} %param.23) | copy-start | bytes 491524
  3.3 43.8 %copy-start.9 = (bf16[128,640]{1,0:T(8,128)(2,1)S(1)}, bf16[128,640]{1,0:T(8,128)(2,1)}, u32[]{:S(2)}) copy-start(bf16[128,640]{1,0:T(8,128)(2,1)} %latent_ref.3) | copy-start | bytes 491524
  3.3 31.1 %all-to-all-start = ((f32[32,8,128]{2,1,0:T(8,128)}), f32[32,8,128]{2,1,0:T(8,128)S(1)}, u32[]{:S(2)}, u32[]{:S(2)}) async-start(f32[32,8,128]{2,1,0:T(8,128)} %shard_map.131), calls=%async_computation | async-start | bytes 262144 | tf_op jit(solution)/shard_map/all_to_all | solution.py:63
  34.3 33.5 %copy-start.1 = (bf16[768,640]{1,0:T(8,128)(2,1)}, bf16[768,640]{1,0:T(8,128)(2,1)S(1)}, u32[]{:S(2)}) copy-start(bf16[768,640]{1,0:T(8,128)(2,1)S(1)} %all-gather.1) | copy-start | bytes 2949124
  35.4 43.7 %all-to-all-start.2 = ((bf16[4,640,128]{2,1,0:T(8,128)(2,1)}), bf16[4,640,128]{2,1,0:T(8,128)(2,1)}, u32[]{:S(2)}, u32[]{:S(2)}) async-start(bf16[4,640,128]{2,1,0:T(8,128)(2,1)} %broadcast_in_dim.24), calls=%async_computation.2 | async-start | bytes 1310720 | tf_op jit(solution)/shard_map/all_to_all | solution.py:308
  40.4 34.8 %copy-start.15 = (f32[640]{0:T(1024)S(1)}, f32[640]{0:T(1024)}, u32[]{:S(2)}) copy-start(f32[640]{0:T(1024)} %param.14) | copy-start | bytes 7684
  40.4 34.8 %copy-start.16 = (f32[640]{0:T(1024)S(1)}, f32[640]{0:T(1024)}, u32[]{:S(2)}) copy-start(f32[640]{0:T(1024)} %param.15) | copy-start | bytes 7684
  40.4 24.8 %collective-permute-start.1 = (bf16[4,192,640]{2,1,0:T(8,128)(2,1)S(1)}, bf16[4,192,640]{2,1,0:T(8,128)(2,1)S(1)}, u32[]{:S(2)}, u32[]{:S(2)}) collective-permute-start(bf16[4,192,640]{2,1,0:T(8,128)(2,1)S(1)} %bitcast.18), channel_id=1, source_target_pairs={{0,8},{1,9},{2,10},{3,11},{4,12},{5,13},{6,14},{7,15},{8,16},{9,17... | collective-permute-start | bytes 2949128 | tf_op jit(solution)/shard_map/ppermute | solution.py:298
  43.7 23.2 %collective-permute-start.2 = (bf16[4,192,640]{2,1,0:T(8,128)(2,1)S(1)}, bf16[4,192,640]{2,1,0:T(8,128)(2,1)S(1)}, u32[]{:S(2)}, u32[]{:S(2)}) collective-permute-start(bf16[4,192,640]{2,1,0:T(8,128)(2,1)S(1)} %bitcast.19), channel_id=1, source_target_pairs={{0,24},{1,25},{2,26},{3,27},{4,28},{5,29},{6,30},{7,31},{8,0},{9,1... | collective-permute-start | bytes 2949128 | tf_op jit(solution)/shard_map/ppermute | solution.py:299
  47.1 6.4 %collective-permute-start = (bf16[128,640]{1,0:T(8,128)(2,1)S(1)}, bf16[128,640]{1,0:T(8,128)(2,1)S(1)}, u32[]{:S(2)}, u32[]{:S(2)}) collective-permute-start(bf16[128,640]{1,0:T(8,128)(2,1)S(1)} %copy-done.9), channel_id=1, source_target_pairs={{2,0},{4,2},{6,4},{8,6},{10,8},{12,10},{14,12},{16,14},{18,16},{20... | collective-permute-start | bytes 491528 | tf_op jit(solution)/shard_map/ppermute | solution.py:300
  65.3 5.7 %copy-start.4 = (bf16[4,192,640]{2,1,0:T(8,128)(2,1)}, bf16[4,192,640]{2,1,0:T(8,128)(2,1)S(1)}, u32[]{:S(2)}) copy-start(bf16[4,192,640]{2,1,0:T(8,128)(2,1)S(1)} %collective-permute-done.1.left_ref) | copy-start | bytes 2949124
  66.9 4.9 %copy-start.6 = (bf16[4,192,640]{2,1,0:T(8,128)(2,1)}, bf16[4,192,640]{2,1,0:T(8,128)(2,1)S(1)}, u32[]{:S(2)}) copy-start(bf16[4,192,640]{2,1,0:T(8,128)(2,1)S(1)} %collective-permute-done.2.right_ref) | copy-start | bytes 2949124
  67.8 22.8 %collective-permute-start.3 = (bf16[2,192,640]{2,1,0:T(8,128)(2,1)}, bf16[2,192,640]{2,1,0:T(8,128)(2,1)}, u32[]{:S(2)}, u32[]{:S(2)}) collective-permute-start(bf16[2,192,640]{2,1,0:T(8,128)(2,1)} %slice.12), channel_id=1, source_target_pairs={{0,8},{1,9},{2,10},{3,11},{4,12},{5,13},{6,14},{7,15},{8,16},{9,17... | collective-permute-start | bytes 1474568 | tf_op jit(solution)/shard_map/ppermute | solution.py:317
  71.8 18.8 %collective-permute-start.4 = (bf16[2,192,640]{2,1,0:T(8,128)(2,1)}, bf16[2,192,640]{2,1,0:T(8,128)(2,1)}, u32[]{:S(2)}, u32[]{:S(2)}) collective-permute-start(bf16[2,192,640]{2,1,0:T(8,128)(2,1)} %slice.13), channel_id=1, source_target_pairs={{0,24},{1,25},{2,26},{3,27},{4,28},{5,29},{6,30},{7,31},{8,0},{9,1... | collective-permute-start | bytes 1474568 | tf_op jit(solution)/shard_map/ppermute | solution.py:318
  75.3 1.1 copy-start.3
  79.1 30.3 %collective-permute-start.8 = (bf16[4,640,128]{2,1,0:T(8,128)(2,1)}, bf16[4,640,128]{2,1,0:T(8,128)(2,1)}, u32[]{:S(2)}, u32[]{:S(2)}) collective-permute-start(bf16[4,640,128]{2,1,0:T(8,128)(2,1)} %all-to-all-done.2.own_ref), channel_id=1, source_target_pairs={{0,24},{1,25},{2,26},{3,27},{4,28},{5,29},{6,30},{7,31},{8,0},{9,1... | collective-permute-start | bytes 1966088 | tf_op jit(solution)/shard_map/ppermute | solution.py:332
  82.5 32.5 %collective-permute-start.7 = (bf16[4,640,128]{2,1,0:T(8,128)(2,1)}, bf16[4,640,128]{2,1,0:T(8,128)(2,1)}, u32[]{:S(2)}, u32[]{:S(2)}) collective-permute-start(bf16[4,640,128]{2,1,0:T(8,128)(2,1)} %all-to-all-done.2.own_ref), channel_id=1, source_target_pairs={{0,8},{1,9},{2,10},{3,11},{4,12},{5,13},{6,14},{7,15},{8,16},{9,17... | collective-permute-start | bytes 1966088 | tf_op jit(solution)/shard_map/ppermute | solution.py:331
  85.1 1.2 copy-start.2
  86.3 1.2 copy-start.5
  87.5 1.2 copy-start.7
  90.6 8.5 %copy-start.14 = (f32[640]{0:T(1024)S(1)}, f32[640]{0:T(1024)}, u32[]{:S(2)}) copy-start(f32[640]{0:T(1024)} %param.17) | copy-start | bytes 7684
  92.4 26.2 %copy-start.17 = (f32[640]{0:T(1024)S(1)}, f32[640]{0:T(1024)}, u32[]{:S(2)}) copy-start(f32[640]{0:T(1024)} %param.19) | copy-start | bytes 7684
  92.4 26.2 %copy-start.18 = (f32[640]{0:T(1024)S(1)}, f32[640]{0:T(1024)}, u32[]{:S(2)}) copy-start(f32[640]{0:T(1024)} %param.20) | copy-start | bytes 7684
  92.4 26.3 %copy-start.10 = (bf16[640,960]{0,1:T(8,128)(2,1)S(1)}, bf16[640,960]{0,1:T(8,128)(2,1)}, u32[]{:S(2)}) copy-start(bf16[640,960]{0,1:T(8,128)(2,1)} %param.21) | copy-start | bytes 3686404
  92.4 7.2 %collective-permute-start.5 = (f32[128,640]{1,0:T(8,128)S(1)}, f32[128,640]{1,0:T(8,128)S(1)}, u32[]{:S(2)}, u32[]{:S(2)}) collective-permute-start(f32[128,640]{1,0:T(8,128)S(1)} %get-tuple-element.22), channel_id=1, source_target_pairs={{0,1},{1,0},{2,3},{3,2},{4,5},{5,4},{6,7},{7,6},{8,9},{9,8},{10,11... | collective-permute-start | bytes 983048 | tf_op jit(solution)/shard_map/ppermute | solution.py:342
  101.3 17.4 %all-to-all-start.1 = ((f32[32,8,128]{2,1,0:T(8,128)}), f32[32,8,128]{2,1,0:T(8,128)S(1)}, u32[]{:S(2)}, u32[]{:S(2)}) async-start(f32[32,8,128]{2,1,0:T(8,128)} %get-tuple-element.24), calls=%async_computation.1 | async-start | bytes 262144 | tf_op jit(solution)/shard_map/all_to_all | solution.py:63
  110.4 13.4 %collective-permute-start.10 = (bf16[2,640,128]{2,1,0:T(8,128)(2,1)S(1)}, bf16[2,640,128]{2,1,0:T(8,128)(2,1)S(1)}, u32[]{:S(2)}, u32[]{:S(2)}) collective-permute-start(bf16[2,640,128]{2,1,0:T(8,128)(2,1)S(1)} %slice.17), channel_id=1, source_target_pairs={{0,24},{1,25},{2,26},{3,27},{4,28},{5,29},{6,30},{7,31},{8,0},{9,1... | collective-permute-start | bytes 983048 | tf_op jit(solution)/shard_map/ppermute | solution.py:346
  116.7 11.9 %collective-permute-start.9 = (bf16[2,640,128]{2,1,0:T(8,128)(2,1)}, bf16[2,640,128]{2,1,0:T(8,128)(2,1)S(1)}, u32[]{:S(2)}, u32[]{:S(2)}) collective-permute-start(bf16[2,640,128]{2,1,0:T(8,128)(2,1)} %slice.16), channel_id=1, source_target_pairs={{0,8},{1,9},{2,10},{3,11},{4,12},{5,13},{6,14},{7,15},{8,16},{9,17... | collective-permute-start | bytes 983048 | tf_op jit(solution)/shard_map/ppermute | solution.py:345
  118.7 21.6 %copy-start.11 = (bf16[320,640]{1,0:T(8,128)(2,1)S(1)}, bf16[320,640]{1,0:T(8,128)(2,1)}, u32[]{:S(2)}) copy-start(bf16[320,640]{1,0:T(8,128)(2,1)} %weight_ref.1) | copy-start | bytes 1228804
  120.3 3.5 %collective-permute-start.6 = (bf16[128,384]{1,0:T(8,128)(2,1)S(1)}, bf16[128,384]{1,0:T(8,128)(2,1)S(1)}, u32[]{:S(2)}, u32[]{:S(2)}) collective-permute-start(bf16[128,384]{1,0:T(8,128)(2,1)S(1)} %get-tuple-element.26.q_ref), channel_id=1, source_target_pairs={{0,1},{1,0},{2,3},{3,2},{4,5},{5,4},{6,7},{7,6},{8,9},{9,8},{10,11... | collective-permute-start | bytes 294920 | tf_op jit(solution)/shard_map/ppermute | solution.py:365
  135.8 4.5 %collective-permute-start.11 = (f32[128,384]{1,0:T(8,128)S(1)}, f32[128,384]{1,0:T(8,128)S(1)}, u32[]{:S(2)}, u32[]{:S(2)}) collective-permute-start(f32[128,384]{1,0:T(8,128)S(1)} %get-tuple-element.31), channel_id=1, source_target_pairs={{0,1},{1,0},{2,3},{3,2},{4,5},{5,4},{6,7},{7,6},{8,9},{9,8},{10,11... | collective-permute-start | bytes 589832 | tf_op jit(solution)/shard_map/ppermute | solution.py:373
  (2 other events, 1.9 us)

commit v4 on v3

--- a/solution.py
+++ b/solution.py
@@ -126,26 +126,38 @@
     )
 
 
-def conv_near(where_ref, blocks_ref, own_ref, left_ref, right_ref, out_ref):
-    x = where_ref[2]
+def convolve(
+    where_ref,
+    blocks_ref,
+    own_ref,
+    left_ref,
+    right_ref,
+    low_ref,
+    high_ref,
+    kept_ref,
+    given_ref,
+    held_ref,
+    sems,
+):
+    core, x = where_ref[0], where_ref[2]
+    count = kept_ref.shape[0]
+    sources = ((own_ref, 0, 0), (left_ref, 3, 0), (right_ref, 1, 0), (low_ref, 2, 0), (high_ref, 2, 2))
+    copies, at = [], 0
+    for index, (ref, _, _) in enumerate(sources):
+        size = ref.shape[0]
+        copy = pltpu.make_async_copy(ref, held_ref.at[at : at + size], sems.at[index])
+        copy.start()
+        copies.append((copy, at, size))
+        at += size
     total = None
-    for step, ref in ((0, own_ref), (3, left_ref), (1, right_ref)):
-        first = 4 * ((x + step) & 3)
-        for z in range(4):
-            part = dot32(blocks_ref[first + z], ref[z])
+    for (_, step, first), (copy, at, size) in zip(sources, copies, strict=True):
+        copy.wait()
+        base = 4 * ((x + step) & 3) + first
+        for z in range(size):
+            part = dot32(blocks_ref[base + z], held_ref[at + z])
             total = part if total is None else total + part
-    out_ref[...] = total
-
-
-def conv_far(where_ref, blocks_ref, low_ref, high_ref, near_ref, kept_ref, given_ref):
-    first = 4 * ((where_ref[2] + 2) & 3)
-    total = near_ref[...]
-    for z in range(4):
-        ref = low_ref if z < 2 else high_ref
-        total = total + dot32(blocks_ref[first + z], ref[z % 2])
-    count = kept_ref.shape[0]
-    kept_ref[...] = jnp.where(where_ref[0] == 0, total[:count], total[count:])
-    given_ref[...] = jnp.where(where_ref[0] == 0, total[count:], total[:count])
+    kept_ref[...] = jnp.where(core == 0, total[:count], total[count:])
+    given_ref[...] = jnp.where(core == 0, total[count:], total[:count])
 
 
 def middle(kept_ref, other_ref, latent_ref, bias_ref, mid_ref, stats_ref):
@@ -156,21 +168,23 @@
     stats_ref[...] = jnp.broadcast_to(stats[None], stats_ref.shape)
 
 
-def project(every_ref, mid_ref, gain_ref, shift_ref, weight_ref, query_ref, fresh_ref):
-    mid = mid_ref[...].astype(jnp.float32)
-    mean, inverse = merged_stats(every_ref, mid.shape[0], 1e-06)
+def project(
+    every_ref, mid_ref, other_ref, gain_ref, shift_ref, weight_ref, query_ref, fresh_ref
+):
+    count = mid_ref.shape[0]
+    mean, inverse = merged_stats(every_ref, count, 1e-06)
+    mid = jnp.concatenate([mid_ref[...], other_ref[...]], axis=0).astype(jnp.float32)
     normed = ((mid - mean) * (inverse * gain_ref[...]) + shift_ref[...]).astype(jnp.bfloat16)
     query = dot_t(normed, weight_ref[:384])
     lane = lax.broadcasted_iota(jnp.int32, query.shape, 1)
     query = jnp.where(lane < HEADS * HEAD_DIM, query, 0.0).astype(jnp.bfloat16)
     query_ref[...] = query * jnp.bfloat16(1.0 / math.sqrt(HEAD_DIM))
-    fresh_ref[...] = dot_t(weight_ref[HEADS * HEAD_DIM :], normed).astype(jnp.bfloat16)
+    fresh_ref[...] = dot_t(weight_ref[HEADS * HEAD_DIM :], normed[:count]).astype(jnp.bfloat16)
 
 
 def attend(
     where_ref,
     q_ref,
-    other_ref,
     own_ref,
     left_ref,
     right_ref,
@@ -179,45 +193,53 @@
     fresh_ref,
     out_ref,
     given_ref,
+    held_ref,
+    sems,
 ):
     my_z = where_ref[3]
-    count = q_ref.shape[0]
+    count = out_ref.shape[0]
+    copies, at = [], 0
+    for index, ref in enumerate((own_ref, left_ref, right_ref, low_ref, high_ref)):
+        size = ref.shape[0]
+        copy = pltpu.make_async_copy(ref, held_ref.at[at : at + size], sems.at[index])
+        copy.start()
+        copies.append(copy)
+        at += size
     lane = lax.broadcasted_iota(jnp.int32, (2 * count, 128), 1)
     row = lax.broadcasted_iota(jnp.int32, (2 * count, 4 * count), 0)
     block = lax.broadcasted_iota(jnp.int32, (2 * count, 4 * count), 1) // count
     replaced = (row < count) & (block == my_z)
-    held = (own_ref, left_ref, right_ref, low_ref, high_ref)
     outs = []
     for head in range(HEADS):
         at = 128 * (head // 2)
         mine = (lane < 64) if head % 2 == 0 else (lane >= 64)
-        query = jnp.concatenate(
-            [q_ref[:, at : at + 128], other_ref[:, at : at + 128]], axis=0
-        )
-        query = jnp.where(mine, query.astype(jnp.float32), 0.0).astype(jnp.bfloat16)
+        query = q_ref[:, at : at + 128].astype(jnp.float32)
+        query = jnp.where(mine, query, 0.0).astype(jnp.bfloat16)
+        fresh = dot32(query[:count], fresh_ref[at : at + 128])
+        fresh = jnp.concatenate([fresh, jnp.full((count, count), LOW, jnp.float32)], axis=0)
         scores = []
-        for ref in held:
-            keys = [ref[z, at : at + 128] for z in range(ref.shape[0])]
-            scores.append(dot32(query, jnp.concatenate(keys, axis=1)))
-        scores[0] = jnp.where(replaced, LOW, scores[0])
-        fresh = dot32(query[:count], fresh_ref[at : at + 128])
-        scores.append(jnp.concatenate([fresh, jnp.full((count, count), LOW, jnp.float32)], axis=0))
-        peak = scores[0].max(axis=1, keepdims=True)
-        for s in scores[1:]:
-            peak = jnp.maximum(peak, s.max(axis=1, keepdims=True))
-        total = jnp.zeros((2 * count, 1), jnp.float32)
-        mixed = jnp.zeros((2 * count, 128), jnp.float32)
+        peak = fresh.max(axis=1, keepdims=True)
+        for x in range(4):
+            if head == 0:
+                copies[x].wait()
+                if x == 3:
+                    copies[4].wait()
+            keys = [held_ref[4 * x + z, at : at + 128] for z in range(4)]
+            score = dot32(query, jnp.concatenate(keys, axis=1))
+            if x == 0:
+                score = jnp.where(replaced, LOW, score)
+            peak = jnp.maximum(peak, score.max(axis=1, keepdims=True))
+            scores.append(score)
         v_at = HEADS * HEAD_DIM + at
-        for s, ref in zip(scores, held + (fresh_ref,), strict=True):
-            weights = jnp.exp(s - peak)
+        weights = jnp.exp(fresh - peak)
+        total = weights.sum(axis=1, keepdims=True)
+        tail = (lambda v: jnp.concatenate([v, jnp.zeros_like(v)], axis=0)) if head == HEADS - 1 else (lambda v: v)
+        mixed = dot_t(weights.astype(jnp.bfloat16), tail(fresh_ref[v_at : v_at + 128]))
+        for x in range(4):
+            weights = jnp.exp(scores[x] - peak)
             total = total + weights.sum(axis=1, keepdims=True)
-            if ref is fresh_ref:
-                values = ref[v_at : v_at + 128]
-            else:
-                values = [ref[z, v_at : v_at + 128] for z in range(ref.shape[0])]
-                values = jnp.concatenate(values, axis=1)
-            if head == HEADS - 1:
-                values = jnp.concatenate([values, jnp.zeros_like(values)], axis=0)
+            values = [held_ref[4 * x + z, v_at : v_at + 128] for z in range(4)]
+            values = tail(jnp.concatenate(values, axis=1))
             mixed = mixed + dot_t(weights.astype(jnp.bfloat16), values)
         outs.append((mixed, peak, total))
     last = jnp.where(lane < 64, outs[4][0], 0.0)
@@ -260,11 +282,14 @@
     out_ref[...] = result.astype(jnp.bfloat16)
 
 
-def call(kernel, outs, smem, *args, scratch=()):
+def call(kernel, outs, smem, *args, scratch=(), fetched=()):
     return pl.pallas_call(
         kernel,
         out_shape=[jax.ShapeDtypeStruct(shape, dtype) for shape, dtype in outs],
-        in_specs=[SMEM] * smem + [VMEM] * (len(args) - smem),
+        in_specs=[
+            SMEM if i < smem else pl.BlockSpec(memory_space=pl.ANY) if i in fetched else VMEM
+            for i in range(len(args))
+        ],
         out_specs=[VMEM] * len(outs),
         scratch_shapes=list(scratch),
         compiler_params=pltpu.CompilerParams(vmem_limit_bytes=40 * 1024 * 1024),
@@ -304,7 +329,7 @@
         jnp.stack([latent, outer]), "space", axis=0, axis_index_groups=CORE_GROUPS
     )
     stale = stale_kv.transpose(0, 2, 1).reshape(2 * feats, tok_dev)
-    stale, _ = lax.optimization_barrier((stale, own_w))
+    stale, _ = lax.optimization_barrier((stale, (left_w,right_w,pair)))
     own_kv = lax.all_to_all(
         jnp.broadcast_to(stale[None], (4, 2 * feats, tok_dev)),
         "space",
@@ -313,7 +338,7 @@
         axis_index_groups=Z_GROUPS,
         tiled=True,
     )
-    every1, pair, left_w, right_w = lax.optimization_barrier((every1, pair, left_w, right_w))
+
     low_w = lax.ppermute(left_w[:2], "space", RIGHT)
     high_w = lax.ppermute(right_w[2:], "space", LEFT)
     (blocks,) = call(
@@ -330,27 +355,34 @@
     own_kv, _ = lax.optimization_barrier((own_kv, blocks))
     left_kv = lax.ppermute(own_kv, "space", RIGHT)
     right_kv = lax.ppermute(own_kv, "space", LEFT)
-
     step, _ = lax.optimization_barrier((timestep, blocks))
     bias = (conv_bias + time_embed(step, time_weight)).reshape(1, width)
-    (near,) = call(
-        conv_near, [((2 * tok_dev, width), f32)], 1, where, blocks, own_w, left_w, right_w
-    )
     kept, given = call(
-        conv_far, [((tok_dev, width), f32)] * 2, 1, where, blocks, low_w, high_w, near
+        convolve,
+        [((tok_dev, width), f32)] * 2,
+        1,
+        where,
+        blocks,
+        own_w,
+        left_w,
+        right_w,
+        low_w,
+        high_w,
+        scratch=[pltpu.VMEM((16, ROWS, width), bf16), pltpu.SemaphoreType.DMA((5,))],
+        fetched=(2, 3, 4, 5, 6),
     )
     other = lax.ppermute(given, "space", SWAP)
     mid, stats2 = call(middle, [((tok_dev, width), bf16), table], 0, kept, other, latent, bias)
     every2 = exchanged(stats2)
     low_kv = lax.ppermute(left_kv[:2], "space", RIGHT)
     high_kv = lax.ppermute(right_kv[2:], "space", LEFT)
-
     query, fresh = call(
         project,
-        [((tok_dev, 384), bf16), ((2 * feats, tok_dev), bf16)],
+        [((2 * tok_dev, 384), bf16), ((2 * feats, tok_dev), bf16)],
         0,
         every2,
         mid,
+        lax.ppermute(mid, "space", SWAP),
         norm2_gain[None],
         norm2_shift[None],
         qkv_weight.T,
@@ -362,13 +394,14 @@
         1,
         where,
         query,
-        lax.ppermute(query, "space", SWAP),
         own_kv,
         left_kv,
         right_kv,
         low_kv,
         high_kv,
         fresh,
+        scratch=[pltpu.VMEM((16, 2 * feats, tok_dev), bf16), pltpu.SemaphoreType.DMA((5,))],
+        fetched=(2, 3, 4, 5, 6),
     )
     other = lax.ppermute(theirs, "space", SWAP)
     (result,) = call(finish, [((tok_dev, width), bf16)], 0, mine, other, mid, out_weight)

time: 143 us -> 134 us (0.937)
  waiting for transfers between devices: 17.1 us -> 11.6 us
  starting transfers between devices: 64 us -> 59.9 us
    ppermute x1, waiting for transfers between devices: 5.3 us -> 0.01 us  [on_device(): left_w = lax.ppermute(own_w, 'space', RIGHT)]
    all_to_all x2, starting transfers between devices: 18.6 us -> 13.6 us  [exchanged(): return lax.all_to_all(stats, 'space', 0, 0, tiled=True)]
    ppermute x1, waiting for transfers between devices: 4.83 us -> 0.01 us  [on_device(): low_kv = lax.ppermute(left_kv[:2], 'space', RIGHT)]
    all_to_all x1, waiting for transfers between devices: 0.01 us -> 3.79 us  [on_device(): lax.all_to_all(jnp.broadcast_to(stale[None], (4, 2 * feats, tok_dev)), 's...]
    ppermute x1, waiting for transfers between devices: 0.01 us -> 2.11 us  [on_device(): high_kv = lax.ppermute(right_kv[2:], 'space', LEFT)]
    ppermute x1, starting transfers between devices: 5.95 us -> 4.01 us  [on_device(): other = lax.ppermute(given, 'space', SWAP)]
    all_gather x1, blocking collectives: 6.48 us -> 4.7 us  [on_device(): lax.all_gather(jnp.stack([latent, outer]), 'space', axis=0, axis_index_gr...]
    ppermute x1, waiting for transfers between devices: 1.66 us -> 0.01 us  [on_device(): right_w = lax.ppermute(own_w, 'space', LEFT)]
  transfers between devices with their start and end apart: 15 -> 15, of which waited for: 7 -> 7; matrix products, arithmetic and copies ran while one was open for 4% -> 5% of each run, Pallas kernels for 7% -> 9%
where the time goes in v4:
time: 134 us; the launch traced here: 133 us
  starting transfers between devices  59.9 us (45%)
  blocking collectives  25.9 us (19%)
  Pallas kernels  19.9 us (15%)
  local copies, waits for them, and re-layouts  12.8 us (10%)
  waiting for transfers between devices  11.6 us (9%)
  between operations  1.72 us (1%)
    all_gather x1, blocking collectives, on_device(): own_w = lax.all_gather(weight, 'space', axis=0, axis_index_groups=Z_GROUPS)  21.2 us
    pallas_call x7, Pallas kernels, call(): pl.pallas_call(kernel, out_shape=[jax.ShapeDtypeStruct(shape, dtype) for...  19.9 us
    all_to_all x2, starting transfers between devices, exchanged(): return lax.all_to_all(stats, 'space', 0, 0, tiled=True)  13.6 us
    all_to_all x1, starting transfers between devices, on_device(): lax.all_to_all(jnp.broadcast_to(stale[None], (4, 2 * feats, tok_dev)), 's...  6.7 us
    unnamed x34, local copies, waits for them, and re-layouts  5.37 us
    all_gather x1, blocking collectives, on_device(): lax.all_gather(jnp.stack([latent, outer]), 'space', axis=0, axis_index_gr...  4.7 us
    ppermute x1, starting transfers between devices, on_device(): other = lax.ppermute(given, 'space', SWAP)  4.01 us
    all_to_all x1, waiting for transfers between devices, on_device(): lax.all_to_all(jnp.broadcast_to(stale[None], (4, 2 * feats, tok_dev)), 's...  3.79 us
  transfers between devices with their start and end apart: 15, of which 7 were waited for; matrix products, arithmetic and copies ran while one was open for 5% of the time, Pallas kernels for 9%

profile of v4, /device:TPU:1, one launch (start us, length us, event | category | flops | bytes accessed | tf_op | source)
XLA Modules:
  0.0 132.6 jit_solution(11450418094616007776)
XLA Ops:
  1.7 21.2 %all-gather.1 = bf16[768,640]{1,0:T(8,128)(2,1)S(1)} all-gather(bf16[192,640]{1,0:T(8,128)(2,1)S(1)} %pad.4), channel_id=3, replica_groups={{0,2,4,6},{1,3,5,7},{8,10,12,14},{9,11,13,15},{16,18,20,22},{17,19,21,2..., dimensions={0}, use_global_device_ids=true | all-gather | bytes 1228800 | tf_op jit(solution)/shard_map/all_gather | solution.py:322
  23.0 2.8 %collective-permute-start.1 = (bf16[4,192,640]{2,1,0:T(8,128)(2,1)S(1)}, bf16[4,192,640]{2,1,0:T(8,128)(2,1)S(1)}, u32[]{:S(2)}, u32[]{:S(2)}) collective-permute-start(bf16[4,192,640]{2,1,0:T(8,128)(2,1)S(1)} %bitcast.18), channel_id=1, source_target_pairs={{0,8},{1,9},{2,10},{3,11},{4,12},{5,13},{6,14},{7,15},{8,16},{9,17... | collective-permute-start | bytes 2949128 | tf_op jit(solution)/shard_map/ppermute | solution.py:323
  25.8 3.6 %collective-permute-start.2 = (bf16[4,192,640]{2,1,0:T(8,128)(2,1)S(1)}, bf16[4,192,640]{2,1,0:T(8,128)(2,1)}, u32[]{:S(2)}, u32[]{:S(2)}) collective-permute-start(bf16[4,192,640]{2,1,0:T(8,128)(2,1)S(1)} %bitcast.19), channel_id=1, source_target_pairs={{0,24},{1,25},{2,26},{3,27},{4,28},{5,29},{6,30},{7,31},{8,0},{9,1... | collective-permute-start | bytes 2949128 | tf_op jit(solution)/shard_map/ppermute | solution.py:324
  30.4 1.6 %shard_map.131 = f32[32,8,128]{2,1,0:T(8,128)} custom-call(bf16[128,640]{1,0:T(8,128)(2,1)S(1)} %copy-done.6), custom_call_target="tpu_custom_call" | custom-call | tf_op jit(solution)/shard_map/pallas_call | solution.py:286
  32.0 9.4 %all-to-all-start = ((f32[32,8,128]{2,1,0:T(8,128)}), f32[32,8,128]{2,1,0:T(8,128)S(1)}, u32[]{:S(2)}, u32[]{:S(2)}) async-start(f32[32,8,128]{2,1,0:T(8,128)} %shard_map.131), calls=%async_computation | async-start | bytes 262144 | tf_op jit(solution)/shard_map/all_to_all | solution.py:63
  41.4 3.3 %collective-permute-start = (bf16[128,640]{1,0:T(8,128)(2,1)S(1)}, bf16[128,640]{1,0:T(8,128)(2,1)S(1)}, u32[]{:S(2)}, u32[]{:S(2)}) collective-permute-start(bf16[128,640]{1,0:T(8,128)(2,1)S(1)} %copy-done.7), channel_id=1, source_target_pairs={{2,0},{4,2},{6,4},{8,6},{10,8},{12,10},{14,12},{16,14},{18,16},{20... | collective-permute-start | bytes 491528 | tf_op jit(solution)/shard_map/ppermute | solution.py:325
  44.7 2.2 %collective-permute-done = bf16[128,640]{1,0:T(8,128)(2,1)S(1)} collective-permute-done((bf16[128,640]{1,0:T(8,128)(2,1)S(1)}, bf16[128,640]{1,0:T(8,128)(2,1)S(1)}, u32[]{:S(2)}, u32[]{:S(2)}) %collective-permute-start) | collective-permute-done | bytes 163872 | tf_op jit(solution)/shard_map/ppermute | solution.py:325
  47.0 4.7 %all-gather = bf16[4,128,640]{2,1,0:T(8,128)(2,1)} all-gather(bf16[2,128,640]{2,1,0:T(8,128)(2,1)S(1)} %pad_maximum_fusion), channel_id=2, replica_groups={{0,1},{2,3},{4,5},{6,7},{8,9},{10,11},{12,13},{14,15},{16,17},{18,19},{..., dimensions={0}, use_global_device_ids=true | all-gather | bytes 983040 | tf_op jit(solution)/shard_map/all_gather | solution.py:328
  51.7 1.1 all-to-all-done.every_ref
  53.8 6.7 %all-to-all-start.2 = ((bf16[4,640,128]{2,1,0:T(8,128)(2,1)}), bf16[4,640,128]{2,1,0:T(8,128)(2,1)}, u32[]{:S(2)}, u32[]{:S(2)}) async-start(bf16[4,640,128]{2,1,0:T(8,128)(2,1)} %broadcast_in_dim.24), calls=%async_computation.2 | async-start | bytes 1310720 | tf_op jit(solution)/shard_map/all_to_all | solution.py:333
  61.3 3.4 %collective-permute-start.3 = (bf16[2,192,640]{2,1,0:T(8,128)(2,1)}, bf16[2,192,640]{2,1,0:T(8,128)(2,1)}, u32[]{:S(2)}, u32[]{:S(2)}) collective-permute-start(bf16[2,192,640]{2,1,0:T(8,128)(2,1)} %slice.16), channel_id=1, source_target_pairs={{0,8},{1,9},{2,10},{3,11},{4,12},{5,13},{6,14},{7,15},{8,16},{9,17... | collective-permute-start | bytes 1474568 | tf_op jit(solution)/shard_map/ppermute | solution.py:342
  64.8 1.9 %slice.17 = bf16[2,192,640]{2,1,0:T(8,128)(2,1)} slice(bf16[4,192,640]{2,1,0:T(8,128)(2,1)} %collective-permute-done.2.right_ref), slice={[2:4], [0:192], [0:640]} | slice | bytes 983040 | tf_op jit(solution)/shard_map/slice | solution.py:343
  66.6 3.0 %collective-permute-start.4 = (bf16[2,192,640]{2,1,0:T(8,128)(2,1)}, bf16[2,192,640]{2,1,0:T(8,128)(2,1)}, u32[]{:S(2)}, u32[]{:S(2)}) collective-permute-start(bf16[2,192,640]{2,1,0:T(8,128)(2,1)} %slice.17), channel_id=1, source_target_pairs={{0,24},{1,25},{2,26},{3,27},{4,28},{5,29},{6,30},{7,31},{8,0},{9,1... | collective-permute-start | bytes 1474568 | tf_op jit(solution)/shard_map/ppermute | solution.py:343
  71.0 2.7 %shard_map.132.blocks_ref = bf16[16,256,192]{2,1,0:T(8,128)(2,1)S(1)} custom-call(s32[4]{0:T(128)S(1)} %pad_add_fusion.where_ref, f32[32,8,128]{2,1,0:T(8,128)S(1)} %all-to-all-done.every_ref, bf16[2,2,128,640]{3,2,1,0:T(8,128)(2,1)S(1)} %bitcast.21, f32[1,640]{1,0:T(1,128)S(1)} %broadcast_in_dim.20.gain_ref, f32[1,640]{1,0:T(1,128)S(1)} %broadcast_in_dim.21.shift_ref), custom_call_target="tpu_custom_call" | custom-call | tf_op jit(solution)/shard_map/pallas_call | solution.py:286
  73.6 3.8 %all-to-all-done.2.own_ref = bf16[4,640,128]{2,1,0:T(8,128)(2,1)} async-done(((bf16[4,640,128]{2,1,0:T(8,128)(2,1)}), bf16[4,640,128]{2,1,0:T(8,128)(2,1)}, u32[]{:S(2)}, u32[]{:S(2)}) %all-to-all-start.2) | async-done | bytes 655392 | tf_op jit(solution)/shard_map/all_to_all | solution.py:333
  77.4 3.4 %collective-permute-start.7 = (bf16[4,640,128]{2,1,0:T(8,128)(2,1)}, bf16[4,640,128]{2,1,0:T(8,128)(2,1)}, u32[]{:S(2)}, u32[]{:S(2)}) collective-permute-start(bf16[4,640,128]{2,1,0:T(8,128)(2,1)} %all-to-all-done.2.own_ref), channel_id=1, source_target_pairs={{0,8},{1,9},{2,10},{3,11},{4,12},{5,13},{6,14},{7,15},{8,16},{9,17... | collective-permute-start | bytes 1966088 | tf_op jit(solution)/shard_map/ppermute | solution.py:356
  80.8 3.1 %collective-permute-start.8 = (bf16[4,640,128]{2,1,0:T(8,128)(2,1)}, bf16[4,640,128]{2,1,0:T(8,128)(2,1)}, u32[]{:S(2)}, u32[]{:S(2)}) collective-permute-start(bf16[4,640,128]{2,1,0:T(8,128)(2,1)} %all-to-all-done.2.own_ref), channel_id=1, source_target_pairs={{0,24},{1,25},{2,26},{3,27},{4,28},{5,29},{6,30},{7,31},{8,0},{9,1... | collective-permute-start | bytes 1966088 | tf_op jit(solution)/shard_map/ppermute | solution.py:357
  84.6 1.2 copy-done.2
  85.8 1.2 copy-done.5
  87.0 4.0 %shard_map.133 = (f32[128,640]{1,0:T(8,128)S(1)}, f32[128,640]{1,0:T(8,128)S(1)}) custom-call(s32[4]{0:T(128)S(1)} %pad_add_fusion.where_ref, bf16[16,256,192]{2,1,0:T(8,128)(2,1)S(1)} %shard_map.132.blocks_ref, bf16[4,192,640]{2,1,0:T(8,128)(2,1)S(1)} %bitcast.20, bf16[4,192,640]{2,1,0:T(8,128)(2,1)S(1)} %copy-done.5, ...), custom_call_target="tpu_custom_call" | custom-call | tf_op jit(solution)/shard_map/pallas_call | solution.py:286
  91.1 4.0 %collective-permute-start.5 = (f32[128,640]{1,0:T(8,128)S(1)}, f32[128,640]{1,0:T(8,128)S(1)}, u32[]{:S(2)}, u32[]{:S(2)}) collective-permute-start(f32[128,640]{1,0:T(8,128)S(1)} %get-tuple-element.14), channel_id=1, source_target_pairs={{0,1},{1,0},{2,3},{3,2},{4,5},{5,4},{6,7},{7,6},{8,9},{9,8},{10,11... | collective-permute-start | bytes 983048 | tf_op jit(solution)/shard_map/ppermute | solution.py:374
  96.3 1.7 %shard_map.134 = (bf16[128,640]{1,0:T(8,128)(2,1)S(1)}, f32[32,8,128]{2,1,0:T(8,128)}) custom-call(f32[128,640]{1,0:T(8,128)S(1)} %get-tuple-element.13.kept_ref, f32[128,640]{1,0:T(8,128)S(1)} %collective-permute-done.5.other_ref, bf16[128,640]{1,0:T(8,128)(2,1)S(1)} %copy-done.7, f32[1,640]{1,0:T(1,128)S(1)} %add.19.bias_ref), custom_call_target="tpu_custom_call" | custom-call | tf_op jit(solution)/shard_map/pallas_call | solution.py:286
  98.0 4.2 %all-to-all-start.1 = ((f32[32,8,128]{2,1,0:T(8,128)}), f32[32,8,128]{2,1,0:T(8,128)S(1)}, u32[]{:S(2)}, u32[]{:S(2)}) async-start(f32[32,8,128]{2,1,0:T(8,128)} %get-tuple-element.16), calls=%async_computation.1 | async-start | bytes 262144 | tf_op jit(solution)/shard_map/all_to_all | solution.py:63
  103.2 3.3 %collective-permute-start.9 = (bf16[2,640,128]{2,1,0:T(8,128)(2,1)S(1)}, bf16[2,640,128]{2,1,0:T(8,128)(2,1)S(1)}, u32[]{:S(2)}, u32[]{:S(2)}) collective-permute-start(bf16[2,640,128]{2,1,0:T(8,128)(2,1)S(1)} %slice.18), channel_id=1, source_target_pairs={{0,8},{1,9},{2,10},{3,11},{4,12},{5,13},{6,14},{7,15},{8,16},{9,17... | collective-permute-start | bytes 983048 | tf_op jit(solution)/shard_map/ppermute | solution.py:377
  106.6 1.7 %slice.19 = bf16[2,640,128]{2,1,0:T(8,128)(2,1)} slice(bf16[4,640,128]{2,1,0:T(8,128)(2,1)} %collective-permute-done.8.right_ref), slice={[2:4], [0:640], [0:128]} | slice | bytes 655360 | tf_op jit(solution)/shard_map/slice | solution.py:378
  108.3 3.2 %collective-permute-start.10 = (bf16[2,640,128]{2,1,0:T(8,128)(2,1)}, bf16[2,640,128]{2,1,0:T(8,128)(2,1)S(1)}, u32[]{:S(2)}, u32[]{:S(2)}) collective-permute-start(bf16[2,640,128]{2,1,0:T(8,128)(2,1)} %slice.19), channel_id=1, source_target_pairs={{0,24},{1,25},{2,26},{3,27},{4,28},{5,29},{6,30},{7,31},{8,0},{9,1... | collective-permute-start | bytes 983048 | tf_op jit(solution)/shard_map/ppermute | solution.py:378
  111.5 2.9 %collective-permute-start.6 = (bf16[128,640]{1,0:T(8,128)(2,1)S(1)}, bf16[128,640]{1,0:T(8,128)(2,1)S(1)}, u32[]{:S(2)}, u32[]{:S(2)}) collective-permute-start(bf16[128,640]{1,0:T(8,128)(2,1)S(1)} %get-tuple-element.17.mid_ref), channel_id=1, source_target_pairs={{0,1},{1,0},{2,3},{3,2},{4,5},{5,4},{6,7},{7,6},{8,9},{9,8},{10,11... | collective-permute-start | bytes 491528 | tf_op jit(solution)/shard_map/ppermute | solution.py:385
  115.2 1.7 %shard_map.135 = (bf16[256,384]{1,0:T(8,128)(2,1)S(1)}, bf16[640,128]{1,0:T(8,128)(2,1)}) custom-call(f32[32,8,128]{2,1,0:T(8,128)S(1)} %all-to-all-done.1.every_ref, bf16[128,640]{1,0:T(8,128)(2,1)S(1)} %get-tuple-element.17.mid_ref, bf16[128,640]{1,0:T(8,128)(2,1)S(1)} %collective-permute-done.6.other_ref, f32[1,640]{1,0:T(1,128)S(1)} %broadcast_in_dim.22.gain_ref, ...), custom_call_target="tpu_custom_call" | custom-call | tf_op jit(solution)/shard_map/pallas_call | solution.py:286
  116.9 2.1 %collective-permute-done.10.high_ref = bf16[2,640,128]{2,1,0:T(8,128)(2,1)S(1)} collective-permute-done((bf16[2,640,128]{2,1,0:T(8,128)(2,1)}, bf16[2,640,128]{2,1,0:T(8,128)(2,1)S(1)}, u32[]{:S(2)}, u32[]{:S(2)}) %collective-permute-start.10) | collective-permute-done | bytes 327712 | tf_op jit(solution)/shard_map/ppermute | solution.py:378
  119.9 6.9 %shard_map.136 = (f32[128,384]{1,0:T(8,128)S(1)}, f32[128,384]{1,0:T(8,128)S(1)}) custom-call(s32[4]{0:T(128)S(1)} %pad_add_fusion.where_ref, bf16[256,384]{1,0:T(8,128)(2,1)S(1)} %get-tuple-element.18.q_ref, bf16[4,640,128]{2,1,0:T(8,128)(2,1)} %all-to-all-done.2.own_ref, bf16[4,640,128]{2,1,0:T(8,128)(2,1)} %collective-permute-done.7.left_ref, ...), custom_call_target="tpu_custom_call" | custom-call | tf_op jit(solution)/shard_map/pallas_call | solution.py:286
  126.8 3.4 %collective-permute-start.11 = (f32[128,384]{1,0:T(8,128)S(1)}, f32[128,384]{1,0:T(8,128)S(1)}, u32[]{:S(2)}, u32[]{:S(2)}) collective-permute-start(f32[128,384]{1,0:T(8,128)S(1)} %get-tuple-element.23), channel_id=1, source_target_pairs={{0,1},{1,0},{2,3},{3,2},{4,5},{5,4},{6,7},{7,6},{8,9},{9,8},{10,11... | collective-permute-start | bytes 589832 | tf_op jit(solution)/shard_map/ppermute | solution.py:406
  131.3 1.3 shard_map.137
  (59 shorter events, 10.0 us)
Async XLA Ops:
  0.6 94.6 %copy-start = (f32[320,640]{1,0:T(8,128)S(1)}, f32[320,640]{1,0:T(8,128)}, u32[]{:S(2)}) copy-start(f32[320,640]{1,0:T(8,128)} %param.18) | copy-start | bytes 2457604
  0.6 40.8 %copy-start.7 = (bf16[128,640]{1,0:T(8,128)(2,1)S(1)}, bf16[128,640]{1,0:T(8,128)(2,1)}, u32[]{:S(2)}) copy-start(bf16[128,640]{1,0:T(8,128)(2,1)} %latent_ref.3) | copy-start | bytes 491524
  0.7 52.2 %copy-start.11 = (bf16[2,128,320]{1,2,0:T(8,128)(2,1)S(1)}, bf16[2,128,320]{1,2,0:T(8,128)(2,1)}, u32[]{:S(2)}) copy-start(bf16[2,128,320]{1,2,0:T(8,128)(2,1)} %param.23) | copy-start | bytes 491524
  23.0 30.8 %copy-start.1 = (bf16[768,640]{1,0:T(8,128)(2,1)}, bf16[768,640]{1,0:T(8,128)(2,1)S(1)}, u32[]{:S(2)}) copy-start(bf16[768,640]{1,0:T(8,128)(2,1)S(1)} %all-gather.1) | copy-start | bytes 2949124
  23.0 28.8 %collective-permute-start.1 = (bf16[4,192,640]{2,1,0:T(8,128)(2,1)S(1)}, bf16[4,192,640]{2,1,0:T(8,128)(2,1)S(1)}, u32[]{:S(2)}, u32[]{:S(2)}) collective-permute-start(bf16[4,192,640]{2,1,0:T(8,128)(2,1)S(1)} %bitcast.18), channel_id=1, source_target_pairs={{0,8},{1,9},{2,10},{3,11},{4,12},{5,13},{6,14},{7,15},{8,16},{9,17... | collective-permute-start | bytes 2949128 | tf_op jit(solution)/shard_map/ppermute | solution.py:323
  25.8 25.9 %collective-permute-start.2 = (bf16[4,192,640]{2,1,0:T(8,128)(2,1)S(1)}, bf16[4,192,640]{2,1,0:T(8,128)(2,1)}, u32[]{:S(2)}, u32[]{:S(2)}) collective-permute-start(bf16[4,192,640]{2,1,0:T(8,128)(2,1)S(1)} %bitcast.19), channel_id=1, source_target_pairs={{0,24},{1,25},{2,26},{3,27},{4,28},{5,29},{6,30},{7,31},{8,0},{9,1... | collective-permute-start | bytes 2949128 | tf_op jit(solution)/shard_map/ppermute | solution.py:324
  29.5 0.9 copy-start.6
  32.0 20.8 %all-to-all-start = ((f32[32,8,128]{2,1,0:T(8,128)}), f32[32,8,128]{2,1,0:T(8,128)S(1)}, u32[]{:S(2)}, u32[]{:S(2)}) async-start(f32[32,8,128]{2,1,0:T(8,128)} %shard_map.131), calls=%async_computation | async-start | bytes 262144 | tf_op jit(solution)/shard_map/all_to_all | solution.py:63
  41.4 5.5 %collective-permute-start = (bf16[128,640]{1,0:T(8,128)(2,1)S(1)}, bf16[128,640]{1,0:T(8,128)(2,1)S(1)}, u32[]{:S(2)}, u32[]{:S(2)}) collective-permute-start(bf16[128,640]{1,0:T(8,128)(2,1)S(1)} %copy-done.7), channel_id=1, source_target_pairs={{2,0},{4,2},{6,4},{8,6},{10,8},{12,10},{14,12},{16,14},{18,16},{20... | collective-permute-start | bytes 491528 | tf_op jit(solution)/shard_map/ppermute | solution.py:325
  51.7 18.0 %copy-start.13 = (f32[640]{0:T(1024)S(1)}, f32[640]{0:T(1024)}, u32[]{:S(2)}) copy-start(f32[640]{0:T(1024)} %param.14) | copy-start | bytes 7684
  51.7 18.0 %copy-start.14 = (f32[640]{0:T(1024)S(1)}, f32[640]{0:T(1024)}, u32[]{:S(2)}) copy-start(f32[640]{0:T(1024)} %param.15) | copy-start | bytes 7684
  51.7 18.1 %copy-start.4 = (bf16[4,192,640]{2,1,0:T(8,128)(2,1)}, bf16[4,192,640]{2,1,0:T(8,128)(2,1)S(1)}, u32[]{:S(2)}) copy-start(bf16[4,192,640]{2,1,0:T(8,128)(2,1)S(1)} %collective-permute-done.1.left_ref) | copy-start | bytes 2949124
  53.8 23.7 %all-to-all-start.2 = ((bf16[4,640,128]{2,1,0:T(8,128)(2,1)}), bf16[4,640,128]{2,1,0:T(8,128)(2,1)}, u32[]{:S(2)}, u32[]{:S(2)}) async-start(bf16[4,640,128]{2,1,0:T(8,128)(2,1)} %broadcast_in_dim.24), calls=%async_computation.2 | async-start | bytes 1310720 | tf_op jit(solution)/shard_map/all_to_all | solution.py:333
  61.3 23.3 %collective-permute-start.3 = (bf16[2,192,640]{2,1,0:T(8,128)(2,1)}, bf16[2,192,640]{2,1,0:T(8,128)(2,1)}, u32[]{:S(2)}, u32[]{:S(2)}) collective-permute-start(bf16[2,192,640]{2,1,0:T(8,128)(2,1)} %slice.16), channel_id=1, source_target_pairs={{0,8},{1,9},{2,10},{3,11},{4,12},{5,13},{6,14},{7,15},{8,16},{9,17... | collective-permute-start | bytes 1474568 | tf_op jit(solution)/shard_map/ppermute | solution.py:342
  66.6 18.0 %collective-permute-start.4 = (bf16[2,192,640]{2,1,0:T(8,128)(2,1)}, bf16[2,192,640]{2,1,0:T(8,128)(2,1)}, u32[]{:S(2)}, u32[]{:S(2)}) collective-permute-start(bf16[2,192,640]{2,1,0:T(8,128)(2,1)} %slice.17), channel_id=1, source_target_pairs={{0,24},{1,25},{2,26},{3,27},{4,28},{5,29},{6,30},{7,31},{8,0},{9,1... | collective-permute-start | bytes 1474568 | tf_op jit(solution)/shard_map/ppermute | solution.py:343
  69.9 1.1 copy-start.3
  77.4 24.8 %collective-permute-start.7 = (bf16[4,640,128]{2,1,0:T(8,128)(2,1)}, bf16[4,640,128]{2,1,0:T(8,128)(2,1)}, u32[]{:S(2)}, u32[]{:S(2)}) collective-permute-start(bf16[4,640,128]{2,1,0:T(8,128)(2,1)} %all-to-all-done.2.own_ref), channel_id=1, source_target_pairs={{0,8},{1,9},{2,10},{3,11},{4,12},{5,13},{6,14},{7,15},{8,16},{9,17... | collective-permute-start | bytes 1966088 | tf_op jit(solution)/shard_map/ppermute | solution.py:356
  80.8 25.7 %collective-permute-start.8 = (bf16[4,640,128]{2,1,0:T(8,128)(2,1)}, bf16[4,640,128]{2,1,0:T(8,128)(2,1)}, u32[]{:S(2)}, u32[]{:S(2)}) collective-permute-start(bf16[4,640,128]{2,1,0:T(8,128)(2,1)} %all-to-all-done.2.own_ref), channel_id=1, source_target_pairs={{0,24},{1,25},{2,26},{3,27},{4,28},{5,29},{6,30},{7,31},{8,0},{9,1... | collective-permute-start | bytes 1966088 | tf_op jit(solution)/shard_map/ppermute | solution.py:357
  84.6 1.2 copy-start.2
  85.8 1.2 copy-start.5
  87.0 8.8 %copy-start.12 = (f32[640]{0:T(1024)S(1)}, f32[640]{0:T(1024)}, u32[]{:S(2)}) copy-start(f32[640]{0:T(1024)} %param.17) | copy-start | bytes 7684
  91.0 23.3 %copy-start.15 = (f32[640]{0:T(1024)S(1)}, f32[640]{0:T(1024)}, u32[]{:S(2)}) copy-start(f32[640]{0:T(1024)} %param.19) | copy-start | bytes 7684
  91.1 23.3 %copy-start.16 = (f32[640]{0:T(1024)S(1)}, f32[640]{0:T(1024)}, u32[]{:S(2)}) copy-start(f32[640]{0:T(1024)} %param.20) | copy-start | bytes 7684
  91.1 24.1 %copy-start.8 = (bf16[640,960]{0,1:T(8,128)(2,1)S(1)}, bf16[640,960]{0,1:T(8,128)(2,1)}, u32[]{:S(2)}) copy-start(bf16[640,960]{0,1:T(8,128)(2,1)} %param.21) | copy-start | bytes 3686404
  91.1 5.3 %collective-permute-start.5 = (f32[128,640]{1,0:T(8,128)S(1)}, f32[128,640]{1,0:T(8,128)S(1)}, u32[]{:S(2)}, u32[]{:S(2)}) collective-permute-start(f32[128,640]{1,0:T(8,128)S(1)} %get-tuple-element.14), channel_id=1, source_target_pairs={{0,1},{1,0},{2,3},{3,2},{4,5},{5,4},{6,7},{7,6},{8,9},{9,8},{10,11... | collective-permute-start | bytes 983048 | tf_op jit(solution)/shard_map/ppermute | solution.py:374
  98.0 17.2 %all-to-all-start.1 = ((f32[32,8,128]{2,1,0:T(8,128)}), f32[32,8,128]{2,1,0:T(8,128)S(1)}, u32[]{:S(2)}, u32[]{:S(2)}) async-start(f32[32,8,128]{2,1,0:T(8,128)} %get-tuple-element.16), calls=%async_computation.1 | async-start | bytes 262144 | tf_op jit(solution)/shard_map/all_to_all | solution.py:63
  103.2 13.6 %collective-permute-start.9 = (bf16[2,640,128]{2,1,0:T(8,128)(2,1)S(1)}, bf16[2,640,128]{2,1,0:T(8,128)(2,1)S(1)}, u32[]{:S(2)}, u32[]{:S(2)}) collective-permute-start(bf16[2,640,128]{2,1,0:T(8,128)(2,1)S(1)} %slice.18), channel_id=1, source_target_pairs={{0,8},{1,9},{2,10},{3,11},{4,12},{5,13},{6,14},{7,15},{8,16},{9,17... | collective-permute-start | bytes 983048 | tf_op jit(solution)/shard_map/ppermute | solution.py:377
  108.3 10.7 %collective-permute-start.10 = (bf16[2,640,128]{2,1,0:T(8,128)(2,1)}, bf16[2,640,128]{2,1,0:T(8,128)(2,1)S(1)}, u32[]{:S(2)}, u32[]{:S(2)}) collective-permute-start(bf16[2,640,128]{2,1,0:T(8,128)(2,1)} %slice.19), channel_id=1, source_target_pairs={{0,24},{1,25},{2,26},{3,27},{4,28},{5,29},{6,30},{7,31},{8,0},{9,1... | collective-permute-start | bytes 983048 | tf_op jit(solution)/shard_map/ppermute | solution.py:378
  111.5 3.7 %collective-permute-start.6 = (bf16[128,640]{1,0:T(8,128)(2,1)S(1)}, bf16[128,640]{1,0:T(8,128)(2,1)S(1)}, u32[]{:S(2)}, u32[]{:S(2)}) collective-permute-start(bf16[128,640]{1,0:T(8,128)(2,1)S(1)} %get-tuple-element.17.mid_ref), channel_id=1, source_target_pairs={{0,1},{1,0},{2,3},{3,2},{4,5},{5,4},{6,7},{7,6},{8,9},{9,8},{10,11... | collective-permute-start | bytes 491528 | tf_op jit(solution)/shard_map/ppermute | solution.py:385
  115.2 16.1 %copy-start.9 = (bf16[320,640]{1,0:T(8,128)(2,1)S(1)}, bf16[320,640]{1,0:T(8,128)(2,1)}, u32[]{:S(2)}) copy-start(bf16[320,640]{1,0:T(8,128)(2,1)} %weight_ref.1) | copy-start | bytes 1228804
  119.0 0.9 copy-start.10
  126.8 4.5 %collective-permute-start.11 = (f32[128,384]{1,0:T(8,128)S(1)}, f32[128,384]{1,0:T(8,128)S(1)}, u32[]{:S(2)}, u32[]{:S(2)}) collective-permute-start(f32[128,384]{1,0:T(8,128)S(1)} %get-tuple-element.23), channel_id=1, source_target_pairs={{0,1},{1,0},{2,3},{3,2},{4,5},{5,4},{6,7},{7,6},{8,9},{9,8},{10,11... | collective-permute-start | bytes 589832 | tf_op jit(solution)/shard_map/ppermute | solution.py:406

commit v5 on v4

--- a/solution.py
+++ b/solution.py
@@ -14,12 +14,13 @@
 PER = 20
 PEERS = 32
 Z_GROUPS = [[8 * x + 2 * z + c for z in range(4)] for x in range(4) for c in range(2)]
-CORE_GROUPS = [[2 * k, 2 * k + 1] for k in range(16)]
 RIGHT = [(i, (i + 8) % PEERS) for i in range(PEERS)]
 LEFT = [(i, (i + 24) % PEERS) for i in range(PEERS)]
 SWAP = [(i, i ^ 1) for i in range(PEERS)]
-OUTER = [(i, i - 2) for i in range(2, PEERS, 2)] + [(i, i + 2) for i in range(1, PEERS - 2, 2)]
+UP = [(i, i + 1) for i in range(PEERS - 1)]
+DOWN = [(i + 1, i) for i in range(PEERS - 1)]
 ROWS = 192
+CHUNKS = 8
 LOW = -1e30
 VMEM = pl.BlockSpec(memory_space=pltpu.VMEM)
 SMEM = pl.BlockSpec(memory_space=pltpu.SMEM)
@@ -68,21 +69,22 @@
     out_ref[...] = jnp.broadcast_to(stats[None], out_ref.shape)
 
 
-def prepare(where_ref, every_ref, pair_ref, gain_ref, shift_ref, out_ref, flat_ref):
-    core, chip = where_ref[0], where_ref[1]
-    count = pair_ref.shape[2]
+def prepare(
+    where_ref, every_ref, before_ref, latent_ref, after_ref, gain_ref, shift_ref, out_ref
+):
+    me = where_ref[0]
+    count = latent_ref.shape[0]
     mean, inverse = merged_stats(every_ref, count, 1e-05)
     factor = inverse * gain_ref[...]
     token = lax.broadcasted_iota(jnp.int32, (count, 640), 0)
-    flat_ref[:, 5760:] = jnp.zeros((2 * count, 128), jnp.bfloat16)
-    for row, (holder, which) in enumerate(((1, 1), (0, 0), (1, 0), (0, 1))):
-        value = pair_ref[holder, which].astype(jnp.float32)
+    for down, ref in enumerate((before_ref, latent_ref, after_ref)):
+        value = ref[...].astype(jnp.float32)
         value = (value - mean) * factor + shift_ref[...]
         value = value / (1.0 + jnp.exp(-value))
-        if row == 0:
-            value = jnp.where(chip > 0, value, 0.0)
-        if row == 3:
-            value = jnp.where(chip < PEERS // 2 - 1, value, 0.0)
+        if down == 0:
+            value = jnp.where(me > 0, value, 0.0)
+        if down == 2:
+            value = jnp.where(me < PEERS - 1, value, 0.0)
         value = value.astype(jnp.bfloat16).astype(jnp.float32)
         shifts = (
             jnp.where(token == 0, 0.0, pltpu.roll(value, 1, 0)),
@@ -90,21 +92,8 @@
             jnp.where(token == count - 1, 0.0, pltpu.roll(value, count - 1, 0)),
         )
         for across, shifted in enumerate(shifts):
-            shifted = shifted.astype(jnp.bfloat16)
-            for out in range(2):
-                down = row - out
-                if 0 <= down <= 2:
-                    at = (3 * down + across) * 640
-                    flat_ref[out * count : (out + 1) * count, at : at + 640] = shifted
-    for parity in range(2):
-
-        @pl.when(core == parity)
-        def _():
-            for index in range(16):
-                at = 360 * index + 180 * parity
-                low = at // 128 * 128
-                wide = flat_ref[:, low : low + 384]
-                out_ref[index] = wide[:, at - low : at - low + ROWS]
+            at = (3 * down + across) * 640
+            out_ref[:, at : at + 640] = shifted.astype(jnp.bfloat16)
 
 
 def time_embed(timestep, time_weight):
@@ -127,42 +116,23 @@
 
 
 def convolve(
-    where_ref,
-    blocks_ref,
-    own_ref,
-    left_ref,
-    right_ref,
-    low_ref,
-    high_ref,
-    kept_ref,
-    given_ref,
-    held_ref,
-    sems,
-):
-    core, x = where_ref[0], where_ref[2]
-    count = kept_ref.shape[0]
-    sources = ((own_ref, 0, 0), (left_ref, 3, 0), (right_ref, 1, 0), (low_ref, 2, 0), (high_ref, 2, 2))
-    copies, at = [], 0
-    for index, (ref, _, _) in enumerate(sources):
-        size = ref.shape[0]
-        copy = pltpu.make_async_copy(ref, held_ref.at[at : at + size], sems.at[index])
+    unfolded_ref, weight_ref, latent_ref, bias_ref, mid_ref, stats_ref, held_ref, sems
+):
+    rows = weight_ref.shape[0] // CHUNKS
+    copies = []
+    for index in range(CHUNKS):
+        part = pl.ds(index * rows, rows)
+        copy = pltpu.make_async_copy(weight_ref.at[part], held_ref.at[part], sems.at[index])
         copy.start()
-        copies.append((copy, at, size))
-        at += size
-    total = None
-    for (_, step, first), (copy, at, size) in zip(sources, copies, strict=True):
+        copies.append(copy)
+    total = latent_ref[...].astype(jnp.float32) + bias_ref[...]
+    conv = None
+    for index, copy in enumerate(copies):
+        at = index * rows
         copy.wait()
-        base = 4 * ((x + step) & 3) + first
-        for z in range(size):
-            part = dot32(blocks_ref[base + z], held_ref[at + z])
-            total = part if total is None else total + part
-    kept_ref[...] = jnp.where(core == 0, total[:count], total[count:])
-    given_ref[...] = jnp.where(core == 0, total[count:], total[:count])
-
-
-def middle(kept_ref, other_ref, latent_ref, bias_ref, mid_ref, stats_ref):
-    conv = kept_ref[...] + other_ref[...]
-    mid = (latent_ref[...].astype(jnp.float32) + conv + bias_ref[...]).astype(jnp.bfloat16)
+        part = dot32(unfolded_ref[:, at : at + rows], held_ref[at : at + rows])
+        conv = part if conv is None else conv + part
+    mid = (total + conv).astype(jnp.bfloat16)
     mid_ref[...] = mid
     stats = local_stats(mid.astype(jnp.float32))
     stats_ref[...] = jnp.broadcast_to(stats[None], stats_ref.shape)
@@ -193,18 +163,11 @@
     fresh_ref,
     out_ref,
     given_ref,
-    held_ref,
-    sems,
-):
-    my_z = where_ref[3]
+):
+    my_z = where_ref[1]
     count = out_ref.shape[0]
-    copies, at = [], 0
-    for index, ref in enumerate((own_ref, left_ref, right_ref, low_ref, high_ref)):
-        size = ref.shape[0]
-        copy = pltpu.make_async_copy(ref, held_ref.at[at : at + size], sems.at[index])
-        copy.start()
-        copies.append(copy)
-        at += size
+    held = [[(ref, z) for z in range(4)] for ref in (own_ref, left_ref, right_ref)]
+    held.append([(low_ref, 0), (low_ref, 1), (high_ref, 0), (high_ref, 1)])
     lane = lax.broadcasted_iota(jnp.int32, (2 * count, 128), 1)
     row = lax.broadcasted_iota(jnp.int32, (2 * count, 4 * count), 0)
     block = lax.broadcasted_iota(jnp.int32, (2 * count, 4 * count), 1) // count
@@ -220,11 +183,7 @@
         scores = []
         peak = fresh.max(axis=1, keepdims=True)
         for x in range(4):
-            if head == 0:
-                copies[x].wait()
-                if x == 3:
-                    copies[4].wait()
-            keys = [held_ref[4 * x + z, at : at + 128] for z in range(4)]
+            keys = [ref[z, at : at + 128] for ref, z in held[x]]
             score = dot32(query, jnp.concatenate(keys, axis=1))
             if x == 0:
                 score = jnp.where(replaced, LOW, score)
@@ -238,7 +197,7 @@
         for x in range(4):
             weights = jnp.exp(scores[x] - peak)
             total = total + weights.sum(axis=1, keepdims=True)
-            values = [held_ref[4 * x + z, v_at : v_at + 128] for z in range(4)]
+            values = [ref[z, v_at : v_at + 128] for ref, z in held[x]]
             values = tail(jnp.concatenate(values, axis=1))
             mixed = mixed + dot_t(weights.astype(jnp.bfloat16), values)
         outs.append((mixed, peak, total))
@@ -282,17 +241,17 @@
     out_ref[...] = result.astype(jnp.bfloat16)
 
 
-def call(kernel, outs, smem, *args, scratch=(), fetched=()):
+def call(kernel, outs, smem, *args, scratch=(), fetched=(), mib=32):
     return pl.pallas_call(
         kernel,
         out_shape=[jax.ShapeDtypeStruct(shape, dtype) for shape, dtype in outs],
         in_specs=[
-            SMEM if i < smem else pl.BlockSpec(memory_space=pl.ANY) if i in fetched else VMEM
+            SMEM if i < smem else pl.BlockSpec(memory_space=pltpu.HBM) if i in fetched else VMEM
             for i in range(len(args))
         ],
         out_specs=[VMEM] * len(outs),
         scratch_shapes=list(scratch),
-        compiler_params=pltpu.CompilerParams(vmem_limit_bytes=40 * 1024 * 1024),
+        compiler_params=pltpu.CompilerParams(vmem_limit_bytes=mib * 1024 * 1024),
     )(*args)
 
 
@@ -313,23 +272,34 @@
     tok_dev, width = latent.shape
     feats = qkv_weight.shape[1] // 3
     me = lax.axis_index("space")
-    where = jnp.stack([me % 2, me // 2, me // 8, (me // 2) % 4])
+    where = jnp.stack([me, (me // 2) % 4])
     rows = conv_weight.shape[0]
     f32, bf16 = jnp.float32, jnp.bfloat16
     table = ((PEERS, 8, 128), f32)
 
     weight = jnp.pad(conv_weight, ((0, ROWS - rows), (0, 0)))
-    own_w = lax.all_gather(weight, "space", axis=0, axis_index_groups=Z_GROUPS)
-    left_w = lax.ppermute(own_w, "space", RIGHT)
-    right_w = lax.ppermute(own_w, "space", LEFT)
-    outer = lax.ppermute(latent, "space", OUTER)
+    weight = lax.all_gather(weight, "space", axis=0, tiled=True)
+
     (stats1,) = call(first_stats, [table], 0, latent)
     every1 = exchanged(stats1)
-    pair = lax.all_gather(
-        jnp.stack([latent, outer]), "space", axis=0, axis_index_groups=CORE_GROUPS
-    )
+    before = lax.ppermute(latent, "space", UP)
+    after = lax.ppermute(latent, "space", DOWN)
+    (unfolded,) = call(
+        prepare,
+        [((tok_dev, 9 * width), bf16)],
+        1,
+        where,
+        every1,
+        before,
+        latent,
+        after,
+        norm1_gain[None],
+        norm1_shift[None],
+    )
+    unfolded = jnp.pad(unfolded.reshape(tok_dev, PEERS, rows), ((0, 0), (0, 0), (0, ROWS - rows)))
+    unfolded = unfolded.reshape(tok_dev, PEERS * ROWS)
+
     stale = stale_kv.transpose(0, 2, 1).reshape(2 * feats, tok_dev)
-    stale, _ = lax.optimization_barrier((stale, (left_w,right_w,pair)))
     own_kv = lax.all_to_all(
         jnp.broadcast_to(stale[None], (4, 2 * feats, tok_dev)),
         "space",
@@ -338,44 +308,25 @@
         axis_index_groups=Z_GROUPS,
         tiled=True,
     )
-
-    low_w = lax.ppermute(left_w[:2], "space", RIGHT)
-    high_w = lax.ppermute(right_w[2:], "space", LEFT)
-    (blocks,) = call(
-        prepare,
-        [((16, 2 * tok_dev, ROWS), bf16)],
-        1,
-        where,
-        every1,
-        pair,
-        norm1_gain[None],
-        norm1_shift[None],
-        scratch=[pltpu.VMEM((2 * tok_dev, 5760 + 128), bf16)],
-    )
-    own_kv, _ = lax.optimization_barrier((own_kv, blocks))
     left_kv = lax.ppermute(own_kv, "space", RIGHT)
     right_kv = lax.ppermute(own_kv, "space", LEFT)
-    step, _ = lax.optimization_barrier((timestep, blocks))
-    bias = (conv_bias + time_embed(step, time_weight)).reshape(1, width)
-    kept, given = call(
-        convolve,
-        [((tok_dev, width), f32)] * 2,
-        1,
-        where,
-        blocks,
-        own_w,
-        left_w,
-        right_w,
-        low_w,
-        high_w,
-        scratch=[pltpu.VMEM((16, ROWS, width), bf16), pltpu.SemaphoreType.DMA((5,))],
-        fetched=(2, 3, 4, 5, 6),
-    )
-    other = lax.ppermute(given, "space", SWAP)
-    mid, stats2 = call(middle, [((tok_dev, width), bf16), table], 0, kept, other, latent, bias)
-    every2 = exchanged(stats2)
     low_kv = lax.ppermute(left_kv[:2], "space", RIGHT)
     high_kv = lax.ppermute(right_kv[2:], "space", LEFT)
+    bias = (conv_bias + time_embed(timestep, time_weight)).reshape(1, width)
+    unfolded, low_kv, high_kv, bias = lax.optimization_barrier((unfolded, low_kv, high_kv, bias))
+    mid, stats2 = call(
+        convolve,
+        [((tok_dev, width), bf16), table],
+        0,
+        unfolded,
+        weight,
+        latent,
+        bias,
+        scratch=[pltpu.VMEM((PEERS * ROWS, width), bf16), pltpu.SemaphoreType.DMA((CHUNKS,))],
+        fetched=(1,),
+        mib=56,
+    )
+    every2 = exchanged(stats2)
     query, fresh = call(
         project,
         [((2 * tok_dev, 384), bf16), ((2 * feats, tok_dev), bf16)],
@@ -400,8 +351,6 @@
         low_kv,
         high_kv,
         fresh,
-        scratch=[pltpu.VMEM((16, 2 * feats, tok_dev), bf16), pltpu.SemaphoreType.DMA((5,))],
-        fetched=(2, 3, 4, 5, 6),
     )
     other = lax.ppermute(theirs, "space", SWAP)
     (result,) = call(finish, [((tok_dev, width), bf16)], 0, mine, other, mid, out_weight)

time: 134 us -> 150 us (1.12)
  waiting for transfers between devices: 11.6 us -> 36.1 us
  starting transfers between devices: 59.9 us -> 36.5 us
  between operations: 1.72 us -> 15 us
  local copies, waits for them, and re-layouts: 12.8 us -> 20.1 us
  blocking collectives: 25.9 us -> 22 us
    all_gather x2 -> x0, blocking collectives: 25.9 us -> none  [the longest x1 21.2 us: on_device(): own_w = lax.all_gather(weight, 'space', axis=0, axis_index_groups=Z_GROUPS)]
    all_to_all x0 -> x1, blocking collectives: none -> 22 us  [on_device(): lax.all_to_all(jnp.broadcast_to(stale[None], (4, 2 * feats, tok_dev)), 's...]
    all_gather x0 -> x1, waiting for transfers between devices: none -> 15.4 us  [on_device(): weight = lax.all_gather(weight, 'space', axis=0, tiled=True)]
    ppermute x6 -> x2, starting transfers between devices: 20.3 us -> 5.46 us  [the longest x1 3.54 us: on_device(): before = lax.ppermute(latent, 'space', UP)]
    ppermute x1, waiting for transfers between devices: 0.01 us -> 12.5 us  [on_device(): left_kv = lax.ppermute(own_kv, 'space', RIGHT)]
    all_to_all x1 -> x0, starting transfers between devices: 6.7 us -> none  [on_device(): lax.all_to_all(jnp.broadcast_to(stale[None], (4, 2 * feats, tok_dev)), 's...]
    all_to_all x2, waiting for transfers between devices: 1.1 us -> 5.21 us  [exchanged(): return lax.all_to_all(stats, 'space', 0, 0, tiled=True)]
    all_to_all x1 -> x0, waiting for transfers between devices: 3.79 us -> none  [on_device(): lax.all_to_all(jnp.broadcast_to(stale[None], (4, 2 * feats, tok_dev)), 's...]
  transfers between devices with their start and end apart: 15 -> 11, of which waited for: 7 -> 6; matrix products, arithmetic and copies ran while one was open for 5% -> 10% of each run, Pallas kernels for 9% -> 2%
where the time goes in v5:
time: 150 us; the launch traced here: 149 us
  starting transfers between devices  36.5 us (24%)
  waiting for transfers between devices  36.1 us (24%)
  blocking collectives  22 us (15%)
  local copies, waits for them, and re-layouts  20.1 us (13%)
  Pallas kernels  19 us (13%)
  between operations  15 us (10%)
    all_to_all x1, blocking collectives, on_device(): lax.all_to_all(jnp.broadcast_to(stale[None], (4, 2 * feats, tok_dev)), 's...  22 us
    pallas_call x6, Pallas kernels, call(): pl.pallas_call(kernel, out_shape=[jax.ShapeDtypeStruct(shape, dtype) for...  19 us
    all_gather x1, waiting for transfers between devices, on_device(): weight = lax.all_gather(weight, 'space', axis=0, tiled=True)  15.4 us
    ppermute x1, waiting for transfers between devices, on_device(): left_kv = lax.ppermute(own_kv, 'space', RIGHT)  12.5 us
    all_to_all x2, starting transfers between devices, exchanged(): return lax.all_to_all(stats, 'space', 0, 0, tiled=True)  11.8 us
    all_to_all x2, waiting for transfers between devices, exchanged(): return lax.all_to_all(stats, 'space', 0, 0, tiled=True)  5.21 us
    unnamed x36, local copies, waits for them, and re-layouts  4.81 us
    ppermute x1, starting transfers between devices, on_device(): low_kv = lax.ppermute(left_kv[:2], 'space', RIGHT)  4.2 us
  transfers between devices with their start and end apart: 11, of which 6 were waited for; matrix products, arithmetic and copies ran while one was open for 10% of the time, Pallas kernels for 2%

profile of v5, /device:TPU:1, one launch (start us, length us, event | category | flops | bytes accessed | tf_op | source)
XLA Modules:
  0.0 149.4 jit_solution(4614791554207032906)
XLA Ops:
  7.2 1.7 %pad.9 = bf16[192,640]{1,0:T(8,128)(2,1)} pad(bf16[180,640]{1,0:T(8,128)(2,1)} %param.16, bf16[]{:T(256)} %constant.36.clone.1), padding=0_12x0_0 | pad | bytes 476162 | tf_op jit(solution)/shard_map/jit(_pad)/pad | solution.py:280
  9.0 1.0 broadcast_in_dim.24
  10.0 22.0 %all_to_all.15.own_ref = bf16[4,640,128]{2,1,0:T(8,128)(2,1)S(1)} all-to-all(bf16[4,640,128]{2,1,0:T(8,128)(2,1)S(1)} %broadcast_in_dim.24), channel_id=1, replica_groups={{0,2,4,6},{1,3,5,7},{8,10,12,14},{9,11,13,15},{16,18,20,22},{17,19,21,2..., dimensions={0} | all-to-all | bytes 1310720 | tf_op jit(solution)/shard_map/all_to_all | solution.py:303
  32.0 3.9 %collective-permute-start.2 = (bf16[4,640,128]{2,1,0:T(8,128)(2,1)S(1)}, bf16[4,640,128]{2,1,0:T(8,128)(2,1)S(1)}, u32[]{:S(2)}, u32[]{:S(2)}) collective-permute-start(bf16[4,640,128]{2,1,0:T(8,128)(2,1)S(1)} %all_to_all.15.own_ref), channel_id=1, source_target_pairs={{0,8},{1,9},{2,10},{3,11},{4,12},{5,13},{6,14},{7,15},{8,16},{9,17... | collective-permute-start | bytes 1966088 | tf_op jit(solution)/shard_map/ppermute | solution.py:311
  36.0 3.2 %collective-permute-start.4 = (bf16[4,640,128]{2,1,0:T(8,128)(2,1)S(1)}, bf16[4,640,128]{2,1,0:T(8,128)(2,1)S(1)}, u32[]{:S(2)}, u32[]{:S(2)}) collective-permute-start(bf16[4,640,128]{2,1,0:T(8,128)(2,1)S(1)} %all_to_all.15.own_ref), channel_id=1, source_target_pairs={{0,24},{1,25},{2,26},{3,27},{4,28},{5,29},{6,30},{7,31},{8,0},{9,1... | collective-permute-start | bytes 1966088 | tf_op jit(solution)/shard_map/ppermute | solution.py:312
  39.2 1.6 %shard_map.131 = f32[32,8,128]{2,1,0:T(8,128)} custom-call(bf16[128,640]{1,0:T(8,128)(2,1)S(1)} %copy-done.5), custom_call_target="tpu_custom_call" | custom-call | tf_op jit(solution)/shard_map/pallas_call | solution.py:245
  40.8 6.7 %all-to-all-start = ((f32[32,8,128]{2,1,0:T(8,128)}), f32[32,8,128]{2,1,0:T(8,128)S(1)}, u32[]{:S(2)}, u32[]{:S(2)}) async-start(f32[32,8,128]{2,1,0:T(8,128)} %shard_map.131), calls=%async_computation | async-start | bytes 262144 | tf_op jit(solution)/shard_map/all_to_all | solution.py:64
  47.5 3.5 %collective-permute-start = (bf16[128,640]{1,0:T(8,128)(2,1)S(1)}, bf16[128,640]{1,0:T(8,128)(2,1)S(1)}, u32[]{:S(2)}, u32[]{:S(2)}) collective-permute-start(bf16[128,640]{1,0:T(8,128)(2,1)S(1)} %copy-done.5), channel_id=1, source_target_pairs={{0,1},{1,2},{2,3},{3,4},{4,5},{5,6},{6,7},{7,8},{8,9},{9,10},{10,1... | collective-permute-start | bytes 491528 | tf_op jit(solution)/shard_map/ppermute | solution.py:285
  51.0 1.9 %collective-permute-start.1 = (bf16[128,640]{1,0:T(8,128)(2,1)S(1)}, bf16[128,640]{1,0:T(8,128)(2,1)S(1)}, u32[]{:S(2)}, u32[]{:S(2)}) collective-permute-start(bf16[128,640]{1,0:T(8,128)(2,1)S(1)} %copy-done.5), channel_id=1, source_target_pairs={{1,0},{2,1},{3,2},{4,3},{5,4},{6,5},{7,6},{8,7},{9,8},{10,9},{11,1... | collective-permute-start | bytes 491528 | tf_op jit(solution)/shard_map/ppermute | solution.py:286
  53.7 12.5 %collective-permute-done.2.left_ref = bf16[4,640,128]{2,1,0:T(8,128)(2,1)S(1)} collective-permute-done((bf16[4,640,128]{2,1,0:T(8,128)(2,1)S(1)}, bf16[4,640,128]{2,1,0:T(8,128)(2,1)S(1)}, u32[]{:S(2)}, u32[]{:S(2)}) %collective-permute-start.2) | collective-permute-done | bytes 655392 | tf_op jit(solution)/shard_map/ppermute | solution.py:311
  67.0 4.2 %collective-permute-start.3 = (bf16[2,640,128]{2,1,0:T(8,128)(2,1)}, bf16[2,640,128]{2,1,0:T(8,128)(2,1)}, u32[]{:S(2)}, u32[]{:S(2)}) collective-permute-start(bf16[2,640,128]{2,1,0:T(8,128)(2,1)} %slice.8), channel_id=1, source_target_pairs={{0,8},{1,9},{2,10},{3,11},{4,12},{5,13},{6,14},{7,15},{8,16},{9,17... | collective-permute-start | bytes 983048 | tf_op jit(solution)/shard_map/ppermute | solution.py:313
  72.0 3.3 %collective-permute-start.5 = (bf16[2,640,128]{2,1,0:T(8,128)(2,1)}, bf16[2,640,128]{2,1,0:T(8,128)(2,1)}, u32[]{:S(2)}, u32[]{:S(2)}) collective-permute-start(bf16[2,640,128]{2,1,0:T(8,128)(2,1)} %slice.9), channel_id=1, source_target_pairs={{0,24},{1,25},{2,26},{3,27},{4,28},{5,29},{6,30},{7,31},{8,0},{9,1... | collective-permute-start | bytes 983048 | tf_op jit(solution)/shard_map/ppermute | solution.py:314
  77.4 0.9 copy-done.11
  78.3 1.6 %shard_map.132 = bf16[128,5760]{1,0:T(8,128)(2,1)S(1)} custom-call(s32[2]{0:T(128)S(1)} %pad_add_fusion.where_ref, f32[32,8,128]{2,1,0:T(8,128)S(1)} %all-to-all-done.every_ref, bf16[128,640]{1,0:T(8,128)(2,1)S(1)} %collective-permute-done.before_ref, bf16[128,640]{1,0:T(8,128)(2,1)S(1)} %copy-done.5, bf16[128,640]{1,0:T(8,128)(2,1)S(1)} %copy-done.11, ...), custom_call_target="tpu_custom_call" | custom-call | tf_op jit(solution)/shard_map/pallas_call | solution.py:245
  79.8 1.7 %copy.14 = bf16[128,5760]{0,1:T(8,128)(2,1)} copy(bf16[128,5760]{1,0:T(8,128)(2,1)S(1)} %shard_map.132) | data formatting | bytes 2949120 | tf_op jit(solution)/shard_map/pallas_call | solution.py:245
  81.5 3.3 %reshape.18 = bf16[128,32,180]{0,2,1:T(8,128)(2,1)} reshape(bf16[128,5760]{0,1:T(8,128)(2,1)} %copy.14) | data formatting | bytes 2949120 | tf_op jit(solution)/shard_map/reshape | solution.py:299
  84.8 2.8 %pad.8 = bf16[128,32,192]{0,2,1:T(8,128)(2,1)} pad(bf16[128,32,180]{0,2,1:T(8,128)(2,1)} %reshape.18, bf16[]{:T(256)} %constant.36.clone.1), padding=0_0x0_0x0_12 | pad | bytes 3047426 | tf_op jit(solution)/shard_map/jit(_pad)/pad | solution.py:299
  88.3 2.6 %copy.15.unfolded_ref = bf16[128,6144]{1,0:T(8,128)(2,1)} copy(bf16[128,6144]{0,1:T(8,128)(2,1)} %bitcast.17) | data formatting | bytes 3145728 | tf_op jit(solution)/shard_map/optimization_barrier | solution.py:316
  91.0 15.4 %all-gather.2.cloned.1.call-done.weight_ref = bf16[6144,640]{1,0:T(8,128)(2,1)} async-done(((bf16[192,640]{1,0:T(8,128)(2,1)}), bf16[6144,640]{1,0:T(8,128)(2,1)}) %all-gather.2.cloned.1.call-update) | async-done | bytes 7864336 | tf_op jit(solution)/shard_map/all_gather | solution.py:281
  106.4 7.2 %shard_map.133 = (bf16[128,640]{1,0:T(8,128)(2,1)}, f32[32,8,128]{2,1,0:T(8,128)}) custom-call(bf16[128,6144]{1,0:T(8,128)(2,1)} %copy.15.unfolded_ref, bf16[6144,640]{1,0:T(8,128)(2,1)} %all-gather.2.cloned.1.call-done.weight_ref, bf16[128,640]{1,0:T(8,128)(2,1)} %latent_ref.5, f32[1,640]{1,0:T(1,128)} %add.17.bias_ref), custom_call_target="tpu_custom_call" | custom-call | tf_op jit(solution)/shard_map/pallas_call | solution.py:245
  113.6 5.1 %all-to-all-start.2 = ((f32[32,8,128]{2,1,0:T(8,128)}), f32[32,8,128]{2,1,0:T(8,128)S(1)}, u32[]{:S(2)}, u32[]{:S(2)}) async-start(f32[32,8,128]{2,1,0:T(8,128)} %get-tuple-element.14), calls=%async_computation.2 | async-start | bytes 262144 | tf_op jit(solution)/shard_map/all_to_all | solution.py:64
  118.7 2.3 %collective-permute-start.6 = (bf16[128,640]{1,0:T(8,128)(2,1)}, bf16[128,640]{1,0:T(8,128)(2,1)S(1)}, u32[]{:S(2)}, u32[]{:S(2)}) collective-permute-start(bf16[128,640]{1,0:T(8,128)(2,1)} %get-tuple-element.15.mid_ref), channel_id=1, source_target_pairs={{0,1},{1,0},{2,3},{3,2},{4,5},{5,4},{6,7},{7,6},{8,9},{9,8},{10,11... | collective-permute-start | bytes 491528 | tf_op jit(solution)/shard_map/ppermute | solution.py:336
  121.0 1.1 collective-permute-done.6.other_ref
  122.2 5.2 %all-to-all-done.2.every_ref = f32[32,8,128]{2,1,0:T(8,128)S(1)} async-done(((f32[32,8,128]{2,1,0:T(8,128)}), f32[32,8,128]{2,1,0:T(8,128)S(1)}, u32[]{:S(2)}, u32[]{:S(2)}) %all-to-all-start.2) | async-done | bytes 131104 | tf_op jit(solution)/shard_map/all_to_all | solution.py:64
  127.4 1.3 copy-done.6
  128.7 0.9 copy-done.7
  129.6 1.7 %shard_map.134 = (bf16[256,384]{1,0:T(8,128)(2,1)S(1)}, bf16[640,128]{1,0:T(8,128)(2,1)}) custom-call(f32[32,8,128]{2,1,0:T(8,128)S(1)} %all-to-all-done.2.every_ref, bf16[128,640]{1,0:T(8,128)(2,1)S(1)} %copy-done.7, bf16[128,640]{1,0:T(8,128)(2,1)S(1)} %collective-permute-done.6.other_ref, f32[1,640]{1,0:T(1,128)S(1)} %broadcast_in_dim.25.gain_ref, ...), custom_call_target="tpu_custom_call" | custom-call | tf_op jit(solution)/shard_map/pallas_call | solution.py:245
  131.3 1.0 copy-done.12
  132.2 5.6 %shard_map.135 = (f32[128,384]{1,0:T(8,128)S(1)}, f32[128,384]{1,0:T(8,128)S(1)}) custom-call(s32[2]{0:T(128)S(1)} %pad_add_fusion.where_ref, bf16[256,384]{1,0:T(8,128)(2,1)S(1)} %get-tuple-element.16.q_ref, bf16[4,640,128]{2,1,0:T(8,128)(2,1)S(1)} %all_to_all.15.own_ref, bf16[4,640,128]{2,1,0:T(8,128)(2,1)S(1)} %copy-done.2, ...), custom_call_target="tpu_custom_call" | custom-call | tf_op jit(solution)/shard_map/pallas_call | solution.py:245
  137.9 2.3 %collective-permute-start.7 = (f32[128,384]{1,0:T(8,128)S(1)}, f32[128,384]{1,0:T(8,128)S(1)}, u32[]{:S(2)}, u32[]{:S(2)}) collective-permute-start(f32[128,384]{1,0:T(8,128)S(1)} %get-tuple-element.21), channel_id=1, source_target_pairs={{0,1},{1,0},{2,3},{3,2},{4,5},{5,4},{6,7},{7,6},{8,9},{9,8},{10,11... | collective-permute-start | bytes 589832 | tf_op jit(solution)/shard_map/ppermute | solution.py:355
  140.2 1.0 collective-permute-done.7.other_ref
  141.3 1.3 shard_map.136
  (53 shorter events, 4.4 us)
Async XLA Ops:
  7.2 68.2 %copy-start = (f32[320,640]{1,0:T(8,128)S(1)}, f32[320,640]{1,0:T(8,128)}, u32[]{:S(2)}) copy-start(f32[320,640]{1,0:T(8,128)} %param.18) | copy-start | bytes 2457604
  7.2 32.0 %copy-start.5 = (bf16[128,640]{1,0:T(8,128)(2,1)S(1)}, bf16[128,640]{1,0:T(8,128)(2,1)}, u32[]{:S(2)}) copy-start(bf16[128,640]{1,0:T(8,128)(2,1)} %latent_ref.5) | copy-start | bytes 491524
  7.2 99.2 %all-gather.2.cloned.1.call-start = ((), (), s32[]{:S(2)}) async-start(), calls=%async_computation.3 | async-start | bytes 8110080 | tf_op jit(solution)/shard_map/all_gather | solution.py:281
  32.0 43.9 %copy-start.14 = (f32[640]{0:T(1024)S(1)}, f32[640]{0:T(1024)}, u32[]{:S(2)}) copy-start(f32[640]{0:T(1024)} %param.14) | copy-start | bytes 7684
  32.0 44.0 %copy-start.15 = (f32[640]{0:T(1024)S(1)}, f32[640]{0:T(1024)}, u32[]{:S(2)}) copy-start(f32[640]{0:T(1024)} %param.15) | copy-start | bytes 7684
  32.0 44.0 %copy-start.13 = (f32[640]{0:T(1024)S(1)}, f32[640]{0:T(1024)}, u32[]{:S(2)}) copy-start(f32[640]{0:T(1024)} %param.17) | copy-start | bytes 7684
  32.0 34.2 %collective-permute-start.2 = (bf16[4,640,128]{2,1,0:T(8,128)(2,1)S(1)}, bf16[4,640,128]{2,1,0:T(8,128)(2,1)S(1)}, u32[]{:S(2)}, u32[]{:S(2)}) collective-permute-start(bf16[4,640,128]{2,1,0:T(8,128)(2,1)S(1)} %all_to_all.15.own_ref), channel_id=1, source_target_pairs={{0,8},{1,9},{2,10},{3,11},{4,12},{5,13},{6,14},{7,15},{8,16},{9,17... | collective-permute-start | bytes 1966088 | tf_op jit(solution)/shard_map/ppermute | solution.py:311
  36.0 35.3 %collective-permute-start.4 = (bf16[4,640,128]{2,1,0:T(8,128)(2,1)S(1)}, bf16[4,640,128]{2,1,0:T(8,128)(2,1)S(1)}, u32[]{:S(2)}, u32[]{:S(2)}) collective-permute-start(bf16[4,640,128]{2,1,0:T(8,128)(2,1)S(1)} %all_to_all.15.own_ref), channel_id=1, source_target_pairs={{0,24},{1,25},{2,26},{3,27},{4,28},{5,29},{6,30},{7,31},{8,0},{9,1... | collective-permute-start | bytes 1966088 | tf_op jit(solution)/shard_map/ppermute | solution.py:312
  40.8 36.6 %all-to-all-start = ((f32[32,8,128]{2,1,0:T(8,128)}), f32[32,8,128]{2,1,0:T(8,128)S(1)}, u32[]{:S(2)}, u32[]{:S(2)}) async-start(f32[32,8,128]{2,1,0:T(8,128)} %shard_map.131), calls=%async_computation | async-start | bytes 262144 | tf_op jit(solution)/shard_map/all_to_all | solution.py:64
  47.5 29.2 %collective-permute-start = (bf16[128,640]{1,0:T(8,128)(2,1)S(1)}, bf16[128,640]{1,0:T(8,128)(2,1)S(1)}, u32[]{:S(2)}, u32[]{:S(2)}) collective-permute-start(bf16[128,640]{1,0:T(8,128)(2,1)S(1)} %copy-done.5), channel_id=1, source_target_pairs={{0,1},{1,2},{2,3},{3,4},{4,5},{5,6},{6,7},{7,8},{8,9},{9,10},{10,1... | collective-permute-start | bytes 491528 | tf_op jit(solution)/shard_map/ppermute | solution.py:285
  51.0 25.6 %collective-permute-start.1 = (bf16[128,640]{1,0:T(8,128)(2,1)S(1)}, bf16[128,640]{1,0:T(8,128)(2,1)S(1)}, u32[]{:S(2)}, u32[]{:S(2)}) collective-permute-start(bf16[128,640]{1,0:T(8,128)(2,1)S(1)} %copy-done.5), channel_id=1, source_target_pairs={{1,0},{2,1},{3,2},{4,3},{5,4},{6,5},{7,6},{8,7},{9,8},{10,9},{11,1... | collective-permute-start | bytes 491528 | tf_op jit(solution)/shard_map/ppermute | solution.py:286
  66.2 10.5 %copy-start.1 = (bf16[4,640,128]{2,1,0:T(8,128)(2,1)}, bf16[4,640,128]{2,1,0:T(8,128)(2,1)S(1)}, u32[]{:S(2)}) copy-start(bf16[4,640,128]{2,1,0:T(8,128)(2,1)S(1)} %collective-permute-done.2.left_ref) | copy-start | bytes 1966084
  67.0 20.6 %collective-permute-start.3 = (bf16[2,640,128]{2,1,0:T(8,128)(2,1)}, bf16[2,640,128]{2,1,0:T(8,128)(2,1)}, u32[]{:S(2)}, u32[]{:S(2)}) collective-permute-start(bf16[2,640,128]{2,1,0:T(8,128)(2,1)} %slice.8), channel_id=1, source_target_pairs={{0,8},{1,9},{2,10},{3,11},{4,12},{5,13},{6,14},{7,15},{8,16},{9,17... | collective-permute-start | bytes 983048 | tf_op jit(solution)/shard_map/ppermute | solution.py:313
  71.2 5.5 %copy-start.3 = (bf16[4,640,128]{2,1,0:T(8,128)(2,1)}, bf16[4,640,128]{2,1,0:T(8,128)(2,1)S(1)}, u32[]{:S(2)}) copy-start(bf16[4,640,128]{2,1,0:T(8,128)(2,1)S(1)} %collective-permute-done.4.right_ref) | copy-start | bytes 1966084
  72.0 16.3 %collective-permute-start.5 = (bf16[2,640,128]{2,1,0:T(8,128)(2,1)}, bf16[2,640,128]{2,1,0:T(8,128)(2,1)}, u32[]{:S(2)}, u32[]{:S(2)}) collective-permute-start(bf16[2,640,128]{2,1,0:T(8,128)(2,1)} %slice.9), channel_id=1, source_target_pairs={{0,24},{1,25},{2,26},{3,27},{4,28},{5,29},{6,30},{7,31},{8,0},{9,1... | collective-permute-start | bytes 983048 | tf_op jit(solution)/shard_map/ppermute | solution.py:314
  76.7 0.7 copy-start.10
  77.4 0.9 copy-start.11
  90.9 30.0 %copy-start.16 = (f32[640]{0:T(1024)S(1)}, f32[640]{0:T(1024)}, u32[]{:S(2)}) copy-start(f32[640]{0:T(1024)} %param.19) | copy-start | bytes 7684
  90.9 30.1 %copy-start.17 = (f32[640]{0:T(1024)S(1)}, f32[640]{0:T(1024)}, u32[]{:S(2)}) copy-start(f32[640]{0:T(1024)} %param.20) | copy-start | bytes 7684
  113.6 17.7 %copy-start.2 = (bf16[4,640,128]{2,1,0:T(8,128)(2,1)S(1)}, bf16[4,640,128]{2,1,0:T(8,128)(2,1)}, u32[]{:S(2)}) copy-start(bf16[4,640,128]{2,1,0:T(8,128)(2,1)} %copy-done.1) | copy-start | bytes 1966084
  113.6 17.7 %copy-start.4 = (bf16[4,640,128]{2,1,0:T(8,128)(2,1)S(1)}, bf16[4,640,128]{2,1,0:T(8,128)(2,1)}, u32[]{:S(2)}) copy-start(bf16[4,640,128]{2,1,0:T(8,128)(2,1)} %copy-done.3) | copy-start | bytes 1966084
  113.6 13.8 %all-to-all-start.2 = ((f32[32,8,128]{2,1,0:T(8,128)}), f32[32,8,128]{2,1,0:T(8,128)S(1)}, u32[]{:S(2)}, u32[]{:S(2)}) async-start(f32[32,8,128]{2,1,0:T(8,128)} %get-tuple-element.14), calls=%async_computation.2 | async-start | bytes 262144 | tf_op jit(solution)/shard_map/all_to_all | solution.py:64
  118.7 3.5 %collective-permute-start.6 = (bf16[128,640]{1,0:T(8,128)(2,1)}, bf16[128,640]{1,0:T(8,128)(2,1)S(1)}, u32[]{:S(2)}, u32[]{:S(2)}) collective-permute-start(bf16[128,640]{1,0:T(8,128)(2,1)} %get-tuple-element.15.mid_ref), channel_id=1, source_target_pairs={{0,1},{1,0},{2,3},{3,2},{4,5},{5,4},{6,7},{7,6},{8,9},{9,8},{10,11... | collective-permute-start | bytes 491528 | tf_op jit(solution)/shard_map/ppermute | solution.py:336
  127.4 1.3 copy-start.6
  128.7 0.9 copy-start.7
  131.3 10.0 %copy-start.8 = (bf16[128,640]{1,0:T(8,128)(2,1)S(1)}, bf16[128,640]{1,0:T(8,128)(2,1)}, u32[]{:S(2)}) copy-start(bf16[128,640]{1,0:T(8,128)(2,1)} %get-tuple-element.15.mid_ref) | copy-start | bytes 491524
  131.3 10.0 %copy-start.9 = (bf16[320,640]{1,0:T(8,128)(2,1)S(1)}, bf16[320,640]{1,0:T(8,128)(2,1)}, u32[]{:S(2)}) copy-start(bf16[320,640]{1,0:T(8,128)(2,1)} %weight_ref.1) | copy-start | bytes 1228804
  131.3 1.0 copy-start.12
  137.9 3.4 %collective-permute-start.7 = (f32[128,384]{1,0:T(8,128)S(1)}, f32[128,384]{1,0:T(8,128)S(1)}, u32[]{:S(2)}, u32[]{:S(2)}) collective-permute-start(f32[128,384]{1,0:T(8,128)S(1)} %get-tuple-element.21), channel_id=1, source_target_pairs={{0,1},{1,0},{2,3},{3,2},{4,5},{5,4},{6,7},{7,6},{8,9},{9,8},{10,11... | collective-permute-start | bytes 589832 | tf_op jit(solution)/shard_map/ppermute | solution.py:355
Sparse Core Ops, SparseCore 0:
  10.2 96.1 all-gather.1

commit v6 on v4

--- a/solution.py
+++ b/solution.py
@@ -132,8 +132,7 @@
     own_ref,
     left_ref,
     right_ref,
-    low_ref,
-    high_ref,
+    far_ref,
     kept_ref,
     given_ref,
     held_ref,
@@ -141,20 +140,18 @@
 ):
     core, x = where_ref[0], where_ref[2]
     count = kept_ref.shape[0]
-    sources = ((own_ref, 0, 0), (left_ref, 3, 0), (right_ref, 1, 0), (low_ref, 2, 0), (high_ref, 2, 2))
-    copies, at = [], 0
-    for index, (ref, _, _) in enumerate(sources):
-        size = ref.shape[0]
-        copy = pltpu.make_async_copy(ref, held_ref.at[at : at + size], sems.at[index])
+    sources = ((own_ref, 0), (left_ref, 3), (right_ref, 1), (far_ref, 2))
+    copies = []
+    for index, (ref, _) in enumerate(sources):
+        copy = pltpu.make_async_copy(ref, held_ref.at[4 * index : 4 * index + 4], sems.at[index])
         copy.start()
-        copies.append((copy, at, size))
-        at += size
+        copies.append(copy)
     total = None
-    for (_, step, first), (copy, at, size) in zip(sources, copies, strict=True):
-        copy.wait()
-        base = 4 * ((x + step) & 3) + first
-        for z in range(size):
-            part = dot32(blocks_ref[base + z], held_ref[at + z])
+    for index, (_, step) in enumerate(sources):
+        copies[index].wait()
+        base = 4 * ((x + step) & 3)
+        for z in range(4):
+            part = dot32(blocks_ref[base + z], held_ref[4 * index + z])
             total = part if total is None else total + part
     kept_ref[...] = jnp.where(core == 0, total[:count], total[count:])
     given_ref[...] = jnp.where(core == 0, total[count:], total[:count])
@@ -182,76 +179,78 @@
     fresh_ref[...] = dot_t(weight_ref[HEADS * HEAD_DIM :], normed[:count]).astype(jnp.bfloat16)
 
 
-def attend(
-    where_ref,
-    q_ref,
-    own_ref,
-    left_ref,
-    right_ref,
-    low_ref,
-    high_ref,
-    fresh_ref,
-    out_ref,
-    given_ref,
-    held_ref,
-    sems,
-):
+def attention(q_ref, blocks, replaced, fresh_ref, before):
+    count = q_ref.shape[0] // 2
+    lane = lax.broadcasted_iota(jnp.int32, (2 * count, 128), 1)
+    outs = []
+    for head in range(HEADS):
+        at = 128 * (head // 2)
+        v_at = HEADS * HEAD_DIM + at
+        mine = (lane < 64) if head % 2 == 0 else (lane >= 64)
+        query = q_ref[:, at : at + 128].astype(jnp.float32)
+        query = jnp.where(mine, query, 0.0).astype(jnp.bfloat16)
+        last = head == HEADS - 1
+        scores = []
+        for index, parts in enumerate(blocks):
+            keys = [ref[z, at : at + 128] for ref, z in parts]
+            score = dot32(query, jnp.concatenate(keys, axis=1))
+            if replaced is not None and index == 0:
+                score = jnp.where(replaced, LOW, score)
+            scores.append(score)
+        values = []
+        for parts in blocks:
+            value = jnp.concatenate([ref[z, v_at : v_at + 128] for ref, z in parts], axis=1)
+            values.append(value)
+        if fresh_ref is not None:
+            score = dot32(query[:count], fresh_ref[at : at + 128])
+            score = jnp.concatenate([score, jnp.full((count, count), LOW, jnp.float32)], axis=0)
+            scores.append(score)
+            values.append(fresh_ref[v_at : v_at + 128])
+        peak = scores[0].max(axis=1, keepdims=True)
+        for score in scores[1:]:
+            peak = jnp.maximum(peak, score.max(axis=1, keepdims=True))
+        if before is None:
+            total = jnp.zeros((2 * count, 1), jnp.float32)
+            mixed = jnp.zeros((2 * count, 128), jnp.float32)
+        else:
+            held = before[:, 320 + head : 321 + head]
+            peak = jnp.maximum(peak, held)
+            factor = jnp.exp(held - peak)
+            total = before[:, 328 + head : 329 + head] * factor
+            mixed = before[:, at : at + 128] * factor
+        for score, value in zip(scores, values, strict=True):
+            weights = jnp.exp(score - peak)
+            total = total + weights.sum(axis=1, keepdims=True)
+            if last:
+                value = jnp.concatenate([value, jnp.zeros_like(value)], axis=0)
+            mixed = mixed + dot_t(weights.astype(jnp.bfloat16), value)
+        outs.append((mixed, peak, total))
+    stats = jnp.where(lane < 64, outs[4][0], 0.0)
+    for head in range(HEADS):
+        stats = jnp.where(lane == 64 + head, outs[head][1], stats)
+        stats = jnp.where(lane == 72 + head, outs[head][2], stats)
+    return (
+        jnp.where(lane < 64, outs[0][0], outs[1][0]),
+        jnp.where(lane < 64, outs[2][0], outs[3][0]),
+        stats,
+    )
+
+
+def attend_near(where_ref, q_ref, own_ref, left_ref, right_ref, fresh_ref, out_ref):
     my_z = where_ref[3]
-    count = out_ref.shape[0]
-    copies, at = [], 0
-    for index, ref in enumerate((own_ref, left_ref, right_ref, low_ref, high_ref)):
-        size = ref.shape[0]
-        copy = pltpu.make_async_copy(ref, held_ref.at[at : at + size], sems.at[index])
-        copy.start()
-        copies.append(copy)
-        at += size
-    lane = lax.broadcasted_iota(jnp.int32, (2 * count, 128), 1)
+    count = q_ref.shape[0] // 2
     row = lax.broadcasted_iota(jnp.int32, (2 * count, 4 * count), 0)
     block = lax.broadcasted_iota(jnp.int32, (2 * count, 4 * count), 1) // count
     replaced = (row < count) & (block == my_z)
-    outs = []
-    for head in range(HEADS):
-        at = 128 * (head // 2)
-        mine = (lane < 64) if head % 2 == 0 else (lane >= 64)
-        query = q_ref[:, at : at + 128].astype(jnp.float32)
-        query = jnp.where(mine, query, 0.0).astype(jnp.bfloat16)
-        fresh = dot32(query[:count], fresh_ref[at : at + 128])
-        fresh = jnp.concatenate([fresh, jnp.full((count, count), LOW, jnp.float32)], axis=0)
-        scores = []
-        peak = fresh.max(axis=1, keepdims=True)
-        for x in range(4):
-            if head == 0:
-                copies[x].wait()
-                if x == 3:
-                    copies[4].wait()
-            keys = [held_ref[4 * x + z, at : at + 128] for z in range(4)]
-            score = dot32(query, jnp.concatenate(keys, axis=1))
-            if x == 0:
-                score = jnp.where(replaced, LOW, score)
-            peak = jnp.maximum(peak, score.max(axis=1, keepdims=True))
-            scores.append(score)
-        v_at = HEADS * HEAD_DIM + at
-        weights = jnp.exp(fresh - peak)
-        total = weights.sum(axis=1, keepdims=True)
-        tail = (lambda v: jnp.concatenate([v, jnp.zeros_like(v)], axis=0)) if head == HEADS - 1 else (lambda v: v)
-        mixed = dot_t(weights.astype(jnp.bfloat16), tail(fresh_ref[v_at : v_at + 128]))
-        for x in range(4):
-            weights = jnp.exp(scores[x] - peak)
-            total = total + weights.sum(axis=1, keepdims=True)
-            values = [held_ref[4 * x + z, v_at : v_at + 128] for z in range(4)]
-            values = tail(jnp.concatenate(values, axis=1))
-            mixed = mixed + dot_t(weights.astype(jnp.bfloat16), values)
-        outs.append((mixed, peak, total))
-    last = jnp.where(lane < 64, outs[4][0], 0.0)
-    for head in range(HEADS):
-        last = jnp.where(lane == 64 + head, outs[head][1], last)
-        last = jnp.where(lane == 72 + head, outs[head][2], last)
-    tiles = (
-        jnp.where(lane < 64, outs[0][0], outs[1][0]),
-        jnp.where(lane < 64, outs[2][0], outs[3][0]),
-        last,
-    )
-    for tile, value in enumerate(tiles):
+    blocks = [[(ref, z) for z in range(4)] for ref in (own_ref, left_ref, right_ref)]
+    for tile, value in enumerate(attention(q_ref, blocks, replaced, fresh_ref, None)):
+        out_ref[:, 128 * tile : 128 * (tile + 1)] = value
+
+
+def attend_far(q_ref, far_ref, near_ref, out_ref, given_ref):
+    count = out_ref.shape[0]
+    blocks = [[(far_ref, z) for z in range(4)]]
+    for tile, value in enumerate(attention(q_ref, blocks, None, None, near_ref)):
         out_ref[:, 128 * tile : 128 * (tile + 1)] = value[:count]
         given_ref[:, 128 * tile : 128 * (tile + 1)] = value[count:]
 
@@ -282,17 +281,17 @@
     out_ref[...] = result.astype(jnp.bfloat16)
 
 
-def call(kernel, outs, smem, *args, scratch=(), fetched=()):
+def call(kernel, outs, smem, *args, scratch=(), fetched=(), mib=32):
     return pl.pallas_call(
         kernel,
         out_shape=[jax.ShapeDtypeStruct(shape, dtype) for shape, dtype in outs],
         in_specs=[
-            SMEM if i < smem else pl.BlockSpec(memory_space=pl.ANY) if i in fetched else VMEM
+            SMEM if i < smem else pl.BlockSpec(memory_space=pltpu.HBM) if i in fetched else VMEM
             for i in range(len(args))
         ],
         out_specs=[VMEM] * len(outs),
         scratch_shapes=list(scratch),
-        compiler_params=pltpu.CompilerParams(vmem_limit_bytes=40 * 1024 * 1024),
+        compiler_params=pltpu.CompilerParams(vmem_limit_bytes=mib * 1024 * 1024),
     )(*args)
 
 
@@ -320,9 +319,10 @@
 
     weight = jnp.pad(conv_weight, ((0, ROWS - rows), (0, 0)))
     own_w = lax.all_gather(weight, "space", axis=0, axis_index_groups=Z_GROUPS)
+    outer = lax.ppermute(latent, "space", OUTER)
+    own_w, outer = lax.optimization_barrier((own_w, outer))
     left_w = lax.ppermute(own_w, "space", RIGHT)
     right_w = lax.ppermute(own_w, "space", LEFT)
-    outer = lax.ppermute(latent, "space", OUTER)
     (stats1,) = call(first_stats, [table], 0, latent)
     every1 = exchanged(stats1)
     pair = lax.all_gather(
@@ -339,8 +339,7 @@
         tiled=True,
     )
 
-    low_w = lax.ppermute(left_w[:2], "space", RIGHT)
-    high_w = lax.ppermute(right_w[2:], "space", LEFT)
+    far_w = lax.ppermute(right_w, "space", LEFT)
     (blocks,) = call(
         prepare,
         [((16, 2 * tok_dev, ROWS), bf16)],
@@ -366,43 +365,41 @@
         own_w,
         left_w,
         right_w,
-        low_w,
-        high_w,
-        scratch=[pltpu.VMEM((16, ROWS, width), bf16), pltpu.SemaphoreType.DMA((5,))],
-        fetched=(2, 3, 4, 5, 6),
+        far_w,
+        scratch=[pltpu.VMEM((16, ROWS, width), bf16), pltpu.SemaphoreType.DMA((4,))],
+        fetched=(2, 3, 4, 5),
+        mib=48,
     )
     other = lax.ppermute(given, "space", SWAP)
     mid, stats2 = call(middle, [((tok_dev, width), bf16), table], 0, kept, other, latent, bias)
     every2 = exchanged(stats2)
-    low_kv = lax.ppermute(left_kv[:2], "space", RIGHT)
-    high_kv = lax.ppermute(right_kv[2:], "space", LEFT)
+    other_mid = lax.ppermute(mid, "space", SWAP)
+    sent_kv, _ = lax.optimization_barrier((left_kv, every2))
+    far_kv = lax.ppermute(sent_kv, "space", RIGHT)
     query, fresh = call(
         project,
         [((2 * tok_dev, 384), bf16), ((2 * feats, tok_dev), bf16)],
         0,
         every2,
         mid,
-        lax.ppermute(mid, "space", SWAP),
+        other_mid,
         norm2_gain[None],
         norm2_shift[None],
         qkv_weight.T,
     )
     fresh_kv = fresh.reshape(2, feats, tok_dev).transpose(0, 2, 1)
-    mine, theirs = call(
-        attend,
-        [((tok_dev, 384), f32)] * 2,
+    (near,) = call(
+        attend_near,
+        [((2 * tok_dev, 384), f32)],
         1,
         where,
         query,
         own_kv,
         left_kv,
         right_kv,
-        low_kv,
-        high_kv,
         fresh,
-        scratch=[pltpu.VMEM((16, 2 * feats, tok_dev), bf16), pltpu.SemaphoreType.DMA((5,))],
-        fetched=(2, 3, 4, 5, 6),
-    )
+    )
+    mine, theirs = call(attend_far, [((tok_dev, 384), f32)] * 2, 0, query, far_kv, near)
     other = lax.ppermute(theirs, "space", SWAP)
     (result,) = call(finish, [((tok_dev, width), bf16)], 0, mine, other, mid, out_weight)
     return (result, fresh_kv)

time: 134 us -> 148 us (1.10)
  waiting for transfers between devices: 11.6 us -> 34.1 us
  local copies, waits for them, and re-layouts: 12.8 us -> 8.12 us
  blocking collectives: 25.9 us -> 21.5 us
  Pallas kernels: 19.9 us -> 21.9 us
    ppermute x5 -> x3, waiting for transfers between devices: 2.9 us -> 19.8 us  [the longest x1 16 us: on_device(): far_w = lax.ppermute(right_w, 'space', LEFT)]
    all_to_all x2, waiting for transfers between devices: 1.1 us -> 11.5 us  [exchanged(): return lax.all_to_all(stats, 'space', 0, 0, tiled=True)]
    ppermute x5 -> x3, starting transfers between devices: 15.8 us -> 8.98 us  [the longest x1 3.98 us: on_device(): far_w = lax.ppermute(right_w, 'space', LEFT)]
    all_to_all x2, starting transfers between devices: 13.6 us -> 19.8 us  [exchanged(): return lax.all_to_all(stats, 'space', 0, 0, tiled=True)]
    slice x4 -> x0, local copies, waits for them, and re-layouts: 5.42 us -> none  [the longest x1 1.86 us: on_device(): high_w = lax.ppermute(right_w[2:], 'space', LEFT)]
    all_to_all x1, waiting for transfers between devices: 3.79 us -> 0.01 us  [on_device(): lax.all_to_all(jnp.broadcast_to(stale[None], (4, 2 * feats, tok_dev)), 's...]
    all_gather x1, blocking collectives: 4.7 us -> 2.28 us  [on_device(): lax.all_gather(jnp.stack([latent, outer]), 'space', axis=0, axis_index_gr...]
    ppermute x1, waiting for transfers between devices: 2.24 us -> 0.01 us  [on_device(): outer = lax.ppermute(latent, 'space', OUTER)]
  transfers between devices with their start and end apart: 15 -> 13, of which waited for: 7 -> 8; matrix products, arithmetic and copies ran while one was open for 5% -> 1% of each run, Pallas kernels for 9% -> 12%
where the time goes in v6:
time: 148 us; the launch traced here: 147 us
  starting transfers between devices  59.1 us (40%)
  waiting for transfers between devices  34.1 us (23%)
  Pallas kernels  21.9 us (15%)
  blocking collectives  21.5 us (15%)
  local copies, waits for them, and re-layouts  8.12 us (5%)
  between operations  1.67 us (1%)
    pallas_call x8, Pallas kernels, call(): pl.pallas_call(kernel, out_shape=[jax.ShapeDtypeStruct(shape, dtype) for...  21.9 us
    all_to_all x2, starting transfers between devices, exchanged(): return lax.all_to_all(stats, 'space', 0, 0, tiled=True)  19.8 us
    all_gather x1, blocking collectives, on_device(): own_w = lax.all_gather(weight, 'space', axis=0, axis_index_groups=Z_GROUPS)  19.2 us
    ppermute x1, waiting for transfers between devices, on_device(): far_w = lax.ppermute(right_w, 'space', LEFT)  16 us
    all_to_all x2, waiting for transfers between devices, exchanged(): return lax.all_to_all(stats, 'space', 0, 0, tiled=True)  11.5 us
    unnamed x30, local copies, waits for them, and re-layouts  6.19 us
    all_to_all x1, starting transfers between devices, on_device(): lax.all_to_all(jnp.broadcast_to(stale[None], (4, 2 * feats, tok_dev)), 's...  5.02 us
    ppermute x1, starting transfers between devices, on_device(): right_kv = lax.ppermute(own_kv, 'space', LEFT)  4.55 us
  transfers between devices with their start and end apart: 13, of which 8 were waited for; matrix products, arithmetic and copies ran while one was open for 1% of the time, Pallas kernels for 12%

profile of v6, /device:TPU:1, one launch (start us, length us, event | category | flops | bytes accessed | tf_op | source)
XLA Modules:
  0.0 147.2 jit_solution(8197272944882740992)
XLA Ops:
  0.7 4.5 %collective-permute-start = (bf16[128,640]{1,0:T(8,128)(2,1)}, bf16[128,640]{1,0:T(8,128)(2,1)S(1)}, u32[]{:S(2)}, u32[]{:S(2)}) collective-permute-start(bf16[128,640]{1,0:T(8,128)(2,1)} %latent_ref.3), channel_id=1, source_target_pairs={{2,0},{4,2},{6,4},{8,6},{10,8},{12,10},{14,12},{16,14},{18,16},{20... | collective-permute-start | bytes 491528 | tf_op jit(solution)/shard_map/ppermute | solution.py:322
  5.2 1.0 pad.4
  6.2 19.2 %all-gather = bf16[768,640]{1,0:T(8,128)(2,1)S(1)} all-gather(bf16[192,640]{1,0:T(8,128)(2,1)S(1)} %pad.4), channel_id=2, replica_groups={{0,2,4,6},{1,3,5,7},{8,10,12,14},{9,11,13,15},{16,18,20,22},{17,19,21,2..., dimensions={0}, use_global_device_ids=true | all-gather | bytes 1228800 | tf_op jit(solution)/shard_map/all_gather | solution.py:321
  25.4 3.8 %collective-permute-start.1 = (bf16[4,192,640]{2,1,0:T(8,128)(2,1)S(1)}, bf16[4,192,640]{2,1,0:T(8,128)(2,1)}, u32[]{:S(2)}, u32[]{:S(2)}) collective-permute-start(bf16[4,192,640]{2,1,0:T(8,128)(2,1)S(1)} %bitcast.18), channel_id=1, source_target_pairs={{0,8},{1,9},{2,10},{3,11},{4,12},{5,13},{6,14},{7,15},{8,16},{9,17... | collective-permute-start | bytes 2949128 | tf_op jit(solution)/shard_map/ppermute | solution.py:324
  29.2 2.7 %collective-permute-start.2 = (bf16[4,192,640]{2,1,0:T(8,128)(2,1)S(1)}, bf16[4,192,640]{2,1,0:T(8,128)(2,1)}, u32[]{:S(2)}, u32[]{:S(2)}) collective-permute-start(bf16[4,192,640]{2,1,0:T(8,128)(2,1)S(1)} %bitcast.19), channel_id=1, source_target_pairs={{0,24},{1,25},{2,26},{3,27},{4,28},{5,29},{6,30},{7,31},{8,0},{9,1... | collective-permute-start | bytes 2949128 | tf_op jit(solution)/shard_map/ppermute | solution.py:325
  32.8 1.6 %shard_map.131 = f32[32,8,128]{2,1,0:T(8,128)} custom-call(bf16[128,640]{1,0:T(8,128)(2,1)S(1)} %copy-done.2), custom_call_target="tpu_custom_call" | custom-call | tf_op jit(solution)/shard_map/pallas_call | solution.py:285
  34.5 11.7 %all-to-all-start = ((f32[32,8,128]{2,1,0:T(8,128)}), f32[32,8,128]{2,1,0:T(8,128)S(1)}, u32[]{:S(2)}, u32[]{:S(2)}) async-start(f32[32,8,128]{2,1,0:T(8,128)} %shard_map.131), calls=%async_computation | async-start | bytes 262144 | tf_op jit(solution)/shard_map/all_to_all | solution.py:63
  46.2 2.3 %all-gather.1 = bf16[4,128,640]{2,1,0:T(8,128)(2,1)S(1)} all-gather(bf16[2,128,640]{2,1,0:T(8,128)(2,1)S(1)} %pad_maximum_fusion), channel_id=3, replica_groups={{0,1},{2,3},{4,5},{6,7},{8,9},{10,11},{12,13},{14,15},{16,17},{18,19},{..., dimensions={0}, use_global_device_ids=true | all-gather | bytes 983040 | tf_op jit(solution)/shard_map/all_gather | solution.py:328
  48.9 7.3 %all-to-all-done.every_ref = f32[32,8,128]{2,1,0:T(8,128)S(1)} async-done(((f32[32,8,128]{2,1,0:T(8,128)}), f32[32,8,128]{2,1,0:T(8,128)S(1)}, u32[]{:S(2)}, u32[]{:S(2)}) %all-to-all-start) | async-done | bytes 131104 | tf_op jit(solution)/shard_map/all_to_all | solution.py:63
  57.1 5.0 %all-to-all-start.2 = ((bf16[4,640,128]{2,1,0:T(8,128)(2,1)}), bf16[4,640,128]{2,1,0:T(8,128)(2,1)S(1)}, u32[]{:S(2)}, u32[]{:S(2)}) async-start(bf16[4,640,128]{2,1,0:T(8,128)(2,1)} %broadcast_in_dim.24), calls=%async_computation.2 | async-start | bytes 1310720 | tf_op jit(solution)/shard_map/all_to_all | solution.py:333
  62.2 4.0 %collective-permute-start.3 = (bf16[4,192,640]{2,1,0:T(8,128)(2,1)}, bf16[4,192,640]{2,1,0:T(8,128)(2,1)}, u32[]{:S(2)}, u32[]{:S(2)}) collective-permute-start(bf16[4,192,640]{2,1,0:T(8,128)(2,1)} %collective-permute-done.2.right_ref), channel_id=1, source_target_pairs={{0,24},{1,25},{2,26},{3,27},{4,28},{5,29},{6,30},{7,31},{8,0},{9,1... | collective-permute-start | bytes 2949128 | tf_op jit(solution)/shard_map/ppermute | solution.py:342
  67.0 2.7 %shard_map.132.blocks_ref = bf16[16,256,192]{2,1,0:T(8,128)(2,1)S(1)} custom-call(s32[4]{0:T(128)S(1)} %pad_add_fusion.where_ref, f32[32,8,128]{2,1,0:T(8,128)S(1)} %all-to-all-done.every_ref, bf16[2,2,128,640]{3,2,1,0:T(8,128)(2,1)S(1)} %bitcast.21, f32[1,640]{1,0:T(1,128)S(1)} %broadcast_in_dim.20.gain_ref, f32[1,640]{1,0:T(1,128)S(1)} %broadcast_in_dim.21.shift_ref), custom_call_target="tpu_custom_call" | custom-call | tf_op jit(solution)/shard_map/pallas_call | solution.py:285
  69.7 1.3 copy-done.1
  71.0 16.0 %collective-permute-done.3.far_ref = bf16[4,192,640]{2,1,0:T(8,128)(2,1)} collective-permute-done((bf16[4,192,640]{2,1,0:T(8,128)(2,1)}, bf16[4,192,640]{2,1,0:T(8,128)(2,1)}, u32[]{:S(2)}, u32[]{:S(2)}) %collective-permute-start.3) | collective-permute-done | bytes 983072 | tf_op jit(solution)/shard_map/ppermute | solution.py:342
  87.0 5.7 %shard_map.133 = (f32[128,640]{1,0:T(8,128)S(1)}, f32[128,640]{1,0:T(8,128)}) custom-call(s32[4]{0:T(128)S(1)} %pad_add_fusion.where_ref, bf16[16,256,192]{2,1,0:T(8,128)(2,1)} %copy-done.1, bf16[4,192,640]{2,1,0:T(8,128)(2,1)S(1)} %bitcast.20, bf16[4,192,640]{2,1,0:T(8,128)(2,1)} %collective-permute-done.1.left_ref, ...), custom_call_target="tpu_custom_call" | custom-call | tf_op jit(solution)/shard_map/pallas_call | solution.py:285
  93.4 3.4 %collective-permute-start.4 = (f32[128,640]{1,0:T(8,128)}, f32[128,640]{1,0:T(8,128)S(1)}, u32[]{:S(2)}, u32[]{:S(2)}) collective-permute-start(f32[128,640]{1,0:T(8,128)} %get-tuple-element.19), channel_id=1, source_target_pairs={{0,1},{1,0},{2,3},{3,2},{4,5},{5,4},{6,7},{7,6},{8,9},{9,8},{10,11... | collective-permute-start | bytes 983048 | tf_op jit(solution)/shard_map/ppermute | solution.py:373
  96.9 3.2 %collective-permute-start.6 = (bf16[4,640,128]{2,1,0:T(8,128)(2,1)S(1)}, bf16[4,640,128]{2,1,0:T(8,128)(2,1)S(1)}, u32[]{:S(2)}, u32[]{:S(2)}) collective-permute-start(bf16[4,640,128]{2,1,0:T(8,128)(2,1)S(1)} %all-to-all-done.2.own_ref), channel_id=1, source_target_pairs={{0,8},{1,9},{2,10},{3,11},{4,12},{5,13},{6,14},{7,15},{8,16},{9,17... | collective-permute-start | bytes 1966088 | tf_op jit(solution)/shard_map/ppermute | solution.py:355
  101.8 1.7 %shard_map.134 = (bf16[128,640]{1,0:T(8,128)(2,1)S(1)}, f32[32,8,128]{2,1,0:T(8,128)}) custom-call(f32[128,640]{1,0:T(8,128)S(1)} %copy-done.7, f32[128,640]{1,0:T(8,128)S(1)} %collective-permute-done.4.other_ref, bf16[128,640]{1,0:T(8,128)(2,1)S(1)} %copy-done.3, f32[1,640]{1,0:T(1,128)S(1)} %add.19.bias_ref), custom_call_target="tpu_custom_call" | custom-call | tf_op jit(solution)/shard_map/pallas_call | solution.py:285
  103.4 8.2 %all-to-all-start.1 = ((f32[32,8,128]{2,1,0:T(8,128)}), f32[32,8,128]{2,1,0:T(8,128)S(1)}, u32[]{:S(2)}, u32[]{:S(2)}) async-start(f32[32,8,128]{2,1,0:T(8,128)} %get-tuple-element.21), calls=%async_computation.1 | async-start | bytes 262144 | tf_op jit(solution)/shard_map/all_to_all | solution.py:63
  111.6 4.5 %collective-permute-start.8 = (bf16[4,640,128]{2,1,0:T(8,128)(2,1)S(1)}, bf16[4,640,128]{2,1,0:T(8,128)(2,1)}, u32[]{:S(2)}, u32[]{:S(2)}) collective-permute-start(bf16[4,640,128]{2,1,0:T(8,128)(2,1)S(1)} %all-to-all-done.2.own_ref), channel_id=1, source_target_pairs={{0,24},{1,25},{2,26},{3,27},{4,28},{5,29},{6,30},{7,31},{8,0},{9,1... | collective-permute-start | bytes 1966088 | tf_op jit(solution)/shard_map/ppermute | solution.py:356
  116.2 4.2 %all-to-all-done.1.every_ref = f32[32,8,128]{2,1,0:T(8,128)S(1)} async-done(((f32[32,8,128]{2,1,0:T(8,128)}), f32[32,8,128]{2,1,0:T(8,128)S(1)}, u32[]{:S(2)}, u32[]{:S(2)}) %all-to-all-start.1) | async-done | bytes 131104 | tf_op jit(solution)/shard_map/all_to_all | solution.py:63
  120.3 1.9 %collective-permute-start.7 = (bf16[4,640,128]{2,1,0:T(8,128)(2,1)S(1)}, bf16[4,640,128]{2,1,0:T(8,128)(2,1)S(1)}, u32[]{:S(2)}, u32[]{:S(2)}) collective-permute-start(bf16[4,640,128]{2,1,0:T(8,128)(2,1)S(1)} %collective-permute-done.6.left_ref), channel_id=1, source_target_pairs={{0,8},{1,9},{2,10},{3,11},{4,12},{5,13},{6,14},{7,15},{8,16},{9,17... | collective-permute-start | bytes 1966088 | tf_op jit(solution)/shard_map/ppermute | solution.py:378
  122.2 3.1 %collective-permute-start.5 = (bf16[128,640]{1,0:T(8,128)(2,1)S(1)}, bf16[128,640]{1,0:T(8,128)(2,1)S(1)}, u32[]{:S(2)}, u32[]{:S(2)}) collective-permute-start(bf16[128,640]{1,0:T(8,128)(2,1)S(1)} %get-tuple-element.22.mid_ref), channel_id=1, source_target_pairs={{0,1},{1,0},{2,3},{3,2},{4,5},{5,4},{6,7},{7,6},{8,9},{9,8},{10,11... | collective-permute-start | bytes 491528 | tf_op jit(solution)/shard_map/ppermute | solution.py:376
  126.2 1.3 copy-done.4
  127.5 1.7 %shard_map.135 = (bf16[256,384]{1,0:T(8,128)(2,1)S(1)}, bf16[640,128]{1,0:T(8,128)(2,1)}) custom-call(f32[32,8,128]{2,1,0:T(8,128)S(1)} %all-to-all-done.1.every_ref, bf16[128,640]{1,0:T(8,128)(2,1)S(1)} %get-tuple-element.22.mid_ref, bf16[128,640]{1,0:T(8,128)(2,1)S(1)} %collective-permute-done.5.other_ref, f32[1,640]{1,0:T(1,128)S(1)} %broadcast_in_dim.22.gain_ref, ...), custom_call_target="tpu_custom_call" | custom-call | tf_op jit(solution)/shard_map/pallas_call | solution.py:285
  129.1 1.4 collective-permute-done.8.right_ref
  131.4 4.9 %shard_map.136.near_ref = f32[256,384]{1,0:T(8,128)S(1)} custom-call(s32[4]{0:T(128)S(1)} %pad_add_fusion.where_ref, bf16[256,384]{1,0:T(8,128)(2,1)S(1)} %get-tuple-element.23.q_ref, bf16[4,640,128]{2,1,0:T(8,128)(2,1)S(1)} %all-to-all-done.2.own_ref, bf16[4,640,128]{2,1,0:T(8,128)(2,1)S(1)} %collective-permute-done.6.left_ref, ...), custom_call_target="tpu_custom_call" | custom-call | tf_op jit(solution)/shard_map/pallas_call | solution.py:285
  136.3 3.0 %collective-permute-done.7.far_ref = bf16[4,640,128]{2,1,0:T(8,128)(2,1)S(1)} collective-permute-done((bf16[4,640,128]{2,1,0:T(8,128)(2,1)S(1)}, bf16[4,640,128]{2,1,0:T(8,128)(2,1)S(1)}, u32[]{:S(2)}, u32[]{:S(2)}) %collective-permute-start.7) | collective-permute-done | bytes 655392 | tf_op jit(solution)/shard_map/ppermute | solution.py:378
  139.3 2.3 %shard_map.137 = (f32[128,384]{1,0:T(8,128)S(1)}, f32[128,384]{1,0:T(8,128)S(1)}) custom-call(bf16[256,384]{1,0:T(8,128)(2,1)S(1)} %get-tuple-element.23.q_ref, bf16[4,640,128]{2,1,0:T(8,128)(2,1)S(1)} %collective-permute-done.7.far_ref, f32[256,384]{1,0:T(8,128)S(1)} %shard_map.136.near_ref), custom_call_target="tpu_custom_call" | custom-call | tf_op jit(solution)/shard_map/pallas_call | solution.py:285
  141.7 3.1 %collective-permute-start.9 = (f32[128,384]{1,0:T(8,128)S(1)}, f32[128,384]{1,0:T(8,128)S(1)}, u32[]{:S(2)}, u32[]{:S(2)}) collective-permute-start(f32[128,384]{1,0:T(8,128)S(1)} %get-tuple-element.29), channel_id=1, source_target_pairs={{0,1},{1,0},{2,3},{3,2},{4,5},{5,4},{6,7},{7,6},{8,9},{9,8},{10,11... | collective-permute-start | bytes 589832 | tf_op jit(solution)/shard_map/ppermute | solution.py:403
  144.8 1.0 collective-permute-done.9.other_ref
  145.9 1.3 shard_map.138
  (48 shorter events, 6.5 us)
Async XLA Ops:
  0.6 99.6 %copy-start = (f32[320,640]{1,0:T(8,128)S(1)}, f32[320,640]{1,0:T(8,128)}, u32[]{:S(2)}) copy-start(f32[320,640]{1,0:T(8,128)} %param.18) | copy-start | bytes 2457604
  0.6 45.5 %copy-start.3 = (bf16[128,640]{1,0:T(8,128)(2,1)S(1)}, bf16[128,640]{1,0:T(8,128)(2,1)}, u32[]{:S(2)}) copy-start(bf16[128,640]{1,0:T(8,128)(2,1)} %latent_ref.3) | copy-start | bytes 491524
  0.7 55.5 %copy-start.9 = (bf16[2,128,320]{1,2,0:T(8,128)(2,1)S(1)}, bf16[2,128,320]{1,2,0:T(8,128)(2,1)}, u32[]{:S(2)}) copy-start(bf16[2,128,320]{1,2,0:T(8,128)(2,1)} %param.23) | copy-start | bytes 491524
  0.7 24.7 %collective-permute-start = (bf16[128,640]{1,0:T(8,128)(2,1)}, bf16[128,640]{1,0:T(8,128)(2,1)S(1)}, u32[]{:S(2)}, u32[]{:S(2)}) collective-permute-start(bf16[128,640]{1,0:T(8,128)(2,1)} %latent_ref.3), channel_id=1, source_target_pairs={{2,0},{4,2},{6,4},{8,6},{10,8},{12,10},{14,12},{16,14},{18,16},{20... | collective-permute-start | bytes 491528 | tf_op jit(solution)/shard_map/ppermute | solution.py:322
  25.4 23.0 %collective-permute-start.1 = (bf16[4,192,640]{2,1,0:T(8,128)(2,1)S(1)}, bf16[4,192,640]{2,1,0:T(8,128)(2,1)}, u32[]{:S(2)}, u32[]{:S(2)}) collective-permute-start(bf16[4,192,640]{2,1,0:T(8,128)(2,1)S(1)} %bitcast.18), channel_id=1, source_target_pairs={{0,8},{1,9},{2,10},{3,11},{4,12},{5,13},{6,14},{7,15},{8,16},{9,17... | collective-permute-start | bytes 2949128 | tf_op jit(solution)/shard_map/ppermute | solution.py:324
  29.2 19.7 %collective-permute-start.2 = (bf16[4,192,640]{2,1,0:T(8,128)(2,1)S(1)}, bf16[4,192,640]{2,1,0:T(8,128)(2,1)}, u32[]{:S(2)}, u32[]{:S(2)}) collective-permute-start(bf16[4,192,640]{2,1,0:T(8,128)(2,1)S(1)} %bitcast.19), channel_id=1, source_target_pairs={{0,24},{1,25},{2,26},{3,27},{4,28},{5,29},{6,30},{7,31},{8,0},{9,1... | collective-permute-start | bytes 2949128 | tf_op jit(solution)/shard_map/ppermute | solution.py:325
  31.9 0.9 copy-start.2
  34.4 31.7 %copy-start.11 = (f32[640]{0:T(1024)S(1)}, f32[640]{0:T(1024)}, u32[]{:S(2)}) copy-start(f32[640]{0:T(1024)} %param.14) | copy-start | bytes 7684
  34.5 31.8 %copy-start.12 = (f32[640]{0:T(1024)S(1)}, f32[640]{0:T(1024)}, u32[]{:S(2)}) copy-start(f32[640]{0:T(1024)} %param.15) | copy-start | bytes 7684
  34.5 21.7 %all-to-all-start = ((f32[32,8,128]{2,1,0:T(8,128)}), f32[32,8,128]{2,1,0:T(8,128)S(1)}, u32[]{:S(2)}, u32[]{:S(2)}) async-start(f32[32,8,128]{2,1,0:T(8,128)} %shard_map.131), calls=%async_computation | async-start | bytes 262144 | tf_op jit(solution)/shard_map/all_to_all | solution.py:63
  57.1 39.8 %all-to-all-start.2 = ((bf16[4,640,128]{2,1,0:T(8,128)(2,1)}), bf16[4,640,128]{2,1,0:T(8,128)(2,1)S(1)}, u32[]{:S(2)}, u32[]{:S(2)}) async-start(bf16[4,640,128]{2,1,0:T(8,128)(2,1)} %broadcast_in_dim.24), calls=%async_computation.2 | async-start | bytes 1310720 | tf_op jit(solution)/shard_map/all_to_all | solution.py:333
  62.2 24.8 %collective-permute-start.3 = (bf16[4,192,640]{2,1,0:T(8,128)(2,1)}, bf16[4,192,640]{2,1,0:T(8,128)(2,1)}, u32[]{:S(2)}, u32[]{:S(2)}) collective-permute-start(bf16[4,192,640]{2,1,0:T(8,128)(2,1)} %collective-permute-done.2.right_ref), channel_id=1, source_target_pairs={{0,24},{1,25},{2,26},{3,27},{4,28},{5,29},{6,30},{7,31},{8,0},{9,1... | collective-permute-start | bytes 2949128 | tf_op jit(solution)/shard_map/ppermute | solution.py:342
  69.6 1.4 copy-start.1
  71.0 29.8 %copy-start.10 = (f32[640]{0:T(1024)S(1)}, f32[640]{0:T(1024)}, u32[]{:S(2)}) copy-start(f32[640]{0:T(1024)} %param.17) | copy-start | bytes 7684
  71.0 54.3 %copy-start.13 = (f32[640]{0:T(1024)S(1)}, f32[640]{0:T(1024)}, u32[]{:S(2)}) copy-start(f32[640]{0:T(1024)} %param.19) | copy-start | bytes 7684
  71.0 54.4 %copy-start.14 = (f32[640]{0:T(1024)S(1)}, f32[640]{0:T(1024)}, u32[]{:S(2)}) copy-start(f32[640]{0:T(1024)} %param.20) | copy-start | bytes 7684
  92.7 0.7 copy-start.6
  93.4 7.4 %collective-permute-start.4 = (f32[128,640]{1,0:T(8,128)}, f32[128,640]{1,0:T(8,128)S(1)}, u32[]{:S(2)}, u32[]{:S(2)}) collective-permute-start(f32[128,640]{1,0:T(8,128)} %get-tuple-element.19), channel_id=1, source_target_pairs={{0,1},{1,0},{2,3},{3,2},{4,5},{5,4},{6,7},{7,6},{8,9},{9,8},{10,11... | collective-permute-start | bytes 983048 | tf_op jit(solution)/shard_map/ppermute | solution.py:373
  96.9 23.4 %collective-permute-start.6 = (bf16[4,640,128]{2,1,0:T(8,128)(2,1)S(1)}, bf16[4,640,128]{2,1,0:T(8,128)(2,1)S(1)}, u32[]{:S(2)}, u32[]{:S(2)}) collective-permute-start(bf16[4,640,128]{2,1,0:T(8,128)(2,1)S(1)} %all-to-all-done.2.own_ref), channel_id=1, source_target_pairs={{0,8},{1,9},{2,10},{3,11},{4,12},{5,13},{6,14},{7,15},{8,16},{9,17... | collective-permute-start | bytes 1966088 | tf_op jit(solution)/shard_map/ppermute | solution.py:355
  100.8 1.0 copy-start.7
  103.4 16.9 %all-to-all-start.1 = ((f32[32,8,128]{2,1,0:T(8,128)}), f32[32,8,128]{2,1,0:T(8,128)S(1)}, u32[]{:S(2)}, u32[]{:S(2)}) async-start(f32[32,8,128]{2,1,0:T(8,128)} %get-tuple-element.21), calls=%async_computation.1 | async-start | bytes 262144 | tf_op jit(solution)/shard_map/all_to_all | solution.py:63
  111.6 18.9 %collective-permute-start.8 = (bf16[4,640,128]{2,1,0:T(8,128)(2,1)S(1)}, bf16[4,640,128]{2,1,0:T(8,128)(2,1)}, u32[]{:S(2)}, u32[]{:S(2)}) collective-permute-start(bf16[4,640,128]{2,1,0:T(8,128)(2,1)S(1)} %all-to-all-done.2.own_ref), channel_id=1, source_target_pairs={{0,24},{1,25},{2,26},{3,27},{4,28},{5,29},{6,30},{7,31},{8,0},{9,1... | collective-permute-start | bytes 1966088 | tf_op jit(solution)/shard_map/ppermute | solution.py:356
  120.3 19.0 %collective-permute-start.7 = (bf16[4,640,128]{2,1,0:T(8,128)(2,1)S(1)}, bf16[4,640,128]{2,1,0:T(8,128)(2,1)S(1)}, u32[]{:S(2)}, u32[]{:S(2)}) collective-permute-start(bf16[4,640,128]{2,1,0:T(8,128)(2,1)S(1)} %collective-permute-done.6.left_ref), channel_id=1, source_target_pairs={{0,8},{1,9},{2,10},{3,11},{4,12},{5,13},{6,14},{7,15},{8,16},{9,17... | collective-permute-start | bytes 1966088 | tf_op jit(solution)/shard_map/ppermute | solution.py:378
  122.2 3.9 %collective-permute-start.5 = (bf16[128,640]{1,0:T(8,128)(2,1)S(1)}, bf16[128,640]{1,0:T(8,128)(2,1)S(1)}, u32[]{:S(2)}, u32[]{:S(2)}) collective-permute-start(bf16[128,640]{1,0:T(8,128)(2,1)S(1)} %get-tuple-element.22.mid_ref), channel_id=1, source_target_pairs={{0,1},{1,0},{2,3},{3,2},{4,5},{5,4},{6,7},{7,6},{8,9},{9,8},{10,11... | collective-permute-start | bytes 491528 | tf_op jit(solution)/shard_map/ppermute | solution.py:376
  126.2 1.3 copy-start.4
  129.1 16.7 %copy-start.5 = (bf16[320,640]{1,0:T(8,128)(2,1)S(1)}, bf16[320,640]{1,0:T(8,128)(2,1)}, u32[]{:S(2)}) copy-start(bf16[320,640]{1,0:T(8,128)(2,1)} %weight_ref.1) | copy-start | bytes 1228804
  130.5 0.9 copy-start.8
  141.7 4.2 %collective-permute-start.9 = (f32[128,384]{1,0:T(8,128)S(1)}, f32[128,384]{1,0:T(8,128)S(1)}, u32[]{:S(2)}, u32[]{:S(2)}) collective-permute-start(f32[128,384]{1,0:T(8,128)S(1)} %get-tuple-element.29), channel_id=1, source_target_pairs={{0,1},{1,0},{2,3},{3,2},{4,5},{5,4},{6,7},{7,6},{8,9},{9,8},{10,11... | collective-permute-start | bytes 589832 | tf_op jit(solution)/shard_map/ppermute | solution.py:403

commit v7 on v6

--- a/solution.py
+++ b/solution.py
@@ -132,7 +132,8 @@
     own_ref,
     left_ref,
     right_ref,
-    far_ref,
+    low_ref,
+    high_ref,
     kept_ref,
     given_ref,
     held_ref,
@@ -140,18 +141,20 @@
 ):
     core, x = where_ref[0], where_ref[2]
     count = kept_ref.shape[0]
-    sources = ((own_ref, 0), (left_ref, 3), (right_ref, 1), (far_ref, 2))
-    copies = []
-    for index, (ref, _) in enumerate(sources):
-        copy = pltpu.make_async_copy(ref, held_ref.at[4 * index : 4 * index + 4], sems.at[index])
+    sources = ((own_ref, 0, 0), (left_ref, 3, 0), (right_ref, 1, 0), (low_ref, 2, 0), (high_ref, 2, 2))
+    copies, at = [], 0
+    for index, (ref, _, _) in enumerate(sources):
+        size = ref.shape[0]
+        copy = pltpu.make_async_copy(ref, held_ref.at[at : at + size], sems.at[index])
         copy.start()
-        copies.append(copy)
+        copies.append((copy, at, size))
+        at += size
     total = None
-    for index, (_, step) in enumerate(sources):
-        copies[index].wait()
-        base = 4 * ((x + step) & 3)
-        for z in range(4):
-            part = dot32(blocks_ref[base + z], held_ref[4 * index + z])
+    for (_, step, first), (copy, at, size) in zip(sources, copies, strict=True):
+        copy.wait()
+        base = 4 * ((x + step) & 3) + first
+        for z in range(size):
+            part = dot32(blocks_ref[base + z], held_ref[at + z])
             total = part if total is None else total + part
     kept_ref[...] = jnp.where(core == 0, total[:count], total[count:])
     given_ref[...] = jnp.where(core == 0, total[count:], total[:count])
@@ -247,9 +250,9 @@
         out_ref[:, 128 * tile : 128 * (tile + 1)] = value
 
 
-def attend_far(q_ref, far_ref, near_ref, out_ref, given_ref):
+def attend_far(q_ref, low_ref, high_ref, near_ref, out_ref, given_ref):
     count = out_ref.shape[0]
-    blocks = [[(far_ref, z) for z in range(4)]]
+    blocks = [[(low_ref, 0), (low_ref, 1), (high_ref, 0), (high_ref, 1)]]
     for tile, value in enumerate(attention(q_ref, blocks, None, None, near_ref)):
         out_ref[:, 128 * tile : 128 * (tile + 1)] = value[:count]
         given_ref[:, 128 * tile : 128 * (tile + 1)] = value[count:]
@@ -281,17 +284,17 @@
     out_ref[...] = result.astype(jnp.bfloat16)
 
 
-def call(kernel, outs, smem, *args, scratch=(), fetched=(), mib=32):
+def call(kernel, outs, smem, *args, scratch=(), fetched=()):
     return pl.pallas_call(
         kernel,
         out_shape=[jax.ShapeDtypeStruct(shape, dtype) for shape, dtype in outs],
         in_specs=[
-            SMEM if i < smem else pl.BlockSpec(memory_space=pltpu.HBM) if i in fetched else VMEM
+            SMEM if i < smem else pl.BlockSpec(memory_space=pl.ANY) if i in fetched else VMEM
             for i in range(len(args))
         ],
         out_specs=[VMEM] * len(outs),
         scratch_shapes=list(scratch),
-        compiler_params=pltpu.CompilerParams(vmem_limit_bytes=mib * 1024 * 1024),
+        compiler_params=pltpu.CompilerParams(vmem_limit_bytes=40 * 1024 * 1024),
     )(*args)
 
 
@@ -319,27 +322,19 @@
 
     weight = jnp.pad(conv_weight, ((0, ROWS - rows), (0, 0)))
     own_w = lax.all_gather(weight, "space", axis=0, axis_index_groups=Z_GROUPS)
-    outer = lax.ppermute(latent, "space", OUTER)
-    own_w, outer = lax.optimization_barrier((own_w, outer))
     left_w = lax.ppermute(own_w, "space", RIGHT)
     right_w = lax.ppermute(own_w, "space", LEFT)
+    outer = lax.ppermute(latent, "space", OUTER)
     (stats1,) = call(first_stats, [table], 0, latent)
     every1 = exchanged(stats1)
     pair = lax.all_gather(
         jnp.stack([latent, outer]), "space", axis=0, axis_index_groups=CORE_GROUPS
     )
     stale = stale_kv.transpose(0, 2, 1).reshape(2 * feats, tok_dev)
-    stale, _ = lax.optimization_barrier((stale, (left_w,right_w,pair)))
-    own_kv = lax.all_to_all(
-        jnp.broadcast_to(stale[None], (4, 2 * feats, tok_dev)),
-        "space",
-        0,
-        0,
-        axis_index_groups=Z_GROUPS,
-        tiled=True,
-    )
-
-    far_w = lax.ppermute(right_w, "space", LEFT)
+    stale, _ = lax.optimization_barrier((stale, own_w))
+    own_kv = lax.all_gather(stale, "space", axis=0, axis_index_groups=Z_GROUPS)
+    low_w = lax.ppermute(left_w[:2], "space", RIGHT)
+    high_w = lax.ppermute(right_w[2:], "space", LEFT)
     (blocks,) = call(
         prepare,
         [((16, 2 * tok_dev, ROWS), bf16)],
@@ -365,24 +360,23 @@
         own_w,
         left_w,
         right_w,
-        far_w,
-        scratch=[pltpu.VMEM((16, ROWS, width), bf16), pltpu.SemaphoreType.DMA((4,))],
-        fetched=(2, 3, 4, 5),
-        mib=48,
+        low_w,
+        high_w,
+        scratch=[pltpu.VMEM((16, ROWS, width), bf16), pltpu.SemaphoreType.DMA((5,))],
+        fetched=(2, 3, 4, 5, 6),
     )
     other = lax.ppermute(given, "space", SWAP)
     mid, stats2 = call(middle, [((tok_dev, width), bf16), table], 0, kept, other, latent, bias)
     every2 = exchanged(stats2)
-    other_mid = lax.ppermute(mid, "space", SWAP)
-    sent_kv, _ = lax.optimization_barrier((left_kv, every2))
-    far_kv = lax.ppermute(sent_kv, "space", RIGHT)
+    low_kv = lax.ppermute(left_kv[:2], "space", RIGHT)
+    high_kv = lax.ppermute(right_kv[2:], "space", LEFT)
     query, fresh = call(
         project,
         [((2 * tok_dev, 384), bf16), ((2 * feats, tok_dev), bf16)],
         0,
         every2,
         mid,
-        other_mid,
+        lax.ppermute(mid, "space", SWAP),
         norm2_gain[None],
         norm2_shift[None],
         qkv_weight.T,
@@ -399,7 +393,9 @@
         right_kv,
         fresh,
     )
-    mine, theirs = call(attend_far, [((tok_dev, 384), f32)] * 2, 0, query, far_kv, near)
+    mine, theirs = call(
+        attend_far, [((tok_dev, 384), f32)] * 2, 0, query, low_kv, high_kv, near
+    )
     other = lax.ppermute(theirs, "space", SWAP)
     (result,) = call(finish, [((tok_dev, width), bf16)], 0, mine, other, mid, out_weight)
     return (result, fresh_kv)

time: 148 us -> 131 us (0.89)
  waiting for transfers between devices: 34.1 us -> 2.39 us
  blocking collectives: 21.5 us -> 42.4 us
  starting transfers between devices: 59.1 us -> 51.7 us
    ppermute x3 -> x5, waiting for transfers between devices: 19.8 us -> 0.79 us  [the longest x1 0.78 us: on_device(): lax.ppermute(mid, 'space', SWAP)]
    all_gather x0 -> x1, blocking collectives: none -> 15.9 us  [on_device(): own_kv = lax.all_gather(stale, 'space', axis=0, axis_index_groups=Z_GROUPS)]
    all_to_all x2, waiting for transfers between devices: 11.5 us -> 0.01 us  [exchanged(): return lax.all_to_all(stats, 'space', 0, 0, tiled=True)]
    ppermute x3 -> x5, starting transfers between devices: 8.98 us -> 15.7 us  [the longest x1 4.55 us: on_device(): high_kv = lax.ppermute(right_kv[2:], 'space', LEFT)]
    all_to_all x1 -> x0, starting transfers between devices: 5.02 us -> none  [on_device(): lax.all_to_all(jnp.broadcast_to(stale[None], (4, 2 * feats, tok_dev)), 's...]
    slice x0 -> x4, local copies, waits for them, and re-layouts: none -> 4.49 us  [the longest x1 1.87 us: on_device(): high_w = lax.ppermute(right_w[2:], 'space', LEFT)]
    all_to_all x2, starting transfers between devices: 19.8 us -> 15.6 us  [exchanged(): return lax.all_to_all(stats, 'space', 0, 0, tiled=True)]
    all_gather x1, blocking collectives: 2.28 us -> 5.24 us  [on_device(): lax.all_gather(jnp.stack([latent, outer]), 'space', axis=0, axis_index_gr...]
  transfers between devices with their start and end apart: 13 -> 14, of which waited for: 8 -> 3; matrix products, arithmetic and copies ran while one was open for 1% -> 5% of each run, Pallas kernels for 12% -> 13%
where the time goes in v7:
time: 131 us; the launch traced here: 130 us
  starting transfers between devices  51.7 us (39%)
  blocking collectives  42.4 us (32%)
  Pallas kernels  21.6 us (16%)
  local copies, waits for them, and re-layouts  8.78 us (7%)
  waiting for transfers between devices  2.39 us (2%)
  between operations  1.68 us (1%)
    pallas_call x8, Pallas kernels, call(): pl.pallas_call(kernel, out_shape=[jax.ShapeDtypeStruct(shape, dtype) for...  21.6 us
    all_gather x1, blocking collectives, on_device(): own_w = lax.all_gather(weight, 'space', axis=0, axis_index_groups=Z_GROUPS)  21.2 us
    all_gather x1, blocking collectives, on_device(): own_kv = lax.all_gather(stale, 'space', axis=0, axis_index_groups=Z_GROUPS)  15.9 us
    all_to_all x2, starting transfers between devices, exchanged(): return lax.all_to_all(stats, 'space', 0, 0, tiled=True)  15.6 us
    all_gather x1, blocking collectives, on_device(): lax.all_gather(jnp.stack([latent, outer]), 'space', axis=0, axis_index_gr...  5.24 us
    ppermute x1, starting transfers between devices, on_device(): high_kv = lax.ppermute(right_kv[2:], 'space', LEFT)  4.55 us
    ppermute x1, starting transfers between devices, on_device(): outer = lax.ppermute(latent, 'space', OUTER)  3.67 us
    ppermute x1, starting transfers between devices, on_device(): right_w = lax.ppermute(own_w, 'space', LEFT)  3.64 us
  transfers between devices with their start and end apart: 14, of which 3 were waited for; matrix products, arithmetic and copies ran while one was open for 5% of the time, Pallas kernels for 13%

profile of v7, /device:TPU:1, one launch (start us, length us, event | category | flops | bytes accessed | tf_op | source)
XLA Modules:
  0.0 130.4 jit_solution(8599769609914500407)
XLA Ops:
  0.7 1.0 pad.4
  1.7 21.2 %all-gather.1 = bf16[768,640]{1,0:T(8,128)(2,1)S(1)} all-gather(bf16[192,640]{1,0:T(8,128)(2,1)S(1)} %pad.4), channel_id=3, replica_groups={{0,2,4,6},{1,3,5,7},{8,10,12,14},{9,11,13,15},{16,18,20,22},{17,19,21,2..., dimensions={0}, use_global_device_ids=true | all-gather | bytes 1228800 | tf_op jit(solution)/shard_map/all_gather | solution.py:324
  22.9 2.8 %collective-permute-start.1 = (bf16[4,192,640]{2,1,0:T(8,128)(2,1)S(1)}, bf16[4,192,640]{2,1,0:T(8,128)(2,1)S(1)}, u32[]{:S(2)}, u32[]{:S(2)}) collective-permute-start(bf16[4,192,640]{2,1,0:T(8,128)(2,1)S(1)} %bitcast.19), channel_id=1, source_target_pairs={{0,8},{1,9},{2,10},{3,11},{4,12},{5,13},{6,14},{7,15},{8,16},{9,17... | collective-permute-start | bytes 2949128 | tf_op jit(solution)/shard_map/ppermute | solution.py:325
  25.8 3.6 %collective-permute-start.2 = (bf16[4,192,640]{2,1,0:T(8,128)(2,1)S(1)}, bf16[4,192,640]{2,1,0:T(8,128)(2,1)}, u32[]{:S(2)}, u32[]{:S(2)}) collective-permute-start(bf16[4,192,640]{2,1,0:T(8,128)(2,1)S(1)} %bitcast.20), channel_id=1, source_target_pairs={{0,24},{1,25},{2,26},{3,27},{4,28},{5,29},{6,30},{7,31},{8,0},{9,1... | collective-permute-start | bytes 2949128 | tf_op jit(solution)/shard_map/ppermute | solution.py:326
  29.4 3.7 %collective-permute-start = (bf16[128,640]{1,0:T(8,128)(2,1)}, bf16[128,640]{1,0:T(8,128)(2,1)}, u32[]{:S(2)}, u32[]{:S(2)}) collective-permute-start(bf16[128,640]{1,0:T(8,128)(2,1)} %latent_ref.3), channel_id=1, source_target_pairs={{2,0},{4,2},{6,4},{8,6},{10,8},{12,10},{14,12},{16,14},{18,16},{20... | collective-permute-start | bytes 491528 | tf_op jit(solution)/shard_map/ppermute | solution.py:327
  34.0 1.6 %shard_map.131 = f32[32,8,128]{2,1,0:T(8,128)} custom-call(bf16[128,640]{1,0:T(8,128)(2,1)S(1)} %copy-done.3), custom_call_target="tpu_custom_call" | custom-call | tf_op jit(solution)/shard_map/pallas_call | solution.py:288
  35.7 9.2 %all-to-all-start = ((f32[32,8,128]{2,1,0:T(8,128)}), f32[32,8,128]{2,1,0:T(8,128)}, u32[]{:S(2)}, u32[]{:S(2)}) async-start(f32[32,8,128]{2,1,0:T(8,128)} %shard_map.131), calls=%async_computation | async-start | bytes 262144 | tf_op jit(solution)/shard_map/all_to_all | solution.py:63
  44.8 15.9 %all-gather.2 = bf16[2560,128]{1,0:T(8,128)(2,1)S(1)} all-gather(bf16[640,128]{1,0:T(8,128)(2,1)} %bitcast.29), channel_id=4, replica_groups={{0,2,4,6},{1,3,5,7},{8,10,12,14},{9,11,13,15},{16,18,20,22},{17,19,21,2..., dimensions={0}, use_global_device_ids=true | all-gather | bytes 819200 | tf_op jit(solution)/shard_map/all_gather | solution.py:335
  61.7 3.1 %collective-permute-start.3 = (bf16[2,192,640]{2,1,0:T(8,128)(2,1)}, bf16[2,192,640]{2,1,0:T(8,128)(2,1)}, u32[]{:S(2)}, u32[]{:S(2)}) collective-permute-start(bf16[2,192,640]{2,1,0:T(8,128)(2,1)} %slice.16), channel_id=1, source_target_pairs={{0,8},{1,9},{2,10},{3,11},{4,12},{5,13},{6,14},{7,15},{8,16},{9,17... | collective-permute-start | bytes 1474568 | tf_op jit(solution)/shard_map/ppermute | solution.py:336
  64.9 1.9 %slice.17 = bf16[2,192,640]{2,1,0:T(8,128)(2,1)} slice(bf16[4,192,640]{2,1,0:T(8,128)(2,1)} %collective-permute-done.2.right_ref), slice={[2:4], [0:192], [0:640]} | slice | bytes 983040 | tf_op jit(solution)/shard_map/slice | solution.py:337
  66.7 3.4 %collective-permute-start.4 = (bf16[2,192,640]{2,1,0:T(8,128)(2,1)}, bf16[2,192,640]{2,1,0:T(8,128)(2,1)}, u32[]{:S(2)}, u32[]{:S(2)}) collective-permute-start(bf16[2,192,640]{2,1,0:T(8,128)(2,1)} %slice.17), channel_id=1, source_target_pairs={{0,24},{1,25},{2,26},{3,27},{4,28},{5,29},{6,30},{7,31},{8,0},{9,1... | collective-permute-start | bytes 1474568 | tf_op jit(solution)/shard_map/ppermute | solution.py:337
  70.2 1.0 pad_maximum_fusion
  71.2 5.2 %all-gather = bf16[4,128,640]{2,1,0:T(8,128)(2,1)S(1)} all-gather(bf16[2,128,640]{2,1,0:T(8,128)(2,1)S(1)} %pad_maximum_fusion), channel_id=2, replica_groups={{0,1},{2,3},{4,5},{6,7},{8,9},{10,11},{12,13},{14,15},{16,17},{18,19},{..., dimensions={0}, use_global_device_ids=true | all-gather | bytes 983040 | tf_op jit(solution)/shard_map/all_gather | solution.py:330
  76.5 3.1 %shard_map.132.blocks_ref = bf16[16,256,192]{2,1,0:T(8,128)(2,1)S(1)} custom-call(s32[4]{0:T(128)S(1)} %pad_add_fusion.where_ref, f32[32,8,128]{2,1,0:T(8,128)} %all-to-all-done.every_ref, bf16[2,2,128,640]{3,2,1,0:T(8,128)(2,1)S(1)} %bitcast.25, f32[1,640]{1,0:T(1,128)S(1)} %broadcast_in_dim.14.gain_ref, f32[1,640]{1,0:T(1,128)S(1)} %broadcast_in_dim.15.shift_ref), custom_call_target="tpu_custom_call" | custom-call | tf_op jit(solution)/shard_map/pallas_call | solution.py:288
  79.6 3.3 %collective-permute-start.9 = (bf16[4,640,128]{2,1,0:T(8,128)(2,1)S(1)}, bf16[4,640,128]{2,1,0:T(8,128)(2,1)S(1)}, u32[]{:S(2)}, u32[]{:S(2)}) collective-permute-start(bf16[4,640,128]{2,1,0:T(8,128)(2,1)S(1)} %bitcast.22), channel_id=1, source_target_pairs={{0,24},{1,25},{2,26},{3,27},{4,28},{5,29},{6,30},{7,31},{8,0},{9,1... | collective-permute-start | bytes 1966088 | tf_op jit(solution)/shard_map/ppermute | solution.py:351
  82.9 2.0 %collective-permute-start.7 = (bf16[4,640,128]{2,1,0:T(8,128)(2,1)S(1)}, bf16[4,640,128]{2,1,0:T(8,128)(2,1)}, u32[]{:S(2)}, u32[]{:S(2)}) collective-permute-start(bf16[4,640,128]{2,1,0:T(8,128)(2,1)S(1)} %bitcast.23), channel_id=1, source_target_pairs={{0,8},{1,9},{2,10},{3,11},{4,12},{5,13},{6,14},{7,15},{8,16},{9,17... | collective-permute-start | bytes 1966088 | tf_op jit(solution)/shard_map/ppermute | solution.py:350
  85.6 4.0 %shard_map.133 = (f32[128,640]{1,0:T(8,128)S(1)}, f32[128,640]{1,0:T(8,128)S(1)}) custom-call(s32[4]{0:T(128)S(1)} %pad_add_fusion.where_ref, bf16[16,256,192]{2,1,0:T(8,128)(2,1)S(1)} %shard_map.132.blocks_ref, bf16[4,192,640]{2,1,0:T(8,128)(2,1)S(1)} %bitcast.21, bf16[4,192,640]{2,1,0:T(8,128)(2,1)S(1)} %copy-done.2, ...), custom_call_target="tpu_custom_call" | custom-call | tf_op jit(solution)/shard_map/pallas_call | solution.py:288
  89.7 2.8 %collective-permute-start.5 = (f32[128,640]{1,0:T(8,128)S(1)}, f32[128,640]{1,0:T(8,128)S(1)}, u32[]{:S(2)}, u32[]{:S(2)}) collective-permute-start(f32[128,640]{1,0:T(8,128)S(1)} %get-tuple-element.14), channel_id=1, source_target_pairs={{0,1},{1,0},{2,3},{3,2},{4,5},{5,4},{6,7},{7,6},{8,9},{9,8},{10,11... | collective-permute-start | bytes 983048 | tf_op jit(solution)/shard_map/ppermute | solution.py:368
  93.7 1.7 %shard_map.134 = (bf16[128,640]{1,0:T(8,128)(2,1)S(1)}, f32[32,8,128]{2,1,0:T(8,128)}) custom-call(f32[128,640]{1,0:T(8,128)S(1)} %get-tuple-element.13.kept_ref, f32[128,640]{1,0:T(8,128)S(1)} %collective-permute-done.5.other_ref, bf16[128,640]{1,0:T(8,128)(2,1)S(1)} %copy-done.4, f32[1,640]{1,0:T(1,128)S(1)} %add.19.bias_ref), custom_call_target="tpu_custom_call" | custom-call | tf_op jit(solution)/shard_map/pallas_call | solution.py:288
  95.4 6.4 %all-to-all-start.1 = ((f32[32,8,128]{2,1,0:T(8,128)}), f32[32,8,128]{2,1,0:T(8,128)S(1)}, u32[]{:S(2)}, u32[]{:S(2)}) async-start(f32[32,8,128]{2,1,0:T(8,128)} %get-tuple-element.16), calls=%async_computation.1 | async-start | bytes 262144 | tf_op jit(solution)/shard_map/all_to_all | solution.py:63
  101.8 4.5 %collective-permute-start.10 = (bf16[2,640,128]{2,1,0:T(8,128)(2,1)S(1)}, bf16[2,640,128]{2,1,0:T(8,128)(2,1)S(1)}, u32[]{:S(2)}, u32[]{:S(2)}) collective-permute-start(bf16[2,640,128]{2,1,0:T(8,128)(2,1)S(1)} %slice.19), channel_id=1, source_target_pairs={{0,24},{1,25},{2,26},{3,27},{4,28},{5,29},{6,30},{7,31},{8,0},{9,1... | collective-permute-start | bytes 983048 | tf_op jit(solution)/shard_map/ppermute | solution.py:372
  106.4 1.7 %slice.18 = bf16[2,640,128]{2,1,0:T(8,128)(2,1)} slice(bf16[4,640,128]{2,1,0:T(8,128)(2,1)} %collective-permute-done.7.left_ref), slice={[0:2], [0:640], [0:128]} | slice | bytes 655360 | tf_op jit(solution)/shard_map/slice | solution.py:371
  108.1 1.9 %collective-permute-start.8 = (bf16[2,640,128]{2,1,0:T(8,128)(2,1)}, bf16[2,640,128]{2,1,0:T(8,128)(2,1)}, u32[]{:S(2)}, u32[]{:S(2)}) collective-permute-start(bf16[2,640,128]{2,1,0:T(8,128)(2,1)} %slice.18), channel_id=1, source_target_pairs={{0,8},{1,9},{2,10},{3,11},{4,12},{5,13},{6,14},{7,15},{8,16},{9,17... | collective-permute-start | bytes 983048 | tf_op jit(solution)/shard_map/ppermute | solution.py:371
  110.0 2.7 %collective-permute-start.6 = (bf16[128,640]{1,0:T(8,128)(2,1)S(1)}, bf16[128,640]{1,0:T(8,128)(2,1)S(1)}, u32[]{:S(2)}, u32[]{:S(2)}) collective-permute-start(bf16[128,640]{1,0:T(8,128)(2,1)S(1)} %get-tuple-element.17.mid_ref), channel_id=1, source_target_pairs={{0,1},{1,0},{2,3},{3,2},{4,5},{5,4},{6,7},{7,6},{8,9},{9,8},{10,11... | collective-permute-start | bytes 491528 | tf_op jit(solution)/shard_map/ppermute | solution.py:379
  113.6 1.3 copy-done.5
  114.9 1.7 %shard_map.135 = (bf16[256,384]{1,0:T(8,128)(2,1)S(1)}, bf16[640,128]{1,0:T(8,128)(2,1)}) custom-call(f32[32,8,128]{2,1,0:T(8,128)S(1)} %all-to-all-done.1.every_ref, bf16[128,640]{1,0:T(8,128)(2,1)S(1)} %get-tuple-element.17.mid_ref, bf16[128,640]{1,0:T(8,128)(2,1)S(1)} %collective-permute-done.6.other_ref, f32[1,640]{1,0:T(1,128)S(1)} %broadcast_in_dim.16.gain_ref, ...), custom_call_target="tpu_custom_call" | custom-call | tf_op jit(solution)/shard_map/pallas_call | solution.py:288
  116.5 1.0 copy-done.7
  117.5 4.9 %shard_map.136.near_ref = f32[256,384]{1,0:T(8,128)S(1)} custom-call(s32[4]{0:T(128)S(1)} %pad_add_fusion.where_ref, bf16[256,384]{1,0:T(8,128)(2,1)S(1)} %get-tuple-element.18.q_ref, bf16[4,640,128]{2,1,0:T(8,128)(2,1)S(1)} %bitcast.24, bf16[4,640,128]{2,1,0:T(8,128)(2,1)} %collective-permute-done.7.left_ref, ...), custom_call_target="tpu_custom_call" | custom-call | tf_op jit(solution)/shard_map/pallas_call | solution.py:288
  122.4 3.3 %shard_map.137 = (f32[128,384]{1,0:T(8,128)S(1)}, f32[128,384]{1,0:T(8,128)S(1)}) custom-call(bf16[256,384]{1,0:T(8,128)(2,1)S(1)} %get-tuple-element.18.q_ref, bf16[2,640,128]{2,1,0:T(8,128)(2,1)} %collective-permute-done.8.low_ref, bf16[2,640,128]{2,1,0:T(8,128)(2,1)S(1)} %collective-permute-done.10.high_ref, f32[256,384]{1,0:T(8,128)S(1)} %shard_map.136.near_ref), custom_call_target="tpu_custom_call" | custom-call | tf_op jit(solution)/shard_map/pallas_call | solution.py:288
  125.7 2.3 %collective-permute-start.11 = (f32[128,384]{1,0:T(8,128)S(1)}, f32[128,384]{1,0:T(8,128)S(1)}, u32[]{:S(2)}, u32[]{:S(2)}) collective-permute-start(f32[128,384]{1,0:T(8,128)S(1)} %get-tuple-element.23), channel_id=1, source_target_pairs={{0,1},{1,0},{2,3},{3,2},{4,5},{5,4},{6,7},{7,6},{8,9},{9,8},{10,11... | collective-permute-start | bytes 589832 | tf_op jit(solution)/shard_map/ppermute | solution.py:399
  128.0 1.0 collective-permute-done.11.other_ref
  129.1 1.3 %shard_map.138 = bf16[128,640]{1,0:T(8,128)(2,1)} custom-call(f32[128,384]{1,0:T(8,128)S(1)} %get-tuple-element.22.own_ref, f32[128,384]{1,0:T(8,128)S(1)} %collective-permute-done.11.other_ref, bf16[128,640]{1,0:T(8,128)(2,1)S(1)} %get-tuple-element.17.mid_ref, bf16[320,640]{1,0:T(8,128)(2,1)S(1)} %copy-done.6), custom_call_target="tpu_custom_call" | custom-call | tf_op jit(solution)/shard_map/pallas_call | solution.py:288
  (50 shorter events, 4.0 us)
Async XLA Ops:
  0.6 92.0 %copy-start = (f32[320,640]{1,0:T(8,128)S(1)}, f32[320,640]{1,0:T(8,128)}, u32[]{:S(2)}) copy-start(f32[320,640]{1,0:T(8,128)} %param.18) | copy-start | bytes 2457604
  0.6 60.1 %copy-start.9 = (f32[640]{0:T(1024)S(1)}, f32[640]{0:T(1024)}, u32[]{:S(2)}) copy-start(f32[640]{0:T(1024)} %param.14) | copy-start | bytes 7684
  0.7 60.1 %copy-start.10 = (f32[640]{0:T(1024)S(1)}, f32[640]{0:T(1024)}, u32[]{:S(2)}) copy-start(f32[640]{0:T(1024)} %param.15) | copy-start | bytes 7684
  22.9 37.9 %collective-permute-start.1 = (bf16[4,192,640]{2,1,0:T(8,128)(2,1)S(1)}, bf16[4,192,640]{2,1,0:T(8,128)(2,1)S(1)}, u32[]{:S(2)}, u32[]{:S(2)}) collective-permute-start(bf16[4,192,640]{2,1,0:T(8,128)(2,1)S(1)} %bitcast.19), channel_id=1, source_target_pairs={{0,8},{1,9},{2,10},{3,11},{4,12},{5,13},{6,14},{7,15},{8,16},{9,17... | collective-permute-start | bytes 2949128 | tf_op jit(solution)/shard_map/ppermute | solution.py:325
  25.8 39.0 %collective-permute-start.2 = (bf16[4,192,640]{2,1,0:T(8,128)(2,1)S(1)}, bf16[4,192,640]{2,1,0:T(8,128)(2,1)}, u32[]{:S(2)}, u32[]{:S(2)}) collective-permute-start(bf16[4,192,640]{2,1,0:T(8,128)(2,1)S(1)} %bitcast.20), channel_id=1, source_target_pairs={{0,24},{1,25},{2,26},{3,27},{4,28},{5,29},{6,30},{7,31},{8,0},{9,1... | collective-permute-start | bytes 2949128 | tf_op jit(solution)/shard_map/ppermute | solution.py:326
  29.4 40.7 %collective-permute-start = (bf16[128,640]{1,0:T(8,128)(2,1)}, bf16[128,640]{1,0:T(8,128)(2,1)}, u32[]{:S(2)}, u32[]{:S(2)}) collective-permute-start(bf16[128,640]{1,0:T(8,128)(2,1)} %latent_ref.3), channel_id=1, source_target_pairs={{2,0},{4,2},{6,4},{8,6},{10,8},{12,10},{14,12},{16,14},{18,16},{20... | collective-permute-start | bytes 491528 | tf_op jit(solution)/shard_map/ppermute | solution.py:327
  33.1 0.9 copy-start.3
  35.7 40.8 %all-to-all-start = ((f32[32,8,128]{2,1,0:T(8,128)}), f32[32,8,128]{2,1,0:T(8,128)}, u32[]{:S(2)}, u32[]{:S(2)}) async-start(f32[32,8,128]{2,1,0:T(8,128)} %shard_map.131), calls=%async_computation | async-start | bytes 262144 | tf_op jit(solution)/shard_map/all_to_all | solution.py:63
  60.9 9.3 %copy-start.1 = (bf16[4,192,640]{2,1,0:T(8,128)(2,1)}, bf16[4,192,640]{2,1,0:T(8,128)(2,1)S(1)}, u32[]{:S(2)}) copy-start(bf16[4,192,640]{2,1,0:T(8,128)(2,1)S(1)} %collective-permute-done.1.left_ref) | copy-start | bytes 2949124
  61.7 23.8 %collective-permute-start.3 = (bf16[2,192,640]{2,1,0:T(8,128)(2,1)}, bf16[2,192,640]{2,1,0:T(8,128)(2,1)}, u32[]{:S(2)}, u32[]{:S(2)}) collective-permute-start(bf16[2,192,640]{2,1,0:T(8,128)(2,1)} %slice.16), channel_id=1, source_target_pairs={{0,8},{1,9},{2,10},{3,11},{4,12},{5,13},{6,14},{7,15},{8,16},{9,17... | collective-permute-start | bytes 1474568 | tf_op jit(solution)/shard_map/ppermute | solution.py:336
  66.7 18.9 %collective-permute-start.4 = (bf16[2,192,640]{2,1,0:T(8,128)(2,1)}, bf16[2,192,640]{2,1,0:T(8,128)(2,1)}, u32[]{:S(2)}, u32[]{:S(2)}) collective-permute-start(bf16[2,192,640]{2,1,0:T(8,128)(2,1)} %slice.17), channel_id=1, source_target_pairs={{0,24},{1,25},{2,26},{3,27},{4,28},{5,29},{6,30},{7,31},{8,0},{9,1... | collective-permute-start | bytes 1474568 | tf_op jit(solution)/shard_map/ppermute | solution.py:337
  76.5 9.1 %copy-start.2 = (bf16[4,192,640]{2,1,0:T(8,128)(2,1)S(1)}, bf16[4,192,640]{2,1,0:T(8,128)(2,1)}, u32[]{:S(2)}) copy-start(bf16[4,192,640]{2,1,0:T(8,128)(2,1)} %copy-done.1) | copy-start | bytes 2949124
  79.6 22.2 %collective-permute-start.9 = (bf16[4,640,128]{2,1,0:T(8,128)(2,1)S(1)}, bf16[4,640,128]{2,1,0:T(8,128)(2,1)S(1)}, u32[]{:S(2)}, u32[]{:S(2)}) collective-permute-start(bf16[4,640,128]{2,1,0:T(8,128)(2,1)S(1)} %bitcast.22), channel_id=1, source_target_pairs={{0,24},{1,25},{2,26},{3,27},{4,28},{5,29},{6,30},{7,31},{8,0},{9,1... | collective-permute-start | bytes 1966088 | tf_op jit(solution)/shard_map/ppermute | solution.py:351
  82.9 23.5 %collective-permute-start.7 = (bf16[4,640,128]{2,1,0:T(8,128)(2,1)S(1)}, bf16[4,640,128]{2,1,0:T(8,128)(2,1)}, u32[]{:S(2)}, u32[]{:S(2)}) collective-permute-start(bf16[4,640,128]{2,1,0:T(8,128)(2,1)S(1)} %bitcast.23), channel_id=1, source_target_pairs={{0,8},{1,9},{2,10},{3,11},{4,12},{5,13},{6,14},{7,15},{8,16},{9,17... | collective-permute-start | bytes 1966088 | tf_op jit(solution)/shard_map/ppermute | solution.py:350
  85.6 7.6 %copy-start.8 = (f32[640]{0:T(1024)S(1)}, f32[640]{0:T(1024)}, u32[]{:S(2)}) copy-start(f32[640]{0:T(1024)} %param.17) | copy-start | bytes 7684
  85.6 8.1 %copy-start.4 = (bf16[128,640]{1,0:T(8,128)(2,1)S(1)}, bf16[128,640]{1,0:T(8,128)(2,1)}, u32[]{:S(2)}) copy-start(bf16[128,640]{1,0:T(8,128)(2,1)} %latent_ref.3) | copy-start | bytes 491524
  89.6 23.1 %copy-start.11 = (f32[640]{0:T(1024)S(1)}, f32[640]{0:T(1024)}, u32[]{:S(2)}) copy-start(f32[640]{0:T(1024)} %param.19) | copy-start | bytes 7684
  89.7 23.1 %copy-start.12 = (f32[640]{0:T(1024)S(1)}, f32[640]{0:T(1024)}, u32[]{:S(2)}) copy-start(f32[640]{0:T(1024)} %param.20) | copy-start | bytes 7684
  89.7 4.0 %collective-permute-start.5 = (f32[128,640]{1,0:T(8,128)S(1)}, f32[128,640]{1,0:T(8,128)S(1)}, u32[]{:S(2)}, u32[]{:S(2)}) collective-permute-start(f32[128,640]{1,0:T(8,128)S(1)} %get-tuple-element.14), channel_id=1, source_target_pairs={{0,1},{1,0},{2,3},{3,2},{4,5},{5,4},{6,7},{7,6},{8,9},{9,8},{10,11... | collective-permute-start | bytes 983048 | tf_op jit(solution)/shard_map/ppermute | solution.py:368
  95.4 18.2 %all-to-all-start.1 = ((f32[32,8,128]{2,1,0:T(8,128)}), f32[32,8,128]{2,1,0:T(8,128)S(1)}, u32[]{:S(2)}, u32[]{:S(2)}) async-start(f32[32,8,128]{2,1,0:T(8,128)} %get-tuple-element.16), calls=%async_computation.1 | async-start | bytes 262144 | tf_op jit(solution)/shard_map/all_to_all | solution.py:63
  101.8 20.6 %collective-permute-start.10 = (bf16[2,640,128]{2,1,0:T(8,128)(2,1)S(1)}, bf16[2,640,128]{2,1,0:T(8,128)(2,1)S(1)}, u32[]{:S(2)}, u32[]{:S(2)}) collective-permute-start(bf16[2,640,128]{2,1,0:T(8,128)(2,1)S(1)} %slice.19), channel_id=1, source_target_pairs={{0,24},{1,25},{2,26},{3,27},{4,28},{5,29},{6,30},{7,31},{8,0},{9,1... | collective-permute-start | bytes 983048 | tf_op jit(solution)/shard_map/ppermute | solution.py:372
  108.1 14.3 %collective-permute-start.8 = (bf16[2,640,128]{2,1,0:T(8,128)(2,1)}, bf16[2,640,128]{2,1,0:T(8,128)(2,1)}, u32[]{:S(2)}, u32[]{:S(2)}) collective-permute-start(bf16[2,640,128]{2,1,0:T(8,128)(2,1)} %slice.18), channel_id=1, source_target_pairs={{0,8},{1,9},{2,10},{3,11},{4,12},{5,13},{6,14},{7,15},{8,16},{9,17... | collective-permute-start | bytes 983048 | tf_op jit(solution)/shard_map/ppermute | solution.py:371
  110.0 3.6 %collective-permute-start.6 = (bf16[128,640]{1,0:T(8,128)(2,1)S(1)}, bf16[128,640]{1,0:T(8,128)(2,1)S(1)}, u32[]{:S(2)}, u32[]{:S(2)}) collective-permute-start(bf16[128,640]{1,0:T(8,128)(2,1)S(1)} %get-tuple-element.17.mid_ref), channel_id=1, source_target_pairs={{0,1},{1,0},{2,3},{3,2},{4,5},{5,4},{6,7},{7,6},{8,9},{9,8},{10,11... | collective-permute-start | bytes 491528 | tf_op jit(solution)/shard_map/ppermute | solution.py:379
  113.6 1.3 copy-start.5
  116.5 12.5 %copy-start.6 = (bf16[320,640]{1,0:T(8,128)(2,1)S(1)}, bf16[320,640]{1,0:T(8,128)(2,1)}, u32[]{:S(2)}) copy-start(bf16[320,640]{1,0:T(8,128)(2,1)} %weight_ref.1) | copy-start | bytes 1228804
  116.5 1.0 copy-start.7
  125.7 3.3 %collective-permute-start.11 = (f32[128,384]{1,0:T(8,128)S(1)}, f32[128,384]{1,0:T(8,128)S(1)}, u32[]{:S(2)}, u32[]{:S(2)}) collective-permute-start(f32[128,384]{1,0:T(8,128)S(1)} %get-tuple-element.23), channel_id=1, source_target_pairs={{0,1},{1,0},{2,3},{3,2},{4,5},{5,4},{6,7},{7,6},{8,9},{9,8},{10,11... | collective-permute-start | bytes 589832 | tf_op jit(solution)/shard_map/ppermute | solution.py:399

commit v8 on v7

--- a/solution.py
+++ b/solution.py
@@ -169,7 +169,7 @@
 
 
 def project(
-    every_ref, mid_ref, other_ref, gain_ref, shift_ref, weight_ref, query_ref, fresh_ref
+    every_ref, mid_ref, other_ref, gain_ref, shift_ref, weight_ref, query_ref, fresh_ref, kept_ref
 ):
     count = mid_ref.shape[0]
     mean, inverse = merged_stats(every_ref, count, 1e-06)
@@ -179,7 +179,9 @@
     lane = lax.broadcasted_iota(jnp.int32, query.shape, 1)
     query = jnp.where(lane < HEADS * HEAD_DIM, query, 0.0).astype(jnp.bfloat16)
     query_ref[...] = query * jnp.bfloat16(1.0 / math.sqrt(HEAD_DIM))
-    fresh_ref[...] = dot_t(weight_ref[HEADS * HEAD_DIM :], normed[:count]).astype(jnp.bfloat16)
+    fresh = dot_t(weight_ref[HEADS * HEAD_DIM :], normed[:count]).astype(jnp.bfloat16)
+    fresh_ref[...] = fresh
+    kept_ref[...] = fresh
 
 
 def attention(q_ref, blocks, replaced, fresh_ref, before):
@@ -250,9 +252,9 @@
         out_ref[:, 128 * tile : 128 * (tile + 1)] = value
 
 
-def attend_far(q_ref, low_ref, high_ref, near_ref, out_ref, given_ref):
+def attend_far(q_ref, far_ref, near_ref, out_ref, given_ref):
     count = out_ref.shape[0]
-    blocks = [[(low_ref, 0), (low_ref, 1), (high_ref, 0), (high_ref, 1)]]
+    blocks = [[(far_ref, z) for z in range(4)]]
     for tile, value in enumerate(attention(q_ref, blocks, None, None, near_ref)):
         out_ref[:, 128 * tile : 128 * (tile + 1)] = value[:count]
         given_ref[:, 128 * tile : 128 * (tile + 1)] = value[count:]
@@ -284,7 +286,7 @@
     out_ref[...] = result.astype(jnp.bfloat16)
 
 
-def call(kernel, outs, smem, *args, scratch=(), fetched=()):
+def call(kernel, outs, smem, *args, scratch=(), fetched=(), cost=None):
     return pl.pallas_call(
         kernel,
         out_shape=[jax.ShapeDtypeStruct(shape, dtype) for shape, dtype in outs],
@@ -294,6 +296,7 @@
         ],
         out_specs=[VMEM] * len(outs),
         scratch_shapes=list(scratch),
+        cost_estimate=cost,
         compiler_params=pltpu.CompilerParams(vmem_limit_bytes=40 * 1024 * 1024),
     )(*args)
 
@@ -368,11 +371,10 @@
     other = lax.ppermute(given, "space", SWAP)
     mid, stats2 = call(middle, [((tok_dev, width), bf16), table], 0, kept, other, latent, bias)
     every2 = exchanged(stats2)
-    low_kv = lax.ppermute(left_kv[:2], "space", RIGHT)
-    high_kv = lax.ppermute(right_kv[2:], "space", LEFT)
-    query, fresh = call(
+    far_kv = lax.ppermute(left_kv, "space", RIGHT)
+    query, fresh, kept_kv = call(
         project,
-        [((2 * tok_dev, 384), bf16), ((2 * feats, tok_dev), bf16)],
+        [((2 * tok_dev, 384), bf16)] + [((2 * feats, tok_dev), bf16)] * 2,
         0,
         every2,
         mid,
@@ -381,7 +383,7 @@
         norm2_shift[None],
         qkv_weight.T,
     )
-    fresh_kv = fresh.reshape(2, feats, tok_dev).transpose(0, 2, 1)
+    fresh_kv = kept_kv.reshape(2, feats, tok_dev).transpose(0, 2, 1)
     (near,) = call(
         attend_near,
         [((2 * tok_dev, 384), f32)],
@@ -392,9 +394,10 @@
         left_kv,
         right_kv,
         fresh,
+        cost=pl.CostEstimate(flops=2000000000, transcendentals=2 * 10**6, bytes_accessed=3 * 10**6),
     )
     mine, theirs = call(
-        attend_far, [((tok_dev, 384), f32)] * 2, 0, query, low_kv, high_kv, near
+        attend_far, [((tok_dev, 384), f32)] * 2, 0, query, far_kv, near
     )
     other = lax.ppermute(theirs, "space", SWAP)
     (result,) = call(finish, [((tok_dev, width), bf16)], 0, mine, other, mid, out_weight)

time: 131 us -> 129 us (0.985)
  waiting for transfers between devices: 2.39 us -> 8.31 us
  local copies, waits for them, and re-layouts: 8.78 us -> 4.73 us
  starting transfers between devices: 51.7 us -> 48.4 us
    ppermute x2 -> x1, waiting for transfers between devices: 0.01 us -> 3.89 us  [on_device(): far_kv = lax.ppermute(left_kv, 'space', RIGHT)]
    ppermute x2 -> x1, starting transfers between devices: 6.46 us -> 3.34 us  [on_device(): far_kv = lax.ppermute(left_kv, 'space', RIGHT)]
    all_to_all x2, waiting for transfers between devices: 0.01 us -> 2.56 us  [exchanged(): return lax.all_to_all(stats, 'space', 0, 0, tiled=True)]
    unnamed x26 -> x24, local copies, waits for them, and re-layouts: 3.23 us -> 0.98 us
    all_to_all x2, starting transfers between devices: 15.6 us -> 13.6 us  [exchanged(): return lax.all_to_all(stats, 'space', 0, 0, tiled=True)]
    slice x2 -> x0, local copies, waits for them, and re-layouts: 1.74 us -> none  [the longest x1 1.72 us: on_device(): low_kv = lax.ppermute(left_kv[:2], 'space', RIGHT)]
  transfers between devices with their start and end apart: 14 -> 13, of which waited for: 3 -> 4; matrix products, arithmetic and copies ran while one was open for 5% -> 3% of each run, Pallas kernels for 13% -> 14%
where the time goes in v8:
time: 129 us; the launch traced here: 128 us
  starting transfers between devices  48.4 us (38%)
  blocking collectives  42.9 us (33%)
  Pallas kernels  21 us (16%)
  waiting for transfers between devices  8.31 us (6%)
  local copies, waits for them, and re-layouts  4.73 us (4%)
  between operations  1.69 us (1%)
    all_gather x1, blocking collectives, on_device(): own_w = lax.all_gather(weight, 'space', axis=0, axis_index_groups=Z_GROUPS)  21.4 us
    pallas_call x8, Pallas kernels, call(): pl.pallas_call(kernel, out_shape=[jax.ShapeDtypeStruct(shape, dtype) for...  21 us
    all_gather x1, blocking collectives, on_device(): own_kv = lax.all_gather(stale, 'space', axis=0, axis_index_groups=Z_GROUPS)  16.2 us
    all_to_all x2, starting transfers between devices, exchanged(): return lax.all_to_all(stats, 'space', 0, 0, tiled=True)  13.6 us
    all_gather x1, blocking collectives, on_device(): lax.all_gather(jnp.stack([latent, outer]), 'space', axis=0, axis_index_gr...  5.26 us
    ppermute x1, starting transfers between devices, on_device(): right_kv = lax.ppermute(own_kv, 'space', LEFT)  4.58 us
    ppermute x1, waiting for transfers between devices, on_device(): far_kv = lax.ppermute(left_kv, 'space', RIGHT)  3.89 us
    ppermute x1, starting transfers between devices, on_device(): right_w = lax.ppermute(own_w, 'space', LEFT)  3.64 us
  transfers between devices with their start and end apart: 13, of which 4 were waited for; matrix products, arithmetic and copies ran while one was open for 3% of the time, Pallas kernels for 14%

profile of v8, /device:TPU:1, one launch (start us, length us, event | category | flops | bytes accessed | tf_op | source)
XLA Modules:
  0.0 127.8 jit_solution(3124027494075705598)
XLA Ops:
  0.7 1.0 pad.4
  1.7 21.4 %all-gather.1 = bf16[768,640]{1,0:T(8,128)(2,1)S(1)} all-gather(bf16[192,640]{1,0:T(8,128)(2,1)S(1)} %pad.4), channel_id=3, replica_groups={{0,2,4,6},{1,3,5,7},{8,10,12,14},{9,11,13,15},{16,18,20,22},{17,19,21,2..., dimensions={0}, use_global_device_ids=true | all-gather | bytes 1228800 | tf_op jit(solution)/shard_map/all_gather | solution.py:327
  23.1 2.8 %collective-permute-start.1 = (bf16[4,192,640]{2,1,0:T(8,128)(2,1)S(1)}, bf16[4,192,640]{2,1,0:T(8,128)(2,1)S(1)}, u32[]{:S(2)}, u32[]{:S(2)}) collective-permute-start(bf16[4,192,640]{2,1,0:T(8,128)(2,1)S(1)} %bitcast.19), channel_id=1, source_target_pairs={{0,8},{1,9},{2,10},{3,11},{4,12},{5,13},{6,14},{7,15},{8,16},{9,17... | collective-permute-start | bytes 2949128 | tf_op jit(solution)/shard_map/ppermute | solution.py:328
  26.0 3.6 %collective-permute-start.2 = (bf16[4,192,640]{2,1,0:T(8,128)(2,1)S(1)}, bf16[4,192,640]{2,1,0:T(8,128)(2,1)}, u32[]{:S(2)}, u32[]{:S(2)}) collective-permute-start(bf16[4,192,640]{2,1,0:T(8,128)(2,1)S(1)} %bitcast.20), channel_id=1, source_target_pairs={{0,24},{1,25},{2,26},{3,27},{4,28},{5,29},{6,30},{7,31},{8,0},{9,1... | collective-permute-start | bytes 2949128 | tf_op jit(solution)/shard_map/ppermute | solution.py:329
  29.6 3.0 %collective-permute-start = (bf16[128,640]{1,0:T(8,128)(2,1)}, bf16[128,640]{1,0:T(8,128)(2,1)S(1)}, u32[]{:S(2)}, u32[]{:S(2)}) collective-permute-start(bf16[128,640]{1,0:T(8,128)(2,1)} %latent_ref.3), channel_id=1, source_target_pairs={{2,0},{4,2},{6,4},{8,6},{10,8},{12,10},{14,12},{16,14},{18,16},{20... | collective-permute-start | bytes 491528 | tf_op jit(solution)/shard_map/ppermute | solution.py:330
  32.6 0.9 copy-done.1
  33.5 1.6 %shard_map.131 = f32[32,8,128]{2,1,0:T(8,128)} custom-call(bf16[128,640]{1,0:T(8,128)(2,1)S(1)} %copy-done.1), custom_call_target="tpu_custom_call" | custom-call | tf_op jit(solution)/shard_map/pallas_call | solution.py:290
  35.2 9.8 %all-to-all-start = ((f32[32,8,128]{2,1,0:T(8,128)}), f32[32,8,128]{2,1,0:T(8,128)}, u32[]{:S(2)}, u32[]{:S(2)}) async-start(f32[32,8,128]{2,1,0:T(8,128)} %shard_map.131), calls=%async_computation | async-start | bytes 262144 | tf_op jit(solution)/shard_map/all_to_all | solution.py:63
  45.0 16.2 %all-gather.2 = bf16[2560,128]{1,0:T(8,128)(2,1)} all-gather(bf16[640,128]{1,0:T(8,128)(2,1)S(1)} %bitcast.26), channel_id=4, replica_groups={{0,2,4,6},{1,3,5,7},{8,10,12,14},{9,11,13,15},{16,18,20,22},{17,19,21,2..., dimensions={0}, use_global_device_ids=true | all-gather | bytes 819200 | tf_op jit(solution)/shard_map/all_gather | solution.py:338
  61.4 0.8 slice.8
  62.2 3.1 %collective-permute-start.3 = (bf16[2,192,640]{2,1,0:T(8,128)(2,1)}, bf16[2,192,640]{2,1,0:T(8,128)(2,1)}, u32[]{:S(2)}, u32[]{:S(2)}) collective-permute-start(bf16[2,192,640]{2,1,0:T(8,128)(2,1)} %slice.8), channel_id=1, source_target_pairs={{0,8},{1,9},{2,10},{3,11},{4,12},{5,13},{6,14},{7,15},{8,16},{9,17... | collective-permute-start | bytes 1474568 | tf_op jit(solution)/shard_map/ppermute | solution.py:339
  65.3 1.9 %slice.9 = bf16[2,192,640]{2,1,0:T(8,128)(2,1)} slice(bf16[4,192,640]{2,1,0:T(8,128)(2,1)} %collective-permute-done.2.right_ref), slice={[2:4], [0:192], [0:640]} | slice | bytes 983040 | tf_op jit(solution)/shard_map/slice | solution.py:340
  67.2 3.4 %collective-permute-start.4 = (bf16[2,192,640]{2,1,0:T(8,128)(2,1)}, bf16[2,192,640]{2,1,0:T(8,128)(2,1)}, u32[]{:S(2)}, u32[]{:S(2)}) collective-permute-start(bf16[2,192,640]{2,1,0:T(8,128)(2,1)} %slice.9), channel_id=1, source_target_pairs={{0,24},{1,25},{2,26},{3,27},{4,28},{5,29},{6,30},{7,31},{8,0},{9,1... | collective-permute-start | bytes 1474568 | tf_op jit(solution)/shard_map/ppermute | solution.py:340
  70.6 5.3 %all-gather = bf16[4,128,640]{2,1,0:T(8,128)(2,1)S(1)} all-gather(bf16[2,128,640]{2,1,0:T(8,128)(2,1)S(1)} %pad_maximum_fusion), channel_id=2, replica_groups={{0,1},{2,3},{4,5},{6,7},{8,9},{10,11},{12,13},{14,15},{16,17},{18,19},{..., dimensions={0}, use_global_device_ids=true | all-gather | bytes 983040 | tf_op jit(solution)/shard_map/all_gather | solution.py:333
  75.9 3.0 %shard_map.132.blocks_ref = bf16[16,256,192]{2,1,0:T(8,128)(2,1)S(1)} custom-call(s32[4]{0:T(128)S(1)} %pad_add_fusion.where_ref, f32[32,8,128]{2,1,0:T(8,128)} %all-to-all-done.every_ref, bf16[2,2,128,640]{3,2,1,0:T(8,128)(2,1)S(1)} %bitcast.22, f32[1,640]{1,0:T(1,128)S(1)} %broadcast_in_dim.14.gain_ref, f32[1,640]{1,0:T(1,128)S(1)} %broadcast_in_dim.15.shift_ref), custom_call_target="tpu_custom_call" | custom-call | tf_op jit(solution)/shard_map/pallas_call | solution.py:290
  78.9 1.9 %collective-permute-start.7 = (bf16[4,640,128]{2,1,0:T(8,128)(2,1)}, bf16[4,640,128]{2,1,0:T(8,128)(2,1)}, u32[]{:S(2)}, u32[]{:S(2)}) collective-permute-start(bf16[4,640,128]{2,1,0:T(8,128)(2,1)} %bitcast.12.own_ref), channel_id=1, source_target_pairs={{0,8},{1,9},{2,10},{3,11},{4,12},{5,13},{6,14},{7,15},{8,16},{9,17... | collective-permute-start | bytes 1966088 | tf_op jit(solution)/shard_map/ppermute | solution.py:353
  81.6 4.0 %shard_map.133 = (f32[128,640]{1,0:T(8,128)S(1)}, f32[128,640]{1,0:T(8,128)S(1)}) custom-call(s32[4]{0:T(128)S(1)} %pad_add_fusion.where_ref, bf16[16,256,192]{2,1,0:T(8,128)(2,1)S(1)} %shard_map.132.blocks_ref, bf16[4,192,640]{2,1,0:T(8,128)(2,1)S(1)} %bitcast.21, bf16[4,192,640]{2,1,0:T(8,128)(2,1)S(1)} %collective-permute-done.1.left_ref, ...), custom_call_target="tpu_custom_call" | custom-call | tf_op jit(solution)/shard_map/pallas_call | solution.py:290
  85.6 3.5 %collective-permute-start.5 = (f32[128,640]{1,0:T(8,128)S(1)}, f32[128,640]{1,0:T(8,128)S(1)}, u32[]{:S(2)}, u32[]{:S(2)}) collective-permute-start(f32[128,640]{1,0:T(8,128)S(1)} %get-tuple-element.15), channel_id=1, source_target_pairs={{0,1},{1,0},{2,3},{3,2},{4,5},{5,4},{6,7},{7,6},{8,9},{9,8},{10,11... | collective-permute-start | bytes 983048 | tf_op jit(solution)/shard_map/ppermute | solution.py:371
  89.2 4.6 %collective-permute-start.9 = (bf16[4,640,128]{2,1,0:T(8,128)(2,1)}, bf16[4,640,128]{2,1,0:T(8,128)(2,1)}, u32[]{:S(2)}, u32[]{:S(2)}) collective-permute-start(bf16[4,640,128]{2,1,0:T(8,128)(2,1)} %bitcast.12.own_ref), channel_id=1, source_target_pairs={{0,24},{1,25},{2,26},{3,27},{4,28},{5,29},{6,30},{7,31},{8,0},{9,1... | collective-permute-start | bytes 1966088 | tf_op jit(solution)/shard_map/ppermute | solution.py:354
  94.4 1.7 %shard_map.134 = (bf16[128,640]{1,0:T(8,128)(2,1)S(1)}, f32[32,8,128]{2,1,0:T(8,128)}) custom-call(f32[128,640]{1,0:T(8,128)S(1)} %get-tuple-element.14.kept_ref, f32[128,640]{1,0:T(8,128)S(1)} %collective-permute-done.5.other_ref, bf16[128,640]{1,0:T(8,128)(2,1)S(1)} %copy-done.3, f32[1,640]{1,0:T(1,128)S(1)} %add.19.bias_ref), custom_call_target="tpu_custom_call" | custom-call | tf_op jit(solution)/shard_map/pallas_call | solution.py:290
  96.1 3.8 %all-to-all-start.1 = ((f32[32,8,128]{2,1,0:T(8,128)}), f32[32,8,128]{2,1,0:T(8,128)S(1)}, u32[]{:S(2)}, u32[]{:S(2)}) async-start(f32[32,8,128]{2,1,0:T(8,128)} %get-tuple-element.17), calls=%async_computation.1 | async-start | bytes 262144 | tf_op jit(solution)/shard_map/all_to_all | solution.py:63
  99.9 3.3 %collective-permute-start.8 = (bf16[4,640,128]{2,1,0:T(8,128)(2,1)}, bf16[4,640,128]{2,1,0:T(8,128)(2,1)S(1)}, u32[]{:S(2)}, u32[]{:S(2)}) collective-permute-start(bf16[4,640,128]{2,1,0:T(8,128)(2,1)} %collective-permute-done.7.left_ref), channel_id=1, source_target_pairs={{0,8},{1,9},{2,10},{3,11},{4,12},{5,13},{6,14},{7,15},{8,16},{9,17... | collective-permute-start | bytes 1966088 | tf_op jit(solution)/shard_map/ppermute | solution.py:374
  103.3 2.7 %collective-permute-start.6 = (bf16[128,640]{1,0:T(8,128)(2,1)S(1)}, bf16[128,640]{1,0:T(8,128)(2,1)S(1)}, u32[]{:S(2)}, u32[]{:S(2)}) collective-permute-start(bf16[128,640]{1,0:T(8,128)(2,1)S(1)} %get-tuple-element.18.mid_ref), channel_id=1, source_target_pairs={{0,1},{1,0},{2,3},{3,2},{4,5},{5,4},{6,7},{7,6},{8,9},{9,8},{10,11... | collective-permute-start | bytes 491528 | tf_op jit(solution)/shard_map/ppermute | solution.py:381
  106.1 0.8 collective-permute-done.6.other_ref
  106.9 2.6 %all-to-all-done.1.every_ref = f32[32,8,128]{2,1,0:T(8,128)S(1)} async-done(((f32[32,8,128]{2,1,0:T(8,128)}), f32[32,8,128]{2,1,0:T(8,128)S(1)}, u32[]{:S(2)}, u32[]{:S(2)}) %all-to-all-start.1) | async-done | bytes 131104 | tf_op jit(solution)/shard_map/all_to_all | solution.py:63
  109.4 1.7 %shard_map.135 = (bf16[256,384]{1,0:T(8,128)(2,1)S(1)}, bf16[640,128]{1,0:T(8,128)(2,1)S(1)}, bf16[640,128]{1,0:T(8,128)(2,1)}) custom-call(f32[32,8,128]{2,1,0:T(8,128)S(1)} %all-to-all-done.1.every_ref, bf16[128,640]{1,0:T(8,128)(2,1)S(1)} %get-tuple-element.18.mid_ref, bf16[128,640]{1,0:T(8,128)(2,1)S(1)} %collective-permute-done.6.other_ref, ...), custom_call_target="tpu_custom_call" | custom-call | tf_op jit(solution)/shard_map/pallas_call | solution.py:290
  111.1 5.3 %shard_map.136.near_ref = f32[256,384]{1,0:T(8,128)S(1)} custom-call(s32[4]{0:T(128)S(1)} %pad_add_fusion.where_ref, bf16[256,384]{1,0:T(8,128)(2,1)S(1)} %get-tuple-element.19.q_ref, bf16[4,640,128]{2,1,0:T(8,128)(2,1)} %bitcast.12.own_ref, bf16[4,640,128]{2,1,0:T(8,128)(2,1)} %collective-permute-done.7.left_ref, ...), custom_call_target="tpu_custom_call" | custom-call | flops 2000000000 | bytes 3000000 | tf_op jit(solution)/shard_map/pallas_call | solution.py:290
  116.4 3.9 %collective-permute-done.8.far_ref = bf16[4,640,128]{2,1,0:T(8,128)(2,1)S(1)} collective-permute-done((bf16[4,640,128]{2,1,0:T(8,128)(2,1)}, bf16[4,640,128]{2,1,0:T(8,128)(2,1)S(1)}, u32[]{:S(2)}, u32[]{:S(2)}) %collective-permute-start.8) | collective-permute-done | bytes 655392 | tf_op jit(solution)/shard_map/ppermute | solution.py:374
  120.3 2.3 %shard_map.137 = (f32[128,384]{1,0:T(8,128)S(1)}, f32[128,384]{1,0:T(8,128)S(1)}) custom-call(bf16[256,384]{1,0:T(8,128)(2,1)S(1)} %get-tuple-element.19.q_ref, bf16[4,640,128]{2,1,0:T(8,128)(2,1)S(1)} %collective-permute-done.8.far_ref, f32[256,384]{1,0:T(8,128)S(1)} %shard_map.136.near_ref), custom_call_target="tpu_custom_call" | custom-call | tf_op jit(solution)/shard_map/pallas_call | solution.py:290
  122.7 2.8 %collective-permute-start.10 = (f32[128,384]{1,0:T(8,128)S(1)}, f32[128,384]{1,0:T(8,128)S(1)}, u32[]{:S(2)}, u32[]{:S(2)}) collective-permute-start(f32[128,384]{1,0:T(8,128)S(1)} %get-tuple-element.24), channel_id=1, source_target_pairs={{0,1},{1,0},{2,3},{3,2},{4,5},{5,4},{6,7},{7,6},{8,9},{9,8},{10,11... | collective-permute-start | bytes 589832 | tf_op jit(solution)/shard_map/ppermute | solution.py:402
  125.5 1.0 collective-permute-done.10.other_ref
  126.5 1.3 %shard_map.138 = bf16[128,640]{1,0:T(8,128)(2,1)} custom-call(f32[128,384]{1,0:T(8,128)S(1)} %get-tuple-element.23.own_ref, f32[128,384]{1,0:T(8,128)S(1)} %collective-permute-done.10.other_ref, bf16[128,640]{1,0:T(8,128)(2,1)S(1)} %get-tuple-element.18.mid_ref, bf16[320,640]{1,0:T(8,128)(2,1)S(1)} %copy-done.5), custom_call_target="tpu_custom_call" | custom-call | tf_op jit(solution)/shard_map/pallas_call | solution.py:290
  (44 shorter events, 0.9 us)
Async XLA Ops:
  0.6 93.2 %copy-start = (f32[320,640]{1,0:T(8,128)S(1)}, f32[320,640]{1,0:T(8,128)}, u32[]{:S(2)}) copy-start(f32[320,640]{1,0:T(8,128)} %param.18) | copy-start | bytes 2457604
  0.6 44.4 %copy-start.6 = (bf16[2,128,320]{1,2,0:T(8,128)(2,1)S(1)}, bf16[2,128,320]{1,2,0:T(8,128)(2,1)}, u32[]{:S(2)}) copy-start(bf16[2,128,320]{1,2,0:T(8,128)(2,1)} %param.23) | copy-start | bytes 491524
  0.7 60.6 %copy-start.8 = (f32[640]{0:T(1024)S(1)}, f32[640]{0:T(1024)}, u32[]{:S(2)}) copy-start(f32[640]{0:T(1024)} %param.14) | copy-start | bytes 7684
  0.7 60.6 %copy-start.9 = (f32[640]{0:T(1024)S(1)}, f32[640]{0:T(1024)}, u32[]{:S(2)}) copy-start(f32[640]{0:T(1024)} %param.15) | copy-start | bytes 7684
  1.7 68.8 %copy-start.2 = (bf16[128,640]{1,0:T(8,128)(2,1)S(1)}, bf16[128,640]{1,0:T(8,128)(2,1)}, u32[]{:S(2)}) copy-start(bf16[128,640]{1,0:T(8,128)(2,1)} %latent_ref.3) | copy-start | bytes 491524
  23.1 38.3 %collective-permute-start.1 = (bf16[4,192,640]{2,1,0:T(8,128)(2,1)S(1)}, bf16[4,192,640]{2,1,0:T(8,128)(2,1)S(1)}, u32[]{:S(2)}, u32[]{:S(2)}) collective-permute-start(bf16[4,192,640]{2,1,0:T(8,128)(2,1)S(1)} %bitcast.19), channel_id=1, source_target_pairs={{0,8},{1,9},{2,10},{3,11},{4,12},{5,13},{6,14},{7,15},{8,16},{9,17... | collective-permute-start | bytes 2949128 | tf_op jit(solution)/shard_map/ppermute | solution.py:328
  26.0 39.4 %collective-permute-start.2 = (bf16[4,192,640]{2,1,0:T(8,128)(2,1)S(1)}, bf16[4,192,640]{2,1,0:T(8,128)(2,1)}, u32[]{:S(2)}, u32[]{:S(2)}) collective-permute-start(bf16[4,192,640]{2,1,0:T(8,128)(2,1)S(1)} %bitcast.20), channel_id=1, source_target_pairs={{0,24},{1,25},{2,26},{3,27},{4,28},{5,29},{6,30},{7,31},{8,0},{9,1... | collective-permute-start | bytes 2949128 | tf_op jit(solution)/shard_map/ppermute | solution.py:329
  29.6 41.0 %collective-permute-start = (bf16[128,640]{1,0:T(8,128)(2,1)}, bf16[128,640]{1,0:T(8,128)(2,1)S(1)}, u32[]{:S(2)}, u32[]{:S(2)}) collective-permute-start(bf16[128,640]{1,0:T(8,128)(2,1)} %latent_ref.3), channel_id=1, source_target_pairs={{2,0},{4,2},{6,4},{8,6},{10,8},{12,10},{14,12},{16,14},{18,16},{20... | collective-permute-start | bytes 491528 | tf_op jit(solution)/shard_map/ppermute | solution.py:330
  32.6 0.9 copy-start.1
  35.2 40.7 %all-to-all-start = ((f32[32,8,128]{2,1,0:T(8,128)}), f32[32,8,128]{2,1,0:T(8,128)}, u32[]{:S(2)}, u32[]{:S(2)}) async-start(f32[32,8,128]{2,1,0:T(8,128)} %shard_map.131), calls=%async_computation | async-start | bytes 262144 | tf_op jit(solution)/shard_map/all_to_all | solution.py:63
  62.2 19.4 %collective-permute-start.3 = (bf16[2,192,640]{2,1,0:T(8,128)(2,1)}, bf16[2,192,640]{2,1,0:T(8,128)(2,1)}, u32[]{:S(2)}, u32[]{:S(2)}) collective-permute-start(bf16[2,192,640]{2,1,0:T(8,128)(2,1)} %slice.8), channel_id=1, source_target_pairs={{0,8},{1,9},{2,10},{3,11},{4,12},{5,13},{6,14},{7,15},{8,16},{9,17... | collective-permute-start | bytes 1474568 | tf_op jit(solution)/shard_map/ppermute | solution.py:339
  67.2 14.4 %collective-permute-start.4 = (bf16[2,192,640]{2,1,0:T(8,128)(2,1)}, bf16[2,192,640]{2,1,0:T(8,128)(2,1)}, u32[]{:S(2)}, u32[]{:S(2)}) collective-permute-start(bf16[2,192,640]{2,1,0:T(8,128)(2,1)} %slice.9), channel_id=1, source_target_pairs={{0,24},{1,25},{2,26},{3,27},{4,28},{5,29},{6,30},{7,31},{8,0},{9,1... | collective-permute-start | bytes 1474568 | tf_op jit(solution)/shard_map/ppermute | solution.py:340
  78.9 21.0 %collective-permute-start.7 = (bf16[4,640,128]{2,1,0:T(8,128)(2,1)}, bf16[4,640,128]{2,1,0:T(8,128)(2,1)}, u32[]{:S(2)}, u32[]{:S(2)}) collective-permute-start(bf16[4,640,128]{2,1,0:T(8,128)(2,1)} %bitcast.12.own_ref), channel_id=1, source_target_pairs={{0,8},{1,9},{2,10},{3,11},{4,12},{5,13},{6,14},{7,15},{8,16},{9,17... | collective-permute-start | bytes 1966088 | tf_op jit(solution)/shard_map/ppermute | solution.py:353
  81.5 12.9 %copy-start.7 = (f32[640]{0:T(1024)S(1)}, f32[640]{0:T(1024)}, u32[]{:S(2)}) copy-start(f32[640]{0:T(1024)} %param.17) | copy-start | bytes 7684
  81.5 12.9 %copy-start.3 = (bf16[128,640]{1,0:T(8,128)(2,1)S(1)}, bf16[128,640]{1,0:T(8,128)(2,1)}, u32[]{:S(2)}) copy-start(bf16[128,640]{1,0:T(8,128)(2,1)} %latent_ref.3) | copy-start | bytes 491524
  81.5 24.5 %copy-start.10 = (f32[640]{0:T(1024)S(1)}, f32[640]{0:T(1024)}, u32[]{:S(2)}) copy-start(f32[640]{0:T(1024)} %param.19) | copy-start | bytes 7684
  81.5 24.5 %copy-start.11 = (f32[640]{0:T(1024)S(1)}, f32[640]{0:T(1024)}, u32[]{:S(2)}) copy-start(f32[640]{0:T(1024)} %param.20) | copy-start | bytes 7684
  85.6 23.8 %copy-start.4 = (bf16[640,960]{0,1:T(8,128)(2,1)S(1)}, bf16[640,960]{0,1:T(8,128)(2,1)}, u32[]{:S(2)}) copy-start(bf16[640,960]{0,1:T(8,128)(2,1)} %param.21) | copy-start | bytes 3686404
  85.6 8.8 %collective-permute-start.5 = (f32[128,640]{1,0:T(8,128)S(1)}, f32[128,640]{1,0:T(8,128)S(1)}, u32[]{:S(2)}, u32[]{:S(2)}) collective-permute-start(f32[128,640]{1,0:T(8,128)S(1)} %get-tuple-element.15), channel_id=1, source_target_pairs={{0,1},{1,0},{2,3},{3,2},{4,5},{5,4},{6,7},{7,6},{8,9},{9,8},{10,11... | collective-permute-start | bytes 983048 | tf_op jit(solution)/shard_map/ppermute | solution.py:371
  89.2 21.9 %collective-permute-start.9 = (bf16[4,640,128]{2,1,0:T(8,128)(2,1)}, bf16[4,640,128]{2,1,0:T(8,128)(2,1)}, u32[]{:S(2)}, u32[]{:S(2)}) collective-permute-start(bf16[4,640,128]{2,1,0:T(8,128)(2,1)} %bitcast.12.own_ref), channel_id=1, source_target_pairs={{0,24},{1,25},{2,26},{3,27},{4,28},{5,29},{6,30},{7,31},{8,0},{9,1... | collective-permute-start | bytes 1966088 | tf_op jit(solution)/shard_map/ppermute | solution.py:354
  96.1 13.3 %all-to-all-start.1 = ((f32[32,8,128]{2,1,0:T(8,128)}), f32[32,8,128]{2,1,0:T(8,128)S(1)}, u32[]{:S(2)}, u32[]{:S(2)}) async-start(f32[32,8,128]{2,1,0:T(8,128)} %get-tuple-element.17), calls=%async_computation.1 | async-start | bytes 262144 | tf_op jit(solution)/shard_map/all_to_all | solution.py:63
  99.9 20.4 %collective-permute-start.8 = (bf16[4,640,128]{2,1,0:T(8,128)(2,1)}, bf16[4,640,128]{2,1,0:T(8,128)(2,1)S(1)}, u32[]{:S(2)}, u32[]{:S(2)}) collective-permute-start(bf16[4,640,128]{2,1,0:T(8,128)(2,1)} %collective-permute-done.7.left_ref), channel_id=1, source_target_pairs={{0,8},{1,9},{2,10},{3,11},{4,12},{5,13},{6,14},{7,15},{8,16},{9,17... | collective-permute-start | bytes 1966088 | tf_op jit(solution)/shard_map/ppermute | solution.py:374
  103.3 3.6 %collective-permute-start.6 = (bf16[128,640]{1,0:T(8,128)(2,1)S(1)}, bf16[128,640]{1,0:T(8,128)(2,1)S(1)}, u32[]{:S(2)}, u32[]{:S(2)}) collective-permute-start(bf16[128,640]{1,0:T(8,128)(2,1)S(1)} %get-tuple-element.18.mid_ref), channel_id=1, source_target_pairs={{0,1},{1,0},{2,3},{3,2},{4,5},{5,4},{6,7},{7,6},{8,9},{9,8},{10,11... | collective-permute-start | bytes 491528 | tf_op jit(solution)/shard_map/ppermute | solution.py:381
  111.1 15.4 %copy-start.5 = (bf16[320,640]{1,0:T(8,128)(2,1)S(1)}, bf16[320,640]{1,0:T(8,128)(2,1)}, u32[]{:S(2)}) copy-start(bf16[320,640]{1,0:T(8,128)(2,1)} %weight_ref.1) | copy-start | bytes 1228804
  122.7 3.8 %collective-permute-start.10 = (f32[128,384]{1,0:T(8,128)S(1)}, f32[128,384]{1,0:T(8,128)S(1)}, u32[]{:S(2)}, u32[]{:S(2)}) collective-permute-start(f32[128,384]{1,0:T(8,128)S(1)} %get-tuple-element.24), channel_id=1, source_target_pairs={{0,1},{1,0},{2,3},{3,2},{4,5},{5,4},{6,7},{7,6},{8,9},{9,8},{10,11... | collective-permute-start | bytes 589832 | tf_op jit(solution)/shard_map/ppermute | solution.py:402

commit v9 on v8

--- a/solution.py
+++ b/solution.py
@@ -104,7 +104,8 @@
                 at = 360 * index + 180 * parity
                 low = at // 128 * 128
                 wide = flat_ref[:, low : low + 384]
-                out_ref[index] = wide[:, at - low : at - low + ROWS]
+                place = ROWS * (index % 4)
+                out_ref[index // 4, :, place : place + ROWS] = wide[:, at - low : at - low + ROWS]
 
 
 def time_embed(timestep, time_weight):
@@ -141,21 +142,21 @@
 ):
     core, x = where_ref[0], where_ref[2]
     count = kept_ref.shape[0]
-    sources = ((own_ref, 0, 0), (left_ref, 3, 0), (right_ref, 1, 0), (low_ref, 2, 0), (high_ref, 2, 2))
     copies, at = [], 0
-    for index, (ref, _, _) in enumerate(sources):
+    for index, ref in enumerate((own_ref, left_ref, right_ref, low_ref, high_ref)):
         size = ref.shape[0]
         copy = pltpu.make_async_copy(ref, held_ref.at[at : at + size], sems.at[index])
         copy.start()
-        copies.append((copy, at, size))
+        copies.append((copy, at))
         at += size
     total = None
-    for (_, step, first), (copy, at, size) in zip(sources, copies, strict=True):
-        copy.wait()
-        base = 4 * ((x + step) & 3) + first
-        for z in range(size):
-            part = dot32(blocks_ref[base + z], held_ref[at + z])
-            total = part if total is None else total + part
+    for step, parts in ((0, (0,)), (3, (1,)), (1, (2,)), (2, (3, 4))):
+        for part in parts:
+            copies[part][0].wait()
+        at = copies[parts[0]][1]
+        weight = held_ref[at : at + 4].reshape(4 * ROWS, -1)
+        product = dot32(blocks_ref[(x + step) & 3], weight)
+        total = product if total is None else total + product
     kept_ref[...] = jnp.where(core == 0, total[:count], total[count:])
     given_ref[...] = jnp.where(core == 0, total[count:], total[:count])
 
@@ -241,20 +242,20 @@
     )
 
 
-def attend_near(where_ref, q_ref, own_ref, left_ref, right_ref, fresh_ref, out_ref):
+def attend_near(where_ref, q_ref, own_ref, left_ref, fresh_ref, out_ref):
     my_z = where_ref[3]
     count = q_ref.shape[0] // 2
     row = lax.broadcasted_iota(jnp.int32, (2 * count, 4 * count), 0)
     block = lax.broadcasted_iota(jnp.int32, (2 * count, 4 * count), 1) // count
     replaced = (row < count) & (block == my_z)
-    blocks = [[(ref, z) for z in range(4)] for ref in (own_ref, left_ref, right_ref)]
+    blocks = [[(ref, z) for z in range(4)] for ref in (own_ref, left_ref)]
     for tile, value in enumerate(attention(q_ref, blocks, replaced, fresh_ref, None)):
         out_ref[:, 128 * tile : 128 * (tile + 1)] = value
 
 
-def attend_far(q_ref, far_ref, near_ref, out_ref, given_ref):
+def attend_far(q_ref, right_ref, far_ref, near_ref, out_ref, given_ref):
     count = out_ref.shape[0]
-    blocks = [[(far_ref, z) for z in range(4)]]
+    blocks = [[(ref, z) for z in range(4)] for ref in (right_ref, far_ref)]
     for tile, value in enumerate(attention(q_ref, blocks, None, None, near_ref)):
         out_ref[:, 128 * tile : 128 * (tile + 1)] = value[:count]
         given_ref[:, 128 * tile : 128 * (tile + 1)] = value[count:]
@@ -340,7 +341,7 @@
     high_w = lax.ppermute(right_w[2:], "space", LEFT)
     (blocks,) = call(
         prepare,
-        [((16, 2 * tok_dev, ROWS), bf16)],
+        [((4, 2 * tok_dev, 4 * ROWS), bf16)],
         1,
         where,
         every1,
@@ -392,12 +393,11 @@
         query,
         own_kv,
         left_kv,
-        right_kv,
         fresh,
         cost=pl.CostEstimate(flops=2000000000, transcendentals=2 * 10**6, bytes_accessed=3 * 10**6),
     )
     mine, theirs = call(
-        attend_far, [((tok_dev, 384), f32)] * 2, 0, query, far_kv, near
+        attend_far, [((tok_dev, 384), f32)] * 2, 0, query, right_kv, far_kv, near
     )
     other = lax.ppermute(theirs, "space", SWAP)
     (result,) = call(finish, [((tok_dev, width), bf16)], 0, mine, other, mid, out_weight)

time: 129 us -> 131 us (1.016)
  waiting for transfers between devices: 8.31 us -> 10 us
    ppermute x1, waiting for transfers between devices: 0.01 us -> 3 us  [on_device(): right_kv = lax.ppermute(own_kv, 'space', LEFT)]
    all_to_all x2, waiting for transfers between devices: 2.56 us -> 0.01 us  [exchanged(): return lax.all_to_all(stats, 'space', 0, 0, tiled=True)]
    all_to_all x2, starting transfers between devices: 13.6 us -> 15.7 us  [exchanged(): return lax.all_to_all(stats, 'space', 0, 0, tiled=True)]
    ppermute x1, starting transfers between devices: 3.34 us -> 1.92 us  [on_device(): far_kv = lax.ppermute(left_kv, 'space', RIGHT)]
  transfers between devices with their start and end apart: 13 -> 13, of which waited for: 4 -> 5; matrix products, arithmetic and copies ran while one was open for 3% -> 3% of each run, Pallas kernels for 14% -> 12%
where the time goes in v9:
time: 131 us; the launch traced here: 130 us
  starting transfers between devices  49.7 us (38%)
  blocking collectives  42.7 us (33%)
  Pallas kernels  21.1 us (16%)
  waiting for transfers between devices  10 us (8%)
  local copies, waits for them, and re-layouts  3.82 us (3%)
  between operations  1.68 us (1%)
    all_gather x1, blocking collectives, on_device(): own_w = lax.all_gather(weight, 'space', axis=0, axis_index_groups=Z_GROUPS)  21.2 us
    pallas_call x8, Pallas kernels, call(): pl.pallas_call(kernel, out_shape=[jax.ShapeDtypeStruct(shape, dtype) for...  21.1 us
    all_gather x1, blocking collectives, on_device(): own_kv = lax.all_gather(stale, 'space', axis=0, axis_index_groups=Z_GROUPS)  16.2 us
    all_to_all x2, starting transfers between devices, exchanged(): return lax.all_to_all(stats, 'space', 0, 0, tiled=True)  15.7 us
    all_gather x1, blocking collectives, on_device(): lax.all_gather(jnp.stack([latent, outer]), 'space', axis=0, axis_index_gr...  5.26 us
    ppermute x1, waiting for transfers between devices, on_device(): far_kv = lax.ppermute(left_kv, 'space', RIGHT)  4.62 us
    ppermute x1, starting transfers between devices, on_device(): right_kv = lax.ppermute(own_kv, 'space', LEFT)  4.55 us
    ppermute x1, starting transfers between devices, on_device(): right_w = lax.ppermute(own_w, 'space', LEFT)  3.64 us
  transfers between devices with their start and end apart: 13, of which 5 were waited for; matrix products, arithmetic and copies ran while one was open for 3% of the time, Pallas kernels for 12%

profile of v9, /device:TPU:1, one launch (start us, length us, event | category | flops | bytes accessed | tf_op | source)
XLA Modules:
  0.0 129.8 jit_solution(4117555019156950127)
XLA Ops:
  0.7 1.1 pad.4
  1.7 21.2 %all-gather.1 = bf16[768,640]{1,0:T(8,128)(2,1)S(1)} all-gather(bf16[192,640]{1,0:T(8,128)(2,1)S(1)} %pad.4), channel_id=3, replica_groups={{0,2,4,6},{1,3,5,7},{8,10,12,14},{9,11,13,15},{16,18,20,22},{17,19,21,2..., dimensions={0}, use_global_device_ids=true | all-gather | bytes 1228800 | tf_op jit(solution)/shard_map/all_gather | solution.py:328
  23.0 2.8 %collective-permute-start.1 = (bf16[4,192,640]{2,1,0:T(8,128)(2,1)S(1)}, bf16[4,192,640]{2,1,0:T(8,128)(2,1)S(1)}, u32[]{:S(2)}, u32[]{:S(2)}) collective-permute-start(bf16[4,192,640]{2,1,0:T(8,128)(2,1)S(1)} %bitcast.19), channel_id=1, source_target_pairs={{0,8},{1,9},{2,10},{3,11},{4,12},{5,13},{6,14},{7,15},{8,16},{9,17... | collective-permute-start | bytes 2949128 | tf_op jit(solution)/shard_map/ppermute | solution.py:329
  25.8 3.6 %collective-permute-start.2 = (bf16[4,192,640]{2,1,0:T(8,128)(2,1)S(1)}, bf16[4,192,640]{2,1,0:T(8,128)(2,1)}, u32[]{:S(2)}, u32[]{:S(2)}) collective-permute-start(bf16[4,192,640]{2,1,0:T(8,128)(2,1)S(1)} %bitcast.20), channel_id=1, source_target_pairs={{0,24},{1,25},{2,26},{3,27},{4,28},{5,29},{6,30},{7,31},{8,0},{9,1... | collective-permute-start | bytes 2949128 | tf_op jit(solution)/shard_map/ppermute | solution.py:330
  29.5 3.0 %collective-permute-start = (bf16[128,640]{1,0:T(8,128)(2,1)S(1)}, bf16[128,640]{1,0:T(8,128)(2,1)S(1)}, u32[]{:S(2)}, u32[]{:S(2)}) collective-permute-start(bf16[128,640]{1,0:T(8,128)(2,1)S(1)} %copy-done.1), channel_id=1, source_target_pairs={{2,0},{4,2},{6,4},{8,6},{10,8},{12,10},{14,12},{16,14},{18,16},{20... | collective-permute-start | bytes 491528 | tf_op jit(solution)/shard_map/ppermute | solution.py:331
  32.5 1.6 %shard_map.131 = f32[32,8,128]{2,1,0:T(8,128)} custom-call(bf16[128,640]{1,0:T(8,128)(2,1)S(1)} %copy-done.1), custom_call_target="tpu_custom_call" | custom-call | tf_op jit(solution)/shard_map/pallas_call | solution.py:291
  34.1 9.8 %all-to-all-start = ((f32[32,8,128]{2,1,0:T(8,128)}), f32[32,8,128]{2,1,0:T(8,128)}, u32[]{:S(2)}, u32[]{:S(2)}) async-start(f32[32,8,128]{2,1,0:T(8,128)} %shard_map.131), calls=%async_computation | async-start | bytes 262144 | tf_op jit(solution)/shard_map/all_to_all | solution.py:63
  44.0 16.2 %all-gather.2 = bf16[2560,128]{1,0:T(8,128)(2,1)} all-gather(bf16[640,128]{1,0:T(8,128)(2,1)S(1)} %bitcast.26), channel_id=4, replica_groups={{0,2,4,6},{1,3,5,7},{8,10,12,14},{9,11,13,15},{16,18,20,22},{17,19,21,2..., dimensions={0}, use_global_device_ids=true | all-gather | bytes 819200 | tf_op jit(solution)/shard_map/all_gather | solution.py:339
  60.3 0.8 slice.8
  61.2 3.1 %collective-permute-start.3 = (bf16[2,192,640]{2,1,0:T(8,128)(2,1)}, bf16[2,192,640]{2,1,0:T(8,128)(2,1)}, u32[]{:S(2)}, u32[]{:S(2)}) collective-permute-start(bf16[2,192,640]{2,1,0:T(8,128)(2,1)} %slice.8), channel_id=1, source_target_pairs={{0,8},{1,9},{2,10},{3,11},{4,12},{5,13},{6,14},{7,15},{8,16},{9,17... | collective-permute-start | bytes 1474568 | tf_op jit(solution)/shard_map/ppermute | solution.py:340
  64.3 1.8 %slice.9 = bf16[2,192,640]{2,1,0:T(8,128)(2,1)} slice(bf16[4,192,640]{2,1,0:T(8,128)(2,1)} %collective-permute-done.2.right_ref), slice={[2:4], [0:192], [0:640]} | slice | bytes 983040 | tf_op jit(solution)/shard_map/slice | solution.py:341
  66.1 3.4 %collective-permute-start.4 = (bf16[2,192,640]{2,1,0:T(8,128)(2,1)}, bf16[2,192,640]{2,1,0:T(8,128)(2,1)}, u32[]{:S(2)}, u32[]{:S(2)}) collective-permute-start(bf16[2,192,640]{2,1,0:T(8,128)(2,1)} %slice.9), channel_id=1, source_target_pairs={{0,24},{1,25},{2,26},{3,27},{4,28},{5,29},{6,30},{7,31},{8,0},{9,1... | collective-permute-start | bytes 1474568 | tf_op jit(solution)/shard_map/ppermute | solution.py:341
  69.6 5.3 %all-gather = bf16[4,128,640]{2,1,0:T(8,128)(2,1)S(1)} all-gather(bf16[2,128,640]{2,1,0:T(8,128)(2,1)S(1)} %pad_maximum_fusion), channel_id=2, replica_groups={{0,1},{2,3},{4,5},{6,7},{8,9},{10,11},{12,13},{14,15},{16,17},{18,19},{..., dimensions={0}, use_global_device_ids=true | all-gather | bytes 983040 | tf_op jit(solution)/shard_map/all_gather | solution.py:334
  74.8 3.0 %shard_map.132.blocks_ref = bf16[4,256,768]{2,1,0:T(8,128)(2,1)S(1)} custom-call(s32[4]{0:T(128)S(1)} %pad_add_fusion.where_ref, f32[32,8,128]{2,1,0:T(8,128)} %all-to-all-done.every_ref, bf16[2,2,128,640]{3,2,1,0:T(8,128)(2,1)S(1)} %bitcast.22, f32[1,640]{1,0:T(1,128)S(1)} %broadcast_in_dim.14.gain_ref, f32[1,640]{1,0:T(1,128)S(1)} %broadcast_in_dim.15.shift_ref), custom_call_target="tpu_custom_call" | custom-call | tf_op jit(solution)/shard_map/pallas_call | solution.py:291
  77.9 1.9 %collective-permute-start.8 = (bf16[4,640,128]{2,1,0:T(8,128)(2,1)}, bf16[4,640,128]{2,1,0:T(8,128)(2,1)}, u32[]{:S(2)}, u32[]{:S(2)}) collective-permute-start(bf16[4,640,128]{2,1,0:T(8,128)(2,1)} %bitcast.12.own_ref), channel_id=1, source_target_pairs={{0,8},{1,9},{2,10},{3,11},{4,12},{5,13},{6,14},{7,15},{8,16},{9,17... | collective-permute-start | bytes 1966088 | tf_op jit(solution)/shard_map/ppermute | solution.py:354
  80.5 3.4 %shard_map.133 = (f32[128,640]{1,0:T(8,128)S(1)}, f32[128,640]{1,0:T(8,128)S(1)}) custom-call(s32[4]{0:T(128)S(1)} %pad_add_fusion.where_ref, bf16[4,256,768]{2,1,0:T(8,128)(2,1)S(1)} %shard_map.132.blocks_ref, bf16[4,192,640]{2,1,0:T(8,128)(2,1)S(1)} %bitcast.21, bf16[4,192,640]{2,1,0:T(8,128)(2,1)S(1)} %collective-permute-done.1.left_ref, ...), custom_call_target="tpu_custom_call" | custom-call | tf_op jit(solution)/shard_map/pallas_call | solution.py:291
  84.0 3.5 %collective-permute-start.5 = (f32[128,640]{1,0:T(8,128)S(1)}, f32[128,640]{1,0:T(8,128)S(1)}, u32[]{:S(2)}, u32[]{:S(2)}) collective-permute-start(f32[128,640]{1,0:T(8,128)S(1)} %get-tuple-element.15), channel_id=1, source_target_pairs={{0,1},{1,0},{2,3},{3,2},{4,5},{5,4},{6,7},{7,6},{8,9},{9,8},{10,11... | collective-permute-start | bytes 983048 | tf_op jit(solution)/shard_map/ppermute | solution.py:372
  88.2 0.5 collective-permute-done.5.other_ref
  88.7 1.7 %shard_map.134 = (bf16[128,640]{1,0:T(8,128)(2,1)S(1)}, f32[32,8,128]{2,1,0:T(8,128)}) custom-call(f32[128,640]{1,0:T(8,128)S(1)} %get-tuple-element.14.kept_ref, f32[128,640]{1,0:T(8,128)S(1)} %collective-permute-done.5.other_ref, bf16[128,640]{1,0:T(8,128)(2,1)S(1)} %copy-done.2, f32[1,640]{1,0:T(1,128)S(1)} %add.19.bias_ref), custom_call_target="tpu_custom_call" | custom-call | tf_op jit(solution)/shard_map/pallas_call | solution.py:291
  90.4 5.8 %all-to-all-start.1 = ((f32[32,8,128]{2,1,0:T(8,128)}), f32[32,8,128]{2,1,0:T(8,128)S(1)}, u32[]{:S(2)}, u32[]{:S(2)}) async-start(f32[32,8,128]{2,1,0:T(8,128)} %get-tuple-element.17), calls=%async_computation.1 | async-start | bytes 262144 | tf_op jit(solution)/shard_map/all_to_all | solution.py:63
  96.2 4.5 %collective-permute-start.7 = (bf16[4,640,128]{2,1,0:T(8,128)(2,1)}, bf16[4,640,128]{2,1,0:T(8,128)(2,1)S(1)}, u32[]{:S(2)}, u32[]{:S(2)}) collective-permute-start(bf16[4,640,128]{2,1,0:T(8,128)(2,1)} %bitcast.12.own_ref), channel_id=1, source_target_pairs={{0,24},{1,25},{2,26},{3,27},{4,28},{5,29},{6,30},{7,31},{8,0},{9,1... | collective-permute-start | bytes 1966088 | tf_op jit(solution)/shard_map/ppermute | solution.py:355
  100.8 1.9 %collective-permute-start.9 = (bf16[4,640,128]{2,1,0:T(8,128)(2,1)}, bf16[4,640,128]{2,1,0:T(8,128)(2,1)}, u32[]{:S(2)}, u32[]{:S(2)}) collective-permute-start(bf16[4,640,128]{2,1,0:T(8,128)(2,1)} %collective-permute-done.8.left_ref), channel_id=1, source_target_pairs={{0,8},{1,9},{2,10},{3,11},{4,12},{5,13},{6,14},{7,15},{8,16},{9,17... | collective-permute-start | bytes 1966088 | tf_op jit(solution)/shard_map/ppermute | solution.py:375
  102.7 2.7 %collective-permute-start.6 = (bf16[128,640]{1,0:T(8,128)(2,1)S(1)}, bf16[128,640]{1,0:T(8,128)(2,1)S(1)}, u32[]{:S(2)}, u32[]{:S(2)}) collective-permute-start(bf16[128,640]{1,0:T(8,128)(2,1)S(1)} %get-tuple-element.18.mid_ref), channel_id=1, source_target_pairs={{0,1},{1,0},{2,3},{3,2},{4,5},{5,4},{6,7},{7,6},{8,9},{9,8},{10,11... | collective-permute-start | bytes 491528 | tf_op jit(solution)/shard_map/ppermute | solution.py:382
  105.5 0.8 collective-permute-done.6.other_ref
  106.3 1.7 %shard_map.135 = (bf16[256,384]{1,0:T(8,128)(2,1)S(1)}, bf16[640,128]{1,0:T(8,128)(2,1)S(1)}, bf16[640,128]{1,0:T(8,128)(2,1)}) custom-call(f32[32,8,128]{2,1,0:T(8,128)S(1)} %all-to-all-done.1.every_ref, bf16[128,640]{1,0:T(8,128)(2,1)S(1)} %get-tuple-element.18.mid_ref, bf16[128,640]{1,0:T(8,128)(2,1)S(1)} %collective-permute-done.6.other_ref, ...), custom_call_target="tpu_custom_call" | custom-call | tf_op jit(solution)/shard_map/pallas_call | solution.py:291
  108.0 4.2 %shard_map.136.near_ref = f32[256,384]{1,0:T(8,128)S(1)} custom-call(s32[4]{0:T(128)S(1)} %pad_add_fusion.where_ref, bf16[256,384]{1,0:T(8,128)(2,1)S(1)} %get-tuple-element.19.q_ref, bf16[4,640,128]{2,1,0:T(8,128)(2,1)} %bitcast.12.own_ref, bf16[4,640,128]{2,1,0:T(8,128)(2,1)} %collective-permute-done.8.left_ref, ...), custom_call_target="tpu_custom_call" | custom-call | flops 2000000000 | bytes 3000000 | tf_op jit(solution)/shard_map/pallas_call | solution.py:291
  112.2 3.0 %collective-permute-done.7.right_ref = bf16[4,640,128]{2,1,0:T(8,128)(2,1)S(1)} collective-permute-done((bf16[4,640,128]{2,1,0:T(8,128)(2,1)}, bf16[4,640,128]{2,1,0:T(8,128)(2,1)S(1)}, u32[]{:S(2)}, u32[]{:S(2)}) %collective-permute-start.7) | collective-permute-done | bytes 655392 | tf_op jit(solution)/shard_map/ppermute | solution.py:355
  115.3 4.6 %collective-permute-done.9.far_ref = bf16[4,640,128]{2,1,0:T(8,128)(2,1)} collective-permute-done((bf16[4,640,128]{2,1,0:T(8,128)(2,1)}, bf16[4,640,128]{2,1,0:T(8,128)(2,1)}, u32[]{:S(2)}, u32[]{:S(2)}) %collective-permute-start.9) | collective-permute-done | bytes 655392 | tf_op jit(solution)/shard_map/ppermute | solution.py:375
  119.9 4.1 %shard_map.137 = (f32[128,384]{1,0:T(8,128)S(1)}, f32[128,384]{1,0:T(8,128)S(1)}) custom-call(bf16[256,384]{1,0:T(8,128)(2,1)S(1)} %get-tuple-element.19.q_ref, bf16[4,640,128]{2,1,0:T(8,128)(2,1)S(1)} %collective-permute-done.7.right_ref, bf16[4,640,128]{2,1,0:T(8,128)(2,1)} %collective-permute-done.9.far_ref, f32[256,384]{1,0:T(8,128)S(1)} %shard_map.136.near_ref), custom_call_target="tpu_custom_call" | custom-call | tf_op jit(solution)/shard_map/pallas_call | solution.py:291
  124.0 3.4 %collective-permute-start.10 = (f32[128,384]{1,0:T(8,128)S(1)}, f32[128,384]{1,0:T(8,128)S(1)}, u32[]{:S(2)}, u32[]{:S(2)}) collective-permute-start(f32[128,384]{1,0:T(8,128)S(1)} %get-tuple-element.24), channel_id=1, source_target_pairs={{0,1},{1,0},{2,3},{3,2},{4,5},{5,4},{6,7},{7,6},{8,9},{9,8},{10,11... | collective-permute-start | bytes 589832 | tf_op jit(solution)/shard_map/ppermute | solution.py:402
  127.4 1.0 collective-permute-done.10.other_ref
  128.5 1.3 %shard_map.138 = bf16[128,640]{1,0:T(8,128)(2,1)} custom-call(f32[128,384]{1,0:T(8,128)S(1)} %get-tuple-element.23.own_ref, f32[128,384]{1,0:T(8,128)S(1)} %collective-permute-done.10.other_ref, bf16[128,640]{1,0:T(8,128)(2,1)S(1)} %get-tuple-element.18.mid_ref, bf16[320,640]{1,0:T(8,128)(2,1)S(1)} %copy-done.4), custom_call_target="tpu_custom_call" | custom-call | tf_op jit(solution)/shard_map/pallas_call | solution.py:291
  (42 shorter events, 0.9 us)
Async XLA Ops:
  0.6 87.0 %copy-start = (f32[320,640]{1,0:T(8,128)S(1)}, f32[320,640]{1,0:T(8,128)}, u32[]{:S(2)}) copy-start(f32[320,640]{1,0:T(8,128)} %param.18) | copy-start | bytes 2457604
  0.6 28.8 %copy-start.1 = (bf16[128,640]{1,0:T(8,128)(2,1)S(1)}, bf16[128,640]{1,0:T(8,128)(2,1)}, u32[]{:S(2)}) copy-start(bf16[128,640]{1,0:T(8,128)(2,1)} %latent_ref.3) | copy-start | bytes 491524
  0.7 43.3 %copy-start.5 = (bf16[2,128,320]{1,2,0:T(8,128)(2,1)S(1)}, bf16[2,128,320]{1,2,0:T(8,128)(2,1)}, u32[]{:S(2)}) copy-start(bf16[2,128,320]{1,2,0:T(8,128)(2,1)} %param.23) | copy-start | bytes 491524
  0.7 59.5 %copy-start.7 = (f32[640]{0:T(1024)S(1)}, f32[640]{0:T(1024)}, u32[]{:S(2)}) copy-start(f32[640]{0:T(1024)} %param.14) | copy-start | bytes 7684
  0.7 59.5 %copy-start.8 = (f32[640]{0:T(1024)S(1)}, f32[640]{0:T(1024)}, u32[]{:S(2)}) copy-start(f32[640]{0:T(1024)} %param.15) | copy-start | bytes 7684
  23.0 37.4 %collective-permute-start.1 = (bf16[4,192,640]{2,1,0:T(8,128)(2,1)S(1)}, bf16[4,192,640]{2,1,0:T(8,128)(2,1)S(1)}, u32[]{:S(2)}, u32[]{:S(2)}) collective-permute-start(bf16[4,192,640]{2,1,0:T(8,128)(2,1)S(1)} %bitcast.19), channel_id=1, source_target_pairs={{0,8},{1,9},{2,10},{3,11},{4,12},{5,13},{6,14},{7,15},{8,16},{9,17... | collective-permute-start | bytes 2949128 | tf_op jit(solution)/shard_map/ppermute | solution.py:329
  25.8 38.5 %collective-permute-start.2 = (bf16[4,192,640]{2,1,0:T(8,128)(2,1)S(1)}, bf16[4,192,640]{2,1,0:T(8,128)(2,1)}, u32[]{:S(2)}, u32[]{:S(2)}) collective-permute-start(bf16[4,192,640]{2,1,0:T(8,128)(2,1)S(1)} %bitcast.20), channel_id=1, source_target_pairs={{0,24},{1,25},{2,26},{3,27},{4,28},{5,29},{6,30},{7,31},{8,0},{9,1... | collective-permute-start | bytes 2949128 | tf_op jit(solution)/shard_map/ppermute | solution.py:330
  29.5 40.0 %collective-permute-start = (bf16[128,640]{1,0:T(8,128)(2,1)S(1)}, bf16[128,640]{1,0:T(8,128)(2,1)S(1)}, u32[]{:S(2)}, u32[]{:S(2)}) collective-permute-start(bf16[128,640]{1,0:T(8,128)(2,1)S(1)} %copy-done.1), channel_id=1, source_target_pairs={{2,0},{4,2},{6,4},{8,6},{10,8},{12,10},{14,12},{16,14},{18,16},{20... | collective-permute-start | bytes 491528 | tf_op jit(solution)/shard_map/ppermute | solution.py:331
  34.1 40.7 %all-to-all-start = ((f32[32,8,128]{2,1,0:T(8,128)}), f32[32,8,128]{2,1,0:T(8,128)}, u32[]{:S(2)}, u32[]{:S(2)}) async-start(f32[32,8,128]{2,1,0:T(8,128)} %shard_map.131), calls=%async_computation | async-start | bytes 262144 | tf_op jit(solution)/shard_map/all_to_all | solution.py:63
  61.2 19.3 %collective-permute-start.3 = (bf16[2,192,640]{2,1,0:T(8,128)(2,1)}, bf16[2,192,640]{2,1,0:T(8,128)(2,1)}, u32[]{:S(2)}, u32[]{:S(2)}) collective-permute-start(bf16[2,192,640]{2,1,0:T(8,128)(2,1)} %slice.8), channel_id=1, source_target_pairs={{0,8},{1,9},{2,10},{3,11},{4,12},{5,13},{6,14},{7,15},{8,16},{9,17... | collective-permute-start | bytes 1474568 | tf_op jit(solution)/shard_map/ppermute | solution.py:340
  66.1 14.3 %collective-permute-start.4 = (bf16[2,192,640]{2,1,0:T(8,128)(2,1)}, bf16[2,192,640]{2,1,0:T(8,128)(2,1)}, u32[]{:S(2)}, u32[]{:S(2)}) collective-permute-start(bf16[2,192,640]{2,1,0:T(8,128)(2,1)} %slice.9), channel_id=1, source_target_pairs={{0,24},{1,25},{2,26},{3,27},{4,28},{5,29},{6,30},{7,31},{8,0},{9,1... | collective-permute-start | bytes 1474568 | tf_op jit(solution)/shard_map/ppermute | solution.py:341
  77.9 22.9 %collective-permute-start.8 = (bf16[4,640,128]{2,1,0:T(8,128)(2,1)}, bf16[4,640,128]{2,1,0:T(8,128)(2,1)}, u32[]{:S(2)}, u32[]{:S(2)}) collective-permute-start(bf16[4,640,128]{2,1,0:T(8,128)(2,1)} %bitcast.12.own_ref), channel_id=1, source_target_pairs={{0,8},{1,9},{2,10},{3,11},{4,12},{5,13},{6,14},{7,15},{8,16},{9,17... | collective-permute-start | bytes 1966088 | tf_op jit(solution)/shard_map/ppermute | solution.py:354
  80.4 7.7 %copy-start.6 = (f32[640]{0:T(1024)S(1)}, f32[640]{0:T(1024)}, u32[]{:S(2)}) copy-start(f32[640]{0:T(1024)} %param.17) | copy-start | bytes 7684
  80.5 8.3 %copy-start.2 = (bf16[128,640]{1,0:T(8,128)(2,1)S(1)}, bf16[128,640]{1,0:T(8,128)(2,1)}, u32[]{:S(2)}) copy-start(bf16[128,640]{1,0:T(8,128)(2,1)} %latent_ref.3) | copy-start | bytes 491524
  83.9 21.5 %copy-start.9 = (f32[640]{0:T(1024)S(1)}, f32[640]{0:T(1024)}, u32[]{:S(2)}) copy-start(f32[640]{0:T(1024)} %param.19) | copy-start | bytes 7684
  83.9 21.6 %copy-start.10 = (f32[640]{0:T(1024)S(1)}, f32[640]{0:T(1024)}, u32[]{:S(2)}) copy-start(f32[640]{0:T(1024)} %param.20) | copy-start | bytes 7684
  84.0 22.3 %copy-start.3 = (bf16[640,960]{0,1:T(8,128)(2,1)S(1)}, bf16[640,960]{0,1:T(8,128)(2,1)}, u32[]{:S(2)}) copy-start(bf16[640,960]{0,1:T(8,128)(2,1)} %param.21) | copy-start | bytes 3686404
  84.0 4.8 %collective-permute-start.5 = (f32[128,640]{1,0:T(8,128)S(1)}, f32[128,640]{1,0:T(8,128)S(1)}, u32[]{:S(2)}, u32[]{:S(2)}) collective-permute-start(f32[128,640]{1,0:T(8,128)S(1)} %get-tuple-element.15), channel_id=1, source_target_pairs={{0,1},{1,0},{2,3},{3,2},{4,5},{5,4},{6,7},{7,6},{8,9},{9,8},{10,11... | collective-permute-start | bytes 983048 | tf_op jit(solution)/shard_map/ppermute | solution.py:372
  90.4 15.9 %all-to-all-start.1 = ((f32[32,8,128]{2,1,0:T(8,128)}), f32[32,8,128]{2,1,0:T(8,128)S(1)}, u32[]{:S(2)}, u32[]{:S(2)}) async-start(f32[32,8,128]{2,1,0:T(8,128)} %get-tuple-element.17), calls=%async_computation.1 | async-start | bytes 262144 | tf_op jit(solution)/shard_map/all_to_all | solution.py:63
  96.2 19.0 %collective-permute-start.7 = (bf16[4,640,128]{2,1,0:T(8,128)(2,1)}, bf16[4,640,128]{2,1,0:T(8,128)(2,1)S(1)}, u32[]{:S(2)}, u32[]{:S(2)}) collective-permute-start(bf16[4,640,128]{2,1,0:T(8,128)(2,1)} %bitcast.12.own_ref), channel_id=1, source_target_pairs={{0,24},{1,25},{2,26},{3,27},{4,28},{5,29},{6,30},{7,31},{8,0},{9,1... | collective-permute-start | bytes 1966088 | tf_op jit(solution)/shard_map/ppermute | solution.py:355
  100.8 19.1 %collective-permute-start.9 = (bf16[4,640,128]{2,1,0:T(8,128)(2,1)}, bf16[4,640,128]{2,1,0:T(8,128)(2,1)}, u32[]{:S(2)}, u32[]{:S(2)}) collective-permute-start(bf16[4,640,128]{2,1,0:T(8,128)(2,1)} %collective-permute-done.8.left_ref), channel_id=1, source_target_pairs={{0,8},{1,9},{2,10},{3,11},{4,12},{5,13},{6,14},{7,15},{8,16},{9,17... | collective-permute-start | bytes 1966088 | tf_op jit(solution)/shard_map/ppermute | solution.py:375
  102.7 3.6 %collective-permute-start.6 = (bf16[128,640]{1,0:T(8,128)(2,1)S(1)}, bf16[128,640]{1,0:T(8,128)(2,1)S(1)}, u32[]{:S(2)}, u32[]{:S(2)}) collective-permute-start(bf16[128,640]{1,0:T(8,128)(2,1)S(1)} %get-tuple-element.18.mid_ref), channel_id=1, source_target_pairs={{0,1},{1,0},{2,3},{3,2},{4,5},{5,4},{6,7},{7,6},{8,9},{9,8},{10,11... | collective-permute-start | bytes 491528 | tf_op jit(solution)/shard_map/ppermute | solution.py:382
  112.2 16.3 %copy-start.4 = (bf16[320,640]{1,0:T(8,128)(2,1)S(1)}, bf16[320,640]{1,0:T(8,128)(2,1)}, u32[]{:S(2)}) copy-start(bf16[320,640]{1,0:T(8,128)(2,1)} %weight_ref.1) | copy-start | bytes 1228804
  124.0 4.5 %collective-permute-start.10 = (f32[128,384]{1,0:T(8,128)S(1)}, f32[128,384]{1,0:T(8,128)S(1)}, u32[]{:S(2)}, u32[]{:S(2)}) collective-permute-start(f32[128,384]{1,0:T(8,128)S(1)} %get-tuple-element.24), channel_id=1, source_target_pairs={{0,1},{1,0},{2,3},{3,2},{4,5},{5,4},{6,7},{7,6},{8,9},{9,8},{10,11... | collective-permute-start | bytes 589832 | tf_op jit(solution)/shard_map/ppermute | solution.py:402

commit v10 on v9

--- a/solution.py
+++ b/solution.py
@@ -242,20 +242,20 @@
     )
 
 
-def attend_near(where_ref, q_ref, own_ref, left_ref, fresh_ref, out_ref):
+def attend_near(where_ref, q_ref, own_ref, left_ref, right_ref, fresh_ref, out_ref):
     my_z = where_ref[3]
     count = q_ref.shape[0] // 2
     row = lax.broadcasted_iota(jnp.int32, (2 * count, 4 * count), 0)
     block = lax.broadcasted_iota(jnp.int32, (2 * count, 4 * count), 1) // count
     replaced = (row < count) & (block == my_z)
-    blocks = [[(ref, z) for z in range(4)] for ref in (own_ref, left_ref)]
+    blocks = [[(ref, z) for z in range(4)] for ref in (own_ref, left_ref, right_ref)]
     for tile, value in enumerate(attention(q_ref, blocks, replaced, fresh_ref, None)):
         out_ref[:, 128 * tile : 128 * (tile + 1)] = value
 
 
-def attend_far(q_ref, right_ref, far_ref, near_ref, out_ref, given_ref):
+def attend_far(q_ref, far_ref, near_ref, out_ref, given_ref):
     count = out_ref.shape[0]
-    blocks = [[(ref, z) for z in range(4)] for ref in (right_ref, far_ref)]
+    blocks = [[(far_ref, z) for z in range(4)]]
     for tile, value in enumerate(attention(q_ref, blocks, None, None, near_ref)):
         out_ref[:, 128 * tile : 128 * (tile + 1)] = value[:count]
         given_ref[:, 128 * tile : 128 * (tile + 1)] = value[count:]
@@ -350,7 +350,7 @@
         norm1_shift[None],
         scratch=[pltpu.VMEM((2 * tok_dev, 5760 + 128), bf16)],
     )
-    own_kv, _ = lax.optimization_barrier((own_kv, blocks))
+    own_kv, _ = lax.optimization_barrier((own_kv, pair))
     left_kv = lax.ppermute(own_kv, "space", RIGHT)
     right_kv = lax.ppermute(own_kv, "space", LEFT)
     step, _ = lax.optimization_barrier((timestep, blocks))
@@ -393,11 +393,12 @@
         query,
         own_kv,
         left_kv,
+        right_kv,
         fresh,
         cost=pl.CostEstimate(flops=2000000000, transcendentals=2 * 10**6, bytes_accessed=3 * 10**6),
     )
     mine, theirs = call(
-        attend_far, [((tok_dev, 384), f32)] * 2, 0, query, right_kv, far_kv, near
+        attend_far, [((tok_dev, 384), f32)] * 2, 0, query, far_kv, near
     )
     other = lax.ppermute(theirs, "space", SWAP)
     (result,) = call(finish, [((tok_dev, width), bf16)], 0, mine, other, mid, out_weight)

time: 131 us -> 127 us (0.969)
  waiting for transfers between devices: 10 us -> 8.32 us
    ppermute x1, waiting for transfers between devices: 3 us -> 0.01 us  [on_device(): right_kv = lax.ppermute(own_kv, 'space', LEFT)]
    all_to_all x2, waiting for transfers between devices: 0.01 us -> 2.57 us  [exchanged(): return lax.all_to_all(stats, 'space', 0, 0, tiled=True)]
    all_to_all x2, starting transfers between devices: 15.7 us -> 13.6 us  [exchanged(): return lax.all_to_all(stats, 'space', 0, 0, tiled=True)]
    ppermute x1, starting transfers between devices: 1.92 us -> 3.34 us  [on_device(): far_kv = lax.ppermute(left_kv, 'space', RIGHT)]
  transfers between devices with their start and end apart: 13 -> 13, of which waited for: 5 -> 4; matrix products, arithmetic and copies ran while one was open for 3% -> 3% of each run, Pallas kernels for 12% -> 13%
where the time goes in v10:
time: 127 us; the launch traced here: 126 us
  starting transfers between devices  48.4 us (38%)
  blocking collectives  42.7 us (34%)
  Pallas kernels  20.4 us (16%)
  waiting for transfers between devices  8.32 us (7%)
  local copies, waits for them, and re-layouts  3.82 us (3%)
  between operations  1.72 us (1%)
    all_gather x1, blocking collectives, on_device(): own_w = lax.all_gather(weight, 'space', axis=0, axis_index_groups=Z_GROUPS)  21.2 us
    pallas_call x8, Pallas kernels, call(): pl.pallas_call(kernel, out_shape=[jax.ShapeDtypeStruct(shape, dtype) for...  20.4 us
    all_gather x1, blocking collectives, on_device(): own_kv = lax.all_gather(stale, 'space', axis=0, axis_index_groups=Z_GROUPS)  16.2 us
    all_to_all x2, starting transfers between devices, exchanged(): return lax.all_to_all(stats, 'space', 0, 0, tiled=True)  13.6 us
    all_gather x1, blocking collectives, on_device(): lax.all_gather(jnp.stack([latent, outer]), 'space', axis=0, axis_index_gr...  5.26 us
    ppermute x1, starting transfers between devices, on_device(): right_kv = lax.ppermute(own_kv, 'space', LEFT)  4.58 us
    ppermute x1, waiting for transfers between devices, on_device(): far_kv = lax.ppermute(left_kv, 'space', RIGHT)  3.9 us
    ppermute x1, starting transfers between devices, on_device(): right_w = lax.ppermute(own_w, 'space', LEFT)  3.64 us
  transfers between devices with their start and end apart: 13, of which 4 were waited for; matrix products, arithmetic and copies ran while one was open for 3% of the time, Pallas kernels for 13%

profile of v10, /device:TPU:1, one launch (start us, length us, event | category | flops | bytes accessed | tf_op | source)
XLA Modules:
  0.0 126.2 jit_solution(9309951209897053157)
XLA Ops:
  0.7 1.1 pad.4
  1.7 21.2 %all-gather.1 = bf16[768,640]{1,0:T(8,128)(2,1)S(1)} all-gather(bf16[192,640]{1,0:T(8,128)(2,1)S(1)} %pad.4), channel_id=3, replica_groups={{0,2,4,6},{1,3,5,7},{8,10,12,14},{9,11,13,15},{16,18,20,22},{17,19,21,2..., dimensions={0}, use_global_device_ids=true | all-gather | bytes 1228800 | tf_op jit(solution)/shard_map/all_gather | solution.py:328
  23.0 2.8 %collective-permute-start.1 = (bf16[4,192,640]{2,1,0:T(8,128)(2,1)S(1)}, bf16[4,192,640]{2,1,0:T(8,128)(2,1)S(1)}, u32[]{:S(2)}, u32[]{:S(2)}) collective-permute-start(bf16[4,192,640]{2,1,0:T(8,128)(2,1)S(1)} %bitcast.19), channel_id=1, source_target_pairs={{0,8},{1,9},{2,10},{3,11},{4,12},{5,13},{6,14},{7,15},{8,16},{9,17... | collective-permute-start | bytes 2949128 | tf_op jit(solution)/shard_map/ppermute | solution.py:329
  25.8 3.6 %collective-permute-start.2 = (bf16[4,192,640]{2,1,0:T(8,128)(2,1)S(1)}, bf16[4,192,640]{2,1,0:T(8,128)(2,1)}, u32[]{:S(2)}, u32[]{:S(2)}) collective-permute-start(bf16[4,192,640]{2,1,0:T(8,128)(2,1)S(1)} %bitcast.20), channel_id=1, source_target_pairs={{0,24},{1,25},{2,26},{3,27},{4,28},{5,29},{6,30},{7,31},{8,0},{9,1... | collective-permute-start | bytes 2949128 | tf_op jit(solution)/shard_map/ppermute | solution.py:330
  29.5 3.0 %collective-permute-start = (bf16[128,640]{1,0:T(8,128)(2,1)S(1)}, bf16[128,640]{1,0:T(8,128)(2,1)S(1)}, u32[]{:S(2)}, u32[]{:S(2)}) collective-permute-start(bf16[128,640]{1,0:T(8,128)(2,1)S(1)} %copy-done.1), channel_id=1, source_target_pairs={{2,0},{4,2},{6,4},{8,6},{10,8},{12,10},{14,12},{16,14},{18,16},{20... | collective-permute-start | bytes 491528 | tf_op jit(solution)/shard_map/ppermute | solution.py:331
  32.5 1.6 %shard_map.131 = f32[32,8,128]{2,1,0:T(8,128)} custom-call(bf16[128,640]{1,0:T(8,128)(2,1)S(1)} %copy-done.1), custom_call_target="tpu_custom_call" | custom-call | tf_op jit(solution)/shard_map/pallas_call | solution.py:291
  34.1 9.8 %all-to-all-start = ((f32[32,8,128]{2,1,0:T(8,128)}), f32[32,8,128]{2,1,0:T(8,128)}, u32[]{:S(2)}, u32[]{:S(2)}) async-start(f32[32,8,128]{2,1,0:T(8,128)} %shard_map.131), calls=%async_computation | async-start | bytes 262144 | tf_op jit(solution)/shard_map/all_to_all | solution.py:63
  44.0 16.2 %all-gather.2 = bf16[2560,128]{1,0:T(8,128)(2,1)} all-gather(bf16[640,128]{1,0:T(8,128)(2,1)S(1)} %bitcast.26), channel_id=4, replica_groups={{0,2,4,6},{1,3,5,7},{8,10,12,14},{9,11,13,15},{16,18,20,22},{17,19,21,2..., dimensions={0}, use_global_device_ids=true | all-gather | bytes 819200 | tf_op jit(solution)/shard_map/all_gather | solution.py:339
  60.2 0.8 slice.8
  61.0 3.2 %collective-permute-start.3 = (bf16[2,192,640]{2,1,0:T(8,128)(2,1)}, bf16[2,192,640]{2,1,0:T(8,128)(2,1)}, u32[]{:S(2)}, u32[]{:S(2)}) collective-permute-start(bf16[2,192,640]{2,1,0:T(8,128)(2,1)} %slice.8), channel_id=1, source_target_pairs={{0,8},{1,9},{2,10},{3,11},{4,12},{5,13},{6,14},{7,15},{8,16},{9,17... | collective-permute-start | bytes 1474568 | tf_op jit(solution)/shard_map/ppermute | solution.py:340
  64.3 1.8 %slice.9 = bf16[2,192,640]{2,1,0:T(8,128)(2,1)} slice(bf16[4,192,640]{2,1,0:T(8,128)(2,1)} %collective-permute-done.2.right_ref), slice={[2:4], [0:192], [0:640]} | slice | bytes 983040 | tf_op jit(solution)/shard_map/slice | solution.py:341
  66.1 3.4 %collective-permute-start.4 = (bf16[2,192,640]{2,1,0:T(8,128)(2,1)}, bf16[2,192,640]{2,1,0:T(8,128)(2,1)}, u32[]{:S(2)}, u32[]{:S(2)}) collective-permute-start(bf16[2,192,640]{2,1,0:T(8,128)(2,1)} %slice.9), channel_id=1, source_target_pairs={{0,24},{1,25},{2,26},{3,27},{4,28},{5,29},{6,30},{7,31},{8,0},{9,1... | collective-permute-start | bytes 1474568 | tf_op jit(solution)/shard_map/ppermute | solution.py:341
  69.6 5.3 %all-gather = bf16[4,128,640]{2,1,0:T(8,128)(2,1)S(1)} all-gather(bf16[2,128,640]{2,1,0:T(8,128)(2,1)S(1)} %pad_maximum_fusion), channel_id=2, replica_groups={{0,1},{2,3},{4,5},{6,7},{8,9},{10,11},{12,13},{14,15},{16,17},{18,19},{..., dimensions={0}, use_global_device_ids=true | all-gather | bytes 983040 | tf_op jit(solution)/shard_map/all_gather | solution.py:334
  74.8 1.9 %collective-permute-start.7 = (bf16[4,640,128]{2,1,0:T(8,128)(2,1)}, bf16[4,640,128]{2,1,0:T(8,128)(2,1)}, u32[]{:S(2)}, u32[]{:S(2)}) collective-permute-start(bf16[4,640,128]{2,1,0:T(8,128)(2,1)} %bitcast.12.own_ref), channel_id=1, source_target_pairs={{0,8},{1,9},{2,10},{3,11},{4,12},{5,13},{6,14},{7,15},{8,16},{9,17... | collective-permute-start | bytes 1966088 | tf_op jit(solution)/shard_map/ppermute | solution.py:354
  77.6 3.0 %shard_map.132.blocks_ref = bf16[4,256,768]{2,1,0:T(8,128)(2,1)S(1)} custom-call(s32[4]{0:T(128)S(1)} %pad_add_fusion.where_ref, f32[32,8,128]{2,1,0:T(8,128)} %all-to-all-done.every_ref, bf16[2,2,128,640]{3,2,1,0:T(8,128)(2,1)S(1)} %bitcast.22, f32[1,640]{1,0:T(1,128)S(1)} %broadcast_in_dim.14.gain_ref, f32[1,640]{1,0:T(1,128)S(1)} %broadcast_in_dim.15.shift_ref), custom_call_target="tpu_custom_call" | custom-call | tf_op jit(solution)/shard_map/pallas_call | solution.py:291
  80.7 3.4 %shard_map.133 = (f32[128,640]{1,0:T(8,128)S(1)}, f32[128,640]{1,0:T(8,128)S(1)}) custom-call(s32[4]{0:T(128)S(1)} %pad_add_fusion.where_ref, bf16[4,256,768]{2,1,0:T(8,128)(2,1)S(1)} %shard_map.132.blocks_ref, bf16[4,192,640]{2,1,0:T(8,128)(2,1)S(1)} %bitcast.21, bf16[4,192,640]{2,1,0:T(8,128)(2,1)S(1)} %collective-permute-done.1.left_ref, ...), custom_call_target="tpu_custom_call" | custom-call | tf_op jit(solution)/shard_map/pallas_call | solution.py:291
  84.1 3.4 %collective-permute-start.5 = (f32[128,640]{1,0:T(8,128)S(1)}, f32[128,640]{1,0:T(8,128)S(1)}, u32[]{:S(2)}, u32[]{:S(2)}) collective-permute-start(f32[128,640]{1,0:T(8,128)S(1)} %get-tuple-element.15), channel_id=1, source_target_pairs={{0,1},{1,0},{2,3},{3,2},{4,5},{5,4},{6,7},{7,6},{8,9},{9,8},{10,11... | collective-permute-start | bytes 983048 | tf_op jit(solution)/shard_map/ppermute | solution.py:372
  87.5 4.6 %collective-permute-start.9 = (bf16[4,640,128]{2,1,0:T(8,128)(2,1)}, bf16[4,640,128]{2,1,0:T(8,128)(2,1)}, u32[]{:S(2)}, u32[]{:S(2)}) collective-permute-start(bf16[4,640,128]{2,1,0:T(8,128)(2,1)} %bitcast.12.own_ref), channel_id=1, source_target_pairs={{0,24},{1,25},{2,26},{3,27},{4,28},{5,29},{6,30},{7,31},{8,0},{9,1... | collective-permute-start | bytes 1966088 | tf_op jit(solution)/shard_map/ppermute | solution.py:355
  92.2 0.5 convolution_reduce_fusion
  92.8 1.7 %shard_map.134 = (bf16[128,640]{1,0:T(8,128)(2,1)S(1)}, f32[32,8,128]{2,1,0:T(8,128)}) custom-call(f32[128,640]{1,0:T(8,128)S(1)} %get-tuple-element.14.kept_ref, f32[128,640]{1,0:T(8,128)S(1)} %collective-permute-done.5.other_ref, bf16[128,640]{1,0:T(8,128)(2,1)S(1)} %copy-done.2, f32[1,640]{1,0:T(1,128)S(1)} %add.19.bias_ref), custom_call_target="tpu_custom_call" | custom-call | tf_op jit(solution)/shard_map/pallas_call | solution.py:291
  94.5 3.8 %all-to-all-start.1 = ((f32[32,8,128]{2,1,0:T(8,128)}), f32[32,8,128]{2,1,0:T(8,128)S(1)}, u32[]{:S(2)}, u32[]{:S(2)}) async-start(f32[32,8,128]{2,1,0:T(8,128)} %get-tuple-element.17), calls=%async_computation.1 | async-start | bytes 262144 | tf_op jit(solution)/shard_map/all_to_all | solution.py:63
  98.3 3.3 %collective-permute-start.8 = (bf16[4,640,128]{2,1,0:T(8,128)(2,1)}, bf16[4,640,128]{2,1,0:T(8,128)(2,1)S(1)}, u32[]{:S(2)}, u32[]{:S(2)}) collective-permute-start(bf16[4,640,128]{2,1,0:T(8,128)(2,1)} %collective-permute-done.7.left_ref), channel_id=1, source_target_pairs={{0,8},{1,9},{2,10},{3,11},{4,12},{5,13},{6,14},{7,15},{8,16},{9,17... | collective-permute-start | bytes 1966088 | tf_op jit(solution)/shard_map/ppermute | solution.py:375
  101.6 2.7 %collective-permute-start.6 = (bf16[128,640]{1,0:T(8,128)(2,1)S(1)}, bf16[128,640]{1,0:T(8,128)(2,1)S(1)}, u32[]{:S(2)}, u32[]{:S(2)}) collective-permute-start(bf16[128,640]{1,0:T(8,128)(2,1)S(1)} %get-tuple-element.18.mid_ref), channel_id=1, source_target_pairs={{0,1},{1,0},{2,3},{3,2},{4,5},{5,4},{6,7},{7,6},{8,9},{9,8},{10,11... | collective-permute-start | bytes 491528 | tf_op jit(solution)/shard_map/ppermute | solution.py:382
  104.4 0.8 collective-permute-done.6.other_ref
  105.2 2.6 %all-to-all-done.1.every_ref = f32[32,8,128]{2,1,0:T(8,128)S(1)} async-done(((f32[32,8,128]{2,1,0:T(8,128)}), f32[32,8,128]{2,1,0:T(8,128)S(1)}, u32[]{:S(2)}, u32[]{:S(2)}) %all-to-all-start.1) | async-done | bytes 131104 | tf_op jit(solution)/shard_map/all_to_all | solution.py:63
  107.8 1.7 %shard_map.135 = (bf16[256,384]{1,0:T(8,128)(2,1)S(1)}, bf16[640,128]{1,0:T(8,128)(2,1)S(1)}, bf16[640,128]{1,0:T(8,128)(2,1)}) custom-call(f32[32,8,128]{2,1,0:T(8,128)S(1)} %all-to-all-done.1.every_ref, bf16[128,640]{1,0:T(8,128)(2,1)S(1)} %get-tuple-element.18.mid_ref, bf16[128,640]{1,0:T(8,128)(2,1)S(1)} %collective-permute-done.6.other_ref, ...), custom_call_target="tpu_custom_call" | custom-call | tf_op jit(solution)/shard_map/pallas_call | solution.py:291
  109.5 5.3 %shard_map.136.near_ref = f32[256,384]{1,0:T(8,128)S(1)} custom-call(s32[4]{0:T(128)S(1)} %pad_add_fusion.where_ref, bf16[256,384]{1,0:T(8,128)(2,1)S(1)} %get-tuple-element.19.q_ref, bf16[4,640,128]{2,1,0:T(8,128)(2,1)} %bitcast.12.own_ref, bf16[4,640,128]{2,1,0:T(8,128)(2,1)} %collective-permute-done.7.left_ref, ...), custom_call_target="tpu_custom_call" | custom-call | flops 2000000000 | bytes 3000000 | tf_op jit(solution)/shard_map/pallas_call | solution.py:291
  114.8 3.9 %collective-permute-done.8.far_ref = bf16[4,640,128]{2,1,0:T(8,128)(2,1)S(1)} collective-permute-done((bf16[4,640,128]{2,1,0:T(8,128)(2,1)}, bf16[4,640,128]{2,1,0:T(8,128)(2,1)S(1)}, u32[]{:S(2)}, u32[]{:S(2)}) %collective-permute-start.8) | collective-permute-done | bytes 655392 | tf_op jit(solution)/shard_map/ppermute | solution.py:375
  118.7 2.3 %shard_map.137 = (f32[128,384]{1,0:T(8,128)S(1)}, f32[128,384]{1,0:T(8,128)S(1)}) custom-call(bf16[256,384]{1,0:T(8,128)(2,1)S(1)} %get-tuple-element.19.q_ref, bf16[4,640,128]{2,1,0:T(8,128)(2,1)S(1)} %collective-permute-done.8.far_ref, f32[256,384]{1,0:T(8,128)S(1)} %shard_map.136.near_ref), custom_call_target="tpu_custom_call" | custom-call | tf_op jit(solution)/shard_map/pallas_call | solution.py:291
  121.0 2.8 %collective-permute-start.10 = (f32[128,384]{1,0:T(8,128)S(1)}, f32[128,384]{1,0:T(8,128)S(1)}, u32[]{:S(2)}, u32[]{:S(2)}) collective-permute-start(f32[128,384]{1,0:T(8,128)S(1)} %get-tuple-element.24), channel_id=1, source_target_pairs={{0,1},{1,0},{2,3},{3,2},{4,5},{5,4},{6,7},{7,6},{8,9},{9,8},{10,11... | collective-permute-start | bytes 589832 | tf_op jit(solution)/shard_map/ppermute | solution.py:403
  123.8 1.0 collective-permute-done.10.other_ref
  124.9 1.3 %shard_map.138 = bf16[128,640]{1,0:T(8,128)(2,1)} custom-call(f32[128,384]{1,0:T(8,128)S(1)} %get-tuple-element.23.own_ref, f32[128,384]{1,0:T(8,128)S(1)} %collective-permute-done.10.other_ref, bf16[128,640]{1,0:T(8,128)(2,1)S(1)} %get-tuple-element.18.mid_ref, bf16[320,640]{1,0:T(8,128)(2,1)S(1)} %copy-done.4), custom_call_target="tpu_custom_call" | custom-call | tf_op jit(solution)/shard_map/pallas_call | solution.py:291
  (42 shorter events, 0.4 us)
Async XLA Ops:
  0.6 91.6 %copy-start = (f32[320,640]{1,0:T(8,128)S(1)}, f32[320,640]{1,0:T(8,128)}, u32[]{:S(2)}) copy-start(f32[320,640]{1,0:T(8,128)} %param.18) | copy-start | bytes 2457604
  0.6 28.8 %copy-start.1 = (bf16[128,640]{1,0:T(8,128)(2,1)S(1)}, bf16[128,640]{1,0:T(8,128)(2,1)}, u32[]{:S(2)}) copy-start(bf16[128,640]{1,0:T(8,128)(2,1)} %latent_ref.3) | copy-start | bytes 491524
  0.7 43.3 %copy-start.5 = (bf16[2,128,320]{1,2,0:T(8,128)(2,1)S(1)}, bf16[2,128,320]{1,2,0:T(8,128)(2,1)}, u32[]{:S(2)}) copy-start(bf16[2,128,320]{1,2,0:T(8,128)(2,1)} %param.23) | copy-start | bytes 491524
  23.0 37.2 %collective-permute-start.1 = (bf16[4,192,640]{2,1,0:T(8,128)(2,1)S(1)}, bf16[4,192,640]{2,1,0:T(8,128)(2,1)S(1)}, u32[]{:S(2)}, u32[]{:S(2)}) collective-permute-start(bf16[4,192,640]{2,1,0:T(8,128)(2,1)S(1)} %bitcast.19), channel_id=1, source_target_pairs={{0,8},{1,9},{2,10},{3,11},{4,12},{5,13},{6,14},{7,15},{8,16},{9,17... | collective-permute-start | bytes 2949128 | tf_op jit(solution)/shard_map/ppermute | solution.py:329
  25.8 38.5 %collective-permute-start.2 = (bf16[4,192,640]{2,1,0:T(8,128)(2,1)S(1)}, bf16[4,192,640]{2,1,0:T(8,128)(2,1)}, u32[]{:S(2)}, u32[]{:S(2)}) collective-permute-start(bf16[4,192,640]{2,1,0:T(8,128)(2,1)S(1)} %bitcast.20), channel_id=1, source_target_pairs={{0,24},{1,25},{2,26},{3,27},{4,28},{5,29},{6,30},{7,31},{8,0},{9,1... | collective-permute-start | bytes 2949128 | tf_op jit(solution)/shard_map/ppermute | solution.py:330
  29.5 40.0 %collective-permute-start = (bf16[128,640]{1,0:T(8,128)(2,1)S(1)}, bf16[128,640]{1,0:T(8,128)(2,1)S(1)}, u32[]{:S(2)}, u32[]{:S(2)}) collective-permute-start(bf16[128,640]{1,0:T(8,128)(2,1)S(1)} %copy-done.1), channel_id=1, source_target_pairs={{2,0},{4,2},{6,4},{8,6},{10,8},{12,10},{14,12},{16,14},{18,16},{20... | collective-permute-start | bytes 491528 | tf_op jit(solution)/shard_map/ppermute | solution.py:331
  34.1 43.5 %all-to-all-start = ((f32[32,8,128]{2,1,0:T(8,128)}), f32[32,8,128]{2,1,0:T(8,128)}, u32[]{:S(2)}, u32[]{:S(2)}) async-start(f32[32,8,128]{2,1,0:T(8,128)} %shard_map.131), calls=%async_computation | async-start | bytes 262144 | tf_op jit(solution)/shard_map/all_to_all | solution.py:63
  61.0 15.8 %copy-start.7 = (f32[640]{0:T(1024)S(1)}, f32[640]{0:T(1024)}, u32[]{:S(2)}) copy-start(f32[640]{0:T(1024)} %param.14) | copy-start | bytes 7684
  61.0 15.8 %copy-start.8 = (f32[640]{0:T(1024)S(1)}, f32[640]{0:T(1024)}, u32[]{:S(2)}) copy-start(f32[640]{0:T(1024)} %param.15) | copy-start | bytes 7684
  61.0 19.6 %collective-permute-start.3 = (bf16[2,192,640]{2,1,0:T(8,128)(2,1)}, bf16[2,192,640]{2,1,0:T(8,128)(2,1)}, u32[]{:S(2)}, u32[]{:S(2)}) collective-permute-start(bf16[2,192,640]{2,1,0:T(8,128)(2,1)} %slice.8), channel_id=1, source_target_pairs={{0,8},{1,9},{2,10},{3,11},{4,12},{5,13},{6,14},{7,15},{8,16},{9,17... | collective-permute-start | bytes 1474568 | tf_op jit(solution)/shard_map/ppermute | solution.py:340
  66.1 14.5 %collective-permute-start.4 = (bf16[2,192,640]{2,1,0:T(8,128)(2,1)}, bf16[2,192,640]{2,1,0:T(8,128)(2,1)}, u32[]{:S(2)}, u32[]{:S(2)}) collective-permute-start(bf16[2,192,640]{2,1,0:T(8,128)(2,1)} %slice.9), channel_id=1, source_target_pairs={{0,24},{1,25},{2,26},{3,27},{4,28},{5,29},{6,30},{7,31},{8,0},{9,1... | collective-permute-start | bytes 1474568 | tf_op jit(solution)/shard_map/ppermute | solution.py:341
  74.8 23.5 %collective-permute-start.7 = (bf16[4,640,128]{2,1,0:T(8,128)(2,1)}, bf16[4,640,128]{2,1,0:T(8,128)(2,1)}, u32[]{:S(2)}, u32[]{:S(2)}) collective-permute-start(bf16[4,640,128]{2,1,0:T(8,128)(2,1)} %bitcast.12.own_ref), channel_id=1, source_target_pairs={{0,8},{1,9},{2,10},{3,11},{4,12},{5,13},{6,14},{7,15},{8,16},{9,17... | collective-permute-start | bytes 1966088 | tf_op jit(solution)/shard_map/ppermute | solution.py:354
  80.6 12.1 %copy-start.6 = (f32[640]{0:T(1024)S(1)}, f32[640]{0:T(1024)}, u32[]{:S(2)}) copy-start(f32[640]{0:T(1024)} %param.17) | copy-start | bytes 7684
  80.6 12.2 %copy-start.2 = (bf16[128,640]{1,0:T(8,128)(2,1)S(1)}, bf16[128,640]{1,0:T(8,128)(2,1)}, u32[]{:S(2)}) copy-start(bf16[128,640]{1,0:T(8,128)(2,1)} %latent_ref.3) | copy-start | bytes 491524
  84.1 20.3 %copy-start.9 = (f32[640]{0:T(1024)S(1)}, f32[640]{0:T(1024)}, u32[]{:S(2)}) copy-start(f32[640]{0:T(1024)} %param.19) | copy-start | bytes 7684
  84.1 20.3 %copy-start.10 = (f32[640]{0:T(1024)S(1)}, f32[640]{0:T(1024)}, u32[]{:S(2)}) copy-start(f32[640]{0:T(1024)} %param.20) | copy-start | bytes 7684
  84.1 23.7 %copy-start.3 = (bf16[640,960]{0,1:T(8,128)(2,1)S(1)}, bf16[640,960]{0,1:T(8,128)(2,1)}, u32[]{:S(2)}) copy-start(bf16[640,960]{0,1:T(8,128)(2,1)} %param.21) | copy-start | bytes 3686404
  84.1 8.6 %collective-permute-start.5 = (f32[128,640]{1,0:T(8,128)S(1)}, f32[128,640]{1,0:T(8,128)S(1)}, u32[]{:S(2)}, u32[]{:S(2)}) collective-permute-start(f32[128,640]{1,0:T(8,128)S(1)} %get-tuple-element.15), channel_id=1, source_target_pairs={{0,1},{1,0},{2,3},{3,2},{4,5},{5,4},{6,7},{7,6},{8,9},{9,8},{10,11... | collective-permute-start | bytes 983048 | tf_op jit(solution)/shard_map/ppermute | solution.py:372
  87.5 21.9 %collective-permute-start.9 = (bf16[4,640,128]{2,1,0:T(8,128)(2,1)}, bf16[4,640,128]{2,1,0:T(8,128)(2,1)}, u32[]{:S(2)}, u32[]{:S(2)}) collective-permute-start(bf16[4,640,128]{2,1,0:T(8,128)(2,1)} %bitcast.12.own_ref), channel_id=1, source_target_pairs={{0,24},{1,25},{2,26},{3,27},{4,28},{5,29},{6,30},{7,31},{8,0},{9,1... | collective-permute-start | bytes 1966088 | tf_op jit(solution)/shard_map/ppermute | solution.py:355
  94.5 13.3 %all-to-all-start.1 = ((f32[32,8,128]{2,1,0:T(8,128)}), f32[32,8,128]{2,1,0:T(8,128)S(1)}, u32[]{:S(2)}, u32[]{:S(2)}) async-start(f32[32,8,128]{2,1,0:T(8,128)} %get-tuple-element.17), calls=%async_computation.1 | async-start | bytes 262144 | tf_op jit(solution)/shard_map/all_to_all | solution.py:63
  98.3 20.4 %collective-permute-start.8 = (bf16[4,640,128]{2,1,0:T(8,128)(2,1)}, bf16[4,640,128]{2,1,0:T(8,128)(2,1)S(1)}, u32[]{:S(2)}, u32[]{:S(2)}) collective-permute-start(bf16[4,640,128]{2,1,0:T(8,128)(2,1)} %collective-permute-done.7.left_ref), channel_id=1, source_target_pairs={{0,8},{1,9},{2,10},{3,11},{4,12},{5,13},{6,14},{7,15},{8,16},{9,17... | collective-permute-start | bytes 1966088 | tf_op jit(solution)/shard_map/ppermute | solution.py:375
  101.6 3.6 %collective-permute-start.6 = (bf16[128,640]{1,0:T(8,128)(2,1)S(1)}, bf16[128,640]{1,0:T(8,128)(2,1)S(1)}, u32[]{:S(2)}, u32[]{:S(2)}) collective-permute-start(bf16[128,640]{1,0:T(8,128)(2,1)S(1)} %get-tuple-element.18.mid_ref), channel_id=1, source_target_pairs={{0,1},{1,0},{2,3},{3,2},{4,5},{5,4},{6,7},{7,6},{8,9},{9,8},{10,11... | collective-permute-start | bytes 491528 | tf_op jit(solution)/shard_map/ppermute | solution.py:382
  109.4 15.4 %copy-start.4 = (bf16[320,640]{1,0:T(8,128)(2,1)S(1)}, bf16[320,640]{1,0:T(8,128)(2,1)}, u32[]{:S(2)}) copy-start(bf16[320,640]{1,0:T(8,128)(2,1)} %weight_ref.1) | copy-start | bytes 1228804
  121.0 3.8 %collective-permute-start.10 = (f32[128,384]{1,0:T(8,128)S(1)}, f32[128,384]{1,0:T(8,128)S(1)}, u32[]{:S(2)}, u32[]{:S(2)}) collective-permute-start(f32[128,384]{1,0:T(8,128)S(1)} %get-tuple-element.24), channel_id=1, source_target_pairs={{0,1},{1,0},{2,3},{3,2},{4,5},{5,4},{6,7},{7,6},{8,9},{9,8},{10,11... | collective-permute-start | bytes 589832 | tf_op jit(solution)/shard_map/ppermute | solution.py:403

commit v11 on v10

--- a/solution.py
+++ b/solution.py
@@ -253,9 +253,9 @@
         out_ref[:, 128 * tile : 128 * (tile + 1)] = value
 
 
-def attend_far(q_ref, far_ref, near_ref, out_ref, given_ref):
+def attend_far(q_ref, low_ref, high_ref, near_ref, out_ref, given_ref):
     count = out_ref.shape[0]
-    blocks = [[(far_ref, z) for z in range(4)]]
+    blocks = [[(low_ref, 0), (low_ref, 1), (high_ref, 0), (high_ref, 1)]]
     for tile, value in enumerate(attention(q_ref, blocks, None, None, near_ref)):
         out_ref[:, 128 * tile : 128 * (tile + 1)] = value[:count]
         given_ref[:, 128 * tile : 128 * (tile + 1)] = value[count:]
@@ -337,6 +337,7 @@
     stale = stale_kv.transpose(0, 2, 1).reshape(2 * feats, tok_dev)
     stale, _ = lax.optimization_barrier((stale, own_w))
     own_kv = lax.all_gather(stale, "space", axis=0, axis_index_groups=Z_GROUPS)
+    left_w, right_w, own_kv = lax.optimization_barrier((left_w, right_w, own_kv))
     low_w = lax.ppermute(left_w[:2], "space", RIGHT)
     high_w = lax.ppermute(right_w[2:], "space", LEFT)
     (blocks,) = call(
@@ -372,7 +373,8 @@
     other = lax.ppermute(given, "space", SWAP)
     mid, stats2 = call(middle, [((tok_dev, width), bf16), table], 0, kept, other, latent, bias)
     every2 = exchanged(stats2)
-    far_kv = lax.ppermute(left_kv, "space", RIGHT)
+    low_kv = lax.ppermute(left_kv[:2], "space", RIGHT)
+    high_kv = lax.ppermute(right_kv[2:], "space", LEFT)
     query, fresh, kept_kv = call(
         project,
         [((2 * tok_dev, 384), bf16)] + [((2 * feats, tok_dev), bf16)] * 2,
@@ -395,10 +397,10 @@
         left_kv,
         right_kv,
         fresh,
-        cost=pl.CostEstimate(flops=2000000000, transcendentals=2 * 10**6, bytes_accessed=3 * 10**6),
+        cost=pl.CostEstimate(flops=1000000000, transcendentals=2 * 10**6, bytes_accessed=3 * 10**6),
     )
     mine, theirs = call(
-        attend_far, [((tok_dev, 384), f32)] * 2, 0, query, far_kv, near
+        attend_far, [((tok_dev, 384), f32)] * 2, 0, query, low_kv, high_kv, near
     )
     other = lax.ppermute(theirs, "space", SWAP)
     (result,) = call(finish, [((tok_dev, width), bf16)], 0, mine, other, mid, out_weight)

time: 127 us -> 128 us (level)
  waiting for transfers between devices: 8.32 us -> 2.37 us
  local copies, waits for them, and re-layouts: 3.82 us -> 7.25 us
  starting transfers between devices: 48.4 us -> 51.6 us
    ppermute x1 -> x2, waiting for transfers between devices: 3.9 us -> 0.01 us  [the longest x1 0.01 us: on_device(): high_kv = lax.ppermute(right_kv[2:], 'space', LEFT)]
    slice x0 -> x2, local copies, waits for them, and re-layouts: none -> 3.43 us  [the longest x1 1.72 us: on_device(): high_kv = lax.ppermute(right_kv[2:], 'space', LEFT)]
    ppermute x1 -> x2, starting transfers between devices: 3.34 us -> 6.44 us  [the longest x1 4.54 us: on_device(): high_kv = lax.ppermute(right_kv[2:], 'space', LEFT)]
    all_to_all x2, waiting for transfers between devices: 2.57 us -> 0.01 us  [exchanged(): return lax.all_to_all(stats, 'space', 0, 0, tiled=True)]
  transfers between devices with their start and end apart: 13 -> 14, of which waited for: 4 -> 3; matrix products, arithmetic and copies ran while one was open for 3% -> 5% of each run, Pallas kernels for 13% -> 13%
where the time goes in v11:
time: 128 us; the launch traced here: 127 us
  starting transfers between devices  51.6 us (40%)
  blocking collectives  42.7 us (33%)
  Pallas kernels  20.4 us (16%)
  local copies, waits for them, and re-layouts  7.25 us (6%)
  waiting for transfers between devices  2.37 us (2%)
  between operations  1.7 us (1%)
    all_gather x1, blocking collectives, on_device(): own_w = lax.all_gather(weight, 'space', axis=0, axis_index_groups=Z_GROUPS)  21.2 us
    pallas_call x8, Pallas kernels, call(): pl.pallas_call(kernel, out_shape=[jax.ShapeDtypeStruct(shape, dtype) for...  20.4 us
    all_gather x1, blocking collectives, on_device(): own_kv = lax.all_gather(stale, 'space', axis=0, axis_index_groups=Z_GROUPS)  16.2 us
    all_to_all x2, starting transfers between devices, exchanged(): return lax.all_to_all(stats, 'space', 0, 0, tiled=True)  14.3 us
    all_gather x1, blocking collectives, on_device(): lax.all_gather(jnp.stack([latent, outer]), 'space', axis=0, axis_index_gr...  5.26 us
    ppermute x1, starting transfers between devices, on_device(): right_kv = lax.ppermute(own_kv, 'space', LEFT)  4.57 us
    ppermute x1, starting transfers between devices, on_device(): high_kv = lax.ppermute(right_kv[2:], 'space', LEFT)  4.54 us
    ppermute x1, starting transfers between devices, on_device(): right_w = lax.ppermute(own_w, 'space', LEFT)  3.64 us
  transfers between devices with their start and end apart: 14, of which 3 were waited for; matrix products, arithmetic and copies ran while one was open for 5% of the time, Pallas kernels for 13%

profile of v11, /device:TPU:1, one launch (start us, length us, event | category | flops | bytes accessed | tf_op | source)
XLA Modules:
  0.0 126.9 jit_solution(6154502623367787855)
XLA Ops:
  0.7 1.1 pad.4
  1.7 21.2 %all-gather.1 = bf16[768,640]{1,0:T(8,128)(2,1)S(1)} all-gather(bf16[192,640]{1,0:T(8,128)(2,1)S(1)} %pad.4), channel_id=3, replica_groups={{0,2,4,6},{1,3,5,7},{8,10,12,14},{9,11,13,15},{16,18,20,22},{17,19,21,2..., dimensions={0}, use_global_device_ids=true | all-gather | bytes 1228800 | tf_op jit(solution)/shard_map/all_gather | solution.py:328
  23.0 2.8 %collective-permute-start.1 = (bf16[4,192,640]{2,1,0:T(8,128)(2,1)S(1)}, bf16[4,192,640]{2,1,0:T(8,128)(2,1)S(1)}, u32[]{:S(2)}, u32[]{:S(2)}) collective-permute-start(bf16[4,192,640]{2,1,0:T(8,128)(2,1)S(1)} %bitcast.19), channel_id=1, source_target_pairs={{0,8},{1,9},{2,10},{3,11},{4,12},{5,13},{6,14},{7,15},{8,16},{9,17... | collective-permute-start | bytes 2949128 | tf_op jit(solution)/shard_map/ppermute | solution.py:329
  25.8 3.6 %collective-permute-start.2 = (bf16[4,192,640]{2,1,0:T(8,128)(2,1)S(1)}, bf16[4,192,640]{2,1,0:T(8,128)(2,1)}, u32[]{:S(2)}, u32[]{:S(2)}) collective-permute-start(bf16[4,192,640]{2,1,0:T(8,128)(2,1)S(1)} %bitcast.20), channel_id=1, source_target_pairs={{0,24},{1,25},{2,26},{3,27},{4,28},{5,29},{6,30},{7,31},{8,0},{9,1... | collective-permute-start | bytes 2949128 | tf_op jit(solution)/shard_map/ppermute | solution.py:330
  29.5 3.0 %collective-permute-start = (bf16[128,640]{1,0:T(8,128)(2,1)S(1)}, bf16[128,640]{1,0:T(8,128)(2,1)S(1)}, u32[]{:S(2)}, u32[]{:S(2)}) collective-permute-start(bf16[128,640]{1,0:T(8,128)(2,1)S(1)} %copy-done.1), channel_id=1, source_target_pairs={{2,0},{4,2},{6,4},{8,6},{10,8},{12,10},{14,12},{16,14},{18,16},{20... | collective-permute-start | bytes 491528 | tf_op jit(solution)/shard_map/ppermute | solution.py:331
  32.5 1.6 %shard_map.131 = f32[32,8,128]{2,1,0:T(8,128)} custom-call(bf16[128,640]{1,0:T(8,128)(2,1)S(1)} %copy-done.1), custom_call_target="tpu_custom_call" | custom-call | tf_op jit(solution)/shard_map/pallas_call | solution.py:291
  34.1 9.8 %all-to-all-start = ((f32[32,8,128]{2,1,0:T(8,128)}), f32[32,8,128]{2,1,0:T(8,128)}, u32[]{:S(2)}, u32[]{:S(2)}) async-start(f32[32,8,128]{2,1,0:T(8,128)} %shard_map.131), calls=%async_computation | async-start | bytes 262144 | tf_op jit(solution)/shard_map/all_to_all | solution.py:63
  44.0 16.2 %all-gather.2 = bf16[2560,128]{1,0:T(8,128)(2,1)} all-gather(bf16[640,128]{1,0:T(8,128)(2,1)S(1)} %bitcast.26), channel_id=4, replica_groups={{0,2,4,6},{1,3,5,7},{8,10,12,14},{9,11,13,15},{16,18,20,22},{17,19,21,2..., dimensions={0}, use_global_device_ids=true | all-gather | bytes 819200 | tf_op jit(solution)/shard_map/all_gather | solution.py:339
  60.2 0.8 slice.12
  61.0 3.2 %collective-permute-start.3 = (bf16[2,192,640]{2,1,0:T(8,128)(2,1)}, bf16[2,192,640]{2,1,0:T(8,128)(2,1)}, u32[]{:S(2)}, u32[]{:S(2)}) collective-permute-start(bf16[2,192,640]{2,1,0:T(8,128)(2,1)} %slice.12), channel_id=1, source_target_pairs={{0,8},{1,9},{2,10},{3,11},{4,12},{5,13},{6,14},{7,15},{8,16},{9,17... | collective-permute-start | bytes 1474568 | tf_op jit(solution)/shard_map/ppermute | solution.py:341
  64.3 1.9 %slice.13 = bf16[2,192,640]{2,1,0:T(8,128)(2,1)} slice(bf16[4,192,640]{2,1,0:T(8,128)(2,1)} %collective-permute-done.2.right_ref), slice={[2:4], [0:192], [0:640]} | slice | bytes 983040 | tf_op jit(solution)/shard_map/slice | solution.py:342
  66.1 3.4 %collective-permute-start.4 = (bf16[2,192,640]{2,1,0:T(8,128)(2,1)}, bf16[2,192,640]{2,1,0:T(8,128)(2,1)}, u32[]{:S(2)}, u32[]{:S(2)}) collective-permute-start(bf16[2,192,640]{2,1,0:T(8,128)(2,1)} %slice.13), channel_id=1, source_target_pairs={{0,24},{1,25},{2,26},{3,27},{4,28},{5,29},{6,30},{7,31},{8,0},{9,1... | collective-permute-start | bytes 1474568 | tf_op jit(solution)/shard_map/ppermute | solution.py:342
  69.6 5.3 %all-gather = bf16[4,128,640]{2,1,0:T(8,128)(2,1)S(1)} all-gather(bf16[2,128,640]{2,1,0:T(8,128)(2,1)S(1)} %pad_maximum_fusion), channel_id=2, replica_groups={{0,1},{2,3},{4,5},{6,7},{8,9},{10,11},{12,13},{14,15},{16,17},{18,19},{..., dimensions={0}, use_global_device_ids=true | all-gather | bytes 983040 | tf_op jit(solution)/shard_map/all_gather | solution.py:334
  74.9 1.9 %collective-permute-start.7 = (bf16[4,640,128]{2,1,0:T(8,128)(2,1)}, bf16[4,640,128]{2,1,0:T(8,128)(2,1)}, u32[]{:S(2)}, u32[]{:S(2)}) collective-permute-start(bf16[4,640,128]{2,1,0:T(8,128)(2,1)} %bitcast.10.own_ref), channel_id=1, source_target_pairs={{0,8},{1,9},{2,10},{3,11},{4,12},{5,13},{6,14},{7,15},{8,16},{9,17... | collective-permute-start | bytes 1966088 | tf_op jit(solution)/shard_map/ppermute | solution.py:355
  76.8 4.6 %collective-permute-start.9 = (bf16[4,640,128]{2,1,0:T(8,128)(2,1)}, bf16[4,640,128]{2,1,0:T(8,128)(2,1)}, u32[]{:S(2)}, u32[]{:S(2)}) collective-permute-start(bf16[4,640,128]{2,1,0:T(8,128)(2,1)} %bitcast.10.own_ref), channel_id=1, source_target_pairs={{0,24},{1,25},{2,26},{3,27},{4,28},{5,29},{6,30},{7,31},{8,0},{9,1... | collective-permute-start | bytes 1966088 | tf_op jit(solution)/shard_map/ppermute | solution.py:356
  82.1 3.0 %shard_map.132.blocks_ref = bf16[4,256,768]{2,1,0:T(8,128)(2,1)S(1)} custom-call(s32[4]{0:T(128)S(1)} %pad_add_fusion.where_ref, f32[32,8,128]{2,1,0:T(8,128)} %all-to-all-done.every_ref, bf16[2,2,128,640]{3,2,1,0:T(8,128)(2,1)S(1)} %bitcast.22, f32[1,640]{1,0:T(1,128)S(1)} %broadcast_in_dim.14.gain_ref, f32[1,640]{1,0:T(1,128)S(1)} %broadcast_in_dim.15.shift_ref), custom_call_target="tpu_custom_call" | custom-call | tf_op jit(solution)/shard_map/pallas_call | solution.py:291
  85.2 3.4 %shard_map.133 = (f32[128,640]{1,0:T(8,128)S(1)}, f32[128,640]{1,0:T(8,128)S(1)}) custom-call(s32[4]{0:T(128)S(1)} %pad_add_fusion.where_ref, bf16[4,256,768]{2,1,0:T(8,128)(2,1)S(1)} %shard_map.132.blocks_ref, bf16[4,192,640]{2,1,0:T(8,128)(2,1)S(1)} %bitcast.21, bf16[4,192,640]{2,1,0:T(8,128)(2,1)S(1)} %collective-permute-done.1.left_ref, ...), custom_call_target="tpu_custom_call" | custom-call | tf_op jit(solution)/shard_map/pallas_call | solution.py:291
  88.7 2.8 %collective-permute-start.5 = (f32[128,640]{1,0:T(8,128)S(1)}, f32[128,640]{1,0:T(8,128)S(1)}, u32[]{:S(2)}, u32[]{:S(2)}) collective-permute-start(f32[128,640]{1,0:T(8,128)S(1)} %get-tuple-element.21), channel_id=1, source_target_pairs={{0,1},{1,0},{2,3},{3,2},{4,5},{5,4},{6,7},{7,6},{8,9},{9,8},{10,11... | collective-permute-start | bytes 983048 | tf_op jit(solution)/shard_map/ppermute | solution.py:373
  92.7 1.7 %shard_map.134 = (bf16[128,640]{1,0:T(8,128)(2,1)S(1)}, f32[32,8,128]{2,1,0:T(8,128)}) custom-call(f32[128,640]{1,0:T(8,128)S(1)} %get-tuple-element.20.kept_ref, f32[128,640]{1,0:T(8,128)S(1)} %collective-permute-done.5.other_ref, bf16[128,640]{1,0:T(8,128)(2,1)S(1)} %copy-done.2, f32[1,640]{1,0:T(1,128)S(1)} %add.19.bias_ref), custom_call_target="tpu_custom_call" | custom-call | tf_op jit(solution)/shard_map/pallas_call | solution.py:291
  94.3 4.5 %all-to-all-start.1 = ((f32[32,8,128]{2,1,0:T(8,128)}), f32[32,8,128]{2,1,0:T(8,128)S(1)}, u32[]{:S(2)}, u32[]{:S(2)}) async-start(f32[32,8,128]{2,1,0:T(8,128)} %get-tuple-element.23), calls=%async_computation.1 | async-start | bytes 262144 | tf_op jit(solution)/shard_map/all_to_all | solution.py:63
  98.8 1.7 %slice.17 = bf16[2,640,128]{2,1,0:T(8,128)(2,1)} slice(bf16[4,640,128]{2,1,0:T(8,128)(2,1)} %collective-permute-done.9.right_ref), slice={[2:4], [0:640], [0:128]} | slice | bytes 655360 | tf_op jit(solution)/shard_map/slice | solution.py:377
  100.6 4.5 %collective-permute-start.10 = (bf16[2,640,128]{2,1,0:T(8,128)(2,1)}, bf16[2,640,128]{2,1,0:T(8,128)(2,1)S(1)}, u32[]{:S(2)}, u32[]{:S(2)}) collective-permute-start(bf16[2,640,128]{2,1,0:T(8,128)(2,1)} %slice.17), channel_id=1, source_target_pairs={{0,24},{1,25},{2,26},{3,27},{4,28},{5,29},{6,30},{7,31},{8,0},{9,1... | collective-permute-start | bytes 983048 | tf_op jit(solution)/shard_map/ppermute | solution.py:377
  105.1 1.7 %slice.16 = bf16[2,640,128]{2,1,0:T(8,128)(2,1)} slice(bf16[4,640,128]{2,1,0:T(8,128)(2,1)} %collective-permute-done.7.left_ref), slice={[0:2], [0:640], [0:128]} | slice | bytes 655360 | tf_op jit(solution)/shard_map/slice | solution.py:376
  106.8 1.9 %collective-permute-start.8 = (bf16[2,640,128]{2,1,0:T(8,128)(2,1)}, bf16[2,640,128]{2,1,0:T(8,128)(2,1)S(1)}, u32[]{:S(2)}, u32[]{:S(2)}) collective-permute-start(bf16[2,640,128]{2,1,0:T(8,128)(2,1)} %slice.16), channel_id=1, source_target_pairs={{0,8},{1,9},{2,10},{3,11},{4,12},{5,13},{6,14},{7,15},{8,16},{9,17... | collective-permute-start | bytes 983048 | tf_op jit(solution)/shard_map/ppermute | solution.py:376
  108.7 2.7 %collective-permute-start.6 = (bf16[128,640]{1,0:T(8,128)(2,1)S(1)}, bf16[128,640]{1,0:T(8,128)(2,1)S(1)}, u32[]{:S(2)}, u32[]{:S(2)}) collective-permute-start(bf16[128,640]{1,0:T(8,128)(2,1)S(1)} %get-tuple-element.24.mid_ref), channel_id=1, source_target_pairs={{0,1},{1,0},{2,3},{3,2},{4,5},{5,4},{6,7},{7,6},{8,9},{9,8},{10,11... | collective-permute-start | bytes 491528 | tf_op jit(solution)/shard_map/ppermute | solution.py:384
  111.5 0.8 collective-permute-done.6.other_ref
  112.3 1.7 %shard_map.135 = (bf16[256,384]{1,0:T(8,128)(2,1)S(1)}, bf16[640,128]{1,0:T(8,128)(2,1)S(1)}, bf16[640,128]{1,0:T(8,128)(2,1)}) custom-call(f32[32,8,128]{2,1,0:T(8,128)S(1)} %all-to-all-done.1.every_ref, bf16[128,640]{1,0:T(8,128)(2,1)S(1)} %get-tuple-element.24.mid_ref, bf16[128,640]{1,0:T(8,128)(2,1)S(1)} %collective-permute-done.6.other_ref, ...), custom_call_target="tpu_custom_call" | custom-call | tf_op jit(solution)/shard_map/pallas_call | solution.py:291
  114.0 5.3 %shard_map.136.near_ref = f32[256,384]{1,0:T(8,128)S(1)} custom-call(s32[4]{0:T(128)S(1)} %pad_add_fusion.where_ref, bf16[256,384]{1,0:T(8,128)(2,1)S(1)} %get-tuple-element.25.q_ref, bf16[4,640,128]{2,1,0:T(8,128)(2,1)} %bitcast.10.own_ref, bf16[4,640,128]{2,1,0:T(8,128)(2,1)} %collective-permute-done.7.left_ref, ...), custom_call_target="tpu_custom_call" | custom-call | flops 1000000000 | bytes 3000000 | tf_op jit(solution)/shard_map/pallas_call | solution.py:291
  119.4 2.4 %shard_map.137 = (f32[128,384]{1,0:T(8,128)S(1)}, f32[128,384]{1,0:T(8,128)S(1)}) custom-call(bf16[256,384]{1,0:T(8,128)(2,1)S(1)} %get-tuple-element.25.q_ref, bf16[2,640,128]{2,1,0:T(8,128)(2,1)S(1)} %collective-permute-done.8.low_ref, bf16[2,640,128]{2,1,0:T(8,128)(2,1)S(1)} %collective-permute-done.10.high_ref, f32[256,384]{1,0:T(8,128)S(1)} %shard_map.136.near_ref), custom_call_target="tpu_custom_call" | custom-call | tf_op jit(solution)/shard_map/pallas_call | solution.py:291
  121.7 2.8 %collective-permute-start.11 = (f32[128,384]{1,0:T(8,128)S(1)}, f32[128,384]{1,0:T(8,128)S(1)}, u32[]{:S(2)}, u32[]{:S(2)}) collective-permute-start(f32[128,384]{1,0:T(8,128)S(1)} %get-tuple-element.30), channel_id=1, source_target_pairs={{0,1},{1,0},{2,3},{3,2},{4,5},{5,4},{6,7},{7,6},{8,9},{9,8},{10,11... | collective-permute-start | bytes 589832 | tf_op jit(solution)/shard_map/ppermute | solution.py:405
  124.5 1.0 collective-permute-done.11.other_ref
  125.6 1.3 %shard_map.138 = bf16[128,640]{1,0:T(8,128)(2,1)} custom-call(f32[128,384]{1,0:T(8,128)S(1)} %get-tuple-element.29.own_ref, f32[128,384]{1,0:T(8,128)S(1)} %collective-permute-done.11.other_ref, bf16[128,640]{1,0:T(8,128)(2,1)S(1)} %get-tuple-element.24.mid_ref, bf16[320,640]{1,0:T(8,128)(2,1)S(1)} %copy-done.4), custom_call_target="tpu_custom_call" | custom-call | tf_op jit(solution)/shard_map/pallas_call | solution.py:291
  (46 shorter events, 1.4 us)
Async XLA Ops:
  0.6 90.9 %copy-start = (f32[320,640]{1,0:T(8,128)S(1)}, f32[320,640]{1,0:T(8,128)}, u32[]{:S(2)}) copy-start(f32[320,640]{1,0:T(8,128)} %param.18) | copy-start | bytes 2457604
  0.6 28.8 %copy-start.1 = (bf16[128,640]{1,0:T(8,128)(2,1)S(1)}, bf16[128,640]{1,0:T(8,128)(2,1)}, u32[]{:S(2)}) copy-start(bf16[128,640]{1,0:T(8,128)(2,1)} %latent_ref.3) | copy-start | bytes 491524
  0.7 43.3 %copy-start.5 = (bf16[2,128,320]{1,2,0:T(8,128)(2,1)S(1)}, bf16[2,128,320]{1,2,0:T(8,128)(2,1)}, u32[]{:S(2)}) copy-start(bf16[2,128,320]{1,2,0:T(8,128)(2,1)} %param.23) | copy-start | bytes 491524
  23.0 37.2 %collective-permute-start.1 = (bf16[4,192,640]{2,1,0:T(8,128)(2,1)S(1)}, bf16[4,192,640]{2,1,0:T(8,128)(2,1)S(1)}, u32[]{:S(2)}, u32[]{:S(2)}) collective-permute-start(bf16[4,192,640]{2,1,0:T(8,128)(2,1)S(1)} %bitcast.19), channel_id=1, source_target_pairs={{0,8},{1,9},{2,10},{3,11},{4,12},{5,13},{6,14},{7,15},{8,16},{9,17... | collective-permute-start | bytes 2949128 | tf_op jit(solution)/shard_map/ppermute | solution.py:329
  25.8 34.4 %collective-permute-start.2 = (bf16[4,192,640]{2,1,0:T(8,128)(2,1)S(1)}, bf16[4,192,640]{2,1,0:T(8,128)(2,1)}, u32[]{:S(2)}, u32[]{:S(2)}) collective-permute-start(bf16[4,192,640]{2,1,0:T(8,128)(2,1)S(1)} %bitcast.20), channel_id=1, source_target_pairs={{0,24},{1,25},{2,26},{3,27},{4,28},{5,29},{6,30},{7,31},{8,0},{9,1... | collective-permute-start | bytes 2949128 | tf_op jit(solution)/shard_map/ppermute | solution.py:330
  29.5 40.1 %collective-permute-start = (bf16[128,640]{1,0:T(8,128)(2,1)S(1)}, bf16[128,640]{1,0:T(8,128)(2,1)S(1)}, u32[]{:S(2)}, u32[]{:S(2)}) collective-permute-start(bf16[128,640]{1,0:T(8,128)(2,1)S(1)} %copy-done.1), channel_id=1, source_target_pairs={{2,0},{4,2},{6,4},{8,6},{10,8},{12,10},{14,12},{16,14},{18,16},{20... | collective-permute-start | bytes 491528 | tf_op jit(solution)/shard_map/ppermute | solution.py:331
  34.1 48.0 %all-to-all-start = ((f32[32,8,128]{2,1,0:T(8,128)}), f32[32,8,128]{2,1,0:T(8,128)}, u32[]{:S(2)}, u32[]{:S(2)}) async-start(f32[32,8,128]{2,1,0:T(8,128)} %shard_map.131), calls=%async_computation | async-start | bytes 262144 | tf_op jit(solution)/shard_map/all_to_all | solution.py:63
  61.0 20.4 %copy-start.7 = (f32[640]{0:T(1024)S(1)}, f32[640]{0:T(1024)}, u32[]{:S(2)}) copy-start(f32[640]{0:T(1024)} %param.14) | copy-start | bytes 7684
  61.0 20.4 %copy-start.8 = (f32[640]{0:T(1024)S(1)}, f32[640]{0:T(1024)}, u32[]{:S(2)}) copy-start(f32[640]{0:T(1024)} %param.15) | copy-start | bytes 7684
  61.0 24.2 %collective-permute-start.3 = (bf16[2,192,640]{2,1,0:T(8,128)(2,1)}, bf16[2,192,640]{2,1,0:T(8,128)(2,1)}, u32[]{:S(2)}, u32[]{:S(2)}) collective-permute-start(bf16[2,192,640]{2,1,0:T(8,128)(2,1)} %slice.12), channel_id=1, source_target_pairs={{0,8},{1,9},{2,10},{3,11},{4,12},{5,13},{6,14},{7,15},{8,16},{9,17... | collective-permute-start | bytes 1474568 | tf_op jit(solution)/shard_map/ppermute | solution.py:341
  66.1 19.1 %collective-permute-start.4 = (bf16[2,192,640]{2,1,0:T(8,128)(2,1)}, bf16[2,192,640]{2,1,0:T(8,128)(2,1)}, u32[]{:S(2)}, u32[]{:S(2)}) collective-permute-start(bf16[2,192,640]{2,1,0:T(8,128)(2,1)} %slice.13), channel_id=1, source_target_pairs={{0,24},{1,25},{2,26},{3,27},{4,28},{5,29},{6,30},{7,31},{8,0},{9,1... | collective-permute-start | bytes 1474568 | tf_op jit(solution)/shard_map/ppermute | solution.py:342
  74.9 30.2 %collective-permute-start.7 = (bf16[4,640,128]{2,1,0:T(8,128)(2,1)}, bf16[4,640,128]{2,1,0:T(8,128)(2,1)}, u32[]{:S(2)}, u32[]{:S(2)}) collective-permute-start(bf16[4,640,128]{2,1,0:T(8,128)(2,1)} %bitcast.10.own_ref), channel_id=1, source_target_pairs={{0,8},{1,9},{2,10},{3,11},{4,12},{5,13},{6,14},{7,15},{8,16},{9,17... | collective-permute-start | bytes 1966088 | tf_op jit(solution)/shard_map/ppermute | solution.py:355
  76.8 22.1 %collective-permute-start.9 = (bf16[4,640,128]{2,1,0:T(8,128)(2,1)}, bf16[4,640,128]{2,1,0:T(8,128)(2,1)}, u32[]{:S(2)}, u32[]{:S(2)}) collective-permute-start(bf16[4,640,128]{2,1,0:T(8,128)(2,1)} %bitcast.10.own_ref), channel_id=1, source_target_pairs={{0,24},{1,25},{2,26},{3,27},{4,28},{5,29},{6,30},{7,31},{8,0},{9,1... | collective-permute-start | bytes 1966088 | tf_op jit(solution)/shard_map/ppermute | solution.py:356
  85.2 7.0 %copy-start.6 = (f32[640]{0:T(1024)S(1)}, f32[640]{0:T(1024)}, u32[]{:S(2)}) copy-start(f32[640]{0:T(1024)} %param.17) | copy-start | bytes 7684
  85.2 7.5 %copy-start.2 = (bf16[128,640]{1,0:T(8,128)(2,1)S(1)}, bf16[128,640]{1,0:T(8,128)(2,1)}, u32[]{:S(2)}) copy-start(bf16[128,640]{1,0:T(8,128)(2,1)} %latent_ref.3) | copy-start | bytes 491524
  88.7 4.0 %collective-permute-start.5 = (f32[128,640]{1,0:T(8,128)S(1)}, f32[128,640]{1,0:T(8,128)S(1)}, u32[]{:S(2)}, u32[]{:S(2)}) collective-permute-start(f32[128,640]{1,0:T(8,128)S(1)} %get-tuple-element.21), channel_id=1, source_target_pairs={{0,1},{1,0},{2,3},{3,2},{4,5},{5,4},{6,7},{7,6},{8,9},{9,8},{10,11... | collective-permute-start | bytes 983048 | tf_op jit(solution)/shard_map/ppermute | solution.py:373
  91.6 19.9 %copy-start.9 = (f32[640]{0:T(1024)S(1)}, f32[640]{0:T(1024)}, u32[]{:S(2)}) copy-start(f32[640]{0:T(1024)} %param.19) | copy-start | bytes 7684
  91.6 19.9 %copy-start.10 = (f32[640]{0:T(1024)S(1)}, f32[640]{0:T(1024)}, u32[]{:S(2)}) copy-start(f32[640]{0:T(1024)} %param.20) | copy-start | bytes 7684
  91.6 20.7 %copy-start.3 = (bf16[640,960]{0,1:T(8,128)(2,1)S(1)}, bf16[640,960]{0,1:T(8,128)(2,1)}, u32[]{:S(2)}) copy-start(bf16[640,960]{0,1:T(8,128)(2,1)} %param.21) | copy-start | bytes 3686404
  94.3 18.0 %all-to-all-start.1 = ((f32[32,8,128]{2,1,0:T(8,128)}), f32[32,8,128]{2,1,0:T(8,128)S(1)}, u32[]{:S(2)}, u32[]{:S(2)}) async-start(f32[32,8,128]{2,1,0:T(8,128)} %get-tuple-element.23), calls=%async_computation.1 | async-start | bytes 262144 | tf_op jit(solution)/shard_map/all_to_all | solution.py:63
  100.6 18.8 %collective-permute-start.10 = (bf16[2,640,128]{2,1,0:T(8,128)(2,1)}, bf16[2,640,128]{2,1,0:T(8,128)(2,1)S(1)}, u32[]{:S(2)}, u32[]{:S(2)}) collective-permute-start(bf16[2,640,128]{2,1,0:T(8,128)(2,1)} %slice.17), channel_id=1, source_target_pairs={{0,24},{1,25},{2,26},{3,27},{4,28},{5,29},{6,30},{7,31},{8,0},{9,1... | collective-permute-start | bytes 983048 | tf_op jit(solution)/shard_map/ppermute | solution.py:377
  106.8 12.5 %collective-permute-start.8 = (bf16[2,640,128]{2,1,0:T(8,128)(2,1)}, bf16[2,640,128]{2,1,0:T(8,128)(2,1)S(1)}, u32[]{:S(2)}, u32[]{:S(2)}) collective-permute-start(bf16[2,640,128]{2,1,0:T(8,128)(2,1)} %slice.16), channel_id=1, source_target_pairs={{0,8},{1,9},{2,10},{3,11},{4,12},{5,13},{6,14},{7,15},{8,16},{9,17... | collective-permute-start | bytes 983048 | tf_op jit(solution)/shard_map/ppermute | solution.py:376
  108.7 3.6 %collective-permute-start.6 = (bf16[128,640]{1,0:T(8,128)(2,1)S(1)}, bf16[128,640]{1,0:T(8,128)(2,1)S(1)}, u32[]{:S(2)}, u32[]{:S(2)}) collective-permute-start(bf16[128,640]{1,0:T(8,128)(2,1)S(1)} %get-tuple-element.24.mid_ref), channel_id=1, source_target_pairs={{0,1},{1,0},{2,3},{3,2},{4,5},{5,4},{6,7},{7,6},{8,9},{9,8},{10,11... | collective-permute-start | bytes 491528 | tf_op jit(solution)/shard_map/ppermute | solution.py:384
  114.0 11.6 %copy-start.4 = (bf16[320,640]{1,0:T(8,128)(2,1)S(1)}, bf16[320,640]{1,0:T(8,128)(2,1)}, u32[]{:S(2)}) copy-start(bf16[320,640]{1,0:T(8,128)(2,1)} %weight_ref.1) | copy-start | bytes 1228804
  121.7 3.9 %collective-permute-start.11 = (f32[128,384]{1,0:T(8,128)S(1)}, f32[128,384]{1,0:T(8,128)S(1)}, u32[]{:S(2)}, u32[]{:S(2)}) collective-permute-start(f32[128,384]{1,0:T(8,128)S(1)} %get-tuple-element.30), channel_id=1, source_target_pairs={{0,1},{1,0},{2,3},{3,2},{4,5},{5,4},{6,7},{7,6},{8,9},{9,8},{10,11... | collective-permute-start | bytes 589832 | tf_op jit(solution)/shard_map/ppermute | solution.py:405
